TPU v7x, 32 devices: a whole 2x2x4 slice. The times are simulated.
32 devices in a mesh: row: 4 (over y, x), col: 8 (over z, core).
Axes of the slice: x: 2, y: 2, z: 4, core: 2. Of those that a mesh axis runs over, the one named last changes fastest.
Arguments:
- g0_values: bfloat16 [4096, 4096], P('row', 'col'), may hold values from -6 to 6
- g0_pattern: int32 [32, 32], P('row', 'col'), may hold values 0 or 1
- sigma_values: bfloat16 [4, 96, 128, 128], P('row', 'col'), may hold values from -0.0029296875 to 0.0029296875
- sigma_pairs: int32 [4, 96, 2], P('row', 'col'), may hold values from 0 to 31, as said below
- sigma_count: int32 [4, 8], P('row', 'col'), may hold values from 1 to 12, as said below
Outputs:
- g_full: bfloat16 [4096, 4096], P('row', 'col')
Inputs may be any that keep to these rules, and one draw needn't show every extreme that they name: `sigma_pairs`: slot pairs of the device at position (g, o) name blocks with block row in g * 8 to g * 8 + 7 and block column in o * 4 to o * 4 + 3; the pairs of one device are distinct. `sigma_count`: count of live slots, which are the first ones of a device.
All inputs are finite; a program needn't handle non-finite values. No bound on the sum of `g0_pattern` on one device may be relied on, other than what follows from the above.
Results may differ from a plain program's by a relative error of at most 0.0037.
Values may be sent and summed in bfloat16 or wider, within the bound.
No kernel may reach another device: no remote copies, remote signals or barrier semaphores. Data moves between devices by JAX's collectives and lax.ppermute only.
A program may use at most 128 MiB of HBM per device.

v0:
```python
import jax
import jax.numpy as jnp
from jax import lax
from jax.sharding import PartitionSpec as P


def per_device(g0_values, g0_pattern, sigma_values, sigma_pairs, sigma_count):
    block_rows = g0_pattern.shape[0]
    block_cols = g0_pattern.shape[1]
    width = sigma_values.shape[-1]
    slot_total = sigma_values.shape[1]
    mask = jnp.repeat(jnp.repeat(g0_pattern, width, axis=0), width, axis=1)
    g0_tile = g0_values * mask.astype(jnp.bfloat16)
    panel = lax.all_gather(g0_tile, "col", axis=1, tiled=True)
    live = jnp.arange(slot_total, dtype=jnp.int32) < sigma_count[0, 0]
    local_k = jnp.where(live, sigma_pairs[0, :, 0] % block_rows, block_rows)
    local_j = sigma_pairs[0, :, 1] % block_cols
    dense = jnp.zeros((block_rows, width, block_cols, width), jnp.bfloat16)
    dense = dense.at[local_k, :, local_j, :].add(sigma_values[0], mode="drop")
    sigma_tile = dense.reshape(block_rows * width, block_cols * width)
    columns = panel
    left_sum = jnp.dot(
        columns,
        lax.all_gather(sigma_tile, "row", axis=0, tiled=True),
        preferred_element_type=jnp.float32,
    )
    left_tile = left_sum.astype(jnp.bfloat16)
    start_value = g0_tile.astype(jnp.float32)
    left_panel = lax.all_gather(left_tile, "col", axis=1, tiled=True)
    columns = left_panel
    result = start_value + jnp.dot(
        columns,
        lax.all_gather(g0_tile, "row", axis=0, tiled=True),
        preferred_element_type=jnp.float32,
    )
    return result.astype(jnp.bfloat16)


def solution(mesh):
    placed = (
        P("row", "col"),
        P("row", "col"),
        P("row", "col", None, None),
        P("row", "col", None),
        P("row", "col"),
    )
    return jax.shard_map(
        per_device, mesh=mesh, in_specs=placed, out_specs=P("row", "col"), check_vma=False
    )
```

profile of v0, /device:TPU:0, one launch (start us, length us, event | category | flops | bytes accessed | tf_op | source)
XLA Modules:
  0.0 305.4 jit_solution(4870501645290470444)
XLA Ops:
  7.2 0.8 fusion.3
  8.0 0.2 broadcast_in_dim.15
  8.2 0.0 copy-start.1
  8.2 2.7 scatter_fusion
  10.9 0.7 copy.8
  11.6 1.3 copy.13
  12.9 0.0 all-gather.7.cloned.1.call-update
  12.9 0.0 all-gather.5.cloned.1.call-start
  13.0 0.1 copy.7
  13.1 2.9 broadcast_in_dim.14
  16.1 0.0 copy-done.1
  16.1 1.2 bitcast_multiply_fusion
  17.2 0.0 all-gather.5.cloned.1.call-update
  17.3 0.0 all-gather.11.cloned.1.call-start
  17.3 0.7 all-gather.11.cloned.1.call-update
  18.0 0.0 copy-start
  18.0 0.0 all-gather.9.cloned.1.call-start
  18.1 50.4 %all-gather.7.cloned.1.call-done = bf16[4096,512]{0,1:T(8,128)(2,1)} async-done(((bf16[1024,512]{0,1:T(8,128)(2,1)}), bf16[4096,512]{0,1:T(8,128)(2,1)}) %all-gather.7.cloned.1.call-update) | async-done | bytes 4194320 | tf_op jit(solution)/shard_map/all_gather | solution.py:24
  68.5 83.7 %all-gather.5.cloned.1.call-done = bf16[1024,4096]{1,0:T(8,128)(2,1)} async-done(((bf16[1024,512]{1,0:T(8,128)(2,1)}), bf16[1024,4096]{1,0:T(8,128)(2,1)}) %all-gather.5.cloned.1.call-update) | async-done | bytes 8388624 | tf_op jit(solution)/shard_map/all_gather | solution.py:14
  152.2 10.1 %convolution_convert_fusion = bf16[1024,512]{1,0:T(8,128)(2,1)} fusion(bf16[1024,4096]{1,0:T(8,128)(2,1)} %all-gather.5.cloned.1.call-done, bf16[4096,512]{0,1:T(8,128)(2,1)} %all-gather.7.cloned.1.call-done), kind=kOutput, calls=%fused_computation.2 | convolution fusion | flops 4295491584 | bytes 13631488 | tf_op jit(solution)/shard_map/dot_general | solution.py:22
  162.2 0.0 all-gather.9.cloned.1.call-update
  162.3 43.0 %all-gather.11.cloned.1.call-done = bf16[4096,512]{1,0:T(8,128)(2,1)} async-done(((bf16[1024,512]{1,0:T(8,128)(2,1)}), bf16[4096,512]{1,0:T(8,128)(2,1)}) %all-gather.11.cloned.1.call-update) | async-done | bytes 4194320 | tf_op jit(solution)/shard_map/all_gather | solution.py:33
  205.3 83.6 %all-gather.9.cloned.1.call-done = bf16[1024,4096]{1,0:T(8,128)(2,1)} async-done(((bf16[1024,512]{1,0:T(8,128)(2,1)}), bf16[1024,4096]{1,0:T(8,128)(2,1)}) %all-gather.9.cloned.1.call-update) | async-done | bytes 8388624 | tf_op jit(solution)/shard_map/all_gather | solution.py:29
  288.8 10.0 %add_convert_fusion = bf16[1024,512]{1,0:T(8,128)(2,1)} fusion(bf16[1024,512]{1,0:T(8,128)(2,1)S(1)} %copy-done, bf16[1024,4096]{1,0:T(8,128)(2,1)} %all-gather.9.cloned.1.call-done, bf16[4096,512]{1,0:T(8,128)(2,1)} %all-gather.11.cloned.1.call-done), kind=kOutput, calls=%fused_computation.1 | convolution fusion | flops 4296540160 | bytes 14680064 | tf_op jit(solution)/shard_map/dot_general | solution.py:31
  (6 shorter events, 0.1 us)
Async XLA Ops:
  6.5 6.4 %copy-start.2 = (s32[8,4]{0,1:T(4,128)S(1)}, s32[8,4]{0,1:T(4,128)}, u32[]{:S(2)}) copy-start(s32[8,4]{0,1:T(4,128)} %param.6) | copy-start | bytes 388
  6.5 61.9 %all-gather.7.cloned.1.call-start = ((), (), s32[]{:S(2)}) async-start(), calls=%async_computation.1 | async-start | bytes 5242880 | tf_op jit(solution)/shard_map/all_gather | solution.py:24
  8.2 7.9 %copy-start.1 = (bf16[1024,512]{1,0:T(8,128)(2,1)S(1)}, bf16[1024,512]{1,0:T(8,128)(2,1)}, u32[]{:S(2)}) copy-start(bf16[1024,512]{1,0:T(8,128)(2,1)} %param.5) | copy-start | bytes 3145732
  12.9 139.2 %all-gather.5.cloned.1.call-start = ((), (), s32[]{:S(2)}) async-start(), calls=%async_computation | async-start | bytes 9437184 | tf_op jit(solution)/shard_map/all_gather | solution.py:14
  17.3 188.0 %all-gather.11.cloned.1.call-start = ((), (), s32[]{:S(2)}) async-start(), calls=%async_computation.3 | async-start | bytes 5242880 | tf_op jit(solution)/shard_map/all_gather | solution.py:33
  18.0 270.8 %copy-start = (bf16[1024,512]{1,0:T(8,128)(2,1)S(1)}, bf16[1024,512]{1,0:T(8,128)(2,1)}, u32[]{:S(2)}) copy-start(bf16[1024,512]{1,0:T(8,128)(2,1)} %bitcast_multiply_fusion) | copy-start | bytes 3145732
  18.0 270.8 %all-gather.9.cloned.1.call-start = ((), (), s32[]{:S(2)}) async-start(), calls=%async_computation.2 | async-start | bytes 9437184 | tf_op jit(solution)/shard_map/all_gather | solution.py:29
Sparse Core Ops, SparseCore 0:
  13.0 55.3 all-gather.6
  70.1 82.0 all-gather.4
  154.0 51.2 all-gather.10
  206.7 82.0 all-gather.8
where the time goes:
time: 306 us; the launch traced here: 305 us
  waiting for transfers between devices  261 us (85%)
  matrix products  20.1 us (7%)
  between operations  13.9 us (5%)
  local copies, waits for them, and re-layouts  5.3 us (2%)
  other arithmetic  4.6 us (2%)
    all_gather x1, waiting for transfers between devices, per_device(): panel = lax.all_gather(g0_tile, 'col', axis=1, tiled=True)  83.7 us
    all_gather x1, waiting for transfers between devices, per_device(): left_panel = lax.all_gather(left_tile, 'col', axis=1, tiled=True)  83.6 us
    all_gather x1, waiting for transfers between devices, per_device(): lax.all_gather(sigma_tile, 'row', axis=0, tiled=True)  50.4 us
    all_gather x1, waiting for transfers between devices, per_device(): lax.all_gather(g0_tile, 'row', axis=0, tiled=True)  43 us
    dot_general x1, matrix products, per_device(): jnp.dot(columns, lax.all_gather(sigma_tile, 'row', axis=0, tiled=True), p...  10.1 us
    dot_general x1, matrix products, per_device(): jnp.dot(columns, lax.all_gather(g0_tile, 'row', axis=0, tiled=True), pref...  10 us
  transfers between devices with their start and end apart: 4, of which 4 were waited for; matrix products, arithmetic and copies ran while one was open for 5% of the time, Pallas kernels for 0%

commit v1 on v0

v1 whole, which is shorter than its diff:
```python
import functools
import math

import jax
import jax.numpy as jnp
from jax import lax
from jax.experimental import pallas as pl
from jax.experimental.pallas import tpu as pltpu
from jax.sharding import PartitionSpec as P

VMEM_BYTES = 48 * 1024 * 1024
ANY = pl.BlockSpec(memory_space=pl.ANY)
SMEM = pl.BlockSpec(memory_space=pltpu.SMEM)
VMEM = pl.BlockSpec(memory_space=pltpu.VMEM)


def mask_kernel(width, pattern_ref, values_ref, upper_ref, lower_ref):
    block_rows, block_cols = pattern_ref.shape
    half = block_rows // 2
    for a in range(block_rows):
        target = upper_ref if a < half else lower_ref
        for b in range(block_cols):
            block = values_ref[pl.ds(a * width, width), pl.ds(b * width, width)]
            keep = pattern_ref[a, b].astype(jnp.float32).astype(jnp.bfloat16)
            target[pl.ds((a % half) * width, width), pl.ds(b * width, width)] = block * keep


def masked_halves(g0_values, g0_pattern):
    rows, cols = g0_values.shape
    half = jax.ShapeDtypeStruct((rows // 2, cols), jnp.bfloat16)
    return pl.pallas_call(
        functools.partial(mask_kernel, rows // g0_pattern.shape[0]),
        out_shape=(half, half),
        in_specs=[SMEM, VMEM],
        out_specs=(VMEM, VMEM),
        compiler_params=pltpu.CompilerParams(vmem_limit_bytes=VMEM_BYTES),
        cost_estimate=pl.CostEstimate(flops=rows * cols, bytes_accessed=4 * rows * cols, transcendentals=0),
        name="mask",
    )(g0_pattern, g0_values)


def turn_kernel(n_slot, n_col, sizes, owner_ref, place_ref, source_ref, *refs):
    rows, cols, width, block_cols, slots = sizes
    slot_refs, col_refs = refs[:n_slot], refs[n_slot:n_slot + n_col]
    upper_ref, lower_ref, sigma, column, slot_sem, col_sem = refs[n_slot + n_col:]
    half = rows // 2

    def column_copy(i):
        start = pl.multiple_of(source_ref[i // 2] * rows + (i % 2) * half, half)
        return pltpu.make_async_copy(col_refs[i], column.at[pl.ds(start, half)], col_sem.at[i])

    def slot_copy(i, s):
        place = place_ref[i, s]
        row = pl.multiple_of((place // block_cols) * width, width)
        col = pl.multiple_of(owner_ref[i] * cols + (place % block_cols) * width, width)
        return pltpu.make_async_copy(
            slot_refs[i].at[s], sigma.at[pl.ds(row, width), pl.ds(col, width)], slot_sem.at[i, s]
        )

    for i in range(n_col):
        column_copy(i).start()
    sigma[...] = jnp.zeros_like(sigma)
    for step in ("start", "wait"):
        for i in range(n_slot):
            @pl.loop(0, slots)
            def _(s):
                @pl.when(place_ref[i, s] >= 0)
                def _():
                    getattr(slot_copy(i, s), step)()
    for i in range(n_col):
        column_copy(i).wait()
    tile = min(256, half)
    for part, out_ref in enumerate((upper_ref, lower_ref)):
        @pl.loop(0, half // tile)
        def _(t):
            at = pl.multiple_of(t * tile, tile)
            out_ref[pl.ds(at, tile), :] = jnp.dot(
                sigma[pl.ds(part * half + at, tile), :], column[...], preferred_element_type=jnp.float32
            ).astype(jnp.bfloat16)


def turn(owners, places, sources, slot_parts, col_parts, rows, cols, block_cols, depth):
    slots, width = slot_parts[0].shape[0], slot_parts[0].shape[1]
    half = jax.ShapeDtypeStruct((rows // 2, cols), jnp.bfloat16)
    n_slot, n_col = len(slot_parts), len(col_parts)
    return pl.pallas_call(
        functools.partial(turn_kernel, n_slot, n_col, (rows, cols, width, block_cols, slots)),
        out_shape=(half, half),
        in_specs=[SMEM, SMEM, SMEM] + [ANY] * (n_slot + n_col),
        out_specs=(VMEM, VMEM),
        scratch_shapes=[
            pltpu.VMEM((rows, depth), jnp.bfloat16),
            pltpu.VMEM((depth, cols), jnp.bfloat16),
            pltpu.SemaphoreType.DMA((n_slot, slots)),
            pltpu.SemaphoreType.DMA((n_col,)),
        ],
        compiler_params=pltpu.CompilerParams(vmem_limit_bytes=VMEM_BYTES),
        cost_estimate=pl.CostEstimate(
            flops=2 * rows * cols * depth, bytes_accessed=2 * depth * cols + 4 * rows * cols, transcendentals=0
        ),
        name="turn",
    )(owners, places, sources, *slot_parts, *col_parts)


def close_kernel(n_row, n_col, sizes, owner_ref, source_ref, *refs):
    rows, cols = sizes
    row_refs, col_refs = refs[:n_row], refs[n_row:n_row + n_col]
    out_ref, panel, column, row_sem, col_sem = refs[n_row + n_col:]
    half = rows // 2

    def column_copy(i):
        start = pl.multiple_of(source_ref[i // 2] * rows + (i % 2) * half, half)
        return pltpu.make_async_copy(col_refs[i], column.at[pl.ds(start, half)], col_sem.at[i])

    def row_copy(i):
        start = pl.multiple_of(owner_ref[i // 2] * cols, cols)
        return pltpu.make_async_copy(
            row_refs[i], panel.at[pl.ds((i % 2) * half, half), pl.ds(start, cols)], row_sem.at[i]
        )

    def each_row(part, step):
        for i in range(part, n_row, 2):
            @pl.when(owner_ref[i // 2] >= 0)
            def _():
                getattr(row_copy(i), step)()

    for i in range(n_col):
        column_copy(i).start()
    each_row(0, "start")
    each_row(1, "start")
    for i in range(n_col):
        column_copy(i).wait()
    tile = min(256, half)
    own = pl.multiple_of(owner_ref[0] * cols, cols)
    for part in range(2):
        each_row(part, "wait")

        @pl.loop(0, half // tile)
        def _(t):
            at = pl.multiple_of(part * half + t * tile, tile)
            total = jnp.dot(panel[pl.ds(at, tile), :], column[...], preferred_element_type=jnp.float32)
            start_value = panel[pl.ds(at, tile), pl.ds(own, cols)].astype(jnp.float32)
            out_ref[pl.ds(at, tile), :] = (start_value + total).astype(jnp.bfloat16)


def close(owners, sources, row_parts, col_parts, rows, cols, depth):
    n_row, n_col = len(row_parts), len(col_parts)
    return pl.pallas_call(
        functools.partial(close_kernel, n_row, n_col, (rows, cols)),
        out_shape=jax.ShapeDtypeStruct((rows, cols), jnp.bfloat16),
        in_specs=[SMEM, SMEM] + [ANY] * (n_row + n_col),
        out_specs=VMEM,
        scratch_shapes=[
            pltpu.VMEM((rows, depth), jnp.bfloat16),
            pltpu.VMEM((depth, cols), jnp.bfloat16),
            pltpu.SemaphoreType.DMA((n_row,)),
            pltpu.SemaphoreType.DMA((n_col,)),
        ],
        compiler_params=pltpu.CompilerParams(vmem_limit_bytes=VMEM_BYTES),
        cost_estimate=pl.CostEstimate(
            flops=2 * rows * cols * depth, bytes_accessed=2 * depth * (rows + cols) + 2 * rows * cols, transcendentals=0
        ),
        name="close",
    )(owners, sources, *row_parts, *col_parts)


class Grid:
    def __init__(self, n_row, n_col):
        side = math.isqrt(n_row)
        self.nx = side if side * side == n_row else n_row
        self.ny = n_row // self.nx
        self.nz, self.nc = n_col // 2, 2
        row, col = lax.axis_index("row"), lax.axis_index("col")
        self.y, self.x = row // self.nx, row % self.nx
        self.z, self.core = col // self.nc, col % self.nc

    def shift(self, value, axis):
        pairs = []
        for y in range(self.ny):
            for x in range(self.nx):
                to = (y, (x + 1) % self.nx) if axis == "x" else ((y + 1) % self.ny, x)
                pairs.append((y * self.nx + x, to[0] * self.nx + to[1]))
        return lax.ppermute(value, "row", pairs)

    def along_z(self, value, step, first):
        pairs = []
        for z in range(self.nz):
            held = z - first if step > 0 else z + first
            if 0 <= z + step < self.nz and 0 <= held < self.nz:
                for core in range(self.nc):
                    pairs.append((z * self.nc + core, (z + step) * self.nc + core))
        return lax.ppermute(value, "col", pairs)

    def twin(self, value):
        pairs = [(z * self.nc + c, z * self.nc + 1 - c) for z in range(self.nz) for c in range(self.nc)]
        return lax.ppermute(value, "col", pairs)

    def plane(self, upper, lower):
        held = {(0, 0, 0): upper, (1, 0, 0): lower}
        for half, axes in ((0, "xy"), (1, "yx")):
            for axis in axes:
                count = self.nx if axis == "x" else self.ny
                for key in [k for k in held if k[0] == half]:
                    value = held[key]
                    for s in range(1, count):
                        value = self.shift(value, axis)
                        held[(half, key[1] + (s if axis == "y" else 0), key[2] + (s if axis == "x" else 0))] = value
        return held

    def plane_order(self):
        return [(dy, dx) for dy in range(self.ny) for dx in range(self.nx)]

    def plane_sources(self):
        found = [
            ((self.y - dy) % self.ny) * self.nx + (self.x - dx) % self.nx for dy, dx in self.plane_order()
        ]
        return jnp.stack(found).astype(jnp.int32)

    def line(self, value):
        found = [value]
        before = after = value
        for s in range(self.nz - 1):
            before = self.along_z(before, 1, s)
            after = self.along_z(after, -1, s)
            found += [before, after]
        return found

    def line_owners(self):
        offsets = [0]
        for s in range(1, self.nz):
            offsets += [-s, s]
        owners = []
        for offset in offsets:
            z = self.z + offset
            there = (z >= 0) & (z < self.nz)
            owners += [
                jnp.where(there, z * self.nc + self.core, -1),
                jnp.where(there, z * self.nc + 1 - self.core, -1),
            ]
        return jnp.stack(owners).astype(jnp.int32)


def per_device(n_row, n_col, g0_values, g0_pattern, sigma_values, sigma_pairs, sigma_count):
    block_rows, block_cols = g0_pattern.shape
    rows, cols = g0_values.shape
    slots = sigma_values.shape[1]
    depth = rows * n_row
    grid = Grid(n_row, n_col)

    live = jnp.arange(slots, dtype=jnp.int32) < sigma_count[0, 0]
    place = (sigma_pairs[0, :, 0] % block_rows) * block_cols + sigma_pairs[0, :, 1] % block_cols
    places = lax.all_gather(jnp.where(live, place, -1), "col", axis=0, tiled=False)

    upper, lower = masked_halves(g0_values, g0_pattern)
    sigma_line = grid.line(sigma_values[0])
    sigma_parts = []
    for value in sigma_line:
        sigma_parts += [value, grid.twin(value)]
    owners = grid.line_owners()
    places = jnp.where(owners[:, None] >= 0, places[jnp.maximum(owners, 0)], -1)
    sources = grid.plane_sources()

    held = grid.plane(upper, lower)
    col_parts = [held[(half, dy, dx)] for dy, dx in grid.plane_order() for half in range(2)]
    turned = turn(owners, places, sources, sigma_parts, col_parts, rows, cols, block_cols, depth)

    lines = [grid.line(upper), grid.line(lower)]
    row_parts = []
    for i in range(len(lines[0])):
        row_parts += [lines[0][i], lines[1][i]]
        row_parts += [grid.twin(lines[0][i]), grid.twin(lines[1][i])]

    held = grid.plane(*turned)
    col_parts = [held[(half, dy, dx)] for dy, dx in grid.plane_order() for half in range(2)]
    return close(owners, sources, row_parts, col_parts, rows, cols, depth)


def solution(mesh):
    placed = (
        P("row", "col"),
        P("row", "col"),
        P("row", "col", None, None),
        P("row", "col", None),
        P("row", "col"),
    )
    return jax.shard_map(
        functools.partial(per_device, mesh.shape["row"], mesh.shape["col"]),
        mesh=mesh, in_specs=placed, out_specs=P("row", "col"), check_vma=False,
    )
```

time: 306 us -> 189 us (0.62)
  waiting for transfers between devices: 261 us -> 73.9 us
  starting transfers between devices: 0.12 us -> 51.1 us
  Pallas kernels: 0 us -> 24.8 us
  blocking collectives: 0 us -> 21.8 us
  matrix products: 20.1 us -> 0 us
  between operations: 13.9 us -> 1.18 us
  local copies, waits for them, and re-layouts: 5.3 us -> 14.2 us
  other arithmetic: 4.6 us -> 0.87 us
    all_gather x4 -> x0, waiting for transfers between devices: 261 us -> none  [the longest x1 83.7 us: per_device(): panel = lax.all_gather(g0_tile, 'col', axis=1, tiled=True)]
    ppermute x0 -> x51, waiting for transfers between devices: none -> 73.9 us  [the longest x12 49.1 us: shift(): return lax.ppermute(value, 'row', pairs)]
    ppermute x0 -> x51, starting transfers between devices: none -> 51.1 us  [the longest x18 34.9 us: along_z(): return lax.ppermute(value, 'col', pairs)]
    pallas_call x0 -> x3, Pallas kernels: none -> 24.8 us  [the longest x1 14.2 us: turn(): pl.pallas_call(functools.partial(turn_kernel, n_slot, n_col, (rows, cols,...]
    all_gather x0 -> x1, blocking collectives: none -> 21.8 us  [per_device(): lax.all_gather(jnp.where(live, place, -1), 'col', axis=0, tiled=False)]
    dot_general x2 -> x0, matrix products: 20.1 us -> none  [the longest x1 10.1 us: per_device(): jnp.dot(columns, lax.all_gather(sigma_tile, 'row', axis=0, tiled=True), p...]
    unnamed x7 -> x81, local copies, waits for them, and re-layouts: 1.27 us -> 12.9 us
    broadcast_in_dim x3 -> x0, local copies, waits for them, and re-layouts: 3.21 us -> none  [the longest x2 2.98 us: per_device(): mask = jnp.repeat(jnp.repeat(g0_pattern, width, axis=0), width, axis=1)]
  transfers between devices with their start and end apart: 4 -> 51, of which waited for: 4 -> 17; matrix products, arithmetic and copies ran while one was open for 5% -> 2% of each run, Pallas kernels for 0% -> 8%
where the time goes in v1:
time: 189 us; the launch traced here: 188 us
  waiting for transfers between devices  73.9 us (39%)
  starting transfers between devices  51.1 us (27%)
  Pallas kernels  24.8 us (13%)
  blocking collectives  21.8 us (12%)
  local copies, waits for them, and re-layouts  14.2 us (8%)
    ppermute x12, waiting for transfers between devices, shift(): return lax.ppermute(value, 'row', pairs)  49.1 us
    ppermute x18, starting transfers between devices, along_z(): return lax.ppermute(value, 'col', pairs)  34.9 us
    ppermute x18, waiting for transfers between devices, along_z(): return lax.ppermute(value, 'col', pairs)  24.8 us
    all_gather x1, blocking collectives, per_device(): lax.all_gather(jnp.where(live, place, -1), 'col', axis=0, tiled=False)  21.8 us
    pallas_call x1, Pallas kernels, turn(): pl.pallas_call(functools.partial(turn_kernel, n_slot, n_col, (rows, cols,...  14.2 us
    unnamed x81, local copies, waits for them, and re-layouts  12.9 us
    ppermute x12, starting transfers between devices, shift(): return lax.ppermute(value, 'row', pairs)  12.1 us
    pallas_call x1, Pallas kernels, close(): pl.pallas_call(functools.partial(close_kernel, n_row, n_col, (rows, cols)...  9.73 us
  transfers between devices with their start and end apart: 51, of which 17 were waited for; matrix products, arithmetic and copies ran while one was open for 2% of the time, Pallas kernels for 8%

profile of v1, /device:TPU:0, one launch (start us, length us, event | category | flops | bytes accessed | tf_op | source)
XLA Modules:
  0.0 187.9 jit_solution(3745573783246608330)
XLA Ops:
  1.3 6.3 %collective-permute-start.27 = (bf16[12,128,128]{2,1,0:T(8,128)(2,1)}, bf16[12,128,128]{2,1,0:T(8,128)(2,1)}, u32[]{:S(2)}, u32[]{:S(2)}) collective-permute-start(bf16[12,128,128]{2,1,0:T(8,128)(2,1)} %bitcast.49), channel_id=1, source_target_pairs={{0,2},{1,3},{2,4},{3,5},{4,6},{5,7},{8,10},{9,11},{10,12},{11,13},... | collective-permute-start | bytes 1179656 | tf_op jit(solution)/shard_map/ppermute | solution.py:192
  10.5 2.0 %collective-permute-start.41 = (bf16[512,512]{1,0:T(8,128)(2,1)S(1)}, bf16[512,512]{1,0:T(8,128)(2,1)S(1)}, u32[]{:S(2)}, u32[]{:S(2)}) collective-permute-start(bf16[512,512]{1,0:T(8,128)(2,1)S(1)} %get-tuple-element.9.refs_14_.refs_0_), channel_id=1, source_target_pairs={{0,16},{8,24},{16,0},{24,8},{1,17},{9,25},{17,1},{25,9},{2,18},{10... | collective-permute-start | bytes 1572872 | tf_op jit(solution)/shard_map/ppermute | solution.py:183
  12.5 1.5 collective-permute-start.39
  15.6 4.6 %collective-permute-start.2 = (bf16[512,512]{1,0:T(8,128)(2,1)S(1)}, bf16[512,512]{1,0:T(8,128)(2,1)S(1)}, u32[]{:S(2)}, u32[]{:S(2)}) collective-permute-start(bf16[512,512]{1,0:T(8,128)(2,1)S(1)} %get-tuple-element.9.refs_14_.refs_0_), channel_id=1, source_target_pairs={{0,2},{1,3},{2,4},{3,5},{4,6},{5,7},{8,10},{9,11},{10,12},{11,13},... | collective-permute-start | bytes 1572872 | tf_op jit(solution)/shard_map/ppermute | solution.py:192
  21.0 4.1 %collective-permute-done.41.refs_18_ = bf16[512,512]{1,0:T(8,128)(2,1)S(1)} collective-permute-done((bf16[512,512]{1,0:T(8,128)(2,1)S(1)}, bf16[512,512]{1,0:T(8,128)(2,1)S(1)}, u32[]{:S(2)}, u32[]{:S(2)}) %collective-permute-start.41) | collective-permute-done | bytes 524320 | tf_op jit(solution)/shard_map/ppermute | solution.py:183
  25.1 1.7 collective-permute-start.42
  26.8 1.5 collective-permute-start.40
  30.9 5.3 %collective-permute-start.3 = (bf16[512,512]{1,0:T(8,128)(2,1)S(1)}, bf16[512,512]{1,0:T(8,128)(2,1)}, u32[]{:S(2)}, u32[]{:S(2)}) collective-permute-start(bf16[512,512]{1,0:T(8,128)(2,1)S(1)} %get-tuple-element.10.refs_15_.refs_1_), channel_id=1, source_target_pairs={{0,2},{1,3},{2,4},{3,5},{4,6},{5,7},{8,10},{9,11},{10,12},{11,13},... | collective-permute-start | bytes 1572872 | tf_op jit(solution)/shard_map/ppermute | solution.py:192
  36.3 2.5 %collective-permute-done.42.refs_19_ = bf16[512,512]{1,0:T(8,128)(2,1)S(1)} collective-permute-done((bf16[512,512]{1,0:T(8,128)(2,1)S(1)}, bf16[512,512]{1,0:T(8,128)(2,1)S(1)}, u32[]{:S(2)}, u32[]{:S(2)}) %collective-permute-start.42) | collective-permute-done | bytes 524320 | tf_op jit(solution)/shard_map/ppermute | solution.py:183
  40.2 5.2 %collective-permute-done.7.refs_9_ = bf16[512,512]{1,0:T(8,128)(2,1)S(1)} collective-permute-done((bf16[512,512]{1,0:T(8,128)(2,1)S(1)}, bf16[512,512]{1,0:T(8,128)(2,1)S(1)}, u32[]{:S(2)}, u32[]{:S(2)}) %collective-permute-start.7) | collective-permute-done | bytes 524320 | tf_op jit(solution)/shard_map/ppermute | solution.py:192
  47.6 4.9 %collective-permute-done.33.refs_8_ = bf16[12,128,128]{2,1,0:T(8,128)(2,1)} collective-permute-done((bf16[12,128,128]{2,1,0:T(8,128)(2,1)}, bf16[12,128,128]{2,1,0:T(8,128)(2,1)}, u32[]{:S(2)}, u32[]{:S(2)}) %collective-permute-start.33) | collective-permute-done | bytes 393248 | tf_op jit(solution)/shard_map/ppermute | solution.py:192
  56.6 5.4 %collective-permute-done.43.refs_20_ = bf16[512,512]{1,0:T(8,128)(2,1)S(1)} collective-permute-done((bf16[512,512]{1,0:T(8,128)(2,1)S(1)}, bf16[512,512]{1,0:T(8,128)(2,1)S(1)}, u32[]{:S(2)}, u32[]{:S(2)}) %collective-permute-start.43) | collective-permute-done | bytes 524320 | tf_op jit(solution)/shard_map/ppermute | solution.py:183
  61.9 5.1 %collective-permute-done.14.refs_16_ = bf16[512,512]{1,0:T(8,128)(2,1)S(1)} collective-permute-done((bf16[512,512]{1,0:T(8,128)(2,1)S(1)}, bf16[512,512]{1,0:T(8,128)(2,1)S(1)}, u32[]{:S(2)}, u32[]{:S(2)}) %collective-permute-start.14) | collective-permute-done | bytes 524320 | tf_op jit(solution)/shard_map/ppermute | solution.py:192
  71.1 4.4 %collective-permute-done.44.refs_21_ = bf16[512,512]{1,0:T(8,128)(2,1)S(1)} collective-permute-done((bf16[512,512]{1,0:T(8,128)(2,1)S(1)}, bf16[512,512]{1,0:T(8,128)(2,1)S(1)}, u32[]{:S(2)}, u32[]{:S(2)}) %collective-permute-start.44) | collective-permute-done | bytes 524320 | tf_op jit(solution)/shard_map/ppermute | solution.py:183
  76.8 3.8 %collective-permute-done.15.refs_17_ = bf16[512,512]{1,0:T(8,128)(2,1)S(1)} collective-permute-done((bf16[512,512]{1,0:T(8,128)(2,1)S(1)}, bf16[512,512]{1,0:T(8,128)(2,1)S(1)}, u32[]{:S(2)}, u32[]{:S(2)}) %collective-permute-start.15) | collective-permute-done | bytes 524320 | tf_op jit(solution)/shard_map/ppermute | solution.py:192
  84.9 4.1 %collective-permute-done.37.refs_12_ = bf16[12,128,128]{2,1,0:T(8,128)(2,1)} collective-permute-done((bf16[12,128,128]{2,1,0:T(8,128)(2,1)}, bf16[12,128,128]{2,1,0:T(8,128)(2,1)}, u32[]{:S(2)}, u32[]{:S(2)}) %collective-permute-start.37) | collective-permute-done | bytes 393248 | tf_op jit(solution)/shard_map/ppermute | solution.py:192
  91.1 21.8 %all-gather = s32[8,1,12]{2,1,0:T(1,128)S(1)} all-gather(s32[1,1,12]{2,1,0:T(1,128)S(1)} %fusion.4), channel_id=1, replica_groups=mesh['row'=4,'col'=8] {'col'}, dimensions={0}, use_global_device_ids=true | all-gather | bytes 432 | tf_op jit(solution)/shard_map/all_gather | solution.py:252
  121.8 14.2 %turn.1 = (bf16[512,512]{1,0:T(8,128)(2,1)S(1)}, bf16[512,512]{1,0:T(8,128)(2,1)}) custom-call(s32[14]{0:T(128)S(1)} %stack.104.owner_ref, s32[14,12]{1,0:T(8,128)S(1)} %broadcast_select_fusion.place_ref, s32[4]{0:T(128)S(1)} %pad_add_fusion.source_ref, bf16[12,128,128]{2,1,0:T(8,128)(2,1)S(1)} %bitcast.51, bf16[12,128,128]{2,1,0:T(8,128)(2,1)S(1)} %copy-done.14, ...), custom_call_target="tpu_custom_call" | custom-call | flops 4294967296 | bytes 6291456 | tf_op jit(solution)/shard_map/turn/pallas_call | solution.py:86
  137.1 1.6 collective-permute-start.45
  139.8 11.6 %collective-permute-done.47.refs_32_ = bf16[512,512]{1,0:T(8,128)(2,1)S(1)} collective-permute-done((bf16[512,512]{1,0:T(8,128)(2,1)S(1)}, bf16[512,512]{1,0:T(8,128)(2,1)S(1)}, u32[]{:S(2)}, u32[]{:S(2)}) %collective-permute-start.47) | collective-permute-done | bytes 524320 | tf_op jit(solution)/shard_map/ppermute | solution.py:183
  153.5 9.2 %collective-permute-done.48.refs_33_ = bf16[512,512]{1,0:T(8,128)(2,1)S(1)} collective-permute-done((bf16[512,512]{1,0:T(8,128)(2,1)}, bf16[512,512]{1,0:T(8,128)(2,1)S(1)}, u32[]{:S(2)}, u32[]{:S(2)}) %collective-permute-start.48) | collective-permute-done | bytes 524320 | tf_op jit(solution)/shard_map/ppermute | solution.py:183
  164.1 8.9 %collective-permute-done.49.refs_34_ = bf16[512,512]{1,0:T(8,128)(2,1)S(1)} collective-permute-done((bf16[512,512]{1,0:T(8,128)(2,1)S(1)}, bf16[512,512]{1,0:T(8,128)(2,1)S(1)}, u32[]{:S(2)}, u32[]{:S(2)}) %collective-permute-start.49) | collective-permute-done | bytes 524320 | tf_op jit(solution)/shard_map/ppermute | solution.py:183
  173.1 2.1 %collective-permute-done.50.refs_35_ = bf16[512,512]{1,0:T(8,128)(2,1)S(1)} collective-permute-done((bf16[512,512]{1,0:T(8,128)(2,1)S(1)}, bf16[512,512]{1,0:T(8,128)(2,1)S(1)}, u32[]{:S(2)}, u32[]{:S(2)}) %collective-permute-start.50) | collective-permute-done | bytes 524320 | tf_op jit(solution)/shard_map/ppermute | solution.py:183
  178.2 9.7 %close.1 = bf16[1024,512]{1,0:T(8,128)(2,1)} custom-call(s32[14]{0:T(128)S(1)} %stack.104.owner_ref, s32[4]{0:T(128)S(1)} %pad_add_fusion.source_ref, bf16[512,512]{1,0:T(8,128)(2,1)S(1)} %copy-done.2, bf16[512,512]{1,0:T(8,128)(2,1)S(1)} %copy-done.4, bf16[512,512]{1,0:T(8,128)(2,1)S(1)} %collective-permute-done.refs_2_, bf16[512,512]{1,0:T(8,128)(2,1)S(1)} %copy-done.6, ...), custom_call_target="tpu_custom_call" | custom-call | flops 4294967296 | bytes 13631488 | tf_op jit(solution)/shard_map/close/pallas_call | solution.py:148
  (172 shorter events, 45.2 us)
Async XLA Ops:
  10.5 14.6 %collective-permute-start.41 = (bf16[512,512]{1,0:T(8,128)(2,1)S(1)}, bf16[512,512]{1,0:T(8,128)(2,1)S(1)}, u32[]{:S(2)}, u32[]{:S(2)}) collective-permute-start(bf16[512,512]{1,0:T(8,128)(2,1)S(1)} %get-tuple-element.9.refs_14_.refs_0_), channel_id=1, source_target_pairs={{0,16},{8,24},{16,0},{24,8},{1,17},{9,25},{17,1},{25,9},{2,18},{10... | collective-permute-start | bytes 1572872 | tf_op jit(solution)/shard_map/ppermute | solution.py:183
  14.3 15.3 %collective-permute-start.6 = (bf16[512,512]{1,0:T(8,128)(2,1)S(1)}, bf16[512,512]{1,0:T(8,128)(2,1)S(1)}, u32[]{:S(2)}, u32[]{:S(2)}) collective-permute-start(bf16[512,512]{1,0:T(8,128)(2,1)S(1)} %get-tuple-element.9.refs_14_.refs_0_), channel_id=1, source_target_pairs={{2,0},{3,1},{4,2},{5,3},{6,4},{7,5},{10,8},{11,9},{12,10},{13,11},... | collective-permute-start | bytes 1572872 | tf_op jit(solution)/shard_map/ppermute | solution.py:192
  15.6 15.3 %collective-permute-start.2 = (bf16[512,512]{1,0:T(8,128)(2,1)S(1)}, bf16[512,512]{1,0:T(8,128)(2,1)S(1)}, u32[]{:S(2)}, u32[]{:S(2)}) collective-permute-start(bf16[512,512]{1,0:T(8,128)(2,1)S(1)} %get-tuple-element.9.refs_14_.refs_0_), channel_id=1, source_target_pairs={{0,2},{1,3},{2,4},{3,5},{4,6},{5,7},{8,10},{9,11},{10,12},{11,13},... | collective-permute-start | bytes 1572872 | tf_op jit(solution)/shard_map/ppermute | solution.py:192
  21.0 15.3 %collective-permute-start = (bf16[512,512]{1,0:T(8,128)(2,1)S(1)}, bf16[512,512]{1,0:T(8,128)(2,1)S(1)}, u32[]{:S(2)}, u32[]{:S(2)}) collective-permute-start(bf16[512,512]{1,0:T(8,128)(2,1)S(1)} %get-tuple-element.9.refs_14_.refs_0_), channel_id=1, source_target_pairs={{0,1},{1,0},{2,3},{3,2},{4,5},{5,4},{6,7},{7,6},{8,9},{9,8},{10,11... | collective-permute-start | bytes 1572872 | tf_op jit(solution)/shard_map/ppermute | solution.py:196
  29.6 15.7 %collective-permute-start.7 = (bf16[512,512]{1,0:T(8,128)(2,1)S(1)}, bf16[512,512]{1,0:T(8,128)(2,1)S(1)}, u32[]{:S(2)}, u32[]{:S(2)}) collective-permute-start(bf16[512,512]{1,0:T(8,128)(2,1)S(1)} %get-tuple-element.10.refs_15_.refs_1_), channel_id=1, source_target_pairs={{2,0},{3,1},{4,2},{5,3},{6,4},{7,5},{10,8},{11,9},{12,10},{13,11},... | collective-permute-start | bytes 1572872 | tf_op jit(solution)/shard_map/ppermute | solution.py:192
  30.9 15.8 %collective-permute-start.3 = (bf16[512,512]{1,0:T(8,128)(2,1)S(1)}, bf16[512,512]{1,0:T(8,128)(2,1)}, u32[]{:S(2)}, u32[]{:S(2)}) collective-permute-start(bf16[512,512]{1,0:T(8,128)(2,1)S(1)} %get-tuple-element.10.refs_15_.refs_1_), channel_id=1, source_target_pairs={{0,2},{1,3},{2,4},{3,5},{4,6},{5,7},{8,10},{9,11},{10,12},{11,13},... | collective-permute-start | bytes 1572872 | tf_op jit(solution)/shard_map/ppermute | solution.py:192
  52.5 14.4 %collective-permute-start.14 = (bf16[512,512]{1,0:T(8,128)(2,1)S(1)}, bf16[512,512]{1,0:T(8,128)(2,1)S(1)}, u32[]{:S(2)}, u32[]{:S(2)}) collective-permute-start(bf16[512,512]{1,0:T(8,128)(2,1)S(1)} %collective-permute-done.6.refs_8_), channel_id=1, source_target_pairs={{2,0},{3,1},{4,2},{5,3},{10,8},{11,9},{12,10},{13,11},{18,16},{19,... | collective-permute-start | bytes 1572872 | tf_op jit(solution)/shard_map/ppermute | solution.py:192
  54.6 14.5 %collective-permute-start.10 = (bf16[512,512]{1,0:T(8,128)(2,1)S(1)}, bf16[512,512]{1,0:T(8,128)(2,1)S(1)}, u32[]{:S(2)}, u32[]{:S(2)}) collective-permute-start(bf16[512,512]{1,0:T(8,128)(2,1)S(1)} %collective-permute-done.2.refs_4_), channel_id=1, source_target_pairs={{2,4},{3,5},{4,6},{5,7},{10,12},{11,13},{12,14},{13,15},{18,20},{1... | collective-permute-start | bytes 1572872 | tf_op jit(solution)/shard_map/ppermute | solution.py:192
  83.6 30.5 %collective-permute-start.22 = (bf16[512,512]{1,0:T(8,128)(2,1)}, bf16[512,512]{1,0:T(8,128)(2,1)}, u32[]{:S(2)}, u32[]{:S(2)}) collective-permute-start(bf16[512,512]{1,0:T(8,128)(2,1)} %copy-done.19), channel_id=1, source_target_pairs={{2,0},{3,1},{10,8},{11,9},{18,16},{19,17},{26,24},{27,25}} | collective-permute-start | bytes 1572872 | tf_op jit(solution)/shard_map/ppermute | solution.py:192
  89.1 25.5 %collective-permute-start.16 = (bf16[512,512]{1,0:T(8,128)(2,1)}, bf16[512,512]{1,0:T(8,128)(2,1)}, u32[]{:S(2)}, u32[]{:S(2)}) collective-permute-start(bf16[512,512]{1,0:T(8,128)(2,1)} %copy-done.19), channel_id=1, source_target_pairs={{0,1},{1,0},{2,3},{3,2},{4,5},{5,4},{6,7},{7,6},{8,9},{9,8},{10,11... | collective-permute-start | bytes 1572872 | tf_op jit(solution)/shard_map/ppermute | solution.py:196
  89.1 26.8 %collective-permute-start.18 = (bf16[512,512]{1,0:T(8,128)(2,1)}, bf16[512,512]{1,0:T(8,128)(2,1)}, u32[]{:S(2)}, u32[]{:S(2)}) collective-permute-start(bf16[512,512]{1,0:T(8,128)(2,1)} %copy-done.20), channel_id=1, source_target_pairs={{4,6},{5,7},{12,14},{13,15},{20,22},{21,23},{28,30},{29,31}} | collective-permute-start | bytes 1572872 | tf_op jit(solution)/shard_map/ppermute | solution.py:192
  90.5 25.6 %collective-permute-start.38 = (bf16[12,128,128]{2,1,0:T(8,128)(2,1)}, bf16[12,128,128]{2,1,0:T(8,128)(2,1)}, u32[]{:S(2)}, u32[]{:S(2)}) collective-permute-start(bf16[12,128,128]{2,1,0:T(8,128)(2,1)} %collective-permute-done.37.refs_12_), channel_id=1, source_target_pairs={{0,1},{1,0},{2,3},{3,2},{4,5},{5,4},{6,7},{7,6},{8,9},{9,8},{10,11... | collective-permute-start | bytes 1179656 | tf_op jit(solution)/shard_map/ppermute | solution.py:196
  91.0 26.6 %collective-permute-start.36 = (bf16[12,128,128]{2,1,0:T(8,128)(2,1)}, bf16[12,128,128]{2,1,0:T(8,128)(2,1)}, u32[]{:S(2)}, u32[]{:S(2)}) collective-permute-start(bf16[12,128,128]{2,1,0:T(8,128)(2,1)} %collective-permute-done.35.refs_10_), channel_id=1, source_target_pairs={{0,1},{1,0},{2,3},{3,2},{4,5},{5,4},{6,7},{7,6},{8,9},{9,8},{10,11... | collective-permute-start | bytes 1179656 | tf_op jit(solution)/shard_map/ppermute | solution.py:196
  114.2 21.8 %collective-permute-start.12 = (bf16[512,512]{1,0:T(8,128)(2,1)}, bf16[512,512]{1,0:T(8,128)(2,1)}, u32[]{:S(2)}, u32[]{:S(2)}) collective-permute-start(bf16[512,512]{1,0:T(8,128)(2,1)} %copy-done.20), channel_id=1, source_target_pairs={{0,1},{1,0},{2,3},{3,2},{4,5},{5,4},{6,7},{7,6},{8,9},{9,8},{10,11... | collective-permute-start | bytes 1572872 | tf_op jit(solution)/shard_map/ppermute | solution.py:196
  114.5 21.7 %collective-permute-start.23 = (bf16[512,512]{1,0:T(8,128)(2,1)}, bf16[512,512]{1,0:T(8,128)(2,1)}, u32[]{:S(2)}, u32[]{:S(2)}) collective-permute-start(bf16[512,512]{1,0:T(8,128)(2,1)} %copy-done.21), channel_id=1, source_target_pairs={{2,0},{3,1},{10,8},{11,9},{18,16},{19,17},{26,24},{27,25}} | collective-permute-start | bytes 1572872 | tf_op jit(solution)/shard_map/ppermute | solution.py:192
  115.8 20.8 %collective-permute-start.17 = (bf16[512,512]{1,0:T(8,128)(2,1)}, bf16[512,512]{1,0:T(8,128)(2,1)}, u32[]{:S(2)}, u32[]{:S(2)}) collective-permute-start(bf16[512,512]{1,0:T(8,128)(2,1)} %copy-done.21), channel_id=1, source_target_pairs={{0,1},{1,0},{2,3},{3,2},{4,5},{5,4},{6,7},{7,6},{8,9},{9,8},{10,11... | collective-permute-start | bytes 1572872 | tf_op jit(solution)/shard_map/ppermute | solution.py:196
  116.1 21.0 %collective-permute-start.19 = (bf16[512,512]{1,0:T(8,128)(2,1)}, bf16[512,512]{1,0:T(8,128)(2,1)}, u32[]{:S(2)}, u32[]{:S(2)}) collective-permute-start(bf16[512,512]{1,0:T(8,128)(2,1)} %copy-done.23), channel_id=1, source_target_pairs={{4,6},{5,7},{12,14},{13,15},{20,22},{21,23},{28,30},{29,31}} | collective-permute-start | bytes 1572872 | tf_op jit(solution)/shard_map/ppermute | solution.py:192
  117.6 21.1 %collective-permute-start.13 = (bf16[512,512]{1,0:T(8,128)(2,1)}, bf16[512,512]{1,0:T(8,128)(2,1)}, u32[]{:S(2)}, u32[]{:S(2)}) collective-permute-start(bf16[512,512]{1,0:T(8,128)(2,1)} %copy-done.23), channel_id=1, source_target_pairs={{0,1},{1,0},{2,3},{3,2},{4,5},{5,4},{6,7},{7,6},{8,9},{9,8},{10,11... | collective-permute-start | bytes 1572872 | tf_op jit(solution)/shard_map/ppermute | solution.py:196
  136.6 14.8 %collective-permute-start.47 = (bf16[512,512]{1,0:T(8,128)(2,1)S(1)}, bf16[512,512]{1,0:T(8,128)(2,1)S(1)}, u32[]{:S(2)}, u32[]{:S(2)}) collective-permute-start(bf16[512,512]{1,0:T(8,128)(2,1)S(1)} %get-tuple-element.11.refs_28_), channel_id=1, source_target_pairs={{0,16},{8,24},{16,0},{24,8},{1,17},{9,25},{17,1},{25,9},{2,18},{10... | collective-permute-start | bytes 1572872 | tf_op jit(solution)/shard_map/ppermute | solution.py:183
  137.1 14.9 %collective-permute-start.45 = (bf16[512,512]{1,0:T(8,128)(2,1)S(1)}, bf16[512,512]{1,0:T(8,128)(2,1)S(1)}, u32[]{:S(2)}, u32[]{:S(2)}) collective-permute-start(bf16[512,512]{1,0:T(8,128)(2,1)S(1)} %get-tuple-element.11.refs_28_), channel_id=1, source_target_pairs={{0,8},{8,0},{16,24},{24,16},{1,9},{9,1},{17,25},{25,17},{2,10},{10... | collective-permute-start | bytes 1572872 | tf_op jit(solution)/shard_map/ppermute | solution.py:183
  138.7 23.9 %collective-permute-start.48 = (bf16[512,512]{1,0:T(8,128)(2,1)}, bf16[512,512]{1,0:T(8,128)(2,1)S(1)}, u32[]{:S(2)}, u32[]{:S(2)}) collective-permute-start(bf16[512,512]{1,0:T(8,128)(2,1)} %get-tuple-element.12.refs_29_), channel_id=1, source_target_pairs={{0,16},{8,24},{16,0},{24,8},{1,17},{9,25},{17,1},{25,9},{2,18},{10... | collective-permute-start | bytes 1572872 | tf_op jit(solution)/shard_map/ppermute | solution.py:183
  139.3 24.8 %collective-permute-start.25 = (bf16[512,512]{1,0:T(8,128)(2,1)}, bf16[512,512]{1,0:T(8,128)(2,1)S(1)}, u32[]{:S(2)}, u32[]{:S(2)}) collective-permute-start(bf16[512,512]{1,0:T(8,128)(2,1)} %collective-permute-done.23.refs_25_), channel_id=1, source_target_pairs={{0,1},{1,0},{2,3},{3,2},{4,5},{5,4},{6,7},{7,6},{8,9},{9,8},{10,11... | collective-permute-start | bytes 1572872 | tf_op jit(solution)/shard_map/ppermute | solution.py:196
  139.3 24.8 %collective-permute-start.21 = (bf16[512,512]{1,0:T(8,128)(2,1)}, bf16[512,512]{1,0:T(8,128)(2,1)S(1)}, u32[]{:S(2)}, u32[]{:S(2)}) collective-permute-start(bf16[512,512]{1,0:T(8,128)(2,1)} %collective-permute-done.19.refs_21_), channel_id=1, source_target_pairs={{0,1},{1,0},{2,3},{3,2},{4,5},{5,4},{6,7},{7,6},{8,9},{9,8},{10,11... | collective-permute-start | bytes 1572872 | tf_op jit(solution)/shard_map/ppermute | solution.py:196
  152.0 21.1 %collective-permute-start.49 = (bf16[512,512]{1,0:T(8,128)(2,1)S(1)}, bf16[512,512]{1,0:T(8,128)(2,1)S(1)}, u32[]{:S(2)}, u32[]{:S(2)}) collective-permute-start(bf16[512,512]{1,0:T(8,128)(2,1)S(1)} %collective-permute-done.45.refs_30_), channel_id=1, source_target_pairs={{0,16},{8,24},{16,0},{24,8},{1,17},{9,25},{17,1},{25,9},{2,18},{10... | collective-permute-start | bytes 1572872 | tf_op jit(solution)/shard_map/ppermute | solution.py:183
  (67 other events, 1244.9 us)

commit v2 on v0

v2 whole, which is shorter than its diff:
```python
import functools
import math

import jax
import jax.numpy as jnp
from jax import lax
from jax.experimental import pallas as pl
from jax.experimental.pallas import tpu as pltpu
from jax.sharding import PartitionSpec as P

VMEM_BYTES = 30 * 1024 * 1024
ANY = pl.BlockSpec(memory_space=pl.ANY)
SMEM = pl.BlockSpec(memory_space=pltpu.SMEM)
VMEM = pl.BlockSpec(memory_space=pltpu.VMEM)
TAIL = 16


def kernel_params():
    return pltpu.CompilerParams(vmem_limit_bytes=VMEM_BYTES)


def after(value, *earlier):
    return lax.optimization_barrier((value, *earlier))[0]


def mask_kernel(width, pattern_ref, values_ref, tile_ref, upper_ref, lower_ref):
    block_rows, block_cols = pattern_ref.shape
    half = block_rows // 2
    for a in range(block_rows):
        target = upper_ref if a < half else lower_ref
        at = pl.ds((a % half) * width, width)
        for b in range(block_cols):
            block = values_ref[pl.ds(a * width, width), pl.ds(b * width, width)]
            block = block * pattern_ref[a, b].astype(jnp.float32).astype(jnp.bfloat16)
            tile_ref[a // half, at, pl.ds(b * width, width)] = block
            target[at, pl.ds(b * width, width)] = block


def masked(g0_values, g0_pattern):
    rows, cols = g0_values.shape
    half = jax.ShapeDtypeStruct((rows // 2, cols), jnp.bfloat16)
    return pl.pallas_call(
        functools.partial(mask_kernel, rows // g0_pattern.shape[0]),
        out_shape=(jax.ShapeDtypeStruct((2, rows // 2, cols), jnp.bfloat16), half, half),
        in_specs=[SMEM, VMEM],
        out_specs=(VMEM, VMEM, VMEM),
        compiler_params=kernel_params(),
        cost_estimate=pl.CostEstimate(flops=rows * cols, bytes_accessed=4 * rows * cols, transcendentals=0),
        name="mask",
    )(g0_pattern, g0_values)


def spread_kernel(count, slots, width, row_ref, col_ref, *refs):
    parts, (dense_ref, spare, sem) = refs[:count], refs[count:]

    dense_ref[...] = jnp.zeros_like(dense_ref)
    for i in range(count):
        for s in range(slots):
            source = parts[i].at[pl.ds(s * width, width)]
            row, col = row_ref[i, s], col_ref[i, s]

            @pl.when(row >= 0)
            def _():
                target = dense_ref.at[pl.ds(pl.multiple_of(row, width), width), pl.ds(pl.multiple_of(col, width), width)]
                pltpu.make_async_copy(source, target, sem.at[i]).start()

            @pl.when(row < 0)
            def _():
                pltpu.make_async_copy(source, spare.at[pl.ds(s * width, width)], sem.at[i]).start()
    for i in range(count):
        pltpu.make_async_copy(parts[i].at[pl.ds(0, slots * width)], spare, sem.at[i]).wait()


def spread(row_at, col_at, parts, slots, rows, depth):
    width = parts[0].shape[1]
    return pl.pallas_call(
        functools.partial(spread_kernel, len(parts), slots, width),
        out_shape=jax.ShapeDtypeStruct((rows, depth), jnp.bfloat16),
        in_specs=[SMEM, SMEM] + [ANY] * len(parts),
        out_specs=VMEM,
        scratch_shapes=[pltpu.VMEM((slots * width, width), jnp.bfloat16), pltpu.SemaphoreType.DMA((len(parts),))],
        compiler_params=kernel_params(),
        cost_estimate=pl.CostEstimate(flops=0, bytes_accessed=4 * rows * depth, transcendentals=0),
        name="spread",
    )(row_at, col_at, *parts)


def turn_kernel(count, source_ref, dense_ref, *refs):
    parts, (out_ref,) = refs[:count], refs[count:]
    half, cols = parts[0].shape
    tile = min(256, half)
    for side in range(2):
        @pl.loop(0, half // tile)
        def _(t):
            at = pl.multiple_of(side * half + t * tile, tile)
            total = jnp.zeros((tile, cols), jnp.float32)
            for i in range(count):
                start = pl.multiple_of(source_ref[i // 2] * (2 * half) + (i % 2) * half, half)
                total += jnp.dot(
                    dense_ref[pl.ds(at, tile), pl.ds(start, half)], parts[i][...], preferred_element_type=jnp.float32
                )
            out_ref[side, pl.ds(pl.multiple_of(t * tile, tile), tile), :] = total.astype(jnp.bfloat16)


def turn(sources, dense, parts):
    rows, depth = dense.shape
    half, cols = parts[0].shape
    return pl.pallas_call(
        functools.partial(turn_kernel, len(parts)),
        out_shape=jax.ShapeDtypeStruct((2, half, cols), jnp.bfloat16),
        in_specs=[SMEM] + [VMEM] * (1 + len(parts)),
        out_specs=VMEM,
        compiler_params=kernel_params(),
        cost_estimate=pl.CostEstimate(
            flops=2 * rows * cols * depth, bytes_accessed=2 * depth * (rows + cols), transcendentals=0
        ),
        name="turn",
    )(sources, dense, *parts)


def close_kernel(n_col, n_row, source_ref, owner_ref, *refs):
    col_refs, row_refs = refs[:n_col], refs[n_col:n_col + n_row]
    total_ref, column_ref, sem = refs[n_col + n_row:]
    half, cols = row_refs[0].shape

    def column_copy(i):
        start = pl.multiple_of(source_ref[i // 2] * (2 * half) + (i % 2) * half, half)
        return pltpu.make_async_copy(col_refs[i], column_ref.at[pl.ds(start, half)], sem.at[i])

    for i in range(n_col):
        column_copy(i).start()
    for i in range(n_col):
        column_copy(i).wait()
    tile = min(256, half)
    for side in range(2):
        @pl.loop(0, half // tile)
        def _(t):
            at = pl.multiple_of(t * tile, tile)
            total = row_refs[side][pl.ds(at, tile), :].astype(jnp.float32)
            for i in range(side, n_row, 2):
                start = pl.multiple_of(jnp.maximum(owner_ref[i // 2], 0) * cols, cols)
                total += jnp.dot(
                    row_refs[i][pl.ds(at, tile), :], column_ref[pl.ds(start, cols), :], preferred_element_type=jnp.float32
                )
            total_ref[side, pl.ds(at, tile), :] = total


def close(sources, owners, col_parts, row_parts):
    half, cols = row_parts[0].shape
    n_col, n_row = len(col_parts), len(row_parts)
    return pl.pallas_call(
        functools.partial(close_kernel, n_col, n_row),
        out_shape=(
            jax.ShapeDtypeStruct((2, half, cols), jnp.float32),
            jax.ShapeDtypeStruct((n_col * half, cols), jnp.bfloat16),
        ),
        in_specs=[SMEM, SMEM] + [ANY] * n_col + [VMEM] * n_row,
        out_specs=(VMEM, VMEM),
        scratch_shapes=[pltpu.SemaphoreType.DMA((n_col,))],
        compiler_params=kernel_params(),
        cost_estimate=pl.CostEstimate(
            flops=2 * n_row * half * cols * cols, bytes_accessed=2 * (n_row + n_col) * half * cols, transcendentals=0
        ),
        name="close",
    )(sources, owners, *col_parts, *row_parts)


def last_kernel(n_row, owner_ref, total_ref, column_ref, *refs):
    row_refs, (out_ref,) = refs[:n_row], refs[n_row:]
    half, cols = row_refs[0].shape
    tile = min(256, half)
    for side in range(2):
        @pl.loop(0, half // tile)
        def _(t):
            at = pl.multiple_of(t * tile, tile)
            total = total_ref[side, pl.ds(at, tile), :]
            for i in range(side, n_row, 2):
                start = pl.multiple_of(jnp.maximum(owner_ref[i // 2], 0) * cols, cols)
                total += jnp.dot(
                    row_refs[i][pl.ds(at, tile), :], column_ref[pl.ds(start, cols), :], preferred_element_type=jnp.float32
                )
            out_ref[pl.ds(pl.multiple_of(side * half + at, tile), tile), :] = total.astype(jnp.bfloat16)


def last(owners, total, column, row_parts):
    half, cols = row_parts[0].shape
    n_row = len(row_parts)
    return pl.pallas_call(
        functools.partial(last_kernel, n_row),
        out_shape=jax.ShapeDtypeStruct((2 * half, cols), jnp.bfloat16),
        in_specs=[SMEM] + [VMEM] * (2 + n_row),
        out_specs=VMEM,
        compiler_params=kernel_params(),
        cost_estimate=pl.CostEstimate(
            flops=2 * n_row * half * cols * cols, bytes_accessed=2 * n_row * half * cols, transcendentals=0
        ),
        name="last",
    )(owners, total, column, *row_parts)


class Grid:
    def __init__(self, n_row, n_col):
        side = math.isqrt(n_row)
        self.nx = side if side * side == n_row else n_row
        self.ny = n_row // self.nx
        self.nz, self.nc = n_col // 2, 2
        row, col = lax.axis_index("row"), lax.axis_index("col")
        self.y, self.x = row // self.nx, row % self.nx
        self.z, self.core = col // self.nc, col % self.nc

    def shift(self, value, axis):
        pairs = []
        for y in range(self.ny):
            for x in range(self.nx):
                to = (y, (x + 1) % self.nx) if axis == "x" else ((y + 1) % self.ny, x)
                pairs.append((y * self.nx + x, to[0] * self.nx + to[1]))
        return lax.ppermute(value, "row", pairs)

    def along_z(self, value, route):
        return lax.ppermute(
            value, "col", [(z * self.nc + c, to * self.nc + c) for z, to in route.items() for c in range(self.nc)]
        )

    def twin(self, value):
        return lax.ppermute(
            value, "col", [(z * self.nc + c, z * self.nc + 1 - c) for z in range(self.nz) for c in range(self.nc)]
        )

    def plane(self, tile):
        if self.nx == 2 and self.ny == 2:
            by_x, by_y = self.shift(tile, "x"), self.shift(tile, "y")
            upper = self.shift(by_x[0], "y")
            lower = self.shift(by_y[1], "x")
            return [tile[0], tile[1], by_x[0], by_x[1], by_y[0], by_y[1], upper, lower]
        found = []
        for dy in range(self.ny):
            along = tile
            for dx in range(self.nx):
                found += [along[0], along[1]]
                along = self.shift(along, "x") if dx + 1 < self.nx else along
            tile = self.shift(tile, "y") if dy + 1 < self.ny else tile
        return found

    def plane_sources(self):
        found = [
            ((self.y - dy) % self.ny) * self.nx + (self.x - dx) % self.nx
            for dy in range(self.ny) for dx in range(self.nx)
        ]
        return jnp.stack(found).astype(jnp.int32)

    def around(self, value):
        found = [value]
        for _ in range(self.nz - 1):
            found.append(self.along_z(found[-1], {z: (z + 1) % self.nz for z in range(self.nz)}))
        return found

    def z_owners(self):
        if self.nz == 4:
            return [self.z, self.z ^ 1, 3 - self.z, 3 - (self.z ^ 1)]
        return [(self.z - s) % self.nz for s in range(self.nz)]

    def col_owners(self):
        found = []
        for z in self.z_owners():
            found += [z * self.nc + self.core, z * self.nc + 1 - self.core]
        return jnp.stack(found).astype(jnp.int32)


NEAR = {0: 1, 1: 0, 2: 3, 3: 2}
MIRROR = {0: 3, 1: 2, 2: 1, 3: 0}


def per_device(n_row, n_col, g0_values, g0_pattern, sigma_values, sigma_pairs, sigma_count):
    block_rows, block_cols = g0_pattern.shape
    rows, cols = g0_values.shape
    slots, width = sigma_values.shape[1], sigma_values.shape[2]
    depth = rows * n_row
    grid = Grid(n_row, n_col)
    owners, sources = grid.col_owners(), grid.plane_sources()

    live = jnp.arange(slots, dtype=jnp.int32) < sigma_count[0, 0]
    block_row = jnp.where(live, sigma_pairs[0, :, 0] % block_rows, -1)
    block_col = sigma_pairs[0, :, 1] % block_cols
    names = jnp.stack([block_row, block_col]).astype(jnp.bfloat16)
    names = jnp.pad(names, ((0, TAIL - 2), (0, width - slots)))
    message = jnp.concatenate([sigma_values[0].reshape(slots * width, width), names])

    tile, upper, lower = masked(g0_values, g0_pattern)

    if grid.nz == 4:
        s_near = grid.along_z(message, NEAR)
        s_far = grid.along_z(message, MIRROR)
        s_cross = grid.along_z(s_far, NEAR)
        line = [message, s_near, s_far, s_cross]
    else:
        line = grid.around(message)
    sigma_parts = []
    for value in line:
        sigma_parts += [value, grid.twin(value)]
    found = jnp.stack([part[slots * width:slots * width + 2, :slots] for part in sigma_parts]).astype(jnp.int32)
    row_at = jnp.where(found[:, 0] >= 0, found[:, 0] * width, -1)
    col_at = owners[:, None] * cols + found[:, 1] * width
    dense = spread(row_at, col_at, sigma_parts, slots, rows, depth)

    turned = turn(sources, dense, grid.plane(tile))

    if grid.nz == 4:
        far_upper = grid.along_z(after(upper, s_near, s_far), MIRROR)
        far_lower = grid.along_z(after(lower, far_upper), MIRROR)
        near = grid.along_z(after(tile, s_cross), NEAR)
        cross_upper = grid.along_z(after(far_upper, far_lower), NEAR)
        cross_lower = grid.along_z(after(far_lower, near), NEAR)
        halves = [(upper, lower), (near[0], near[1]), (far_upper, far_lower), (cross_upper, cross_lower)]
        twins = [(t[0], t[1]) for t in (grid.twin(tile), grid.twin(near))]
        twins += [(grid.twin(a), grid.twin(b)) for a, b in halves[2:]]
    else:
        halves = [(t[0], t[1]) for t in grid.around(tile)]
        twins = [(grid.twin(a), grid.twin(b)) for a, b in halves]
    row_parts = []
    for own, other in zip(halves, twins):
        row_parts += [*own, *other]

    total, column = close(sources, owners[:-2], grid.plane(turned), row_parts[:-4])
    return last(owners[-2:], total, column, row_parts[-4:])


def solution(mesh):
    placed = (
        P("row", "col"),
        P("row", "col"),
        P("row", "col", None, None),
        P("row", "col", None),
        P("row", "col"),
    )
    return jax.shard_map(
        functools.partial(per_device, mesh.shape["row"], mesh.shape["col"]),
        mesh=mesh, in_specs=placed, out_specs=P("row", "col"), check_vma=False,
    )
```

time: 306 us -> 125 us (0.41)
  waiting for transfers between devices: 261 us -> 64.4 us
  starting transfers between devices: 0.12 us -> 26.5 us
  Pallas kernels: 0 us -> 20.8 us
  matrix products: 20.1 us -> 0 us
  between operations: 13.9 us -> 0.94 us
  local copies, waits for them, and re-layouts: 5.3 us -> 10 us
    all_gather x4 -> x0, waiting for transfers between devices: 261 us -> none  [the longest x1 83.7 us: per_device(): panel = lax.all_gather(g0_tile, 'col', axis=1, tiled=True)]
    ppermute x0 -> x26, waiting for transfers between devices: none -> 64.4 us  [the longest x8 54.8 us: along_z(): lax.ppermute(value, 'col', [(z * self.nc + c, to * self.nc + c) for z, to...]
    ppermute x0 -> x26, starting transfers between devices: none -> 26.5 us  [the longest x8 15.5 us: along_z(): lax.ppermute(value, 'col', [(z * self.nc + c, to * self.nc + c) for z, to...]
    pallas_call x0 -> x5, Pallas kernels: none -> 20.8 us  [the longest x1 5.71 us: close(): pl.pallas_call(functools.partial(close_kernel, n_col, n_row), out_shape=(...]
    dot_general x2 -> x0, matrix products: 20.1 us -> none  [the longest x1 10.1 us: per_device(): jnp.dot(columns, lax.all_gather(sigma_tile, 'row', axis=0, tiled=True), p...]
    squeeze x0 -> x9, local copies, waits for them, and re-layouts: none -> 7.82 us  [the longest x6 5.21 us: plane(): return [tile[0], tile[1], by_x[0], by_x[1], by_y[0], by_y[1], upper, lower]]
    broadcast_in_dim x3 -> x0, local copies, waits for them, and re-layouts: 3.21 us -> none  [the longest x2 2.98 us: per_device(): mask = jnp.repeat(jnp.repeat(g0_pattern, width, axis=0), width, axis=1)]
  transfers between devices with their start and end apart: 4 -> 26, of which waited for: 4 -> 9; matrix products, arithmetic and copies ran while one was open for 5% -> 7% of each run, Pallas kernels for 0% -> 14%
where the time goes in v2:
time: 125 us
  waiting for transfers between devices  64.4 us (52%)
  starting transfers between devices  26.5 us (21%)
  Pallas kernels  20.8 us (17%)
  local copies, waits for them, and re-layouts  10 us (8%)
  other arithmetic  2.07 us (2%)
    ppermute x8, waiting for transfers between devices, along_z(): lax.ppermute(value, 'col', [(z * self.nc + c, to * self.nc + c) for z, to...  54.8 us
    ppermute x8, starting transfers between devices, along_z(): lax.ppermute(value, 'col', [(z * self.nc + c, to * self.nc + c) for z, to...  15.5 us
    ppermute x8, starting transfers between devices, shift(): return lax.ppermute(value, 'row', pairs)  9.31 us
    ppermute x8, waiting for transfers between devices, shift(): return lax.ppermute(value, 'row', pairs)  7.81 us
    pallas_call x1, Pallas kernels, close(): pl.pallas_call(functools.partial(close_kernel, n_col, n_row), out_shape=(...  5.71 us
    pallas_call x1, Pallas kernels, turn(): pl.pallas_call(functools.partial(turn_kernel, len(parts)), out_shape=jax....  5.52 us
    squeeze x6, local copies, waits for them, and re-layouts, plane(): return [tile[0], tile[1], by_x[0], by_x[1], by_y[0], by_y[1], upper, lower]  5.21 us
    pallas_call x1, Pallas kernels, spread(): pl.pallas_call(functools.partial(spread_kernel, len(parts), slots, width)...  4.64 us
  transfers between devices with their start and end apart: 26, of which 9 were waited for; matrix products, arithmetic and copies ran while one was open for 7% of the time, Pallas kernels for 14%

profile of v2, /device:TPU:0, one launch (start us, length us, event | category | flops | bytes accessed | tf_op | source)
XLA Modules:
  0.0 124.7 jit_solution(5331116642373699381)
XLA Ops:
  3.0 2.6 %collective-permute-start.1 = (bf16[1552,128]{1,0:T(8,128)(2,1)S(1)}, bf16[1552,128]{1,0:T(8,128)(2,1)S(1)}, u32[]{:S(2)}, u32[]{:S(2)}) collective-permute-start(bf16[1552,128]{1,0:T(8,128)(2,1)S(1)} %pad_maximum_fusion.refs_0_), channel_id=1, source_target_pairs={{0,2},{1,3},{2,0},{3,1},{4,6},{5,7},{6,4},{7,5},{8,10},{9,11},{10,... | collective-permute-start | bytes 1191944 | tf_op jit(solution)/shard_map/ppermute | solution.py:220
  5.6 2.5 %collective-permute-start.3 = (bf16[1552,128]{1,0:T(8,128)(2,1)S(1)}, bf16[1552,128]{1,0:T(8,128)(2,1)S(1)}, u32[]{:S(2)}, u32[]{:S(2)}) collective-permute-start(bf16[1552,128]{1,0:T(8,128)(2,1)S(1)} %pad_maximum_fusion.refs_0_), channel_id=1, source_target_pairs={{0,6},{1,7},{2,4},{3,5},{4,2},{5,3},{6,0},{7,1},{8,14},{9,15},{10,... | collective-permute-start | bytes 1191944 | tf_op jit(solution)/shard_map/ppermute | solution.py:220
  10.1 1.7 %mask.1 = (bf16[2,512,512]{2,1,0:T(8,128)(2,1)S(1)}, bf16[512,512]{1,0:T(8,128)(2,1)S(1)}, bf16[512,512]{1,0:T(8,128)(2,1)}) custom-call(s32[8,4]{1,0:T(8,128)S(1)} %copy.6.pattern_ref, bf16[1024,512]{1,0:T(8,128)(2,1)S(1)} %copy-done), custom_call_target="tpu_custom_call" | custom-call | flops 524288 | bytes 2097152 | tf_op jit(solution)/shard_map/mask/pallas_call | solution.py:42
  11.8 1.5 %collective-permute-start.7 = (bf16[2,512,512]{2,1,0:T(8,128)(2,1)S(1)}, bf16[2,512,512]{2,1,0:T(8,128)(2,1)}, u32[]{:S(2)}, u32[]{:S(2)}) collective-permute-start(bf16[2,512,512]{2,1,0:T(8,128)(2,1)S(1)} %get-tuple-element.18), channel_id=1, source_target_pairs={{0,8},{8,0},{16,24},{24,16},{1,9},{9,1},{17,25},{25,17},{2,10},{10... | collective-permute-start | bytes 3145736 | tf_op jit(solution)/shard_map/ppermute | solution.py:217
  13.3 1.5 %collective-permute-start.8 = (bf16[2,512,512]{2,1,0:T(8,128)(2,1)S(1)}, bf16[2,512,512]{2,1,0:T(8,128)(2,1)}, u32[]{:S(2)}, u32[]{:S(2)}) collective-permute-start(bf16[2,512,512]{2,1,0:T(8,128)(2,1)S(1)} %get-tuple-element.18), channel_id=1, source_target_pairs={{0,16},{8,24},{16,0},{24,8},{1,17},{9,25},{17,1},{25,9},{2,18},{10... | collective-permute-start | bytes 3145736 | tf_op jit(solution)/shard_map/ppermute | solution.py:217
  15.4 10.8 %collective-permute-done.3.refs_4_ = bf16[1552,128]{1,0:T(8,128)(2,1)S(1)} collective-permute-done((bf16[1552,128]{1,0:T(8,128)(2,1)S(1)}, bf16[1552,128]{1,0:T(8,128)(2,1)S(1)}, u32[]{:S(2)}, u32[]{:S(2)}) %collective-permute-start.3) | collective-permute-done | bytes 397344 | tf_op jit(solution)/shard_map/ppermute | solution.py:220
  26.9 11.0 %collective-permute-done.5.refs_6_ = bf16[1552,128]{1,0:T(8,128)(2,1)S(1)} collective-permute-done((bf16[1552,128]{1,0:T(8,128)(2,1)S(1)}, bf16[1552,128]{1,0:T(8,128)(2,1)S(1)}, u32[]{:S(2)}, u32[]{:S(2)}) %collective-permute-start.5) | collective-permute-done | bytes 397344 | tf_op jit(solution)/shard_map/ppermute | solution.py:220
  37.9 1.5 %collective-permute-start.18 = (bf16[512,512]{1,0:T(8,128)(2,1)S(1)}, bf16[512,512]{1,0:T(8,128)(2,1)}, u32[]{:S(2)}, u32[]{:S(2)}) collective-permute-start(bf16[512,512]{1,0:T(8,128)(2,1)S(1)} %get-tuple-element.19.refs_8_), channel_id=1, source_target_pairs={{0,6},{1,7},{2,4},{3,5},{4,2},{5,3},{6,0},{7,1},{8,14},{9,15},{10,... | collective-permute-start | bytes 1572872 | tf_op jit(solution)/shard_map/ppermute | solution.py:220
  39.5 1.7 %collective-permute-done.4.refs_5_ = bf16[1552,128]{1,0:T(8,128)(2,1)S(1)} collective-permute-done((bf16[1552,128]{1,0:T(8,128)(2,1)S(1)}, bf16[1552,128]{1,0:T(8,128)(2,1)S(1)}, u32[]{:S(2)}, u32[]{:S(2)}) %collective-permute-start.4) | collective-permute-done | bytes 397344 | tf_op jit(solution)/shard_map/ppermute | solution.py:225
  42.0 1.3 %slice_bitcast_fusion.14 = (bf16[512,512]{1,0:T(8,128)(2,1)S(1)}, bf16[512,512]{1,0:T(8,128)(2,1)S(1)}) fusion(bf16[2,512,512]{2,1,0:T(8,128)(2,1)} %collective-permute-done.7), kind=kLoop, calls=%fused_computation.14 | loop fusion | bytes 2097152 | tf_op jit(solution)/shard_map/squeeze | solution.py:234
  43.3 1.6 %collective-permute-start.9 = (bf16[512,512]{1,0:T(8,128)(2,1)S(1)}, bf16[512,512]{1,0:T(8,128)(2,1)S(1)}, u32[]{:S(2)}, u32[]{:S(2)}) collective-permute-start(bf16[512,512]{1,0:T(8,128)(2,1)S(1)} %get-tuple-element.40.refs_2_), channel_id=1, source_target_pairs={{0,16},{8,24},{16,0},{24,8},{1,17},{9,25},{17,1},{25,9},{2,18},{10... | collective-permute-start | bytes 1572872 | tf_op jit(solution)/shard_map/ppermute | solution.py:217
  46.2 1.6 %collective-permute-start.10 = (bf16[512,512]{1,0:T(8,128)(2,1)S(1)}, bf16[512,512]{1,0:T(8,128)(2,1)S(1)}, u32[]{:S(2)}, u32[]{:S(2)}) collective-permute-start(bf16[512,512]{1,0:T(8,128)(2,1)S(1)} %get-tuple-element.37.refs_5_), channel_id=1, source_target_pairs={{0,8},{8,0},{16,24},{24,16},{1,9},{9,1},{17,25},{25,17},{2,10},{10... | collective-permute-start | bytes 1572872 | tf_op jit(solution)/shard_map/ppermute | solution.py:217
  47.8 4.6 %spread.1.dense_ref = bf16[1024,4096]{1,0:T(8,128)(2,1)S(1)} custom-call(s32[8,12]{1,0:T(8,128)S(1)} %bitcast.89, s32[8,12]{1,0:T(8,128)S(1)} %broadcast_add_fusion.col_ref, bf16[1552,128]{1,0:T(8,128)(2,1)S(1)} %pad_maximum_fusion.refs_0_, bf16[1552,128]{1,0:T(8,128)(2,1)S(1)} %collective-permute-done.refs_1_, ...), custom_call_target="tpu_custom_call" | custom-call | bytes 16777216 | tf_op jit(solution)/shard_map/spread/pallas_call | solution.py:76
  52.5 5.2 %collective-permute-done.9.refs_6_ = bf16[512,512]{1,0:T(8,128)(2,1)S(1)} collective-permute-done((bf16[512,512]{1,0:T(8,128)(2,1)S(1)}, bf16[512,512]{1,0:T(8,128)(2,1)S(1)}, u32[]{:S(2)}, u32[]{:S(2)}) %collective-permute-start.9) | collective-permute-done | bytes 524320 | tf_op jit(solution)/shard_map/ppermute | solution.py:217
  57.7 2.6 %collective-permute-done.10.refs_7_ = bf16[512,512]{1,0:T(8,128)(2,1)S(1)} collective-permute-done((bf16[512,512]{1,0:T(8,128)(2,1)S(1)}, bf16[512,512]{1,0:T(8,128)(2,1)S(1)}, u32[]{:S(2)}, u32[]{:S(2)}) %collective-permute-start.10) | collective-permute-done | bytes 524320 | tf_op jit(solution)/shard_map/ppermute | solution.py:217
  60.3 5.5 %turn.1 = bf16[2,512,512]{2,1,0:T(8,128)(2,1)S(1)} custom-call(s32[4]{0:T(128)S(1)} %pad_add_fusion.1.source_ref, bf16[1024,4096]{1,0:T(8,128)(2,1)S(1)} %spread.1.dense_ref, bf16[512,512]{1,0:T(8,128)(2,1)S(1)} %get-tuple-element.42.refs_0_, bf16[512,512]{1,0:T(8,128)(2,1)S(1)} %get-tuple-element.41.refs_1_, ...), custom_call_target="tpu_custom_call" | custom-call | flops 4294967296 | bytes 12582912 | tf_op jit(solution)/shard_map/turn/pallas_call | solution.py:108
  65.8 1.6 %collective-permute-start.11 = (bf16[2,512,512]{2,1,0:T(8,128)(2,1)S(1)}, bf16[2,512,512]{2,1,0:T(8,128)(2,1)}, u32[]{:S(2)}, u32[]{:S(2)}) collective-permute-start(bf16[2,512,512]{2,1,0:T(8,128)(2,1)S(1)} %turn.1), channel_id=1, source_target_pairs={{0,8},{8,0},{16,24},{24,16},{1,9},{9,1},{17,25},{25,17},{2,10},{10... | collective-permute-start | bytes 3145736 | tf_op jit(solution)/shard_map/ppermute | solution.py:217
  67.4 1.5 %collective-permute-start.19 = (bf16[512,512]{1,0:T(8,128)(2,1)}, bf16[512,512]{1,0:T(8,128)(2,1)}, u32[]{:S(2)}, u32[]{:S(2)}) collective-permute-start(bf16[512,512]{1,0:T(8,128)(2,1)} %get-tuple-element.20.refs_9_), channel_id=1, source_target_pairs={{0,6},{1,7},{2,4},{3,5},{4,2},{5,3},{6,0},{7,1},{8,14},{9,15},{10,... | collective-permute-start | bytes 1572872 | tf_op jit(solution)/shard_map/ppermute | solution.py:220
  70.8 16.5 %collective-permute-done.19.refs_17_ = bf16[512,512]{1,0:T(8,128)(2,1)} collective-permute-done((bf16[512,512]{1,0:T(8,128)(2,1)}, bf16[512,512]{1,0:T(8,128)(2,1)}, u32[]{:S(2)}, u32[]{:S(2)}) %collective-permute-start.19) | collective-permute-done | bytes 524320 | tf_op jit(solution)/shard_map/ppermute | solution.py:220
  87.3 5.9 %collective-permute-start.22 = (bf16[512,512]{1,0:T(8,128)(2,1)}, bf16[512,512]{1,0:T(8,128)(2,1)S(1)}, u32[]{:S(2)}, u32[]{:S(2)}) collective-permute-start(bf16[512,512]{1,0:T(8,128)(2,1)} %collective-permute-done.18.refs_16_), channel_id=1, source_target_pairs={{0,2},{1,3},{2,0},{3,1},{4,6},{5,7},{6,4},{7,5},{8,10},{9,11},{10,... | collective-permute-start | bytes 1572872 | tf_op jit(solution)/shard_map/ppermute | solution.py:220
  97.1 9.2 %collective-permute-done.22.refs_0_ = bf16[512,512]{1,0:T(8,128)(2,1)S(1)} collective-permute-done((bf16[512,512]{1,0:T(8,128)(2,1)}, bf16[512,512]{1,0:T(8,128)(2,1)S(1)}, u32[]{:S(2)}, u32[]{:S(2)}) %collective-permute-start.22) | collective-permute-done | bytes 524320 | tf_op jit(solution)/shard_map/ppermute | solution.py:220
  108.1 7.0 %collective-permute-done.23.refs_1_ = bf16[512,512]{1,0:T(8,128)(2,1)S(1)} collective-permute-done((bf16[512,512]{1,0:T(8,128)(2,1)}, bf16[512,512]{1,0:T(8,128)(2,1)S(1)}, u32[]{:S(2)}, u32[]{:S(2)}) %collective-permute-start.23) | collective-permute-done | bytes 524320 | tf_op jit(solution)/shard_map/ppermute | solution.py:220
  115.7 5.7 %close.1 = (f32[2,512,512]{2,1,0:T(8,128)S(1)}, bf16[4096,512]{1,0:T(8,128)(2,1)S(1)}) custom-call(s32[4]{0:T(128)S(1)} %pad_add_fusion.1.source_ref, s32[6]{0:T(128)S(1)} %stack.97.owner_ref, bf16[512,512]{1,0:T(8,128)(2,1)S(1)} %get-tuple-element.36.refs_0_, bf16[512,512]{1,0:T(8,128)(2,1)S(1)} %get-tuple-element.35.refs_1_, ...), custom_call_target="tpu_custom_call" | custom-call | flops 3221225472 | bytes 10485760 | tf_op jit(solution)/shard_map/close/pallas_call | solution.py:151
  121.4 3.3 %last.1 = bf16[1024,512]{1,0:T(8,128)(2,1)} custom-call(s32[2]{0:T(128)S(1)} %pad_add_fusion.owner_ref, f32[2,512,512]{2,1,0:T(8,128)S(1)} %get-tuple-element.21.total_ref, bf16[4096,512]{1,0:T(8,128)(2,1)S(1)} %get-tuple-element.22.column_ref, bf16[512,512]{1,0:T(8,128)(2,1)S(1)} %collective-permute-done.22.refs_0_, ...), custom_call_target="tpu_custom_call" | custom-call | flops 1073741824 | bytes 2097152 | tf_op jit(solution)/shard_map/last/pallas_call | solution.py:188
  (64 shorter events, 15.9 us)
Async XLA Ops:
  2.5 23.8 %collective-permute-start = (bf16[1552,128]{1,0:T(8,128)(2,1)S(1)}, bf16[1552,128]{1,0:T(8,128)(2,1)S(1)}, u32[]{:S(2)}, u32[]{:S(2)}) collective-permute-start(bf16[1552,128]{1,0:T(8,128)(2,1)S(1)} %pad_maximum_fusion.refs_0_), channel_id=1, source_target_pairs={{0,1},{1,0},{2,3},{3,2},{4,5},{5,4},{6,7},{7,6},{8,9},{9,8},{10,11... | collective-permute-start | bytes 1191944 | tf_op jit(solution)/shard_map/ppermute | solution.py:225
  3.0 12.4 %collective-permute-start.1 = (bf16[1552,128]{1,0:T(8,128)(2,1)S(1)}, bf16[1552,128]{1,0:T(8,128)(2,1)S(1)}, u32[]{:S(2)}, u32[]{:S(2)}) collective-permute-start(bf16[1552,128]{1,0:T(8,128)(2,1)S(1)} %pad_maximum_fusion.refs_0_), channel_id=1, source_target_pairs={{0,2},{1,3},{2,0},{3,1},{4,6},{5,7},{6,4},{7,5},{8,10},{9,11},{10,... | collective-permute-start | bytes 1191944 | tf_op jit(solution)/shard_map/ppermute | solution.py:220
  5.6 20.6 %collective-permute-start.3 = (bf16[1552,128]{1,0:T(8,128)(2,1)S(1)}, bf16[1552,128]{1,0:T(8,128)(2,1)S(1)}, u32[]{:S(2)}, u32[]{:S(2)}) collective-permute-start(bf16[1552,128]{1,0:T(8,128)(2,1)S(1)} %pad_maximum_fusion.refs_0_), channel_id=1, source_target_pairs={{0,6},{1,7},{2,4},{3,5},{4,2},{5,3},{6,0},{7,1},{8,14},{9,15},{10,... | collective-permute-start | bytes 1191944 | tf_op jit(solution)/shard_map/ppermute | solution.py:220
  11.8 30.2 %collective-permute-start.7 = (bf16[2,512,512]{2,1,0:T(8,128)(2,1)S(1)}, bf16[2,512,512]{2,1,0:T(8,128)(2,1)}, u32[]{:S(2)}, u32[]{:S(2)}) collective-permute-start(bf16[2,512,512]{2,1,0:T(8,128)(2,1)S(1)} %get-tuple-element.18), channel_id=1, source_target_pairs={{0,8},{8,0},{16,24},{24,16},{1,9},{9,1},{17,25},{25,17},{2,10},{10... | collective-permute-start | bytes 3145736 | tf_op jit(solution)/shard_map/ppermute | solution.py:217
  13.3 30.0 %collective-permute-start.8 = (bf16[2,512,512]{2,1,0:T(8,128)(2,1)S(1)}, bf16[2,512,512]{2,1,0:T(8,128)(2,1)}, u32[]{:S(2)}, u32[]{:S(2)}) collective-permute-start(bf16[2,512,512]{2,1,0:T(8,128)(2,1)S(1)} %get-tuple-element.18), channel_id=1, source_target_pairs={{0,16},{8,24},{16,0},{24,8},{1,17},{9,25},{17,1},{25,9},{2,18},{10... | collective-permute-start | bytes 3145736 | tf_op jit(solution)/shard_map/ppermute | solution.py:217
  15.4 54.1 %collective-permute-start.15 = (bf16[2,512,512]{2,1,0:T(8,128)(2,1)S(1)}, bf16[2,512,512]{2,1,0:T(8,128)(2,1)}, u32[]{:S(2)}, u32[]{:S(2)}) collective-permute-start(bf16[2,512,512]{2,1,0:T(8,128)(2,1)S(1)} %get-tuple-element.18), channel_id=1, source_target_pairs={{0,1},{1,0},{2,3},{3,2},{4,5},{5,4},{6,7},{7,6},{8,9},{9,8},{10,11... | collective-permute-start | bytes 3145736 | tf_op jit(solution)/shard_map/ppermute | solution.py:225
  26.3 13.2 %collective-permute-start.2 = (bf16[1552,128]{1,0:T(8,128)(2,1)S(1)}, bf16[1552,128]{1,0:T(8,128)(2,1)S(1)}, u32[]{:S(2)}, u32[]{:S(2)}) collective-permute-start(bf16[1552,128]{1,0:T(8,128)(2,1)S(1)} %collective-permute-done.1.refs_2_), channel_id=1, source_target_pairs={{0,1},{1,0},{2,3},{3,2},{4,5},{5,4},{6,7},{7,6},{8,9},{9,8},{10,11... | collective-permute-start | bytes 1191944 | tf_op jit(solution)/shard_map/ppermute | solution.py:225
  26.3 11.6 %collective-permute-start.5 = (bf16[1552,128]{1,0:T(8,128)(2,1)S(1)}, bf16[1552,128]{1,0:T(8,128)(2,1)S(1)}, u32[]{:S(2)}, u32[]{:S(2)}) collective-permute-start(bf16[1552,128]{1,0:T(8,128)(2,1)S(1)} %collective-permute-done.3.refs_4_), channel_id=1, source_target_pairs={{0,2},{1,3},{2,0},{3,1},{4,6},{5,7},{6,4},{7,5},{8,10},{9,11},{10,... | collective-permute-start | bytes 1191944 | tf_op jit(solution)/shard_map/ppermute | solution.py:220
  37.9 29.5 %collective-permute-start.18 = (bf16[512,512]{1,0:T(8,128)(2,1)S(1)}, bf16[512,512]{1,0:T(8,128)(2,1)}, u32[]{:S(2)}, u32[]{:S(2)}) collective-permute-start(bf16[512,512]{1,0:T(8,128)(2,1)S(1)} %get-tuple-element.19.refs_8_), channel_id=1, source_target_pairs={{0,6},{1,7},{2,4},{3,5},{4,2},{5,3},{6,0},{7,1},{8,14},{9,15},{10,... | collective-permute-start | bytes 1572872 | tf_op jit(solution)/shard_map/ppermute | solution.py:220
  41.2 52.1 %collective-permute-start.16 = (bf16[2,512,512]{2,1,0:T(8,128)(2,1)S(1)}, bf16[2,512,512]{2,1,0:T(8,128)(2,1)}, u32[]{:S(2)}, u32[]{:S(2)}) collective-permute-start(bf16[2,512,512]{2,1,0:T(8,128)(2,1)S(1)} %get-tuple-element.18), channel_id=1, source_target_pairs={{0,2},{1,3},{2,0},{3,1},{4,6},{5,7},{6,4},{7,5},{8,10},{9,11},{10,... | collective-permute-start | bytes 3145736 | tf_op jit(solution)/shard_map/ppermute | solution.py:220
  43.3 14.4 %collective-permute-start.9 = (bf16[512,512]{1,0:T(8,128)(2,1)S(1)}, bf16[512,512]{1,0:T(8,128)(2,1)S(1)}, u32[]{:S(2)}, u32[]{:S(2)}) collective-permute-start(bf16[512,512]{1,0:T(8,128)(2,1)S(1)} %get-tuple-element.40.refs_2_), channel_id=1, source_target_pairs={{0,16},{8,24},{16,0},{24,8},{1,17},{9,25},{17,1},{25,9},{2,18},{10... | collective-permute-start | bytes 1572872 | tf_op jit(solution)/shard_map/ppermute | solution.py:217
  46.2 14.1 %collective-permute-start.10 = (bf16[512,512]{1,0:T(8,128)(2,1)S(1)}, bf16[512,512]{1,0:T(8,128)(2,1)S(1)}, u32[]{:S(2)}, u32[]{:S(2)}) collective-permute-start(bf16[512,512]{1,0:T(8,128)(2,1)S(1)} %get-tuple-element.37.refs_5_), channel_id=1, source_target_pairs={{0,8},{8,0},{16,24},{24,16},{1,9},{9,1},{17,25},{25,17},{2,10},{10... | collective-permute-start | bytes 1572872 | tf_op jit(solution)/shard_map/ppermute | solution.py:217
  65.8 27.5 %collective-permute-start.11 = (bf16[2,512,512]{2,1,0:T(8,128)(2,1)S(1)}, bf16[2,512,512]{2,1,0:T(8,128)(2,1)}, u32[]{:S(2)}, u32[]{:S(2)}) collective-permute-start(bf16[2,512,512]{2,1,0:T(8,128)(2,1)S(1)} %turn.1), channel_id=1, source_target_pairs={{0,8},{8,0},{16,24},{24,16},{1,9},{9,1},{17,25},{25,17},{2,10},{10... | collective-permute-start | bytes 3145736 | tf_op jit(solution)/shard_map/ppermute | solution.py:217
  67.4 20.0 %collective-permute-start.19 = (bf16[512,512]{1,0:T(8,128)(2,1)}, bf16[512,512]{1,0:T(8,128)(2,1)}, u32[]{:S(2)}, u32[]{:S(2)}) collective-permute-start(bf16[512,512]{1,0:T(8,128)(2,1)} %get-tuple-element.20.refs_9_), channel_id=1, source_target_pairs={{0,6},{1,7},{2,4},{3,5},{4,2},{5,3},{6,0},{7,1},{8,14},{9,15},{10,... | collective-permute-start | bytes 1572872 | tf_op jit(solution)/shard_map/ppermute | solution.py:220
  68.9 26.3 %collective-permute-start.12 = (bf16[2,512,512]{2,1,0:T(8,128)(2,1)S(1)}, bf16[2,512,512]{2,1,0:T(8,128)(2,1)}, u32[]{:S(2)}, u32[]{:S(2)}) collective-permute-start(bf16[2,512,512]{2,1,0:T(8,128)(2,1)S(1)} %turn.1), channel_id=1, source_target_pairs={{0,16},{8,24},{16,0},{24,8},{1,17},{9,25},{17,1},{25,9},{2,18},{10... | collective-permute-start | bytes 3145736 | tf_op jit(solution)/shard_map/ppermute | solution.py:217
  69.6 27.0 %collective-permute-start.20 = (bf16[512,512]{1,0:T(8,128)(2,1)}, bf16[512,512]{1,0:T(8,128)(2,1)S(1)}, u32[]{:S(2)}, u32[]{:S(2)}) collective-permute-start(bf16[512,512]{1,0:T(8,128)(2,1)} %collective-permute-done.18.refs_16_), channel_id=1, source_target_pairs={{0,1},{1,0},{2,3},{3,2},{4,5},{5,4},{6,7},{7,6},{8,9},{9,8},{10,11... | collective-permute-start | bytes 1572872 | tf_op jit(solution)/shard_map/ppermute | solution.py:225
  87.3 18.9 %collective-permute-start.22 = (bf16[512,512]{1,0:T(8,128)(2,1)}, bf16[512,512]{1,0:T(8,128)(2,1)S(1)}, u32[]{:S(2)}, u32[]{:S(2)}) collective-permute-start(bf16[512,512]{1,0:T(8,128)(2,1)} %collective-permute-done.18.refs_16_), channel_id=1, source_target_pairs={{0,2},{1,3},{2,0},{3,1},{4,6},{5,7},{6,4},{7,5},{8,10},{9,11},{10,... | collective-permute-start | bytes 1572872 | tf_op jit(solution)/shard_map/ppermute | solution.py:220
  93.2 21.8 %collective-permute-start.17 = (bf16[2,512,512]{2,1,0:T(8,128)(2,1)}, bf16[2,512,512]{2,1,0:T(8,128)(2,1)S(1)}, u32[]{:S(2)}, u32[]{:S(2)}) collective-permute-start(bf16[2,512,512]{2,1,0:T(8,128)(2,1)} %collective-permute-done.16), channel_id=1, source_target_pairs={{0,1},{1,0},{2,3},{3,2},{4,5},{5,4},{6,7},{7,6},{8,9},{9,8},{10,11... | collective-permute-start | bytes 3145736 | tf_op jit(solution)/shard_map/ppermute | solution.py:225
  93.3 22.3 %collective-permute-start.21 = (bf16[512,512]{1,0:T(8,128)(2,1)}, bf16[512,512]{1,0:T(8,128)(2,1)S(1)}, u32[]{:S(2)}, u32[]{:S(2)}) collective-permute-start(bf16[512,512]{1,0:T(8,128)(2,1)} %collective-permute-done.19.refs_17_), channel_id=1, source_target_pairs={{0,1},{1,0},{2,3},{3,2},{4,5},{5,4},{6,7},{7,6},{8,9},{9,8},{10,11... | collective-permute-start | bytes 1572872 | tf_op jit(solution)/shard_map/ppermute | solution.py:225
  95.2 19.9 %collective-permute-start.23 = (bf16[512,512]{1,0:T(8,128)(2,1)}, bf16[512,512]{1,0:T(8,128)(2,1)S(1)}, u32[]{:S(2)}, u32[]{:S(2)}) collective-permute-start(bf16[512,512]{1,0:T(8,128)(2,1)} %collective-permute-done.19.refs_17_), channel_id=1, source_target_pairs={{0,2},{1,3},{2,0},{3,1},{4,6},{5,7},{6,4},{7,5},{8,10},{9,11},{10,... | collective-permute-start | bytes 1572872 | tf_op jit(solution)/shard_map/ppermute | solution.py:220
  96.5 19.1 %collective-permute-start.13 = (bf16[512,512]{1,0:T(8,128)(2,1)S(1)}, bf16[512,512]{1,0:T(8,128)(2,1)S(1)}, u32[]{:S(2)}, u32[]{:S(2)}) collective-permute-start(bf16[512,512]{1,0:T(8,128)(2,1)S(1)} %get-tuple-element.34.refs_2_), channel_id=1, source_target_pairs={{0,16},{8,24},{16,0},{24,8},{1,17},{9,25},{17,1},{25,9},{2,18},{10... | collective-permute-start | bytes 1572872 | tf_op jit(solution)/shard_map/ppermute | solution.py:217
  106.3 9.4 %collective-permute-start.14 = (bf16[512,512]{1,0:T(8,128)(2,1)S(1)}, bf16[512,512]{1,0:T(8,128)(2,1)S(1)}, u32[]{:S(2)}, u32[]{:S(2)}) collective-permute-start(bf16[512,512]{1,0:T(8,128)(2,1)S(1)} %get-tuple-element.31.refs_5_), channel_id=1, source_target_pairs={{0,8},{8,0},{16,24},{24,16},{1,9},{9,1},{17,25},{25,17},{2,10},{10... | collective-permute-start | bytes 1572872 | tf_op jit(solution)/shard_map/ppermute | solution.py:217
  115.0 6.3 %collective-permute-start.24 = (bf16[512,512]{1,0:T(8,128)(2,1)S(1)}, bf16[512,512]{1,0:T(8,128)(2,1)S(1)}, u32[]{:S(2)}, u32[]{:S(2)}) collective-permute-start(bf16[512,512]{1,0:T(8,128)(2,1)S(1)} %collective-permute-done.22.refs_0_), channel_id=1, source_target_pairs={{0,1},{1,0},{2,3},{3,2},{4,5},{5,4},{6,7},{7,6},{8,9},{9,8},{10,11... | collective-permute-start | bytes 1572872 | tf_op jit(solution)/shard_map/ppermute | solution.py:225
  115.1 6.3 %collective-permute-start.25 = (bf16[512,512]{1,0:T(8,128)(2,1)S(1)}, bf16[512,512]{1,0:T(8,128)(2,1)S(1)}, u32[]{:S(2)}, u32[]{:S(2)}) collective-permute-start(bf16[512,512]{1,0:T(8,128)(2,1)S(1)} %collective-permute-done.23.refs_1_), channel_id=1, source_target_pairs={{0,1},{1,0},{2,3},{3,2},{4,5},{5,4},{6,7},{7,6},{8,9},{9,8},{10,11... | collective-permute-start | bytes 1572872 | tf_op jit(solution)/shard_map/ppermute | solution.py:225
  (3 other events, 7.2 us)

commit v3 on v2

v3 whole, which is shorter than its diff:
```python
import functools
import math

import jax
import jax.numpy as jnp
from jax import lax
from jax.experimental import pallas as pl
from jax.experimental.pallas import tpu as pltpu
from jax.sharding import PartitionSpec as P

VMEM_BYTES = 30 * 1024 * 1024
FIRST_VMEM_BYTES = 60 * 1024 * 1024
ANY = pl.BlockSpec(memory_space=pl.ANY)
HBM = pl.BlockSpec(memory_space=pltpu.HBM)
SMEM = pl.BlockSpec(memory_space=pltpu.SMEM)
VMEM = pl.BlockSpec(memory_space=pltpu.VMEM)
TAIL = 16
NO_COST = pl.CostEstimate(flops=0, bytes_accessed=0, transcendentals=0)


def kernel_params():
    return pltpu.CompilerParams(vmem_limit_bytes=VMEM_BYTES)


def after(value, *earlier):
    return lax.optimization_barrier((value, *earlier))[0]


def prepare_kernel(
    slots, width, base_ref, values_ref, pattern_ref, slots_ref, pairs_ref,
    message_ref, tile_ref, upper_ref, lower_ref,
    pattern, values, pairs, names, small_sems, slot_sems, row_sems,
):
    block_cols, block_rows = pattern_ref.shape
    half = block_rows // 2
    small = [
        pltpu.make_async_copy(pairs_ref, pairs, small_sems.at[0]),
        pltpu.make_async_copy(pattern_ref, pattern, small_sems.at[1]),
    ]
    moves = [
        pltpu.make_async_copy(slots_ref.at[0, s], message_ref.at[pl.ds(s * width, width)], slot_sems.at[s])
        for s in range(slots)
    ]
    fetches = [
        pltpu.make_async_copy(values_ref.at[pl.ds(a * width, width)], values.at[pl.ds(a * width, width)], row_sems.at[a])
        for a in range(block_rows)
    ]
    for move in small + fetches + moves:
        move.start()
    for move in small:
        move.wait()
    shape = pairs.shape
    first = lax.broadcasted_iota(jnp.int32, shape, 0) == 0
    local = pairs[...] - jnp.where(first, base_ref[0], base_ref[1])
    live = lax.broadcasted_iota(jnp.int32, shape, 1) < base_ref[2]
    names[...] = jnp.full(names.shape, -1, jnp.int32)
    names[pl.ds(0, shape[0]), pl.ds(0, shape[1])] = jnp.where(live, local, -1)
    message_ref[pl.ds(slots * width, TAIL), :] = names[...].astype(jnp.float32).astype(jnp.bfloat16)
    for a in range(block_rows):
        target = upper_ref if a < half else lower_ref
        at = pl.ds((a % half) * width, width)
        fetches[a].wait()
        for b in range(block_cols):
            keep = pattern[b:b + 1, a:a + 1].astype(jnp.float32)
            keep = jnp.broadcast_to(keep, (width, width)).astype(jnp.bfloat16)
            block = values[pl.ds(a * width, width), pl.ds(b * width, width)] * keep
            tile_ref[a // half, at, pl.ds(b * width, width)] = block
            target[at, pl.ds(b * width, width)] = block
    for move in moves:
        move.wait()


def prepare(base, g0_values, g0_pattern, sigma_values, sigma_pairs):
    rows, cols = g0_values.shape
    slots, width = sigma_values.shape[1], sigma_values.shape[2]
    half = jax.ShapeDtypeStruct((rows // 2, cols), jnp.bfloat16)
    return pl.pallas_call(
        functools.partial(prepare_kernel, slots, width),
        out_shape=(
            jax.ShapeDtypeStruct((slots * width + TAIL, width), jnp.bfloat16),
            jax.ShapeDtypeStruct((2, rows // 2, cols), jnp.bfloat16), half, half,
        ),
        in_specs=[SMEM] + [HBM] * 4,
        out_specs=(VMEM, VMEM, VMEM, VMEM),
        scratch_shapes=[
            pltpu.VMEM((g0_pattern.shape[1], g0_pattern.shape[0]), jnp.int32),
            pltpu.VMEM((rows, cols), jnp.bfloat16),
            pltpu.VMEM((2, slots), jnp.int32),
            pltpu.VMEM((TAIL, width), jnp.int32),
            pltpu.SemaphoreType.DMA((2,)),
            pltpu.SemaphoreType.DMA((slots,)),
            pltpu.SemaphoreType.DMA((g0_pattern.shape[0],)),
        ],
        compiler_params=pltpu.CompilerParams(vmem_limit_bytes=FIRST_VMEM_BYTES),
        cost_estimate=NO_COST,
        name="prepare",
    )(base, g0_values, g0_pattern.T, sigma_values, sigma_pairs[0].T)


def place_slots(slots, width, row_ref, col_ref, parts, dense_ref, spare, sem):
    for i, part in enumerate(parts):
        for s in range(slots):
            source = part.at[pl.ds(s * width, width)]
            row, col = row_ref[i, s], col_ref[i, s]

            @pl.when(row >= 0)
            def _():
                target = dense_ref.at[pl.ds(pl.multiple_of(row, width), width), pl.ds(pl.multiple_of(col, width), width)]
                pltpu.make_async_copy(source, target, sem.at[i]).start()

            @pl.when(row < 0)
            def _():
                pltpu.make_async_copy(source, spare.at[pl.ds(s * width, width)], sem.at[i]).start()
    for i, part in enumerate(parts):
        pltpu.make_async_copy(part.at[pl.ds(0, slots * width)], spare, sem.at[i]).wait()


def spread_kernel(count, slots, width, row_ref, col_ref, *refs):
    parts, (dense_ref, spare, sem) = refs[:count], refs[count:]
    dense_ref[...] = jnp.zeros_like(dense_ref)
    place_slots(slots, width, row_ref, col_ref, parts, dense_ref, spare, sem)


def spread(row_at, col_at, parts, slots, rows, depth):
    width = parts[0].shape[1]
    return pl.pallas_call(
        functools.partial(spread_kernel, len(parts), slots, width),
        out_shape=jax.ShapeDtypeStruct((rows, depth), jnp.bfloat16),
        in_specs=[SMEM, SMEM] + [ANY] * len(parts),
        out_specs=VMEM,
        scratch_shapes=[pltpu.VMEM((slots * width, width), jnp.bfloat16), pltpu.SemaphoreType.DMA((len(parts),))],
        compiler_params=kernel_params(),
        cost_estimate=NO_COST,
        name="spread",
    )(row_at, col_at, *parts)


def fill_kernel(count, slots, width, row_ref, col_ref, *refs):
    parts, (_, dense_ref, spare, sem) = refs[:count], refs[count:]
    place_slots(slots, width, row_ref, col_ref, parts, dense_ref, spare, sem)


def fill(row_at, col_at, parts, dense, slots):
    width = parts[0].shape[1]
    return pl.pallas_call(
        functools.partial(fill_kernel, len(parts), slots, width),
        out_shape=jax.ShapeDtypeStruct(dense.shape, dense.dtype),
        in_specs=[SMEM, SMEM] + [ANY] * (len(parts) + 1),
        out_specs=ANY,
        scratch_shapes=[pltpu.VMEM((slots * width, width), jnp.bfloat16), pltpu.SemaphoreType.DMA((len(parts),))],
        input_output_aliases={2 + len(parts): 0},
        compiler_params=kernel_params(),
        cost_estimate=NO_COST,
        name="fill",
    )(row_at, col_at, *parts, dense)


def turn_kernel(side, source_ref, dense_ref, *refs):
    parts, out_ref = refs[:-1], refs[-1]
    half, cols = parts[0].shape
    tile = min(256, half)

    @pl.loop(0, half // tile)
    def _(t):
        at = pl.multiple_of(t * tile, tile)
        total = jnp.zeros((tile, cols), jnp.float32)
        for i, part in enumerate(parts):
            start = pl.multiple_of(source_ref[i // 2] * (2 * half) + (i % 2) * half, half)
            total += jnp.dot(
                dense_ref[pl.ds(side * half + at, tile), pl.ds(start, half)], part[...], preferred_element_type=jnp.float32
            )
        out_ref[pl.ds(at, tile), :] = total.astype(jnp.bfloat16)


def turn(side, sources, dense, parts):
    depth = dense.shape[1]
    half, cols = parts[0].shape
    return pl.pallas_call(
        functools.partial(turn_kernel, side),
        out_shape=jax.ShapeDtypeStruct((half, cols), jnp.bfloat16),
        in_specs=[SMEM] + [VMEM] * (1 + len(parts)),
        out_specs=VMEM,
        compiler_params=kernel_params(),
        cost_estimate=NO_COST,
        name="turn",
    )(sources, dense, *parts)


def close_kernel(n_col, n_row, source_ref, owner_ref, *refs):
    col_refs, row_refs = refs[:n_col], refs[n_col:n_col + n_row]
    total_ref, column_ref, sem = refs[n_col + n_row:]
    _, half, cols = row_refs[0].shape

    def column_copy(i):
        start = pl.multiple_of(source_ref[i // 2] * (2 * half) + (i % 2) * half, half)
        return pltpu.make_async_copy(col_refs[i], column_ref.at[pl.ds(start, half)], sem.at[i])

    for i in range(n_col):
        column_copy(i).start()
    for i in range(n_col):
        column_copy(i).wait()
    tile = min(256, half)
    for side in range(2):
        @pl.loop(0, half // tile)
        def _(t):
            at = pl.multiple_of(t * tile, tile)
            total = row_refs[0][side, pl.ds(at, tile), :].astype(jnp.float32)
            for i, part in enumerate(row_refs):
                start = pl.multiple_of(owner_ref[i] * cols, cols)
                total += jnp.dot(
                    part[side, pl.ds(at, tile), :], column_ref[pl.ds(start, cols), :], preferred_element_type=jnp.float32
                )
            total_ref[side, pl.ds(at, tile), :] = total


def close(sources, owners, col_parts, row_parts):
    _, half, cols = row_parts[0].shape
    n_col, n_row = len(col_parts), len(row_parts)
    return pl.pallas_call(
        functools.partial(close_kernel, n_col, n_row),
        out_shape=(
            jax.ShapeDtypeStruct((2, half, cols), jnp.float32),
            jax.ShapeDtypeStruct((n_col * half, cols), jnp.bfloat16),
        ),
        in_specs=[SMEM, SMEM] + [ANY] * n_col + [VMEM] * n_row,
        out_specs=(VMEM, VMEM),
        scratch_shapes=[pltpu.SemaphoreType.DMA((n_col,))],
        compiler_params=kernel_params(),
        cost_estimate=NO_COST,
        name="close",
    )(sources, owners, *col_parts, *row_parts)


def last_kernel(side, n_row, owner_ref, total_ref, column_ref, *refs):
    row_refs, out_ref, result, sem = refs[:n_row], refs[-3], refs[-2], refs[-1]
    half, cols = row_refs[0].shape
    tile = min(256, half)
    moves = []
    for t in range(half // tile):
        at = pl.ds(t * tile, tile)
        total = total_ref[side, at, :]
        for i, part in enumerate(row_refs):
            start = pl.multiple_of(owner_ref[i] * cols, cols)
            total += jnp.dot(part[at, :], column_ref[pl.ds(start, cols), :], preferred_element_type=jnp.float32)
        result[at, :] = total.astype(jnp.bfloat16)
        moves.append(
            pltpu.make_async_copy(result.at[at], out_ref.at[pl.ds(side * half + t * tile, tile)], sem.at[t])
        )
        moves[-1].start()
    for move in moves:
        move.wait()


def last(side, owners, total, column, row_parts, earlier=None):
    half, cols = row_parts[0].shape
    n_row = len(row_parts)
    operands = [owners, total, column, *row_parts]
    specs = [SMEM] + [VMEM] * (2 + n_row)
    aliases = {}
    if earlier is not None:
        aliases = {len(operands): 0}
        operands.append(earlier)
        specs.append(HBM)
    return pl.pallas_call(
        functools.partial(last_kernel, side, n_row),
        out_shape=jax.ShapeDtypeStruct((2 * half, cols), jnp.bfloat16),
        in_specs=specs,
        out_specs=HBM,
        scratch_shapes=[
            pltpu.VMEM((half, cols), jnp.bfloat16),
            pltpu.SemaphoreType.DMA((half // min(256, half),)),
        ],
        input_output_aliases=aliases,
        compiler_params=kernel_params(),
        cost_estimate=NO_COST,
        name="last",
    )(*operands)


class Grid:
    def __init__(self, n_row, n_col):
        side = math.isqrt(n_row)
        self.nx = side if side * side == n_row else n_row
        self.ny = n_row // self.nx
        self.nz, self.nc = n_col // 2, 2
        row, col = lax.axis_index("row"), lax.axis_index("col")
        self.y, self.x = row // self.nx, row % self.nx
        self.z, self.core = col // self.nc, col % self.nc

    def shift(self, value, axis):
        pairs = []
        for y in range(self.ny):
            for x in range(self.nx):
                to = (y, (x + 1) % self.nx) if axis == "x" else ((y + 1) % self.ny, x)
                pairs.append((y * self.nx + x, to[0] * self.nx + to[1]))
        return lax.ppermute(value, "row", pairs)

    def along_z(self, value, route):
        return lax.ppermute(
            value, "col", [(z * self.nc + c, to * self.nc + c) for z, to in route.items() for c in range(self.nc)]
        )

    def twin(self, value):
        return lax.ppermute(
            value, "col", [(z * self.nc + c, z * self.nc + 1 - c) for z in range(self.nz) for c in range(self.nc)]
        )

    def plane(self, upper, lower):
        found = []
        for dy in range(self.ny):
            along = upper, lower
            for dx in range(self.nx):
                found += along
                along = [self.shift(v, "x") for v in along] if dx + 1 < self.nx else along
            if dy + 1 < self.ny:
                upper, lower = self.shift(upper, "y"), self.shift(lower, "y")
        return found

    def plane_sources(self):
        found = [
            ((self.y - dy) % self.ny) * self.nx + (self.x - dx) % self.nx
            for dy in range(self.ny) for dx in range(self.nx)
        ]
        return jnp.stack(found).astype(jnp.int32)

    def around(self, value):
        found = [value]
        for _ in range(self.nz - 1):
            found.append(self.along_z(found[-1], {z: (z + 1) % self.nz for z in range(self.nz)}))
        return found

    def z_owners(self):
        if self.nz == 4:
            return [self.z, self.z ^ 1, 3 - self.z, 3 - (self.z ^ 1)]
        return [(self.z - s) % self.nz for s in range(self.nz)]

    def col_owners(self):
        found = []
        for z in self.z_owners():
            found += [z * self.nc + self.core, z * self.nc + 1 - self.core]
        return jnp.stack(found).astype(jnp.int32)


NEAR = {0: 1, 1: 0, 2: 3, 3: 2}
MIRROR = {0: 3, 1: 2, 2: 1, 3: 0}


def per_device(n_row, n_col, g0_values, g0_pattern, sigma_values, sigma_pairs, sigma_count):
    block_rows, block_cols = g0_pattern.shape
    rows, cols = g0_values.shape
    slots, width = sigma_values.shape[1], sigma_values.shape[2]
    depth = rows * n_row
    grid = Grid(n_row, n_col)
    owners, sources = grid.col_owners(), grid.plane_sources()

    base = jnp.stack([lax.axis_index("row") * block_rows, lax.axis_index("col") * block_cols, sigma_count[0, 0]]).astype(jnp.int32)
    message, tile, upper, lower = prepare(base, g0_values, g0_pattern, sigma_values, sigma_pairs)

    def names(parts, held_by):
        found = jnp.stack([part[slots * width:slots * width + 2, :slots] for part in parts]).astype(jnp.int32)
        row_at = jnp.where(found[:, 0] >= 0, found[:, 0] * width, -1)
        return row_at, held_by[:, None] * cols + found[:, 1] * width

    def dense_rows(parts):
        first = spread(*names(parts[:-2], owners[:-2]), parts[:-2], slots, rows, depth)
        return fill(*names(parts[-2:], owners[-2:]), parts[-2:], first, slots)

    def finish(col_parts, row_parts, ends):
        total, column = close(sources, owners[:-2], col_parts, row_parts)
        result = None
        for side, pair in enumerate(ends):
            result = last(side, owners[-2:], total, column, pair, result)
        return result

    if (grid.ny, grid.nx, grid.nz) != (2, 2, 4):
        sigma_parts = []
        for value in grid.around(message):
            sigma_parts += [value, grid.twin(value)]
        dense = dense_rows(sigma_parts)
        found = grid.plane(upper, lower)
        turned = [turn(side, sources, dense, found) for side in range(2)]
        row_parts = []
        for value in grid.around(tile):
            row_parts += [value, grid.twin(value)]
        ends = [[value[side] for value in row_parts[-2:]] for side in range(2)]
        return finish(grid.plane(*turned), row_parts[:-2], ends)

    with jax.named_scope("slots_far"):
        s_far = grid.along_z(message, MIRROR)
    with jax.named_scope("slots_near"):
        s_near = grid.along_z(message, NEAR)
    with jax.named_scope("g0_x_upper"):
        x_upper = grid.shift(upper, "x")
    with jax.named_scope("g0_y_upper"):
        y_upper = grid.shift(upper, "y")
    with jax.named_scope("slots_twin"):
        s_twin = grid.twin(message)
    with jax.named_scope("g0_x_lower"):
        x_lower = grid.shift(after(lower, x_upper), "x")
    with jax.named_scope("g0_y_lower"):
        y_lower = grid.shift(after(lower, y_upper), "y")
    with jax.named_scope("slots_cross"):
        s_cross = grid.along_z(after(s_far, s_near, x_upper, y_upper), NEAR)
    with jax.named_scope("g0_far"):
        far = grid.along_z(after(tile, s_far, s_near, x_upper, y_upper), MIRROR)
    with jax.named_scope("slots_far_twin"):
        s_far_twin = grid.twin(after(s_far, s_near))
    with jax.named_scope("slots_near_twin"):
        s_near_twin = grid.twin(after(s_near, s_far_twin))
    with jax.named_scope("g0_xy_upper"):
        far_upper = grid.shift(after(x_upper, y_lower), "y")
    with jax.named_scope("g0_xy_lower"):
        far_lower = grid.shift(after(y_lower, x_lower), "x")
    with jax.named_scope("slots_cross_twin"):
        s_cross_twin = grid.twin(after(s_cross, s_near_twin))
    with jax.named_scope("g0_near"):
        near = grid.along_z(after(tile, far, far_upper, far_lower), NEAR)
    dense = dense_rows([message, s_twin, s_near, s_near_twin, s_far, s_far_twin, s_cross, s_cross_twin])
    found = [upper, lower, x_upper, x_lower, y_upper, y_lower, far_upper, far_lower]
    turned = [turn(side, sources, dense, found) for side in range(2)]

    with jax.named_scope("turned_x_upper"):
        x_upper = grid.shift(turned[0], "x")
    with jax.named_scope("turned_y_upper"):
        y_upper = grid.shift(turned[0], "y")
    with jax.named_scope("g0_twin"):
        tile_twin = grid.twin(after(tile, far))
    with jax.named_scope("g0_far_twin"):
        far_twin = grid.twin(after(far, tile_twin))
    with jax.named_scope("g0_cross_upper"):
        cross_upper = grid.along_z(after(far[0], near, x_upper, y_upper), NEAR)
    with jax.named_scope("turned_x_lower"):
        x_lower = grid.shift(after(turned[1], x_upper), "x")
    with jax.named_scope("turned_y_lower"):
        y_lower = grid.shift(after(turned[1], y_upper), "y")
    with jax.named_scope("turned_xy_upper"):
        far_upper = grid.shift(after(x_upper, y_lower, far_twin), "y")
    with jax.named_scope("turned_xy_lower"):
        far_lower = grid.shift(after(y_lower, x_lower, far_twin), "x")
    with jax.named_scope("g0_cross_lower"):
        cross_lower = grid.along_z(after(far[1], cross_upper, far_upper, far_lower), NEAR)
    with jax.named_scope("g0_near_twin"):
        near_twin = grid.twin(near)
    with jax.named_scope("g0_cross_upper_twin"):
        cross_upper_twin = grid.twin(after(cross_upper, near_twin))
    with jax.named_scope("g0_cross_lower_twin"):
        cross_lower_twin = grid.twin(cross_lower)
    ends = [[cross_upper, cross_upper_twin], [cross_lower, cross_lower_twin]]
    col_parts = [*turned, x_upper, x_lower, y_upper, y_lower, far_upper, far_lower]
    return finish(col_parts, [tile, tile_twin, near, near_twin, far, far_twin], ends)


def solution(mesh):
    placed = (
        P("row", "col"),
        P("row", "col"),
        P("row", "col", None, None),
        P("row", "col", None),
        P("row", "col"),
    )
    return jax.shard_map(
        functools.partial(per_device, mesh.shape["row"], mesh.shape["col"]),
        mesh=mesh, in_specs=placed, out_specs=P("row", "col"), check_vma=False,
    )
```

time: 125 us -> 153 us (1.22)
  waiting for transfers between devices: 64.4 us -> 83 us
  starting transfers between devices: 26.5 us -> 41.8 us
  local copies, waits for them, and re-layouts: 10 us -> 1.89 us
  Pallas kernels: 20.8 us -> 23.8 us
    ppermute x8 -> x12, waiting for transfers between devices: 7.81 us -> 29.3 us  [shift(): return lax.ppermute(value, 'row', pairs)]
    ppermute x8 -> x7, starting transfers between devices: 15.5 us -> 27.6 us  [along_z(): lax.ppermute(value, 'col', [(z * self.nc + c, to * self.nc + c) for z, to...]
    squeeze x9 -> x1, local copies, waits for them, and re-layouts: 7.82 us -> 0.07 us  [per_device(): cross_upper = grid.along_z(after(far[0], near, x_upper, y_upper), NEAR)]
    pallas_call x3 -> x6, Pallas kernels: 10.5 us -> 15.9 us  [the longest x2 6.13 us: turn(): pl.pallas_call(functools.partial(turn_kernel, side), out_shape=jax.ShapeD...]
    ppermute x8 -> x12, starting transfers between devices: 9.31 us -> 14.2 us  [shift(): return lax.ppermute(value, 'row', pairs)]
    ppermute x10 -> x9, waiting for transfers between devices: 1.73 us -> 0.02 us  [twin(): lax.ppermute(value, 'col', [(z * self.nc + c, z * self.nc + 1 - c) for z...]
    pallas_call x1, Pallas kernels: 4.64 us -> 2.95 us  [spread(): pl.pallas_call(functools.partial(spread_kernel, len(parts), slots, width)...]
    ppermute x10 -> x9, starting transfers between devices: 1.69 us -> 0.04 us  [twin(): lax.ppermute(value, 'col', [(z * self.nc + c, z * self.nc + 1 - c) for z...]
  transfers between devices with their start and end apart: 26 -> 28, of which waited for: 9 -> 14; matrix products, arithmetic and copies ran while one was open for 7% -> 1% of each run, Pallas kernels for 14% -> 11%
where the time goes in v3:
time: 153 us; the launch traced here: 152 us
  waiting for transfers between devices  83 us (54%)
  starting transfers between devices  41.8 us (27%)
  Pallas kernels  23.8 us (16%)
  local copies, waits for them, and re-layouts  1.89 us (1%)
    ppermute x7, waiting for transfers between devices, along_z(): lax.ppermute(value, 'col', [(z * self.nc + c, to * self.nc + c) for z, to...  53.7 us
    ppermute x12, waiting for transfers between devices, shift(): return lax.ppermute(value, 'row', pairs)  29.3 us
    ppermute x7, starting transfers between devices, along_z(): lax.ppermute(value, 'col', [(z * self.nc + c, to * self.nc + c) for z, to...  27.6 us
    ppermute x12, starting transfers between devices, shift(): return lax.ppermute(value, 'row', pairs)  14.2 us
    pallas_call x2, Pallas kernels, turn(): pl.pallas_call(functools.partial(turn_kernel, side), out_shape=jax.ShapeD...  6.13 us
    pallas_call x1, Pallas kernels, close(): pl.pallas_call(functools.partial(close_kernel, n_col, n_row), out_shape=(...  4.87 us
    pallas_call x1, Pallas kernels, prepare(): pl.pallas_call(functools.partial(prepare_kernel, slots, width), out_shape...  4.57 us
    pallas_call x2, Pallas kernels, last(): pl.pallas_call(functools.partial(last_kernel, side, n_row), out_shape=jax...  3.96 us
  transfers between devices with their start and end apart: 28, of which 14 were waited for; matrix products, arithmetic and copies ran while one was open for 1% of the time, Pallas kernels for 11%

profile of v3, /device:TPU:0, one launch (start us, length us, event | category | flops | bytes accessed | tf_op | source)
XLA Modules:
  0.0 152.2 jit_solution(5167700241205309288)
XLA Ops:
  1.2 4.6 %prepare.1 = (bf16[1552,128]{1,0:T(8,128)(2,1)}, bf16[2,512,512]{2,1,0:T(8,128)(2,1)}, bf16[512,512]{1,0:T(8,128)(2,1)}, bf16[512,512]{1,0:T(8,128)(2,1)}) custom-call(s32[3]{0:T(128)} %pad_add_fusion.2.base_ref, bf16[1024,512]{1,0:T(8,128)(2,1)} %values_ref.1, s32[4,8]{1,0:T(4,128)} %bitcast.60, bf16[1,12,128,128]{3,2,1,0:T(8,128)(2,1)} %slots_ref.1, ...), custom_call_target="tpu_custom_call" | custom-call | tf_op jit(solution)/shard_map/prepare/pallas_call | solution.py:77
  5.8 5.1 %collective-permute-start = (bf16[1552,128]{1,0:T(8,128)(2,1)}, bf16[1552,128]{1,0:T(8,128)(2,1)S(1)}, u32[]{:S(2)}, u32[]{:S(2)}) collective-permute-start(bf16[1552,128]{1,0:T(8,128)(2,1)} %get-tuple-element.30.refs_0_), channel_id=1, source_target_pairs={{0,6},{1,7},{2,4},{3,5},{4,2},{5,3},{6,0},{7,1},{8,14},{9,15},{10,... | collective-permute-start | bytes 1191944 | tf_op jit(solution)/shard_map/slots_far/ppermute | solution.py:299
  12.4 1.5 collective-permute-start.3
  14.9 6.4 %collective-permute-done.refs_4_ = bf16[1552,128]{1,0:T(8,128)(2,1)S(1)} collective-permute-done((bf16[1552,128]{1,0:T(8,128)(2,1)}, bf16[1552,128]{1,0:T(8,128)(2,1)S(1)}, u32[]{:S(2)}, u32[]{:S(2)}) %collective-permute-start) | collective-permute-done | bytes 397344 | tf_op jit(solution)/shard_map/slots_far/ppermute | solution.py:299
  21.3 7.7 %collective-permute-done.1.refs_2_ = bf16[1552,128]{1,0:T(8,128)(2,1)S(1)} collective-permute-done((bf16[1552,128]{1,0:T(8,128)(2,1)}, bf16[1552,128]{1,0:T(8,128)(2,1)S(1)}, u32[]{:S(2)}, u32[]{:S(2)}) %collective-permute-start.1) | collective-permute-done | bytes 397344 | tf_op jit(solution)/shard_map/slots_near/ppermute | solution.py:299
  29.0 1.7 %collective-permute-start.4 = (bf16[1552,128]{1,0:T(8,128)(2,1)S(1)}, bf16[1552,128]{1,0:T(8,128)(2,1)S(1)}, u32[]{:S(2)}, u32[]{:S(2)}) collective-permute-start(bf16[1552,128]{1,0:T(8,128)(2,1)S(1)} %collective-permute-done.refs_4_), channel_id=1, source_target_pairs={{0,2},{1,3},{2,0},{3,1},{4,6},{5,7},{6,4},{7,5},{8,10},{9,11},{10,... | collective-permute-start | bytes 1191944 | tf_op jit(solution)/shard_map/slots_cross/ppermute | solution.py:299
  34.2 6.8 %collective-permute-done.4.refs_0_ = bf16[1552,128]{1,0:T(8,128)(2,1)S(1)} collective-permute-done((bf16[1552,128]{1,0:T(8,128)(2,1)S(1)}, bf16[1552,128]{1,0:T(8,128)(2,1)S(1)}, u32[]{:S(2)}, u32[]{:S(2)}) %collective-permute-start.4) | collective-permute-done | bytes 397344 | tf_op jit(solution)/shard_map/slots_cross/ppermute | solution.py:299
  41.0 5.2 %collective-permute-done.10.refs_5_ = bf16[512,512]{1,0:T(8,128)(2,1)S(1)} collective-permute-done((bf16[512,512]{1,0:T(8,128)(2,1)}, bf16[512,512]{1,0:T(8,128)(2,1)S(1)}, u32[]{:S(2)}, u32[]{:S(2)}) %collective-permute-start.10) | collective-permute-done | bytes 524320 | tf_op jit(solution)/shard_map/g0_y_lower/ppermute | solution.py:296
  48.3 15.0 %collective-permute-done.17.refs_12_ = bf16[2,512,512]{2,1,0:T(8,128)(2,1)S(1)} collective-permute-done((bf16[2,512,512]{2,1,0:T(8,128)(2,1)}, bf16[2,512,512]{2,1,0:T(8,128)(2,1)S(1)}, u32[]{:S(2)}, u32[]{:S(2)}) %collective-permute-start.17) | collective-permute-done | bytes 1048608 | tf_op jit(solution)/shard_map/g0_far/ppermute | solution.py:299
  64.4 2.9 %spread.1.refs_2_ = bf16[1024,4096]{1,0:T(8,128)(2,1)S(1)} custom-call(s32[6,12]{1,0:T(8,128)S(1)} %bitcast.57, s32[6,12]{1,0:T(8,128)S(1)} %bitcast_add_fusion.col_ref, bf16[1552,128]{1,0:T(8,128)(2,1)S(1)} %copy-done.3, bf16[1552,128]{1,0:T(8,128)(2,1)S(1)} %collective-permute-done.8.refs_1_, bf16[1552,128]{1,0:T(8,128)(2,1)S(1)} %collective-permute-done.1.refs_2_, ...), custom_call_target="tpu_custom_call" | custom-call | tf_op jit(solution)/shard_map/spread/pallas_call | solution.py:126
  67.4 18.6 %collective-permute-start.22 = (bf16[2,512,512]{2,1,0:T(8,128)(2,1)S(1)}, bf16[2,512,512]{2,1,0:T(8,128)(2,1)S(1)}, u32[]{:S(2)}, u32[]{:S(2)}) collective-permute-start(bf16[2,512,512]{2,1,0:T(8,128)(2,1)S(1)} %copy-done.2), channel_id=1, source_target_pairs={{0,2},{1,3},{2,0},{3,1},{4,6},{5,7},{6,4},{7,5},{8,10},{9,11},{10,... | collective-permute-start | bytes 3145736 | tf_op jit(solution)/shard_map/g0_near/ppermute | solution.py:299
  87.4 3.1 %turn.2.refs_0_ = bf16[512,512]{1,0:T(8,128)(2,1)S(1)} custom-call(s32[4]{0:T(128)S(1)} %pad_add_fusion.1.source_ref, bf16[1024,4096]{1,0:T(8,128)(2,1)S(1)} %fill.1.dense_ref, bf16[512,512]{1,0:T(8,128)(2,1)S(1)} %copy-done, bf16[512,512]{1,0:T(8,128)(2,1)S(1)} %copy-done.1, bf16[512,512]{1,0:T(8,128)(2,1)S(1)} %collective-permute-done.2.refs_2_, ...), custom_call_target="tpu_custom_call" | custom-call | tf_op jit(solution)/shard_map/turn/pallas_call | solution.py:178
  91.1 1.7 %collective-permute-start.13 = (bf16[512,512]{1,0:T(8,128)(2,1)S(1)}, bf16[512,512]{1,0:T(8,128)(2,1)S(1)}, u32[]{:S(2)}, u32[]{:S(2)}) collective-permute-start(bf16[512,512]{1,0:T(8,128)(2,1)S(1)} %turn.2.refs_0_), channel_id=1, source_target_pairs={{0,8},{8,0},{16,24},{24,16},{1,9},{9,1},{17,25},{25,17},{2,10},{10... | collective-permute-start | bytes 1572872 | tf_op jit(solution)/shard_map/turned_x_upper/ppermute | solution.py:296
  92.7 3.1 %turn.3.refs_1_ = bf16[512,512]{1,0:T(8,128)(2,1)S(1)} custom-call(s32[4]{0:T(128)S(1)} %pad_add_fusion.1.source_ref, bf16[1024,4096]{1,0:T(8,128)(2,1)S(1)} %fill.1.dense_ref, bf16[512,512]{1,0:T(8,128)(2,1)S(1)} %copy-done, bf16[512,512]{1,0:T(8,128)(2,1)S(1)} %copy-done.1, bf16[512,512]{1,0:T(8,128)(2,1)S(1)} %collective-permute-done.2.refs_2_, ...), custom_call_target="tpu_custom_call" | custom-call | tf_op jit(solution)/shard_map/turn/pallas_call | solution.py:178
  95.8 8.8 %collective-permute-done.15.refs_4_ = bf16[512,512]{1,0:T(8,128)(2,1)S(1)} collective-permute-done((bf16[512,512]{1,0:T(8,128)(2,1)S(1)}, bf16[512,512]{1,0:T(8,128)(2,1)S(1)}, u32[]{:S(2)}, u32[]{:S(2)}) %collective-permute-start.15) | collective-permute-done | bytes 524320 | tf_op jit(solution)/shard_map/turned_y_upper/ppermute | solution.py:296
  106.9 2.9 %collective-permute-done.22.refs_10_ = bf16[2,512,512]{2,1,0:T(8,128)(2,1)S(1)} collective-permute-done((bf16[2,512,512]{2,1,0:T(8,128)(2,1)S(1)}, bf16[2,512,512]{2,1,0:T(8,128)(2,1)S(1)}, u32[]{:S(2)}, u32[]{:S(2)}) %collective-permute-start.22) | collective-permute-done | bytes 1048608 | tf_op jit(solution)/shard_map/g0_near/ppermute | solution.py:299
  109.8 1.7 %collective-permute-start.24 = (bf16[512,512]{1,0:T(8,128)(2,1)S(1)}, bf16[512,512]{1,0:T(8,128)(2,1)S(1)}, u32[]{:S(2)}, u32[]{:S(2)}) collective-permute-start(bf16[512,512]{1,0:T(8,128)(2,1)S(1)} %get-tuple-element.52), channel_id=1, source_target_pairs={{0,2},{1,3},{2,0},{3,1},{4,6},{5,7},{6,4},{7,5},{8,10},{9,11},{10,... | collective-permute-start | bytes 1572872 | tf_op jit(solution)/shard_map/g0_cross_upper/ppermute | solution.py:299
  111.5 6.3 %collective-permute-done.16.refs_5_ = bf16[512,512]{1,0:T(8,128)(2,1)S(1)} collective-permute-done((bf16[512,512]{1,0:T(8,128)(2,1)S(1)}, bf16[512,512]{1,0:T(8,128)(2,1)S(1)}, u32[]{:S(2)}, u32[]{:S(2)}) %collective-permute-start.16) | collective-permute-done | bytes 524320 | tf_op jit(solution)/shard_map/turned_y_lower/ppermute | solution.py:296
  120.3 3.2 %collective-permute-done.24.refs_0_ = bf16[512,512]{1,0:T(8,128)(2,1)S(1)} collective-permute-done((bf16[512,512]{1,0:T(8,128)(2,1)S(1)}, bf16[512,512]{1,0:T(8,128)(2,1)S(1)}, u32[]{:S(2)}, u32[]{:S(2)}) %collective-permute-start.24) | collective-permute-done | bytes 524320 | tf_op jit(solution)/shard_map/g0_cross_upper/ppermute | solution.py:299
  123.5 6.6 %collective-permute-done.20.refs_6_ = bf16[512,512]{1,0:T(8,128)(2,1)S(1)} collective-permute-done((bf16[512,512]{1,0:T(8,128)(2,1)S(1)}, bf16[512,512]{1,0:T(8,128)(2,1)S(1)}, u32[]{:S(2)}, u32[]{:S(2)}) %collective-permute-start.20) | collective-permute-done | bytes 524320 | tf_op jit(solution)/shard_map/turned_xy_upper/ppermute | solution.py:296
  131.6 11.7 %collective-permute-done.25.refs_0_ = bf16[512,512]{1,0:T(8,128)(2,1)S(1)} collective-permute-done((bf16[512,512]{1,0:T(8,128)(2,1)S(1)}, bf16[512,512]{1,0:T(8,128)(2,1)S(1)}, u32[]{:S(2)}, u32[]{:S(2)}) %collective-permute-start.25) | collective-permute-done | bytes 524320 | tf_op jit(solution)/shard_map/g0_cross_lower/ppermute | solution.py:299
  143.4 4.9 %close.1 = (f32[2,512,512]{2,1,0:T(8,128)S(1)}, bf16[4096,512]{1,0:T(8,128)(2,1)S(1)}) custom-call(s32[4]{0:T(128)S(1)} %pad_add_fusion.1.source_ref, s32[6]{0:T(128)S(1)} %stack.97.owner_ref, bf16[512,512]{1,0:T(8,128)(2,1)S(1)} %turn.2.refs_0_, bf16[512,512]{1,0:T(8,128)(2,1)S(1)} %turn.3.refs_1_, bf16[512,512]{1,0:T(8,128)(2,1)S(1)} %collective-permute-done.13.refs_2_, ...), custom_call_target="tpu_custom_call" | custom-call | tf_op jit(solution)/shard_map/close/pallas_call | solution.py:219
  148.3 2.0 %last.2.refs_2_ = bf16[1024,512]{1,0:T(8,128)(2,1)} custom-call(s32[2]{0:T(128)S(1)} %get-tuple-element.56.owner_ref, f32[2,512,512]{2,1,0:T(8,128)S(1)} %get-tuple-element.50.total_ref, bf16[4096,512]{1,0:T(8,128)(2,1)S(1)} %get-tuple-element.51.column_ref, bf16[512,512]{1,0:T(8,128)(2,1)S(1)} %collective-permute-done.24.refs_0_, ...), custom_call_target="tpu_custom_call" | custom-call | tf_op jit(solution)/shard_map/last/pallas_call | solution.py:264
  150.3 2.0 %last.3 = bf16[1024,512]{1,0:T(8,128)(2,1)} custom-call(s32[2]{0:T(128)S(1)} %get-tuple-element.56.owner_ref, f32[2,512,512]{2,1,0:T(8,128)S(1)} %get-tuple-element.50.total_ref, bf16[4096,512]{1,0:T(8,128)(2,1)S(1)} %get-tuple-element.51.column_ref, bf16[512,512]{1,0:T(8,128)(2,1)S(1)} %collective-permute-done.25.refs_0_, ...), custom_call_target="tpu_custom_call", output_to_operand_aliasing={{}: (5, {})} | custom-call | tf_op jit(solution)/shard_map/last/pallas_call | solution.py:264
  (69 shorter events, 18.0 us)
Async XLA Ops:
  5.8 15.4 %collective-permute-start = (bf16[1552,128]{1,0:T(8,128)(2,1)}, bf16[1552,128]{1,0:T(8,128)(2,1)S(1)}, u32[]{:S(2)}, u32[]{:S(2)}) collective-permute-start(bf16[1552,128]{1,0:T(8,128)(2,1)} %get-tuple-element.30.refs_0_), channel_id=1, source_target_pairs={{0,6},{1,7},{2,4},{3,5},{4,2},{5,3},{6,0},{7,1},{8,14},{9,15},{10,... | collective-permute-start | bytes 1191944 | tf_op jit(solution)/shard_map/slots_far/ppermute | solution.py:299
  10.9 18.0 %collective-permute-start.1 = (bf16[1552,128]{1,0:T(8,128)(2,1)}, bf16[1552,128]{1,0:T(8,128)(2,1)S(1)}, u32[]{:S(2)}, u32[]{:S(2)}) collective-permute-start(bf16[1552,128]{1,0:T(8,128)(2,1)} %get-tuple-element.30.refs_0_), channel_id=1, source_target_pairs={{0,2},{1,3},{2,0},{3,1},{4,6},{5,7},{6,4},{7,5},{8,10},{9,11},{10,... | collective-permute-start | bytes 1191944 | tf_op jit(solution)/shard_map/slots_near/ppermute | solution.py:299
  10.9 18.0 %collective-permute-start.2 = (bf16[512,512]{1,0:T(8,128)(2,1)}, bf16[512,512]{1,0:T(8,128)(2,1)S(1)}, u32[]{:S(2)}, u32[]{:S(2)}) collective-permute-start(bf16[512,512]{1,0:T(8,128)(2,1)} %get-tuple-element.31.refs_0_), channel_id=1, source_target_pairs={{0,8},{8,0},{16,24},{24,16},{1,9},{9,1},{17,25},{25,17},{2,10},{10... | collective-permute-start | bytes 1572872 | tf_op jit(solution)/shard_map/g0_x_upper/ppermute | solution.py:296
  12.4 16.6 %collective-permute-start.3 = (bf16[512,512]{1,0:T(8,128)(2,1)}, bf16[512,512]{1,0:T(8,128)(2,1)S(1)}, u32[]{:S(2)}, u32[]{:S(2)}) collective-permute-start(bf16[512,512]{1,0:T(8,128)(2,1)} %get-tuple-element.31.refs_0_), channel_id=1, source_target_pairs={{0,16},{8,24},{16,0},{24,8},{1,17},{9,25},{17,1},{25,9},{2,18},{10... | collective-permute-start | bytes 1572872 | tf_op jit(solution)/shard_map/g0_y_upper/ppermute | solution.py:296
  14.0 19.8 %collective-permute-start.8 = (bf16[1552,128]{1,0:T(8,128)(2,1)}, bf16[1552,128]{1,0:T(8,128)(2,1)S(1)}, u32[]{:S(2)}, u32[]{:S(2)}) collective-permute-start(bf16[1552,128]{1,0:T(8,128)(2,1)} %get-tuple-element.30.refs_0_), channel_id=1, source_target_pairs={{0,1},{1,0},{2,3},{3,2},{4,5},{5,4},{6,7},{7,6},{8,9},{9,8},{10,11... | collective-permute-start | bytes 1191944 | tf_op jit(solution)/shard_map/slots_twin/ppermute | solution.py:304
  30.7 17.0 %collective-permute-start.9 = (bf16[512,512]{1,0:T(8,128)(2,1)}, bf16[512,512]{1,0:T(8,128)(2,1)S(1)}, u32[]{:S(2)}, u32[]{:S(2)}) collective-permute-start(bf16[512,512]{1,0:T(8,128)(2,1)} %get-tuple-element.38.refs_1_), channel_id=1, source_target_pairs={{0,8},{8,0},{16,24},{24,16},{1,9},{9,1},{17,25},{25,17},{2,10},{10... | collective-permute-start | bytes 1572872 | tf_op jit(solution)/shard_map/g0_x_lower/ppermute | solution.py:296
  32.2 14.0 %collective-permute-start.10 = (bf16[512,512]{1,0:T(8,128)(2,1)}, bf16[512,512]{1,0:T(8,128)(2,1)S(1)}, u32[]{:S(2)}, u32[]{:S(2)}) collective-permute-start(bf16[512,512]{1,0:T(8,128)(2,1)} %get-tuple-element.38.refs_1_), channel_id=1, source_target_pairs={{0,16},{8,24},{16,0},{24,8},{1,17},{9,25},{17,1},{25,9},{2,18},{10... | collective-permute-start | bytes 1572872 | tf_op jit(solution)/shard_map/g0_y_lower/ppermute | solution.py:296
  33.8 29.5 %collective-permute-start.17 = (bf16[2,512,512]{2,1,0:T(8,128)(2,1)}, bf16[2,512,512]{2,1,0:T(8,128)(2,1)S(1)}, u32[]{:S(2)}, u32[]{:S(2)}) collective-permute-start(bf16[2,512,512]{2,1,0:T(8,128)(2,1)} %get-tuple-element.49.refs_8_), channel_id=1, source_target_pairs={{0,6},{1,7},{2,4},{3,5},{4,2},{5,3},{6,0},{7,1},{8,14},{9,15},{10,... | collective-permute-start | bytes 3145736 | tf_op jit(solution)/shard_map/g0_far/ppermute | solution.py:299
  34.2 14.1 %collective-permute-start.6 = (bf16[1552,128]{1,0:T(8,128)(2,1)S(1)}, bf16[1552,128]{1,0:T(8,128)(2,1)S(1)}, u32[]{:S(2)}, u32[]{:S(2)}) collective-permute-start(bf16[1552,128]{1,0:T(8,128)(2,1)S(1)} %collective-permute-done.1.refs_2_), channel_id=1, source_target_pairs={{0,1},{1,0},{2,3},{3,2},{4,5},{5,4},{6,7},{7,6},{8,9},{9,8},{10,11... | collective-permute-start | bytes 1191944 | tf_op jit(solution)/shard_map/slots_near_twin/ppermute | solution.py:304
  46.2 21.1 %collective-permute-start.11 = (bf16[512,512]{1,0:T(8,128)(2,1)S(1)}, bf16[512,512]{1,0:T(8,128)(2,1)S(1)}, u32[]{:S(2)}, u32[]{:S(2)}) collective-permute-start(bf16[512,512]{1,0:T(8,128)(2,1)S(1)} %collective-permute-done.2.refs_2_), channel_id=1, source_target_pairs={{0,16},{8,24},{16,0},{24,8},{1,17},{9,25},{17,1},{25,9},{2,18},{10... | collective-permute-start | bytes 1572872 | tf_op jit(solution)/shard_map/g0_xy_upper/ppermute | solution.py:296
  47.7 19.6 %collective-permute-start.12 = (bf16[512,512]{1,0:T(8,128)(2,1)S(1)}, bf16[512,512]{1,0:T(8,128)(2,1)S(1)}, u32[]{:S(2)}, u32[]{:S(2)}) collective-permute-start(bf16[512,512]{1,0:T(8,128)(2,1)S(1)} %collective-permute-done.10.refs_5_), channel_id=1, source_target_pairs={{0,8},{8,0},{16,24},{24,16},{1,9},{9,1},{17,25},{25,17},{2,10},{10... | collective-permute-start | bytes 1572872 | tf_op jit(solution)/shard_map/g0_xy_lower/ppermute | solution.py:296
  48.3 37.7 %collective-permute-start.7 = (bf16[1552,128]{1,0:T(8,128)(2,1)S(1)}, bf16[1552,128]{1,0:T(8,128)(2,1)S(1)}, u32[]{:S(2)}, u32[]{:S(2)}) collective-permute-start(bf16[1552,128]{1,0:T(8,128)(2,1)S(1)} %collective-permute-done.4.refs_0_), channel_id=1, source_target_pairs={{0,1},{1,0},{2,3},{3,2},{4,5},{5,4},{6,7},{7,6},{8,9},{9,8},{10,11... | collective-permute-start | bytes 1191944 | tf_op jit(solution)/shard_map/slots_cross_twin/ppermute | solution.py:304
  63.3 27.8 %collective-permute-start.18 = (bf16[2,512,512]{2,1,0:T(8,128)(2,1)}, bf16[2,512,512]{2,1,0:T(8,128)(2,1)S(1)}, u32[]{:S(2)}, u32[]{:S(2)}) collective-permute-start(bf16[2,512,512]{2,1,0:T(8,128)(2,1)} %get-tuple-element.49.refs_8_), channel_id=1, source_target_pairs={{0,1},{1,0},{2,3},{3,2},{4,5},{5,4},{6,7},{7,6},{8,9},{9,8},{10,11... | collective-permute-start | bytes 3145736 | tf_op jit(solution)/shard_map/g0_twin/ppermute | solution.py:304
  67.4 42.4 %collective-permute-start.22 = (bf16[2,512,512]{2,1,0:T(8,128)(2,1)S(1)}, bf16[2,512,512]{2,1,0:T(8,128)(2,1)S(1)}, u32[]{:S(2)}, u32[]{:S(2)}) collective-permute-start(bf16[2,512,512]{2,1,0:T(8,128)(2,1)S(1)} %copy-done.2), channel_id=1, source_target_pairs={{0,2},{1,3},{2,0},{3,1},{4,6},{5,7},{6,4},{7,5},{8,10},{9,11},{10,... | collective-permute-start | bytes 3145736 | tf_op jit(solution)/shard_map/g0_near/ppermute | solution.py:299
  90.5 14.1 %collective-permute-start.15 = (bf16[512,512]{1,0:T(8,128)(2,1)S(1)}, bf16[512,512]{1,0:T(8,128)(2,1)S(1)}, u32[]{:S(2)}, u32[]{:S(2)}) collective-permute-start(bf16[512,512]{1,0:T(8,128)(2,1)S(1)} %turn.2.refs_0_), channel_id=1, source_target_pairs={{0,16},{8,24},{16,0},{24,8},{1,17},{9,25},{17,1},{25,9},{2,18},{10... | collective-permute-start | bytes 1572872 | tf_op jit(solution)/shard_map/turned_y_upper/ppermute | solution.py:296
  91.1 26.7 %collective-permute-start.19 = (bf16[2,512,512]{2,1,0:T(8,128)(2,1)S(1)}, bf16[2,512,512]{2,1,0:T(8,128)(2,1)S(1)}, u32[]{:S(2)}, u32[]{:S(2)}) collective-permute-start(bf16[2,512,512]{2,1,0:T(8,128)(2,1)S(1)} %collective-permute-done.17.refs_12_), channel_id=1, source_target_pairs={{0,1},{1,0},{2,3},{3,2},{4,5},{5,4},{6,7},{7,6},{8,9},{9,8},{10,11... | collective-permute-start | bytes 3145736 | tf_op jit(solution)/shard_map/g0_far_twin/ppermute | solution.py:304
  91.1 14.3 %collective-permute-start.13 = (bf16[512,512]{1,0:T(8,128)(2,1)S(1)}, bf16[512,512]{1,0:T(8,128)(2,1)S(1)}, u32[]{:S(2)}, u32[]{:S(2)}) collective-permute-start(bf16[512,512]{1,0:T(8,128)(2,1)S(1)} %turn.2.refs_0_), channel_id=1, source_target_pairs={{0,8},{8,0},{16,24},{24,16},{1,9},{9,1},{17,25},{25,17},{2,10},{10... | collective-permute-start | bytes 1572872 | tf_op jit(solution)/shard_map/turned_x_upper/ppermute | solution.py:296
  104.6 13.2 %collective-permute-start.16 = (bf16[512,512]{1,0:T(8,128)(2,1)S(1)}, bf16[512,512]{1,0:T(8,128)(2,1)S(1)}, u32[]{:S(2)}, u32[]{:S(2)}) collective-permute-start(bf16[512,512]{1,0:T(8,128)(2,1)S(1)} %turn.3.refs_1_), channel_id=1, source_target_pairs={{0,16},{8,24},{16,0},{24,8},{1,17},{9,25},{17,1},{25,9},{2,18},{10... | collective-permute-start | bytes 1572872 | tf_op jit(solution)/shard_map/turned_y_lower/ppermute | solution.py:296
  105.4 13.6 %collective-permute-start.14 = (bf16[512,512]{1,0:T(8,128)(2,1)S(1)}, bf16[512,512]{1,0:T(8,128)(2,1)S(1)}, u32[]{:S(2)}, u32[]{:S(2)}) collective-permute-start(bf16[512,512]{1,0:T(8,128)(2,1)S(1)} %turn.3.refs_1_), channel_id=1, source_target_pairs={{0,8},{8,0},{16,24},{24,16},{1,9},{9,1},{17,25},{25,17},{2,10},{10... | collective-permute-start | bytes 1572872 | tf_op jit(solution)/shard_map/turned_x_lower/ppermute | solution.py:296
  109.8 13.8 %collective-permute-start.24 = (bf16[512,512]{1,0:T(8,128)(2,1)S(1)}, bf16[512,512]{1,0:T(8,128)(2,1)S(1)}, u32[]{:S(2)}, u32[]{:S(2)}) collective-permute-start(bf16[512,512]{1,0:T(8,128)(2,1)S(1)} %get-tuple-element.52), channel_id=1, source_target_pairs={{0,2},{1,3},{2,0},{3,1},{4,6},{5,7},{6,4},{7,5},{8,10},{9,11},{10,... | collective-permute-start | bytes 1572872 | tf_op jit(solution)/shard_map/g0_cross_upper/ppermute | solution.py:299
  111.5 20.1 %collective-permute-start.23 = (bf16[2,512,512]{2,1,0:T(8,128)(2,1)S(1)}, bf16[2,512,512]{2,1,0:T(8,128)(2,1)S(1)}, u32[]{:S(2)}, u32[]{:S(2)}) collective-permute-start(bf16[2,512,512]{2,1,0:T(8,128)(2,1)S(1)} %collective-permute-done.22.refs_10_), channel_id=1, source_target_pairs={{0,1},{1,0},{2,3},{3,2},{4,5},{5,4},{6,7},{7,6},{8,9},{9,8},{10,11... | collective-permute-start | bytes 3145736 | tf_op jit(solution)/shard_map/g0_near_twin/ppermute | solution.py:304
  117.8 12.3 %collective-permute-start.20 = (bf16[512,512]{1,0:T(8,128)(2,1)S(1)}, bf16[512,512]{1,0:T(8,128)(2,1)S(1)}, u32[]{:S(2)}, u32[]{:S(2)}) collective-permute-start(bf16[512,512]{1,0:T(8,128)(2,1)S(1)} %collective-permute-done.13.refs_2_), channel_id=1, source_target_pairs={{0,16},{8,24},{16,0},{24,8},{1,17},{9,25},{17,1},{25,9},{2,18},{10... | collective-permute-start | bytes 1572872 | tf_op jit(solution)/shard_map/turned_xy_upper/ppermute | solution.py:296
  119.0 12.7 %collective-permute-start.21 = (bf16[512,512]{1,0:T(8,128)(2,1)S(1)}, bf16[512,512]{1,0:T(8,128)(2,1)S(1)}, u32[]{:S(2)}, u32[]{:S(2)}) collective-permute-start(bf16[512,512]{1,0:T(8,128)(2,1)S(1)} %collective-permute-done.16.refs_5_), channel_id=1, source_target_pairs={{0,8},{8,0},{16,24},{24,16},{1,9},{9,1},{17,25},{25,17},{2,10},{10... | collective-permute-start | bytes 1572872 | tf_op jit(solution)/shard_map/turned_xy_lower/ppermute | solution.py:296
  131.6 16.6 %collective-permute-start.27 = (bf16[512,512]{1,0:T(8,128)(2,1)S(1)}, bf16[512,512]{1,0:T(8,128)(2,1)S(1)}, u32[]{:S(2)}, u32[]{:S(2)}) collective-permute-start(bf16[512,512]{1,0:T(8,128)(2,1)S(1)} %collective-permute-done.24.refs_0_), channel_id=1, source_target_pairs={{0,1},{1,0},{2,3},{3,2},{4,5},{5,4},{6,7},{7,6},{8,9},{9,8},{10,11... | collective-permute-start | bytes 1572872 | tf_op jit(solution)/shard_map/g0_cross_upper_twin/ppermute | solution.py:304
  (8 other events, 101.0 us)

commit v4 on v3

v4 whole, which is shorter than its diff:
```python
import functools
import math

import jax
import jax.numpy as jnp
from jax import lax
from jax.experimental import pallas as pl
from jax.experimental.pallas import tpu as pltpu
from jax.sharding import PartitionSpec as P

VMEM_BYTES = 30 * 1024 * 1024
FIRST_VMEM_BYTES = 60 * 1024 * 1024
ANY = pl.BlockSpec(memory_space=pl.ANY)
HBM = pl.BlockSpec(memory_space=pltpu.HBM)
SMEM = pl.BlockSpec(memory_space=pltpu.SMEM)
VMEM = pl.BlockSpec(memory_space=pltpu.VMEM)
TAIL = 16
NO_COST = pl.CostEstimate(flops=0, bytes_accessed=0, transcendentals=0)


def kernel_params():
    return pltpu.CompilerParams(vmem_limit_bytes=VMEM_BYTES)


def after(value, *earlier):
    return lax.optimization_barrier((value, *earlier))[0]


def prepare_kernel(
    slots, width, base_ref, values_ref, pattern_ref, slots_ref, pairs_ref,
    message_ref, tile_ref,
    pattern, values, message, pairs, names, small_sems, slot_sem, in_sems, tile_sems, out_sem,
):
    block_cols, block_rows = pattern_ref.shape
    half = block_rows // 2
    small = [
        pltpu.make_async_copy(pairs_ref, pairs, small_sems.at[0]),
        pltpu.make_async_copy(pattern_ref, pattern, small_sems.at[1]),
    ]
    take = pltpu.make_async_copy(slots_ref.at[0], message.at[pl.ds(0, slots)], slot_sem)
    fetches = [
        pltpu.make_async_copy(values_ref.at[pl.ds(a * width, width)], values.at[a], in_sems.at[a])
        for a in range(block_rows)
    ]
    for move in small + [take] + fetches:
        move.start()
    for move in small:
        move.wait()
    shape = pairs.shape
    first = lax.broadcasted_iota(jnp.int32, shape, 0) == 0
    local = pairs[...] - jnp.where(first, base_ref[0], base_ref[1])
    live = lax.broadcasted_iota(jnp.int32, shape, 1) < base_ref[2]
    names[...] = jnp.full(names.shape, -1, jnp.int32)
    names[pl.ds(0, shape[0]), pl.ds(0, shape[1])] = jnp.where(live, local, -1)
    message[slots, pl.ds(0, TAIL), :] = names[...].astype(jnp.float32).astype(jnp.bfloat16)
    take.wait()
    gives = [
        pltpu.make_async_copy(message.at[s], message_ref.at[pl.ds(s * width, width)], out_sem.at[s]) for s in range(slots)
    ]
    gives.append(
        pltpu.make_async_copy(
            message.at[slots, pl.ds(0, TAIL)], message_ref.at[pl.ds(slots * width, TAIL)], out_sem.at[slots]
        )
    )
    for move in gives:
        move.start()
    for a in range(block_rows):
        fetches[a].wait()
        for b in range(block_cols):
            keep = pattern[b:b + 1, a:a + 1].astype(jnp.float32)
            keep = jnp.broadcast_to(keep, (width, width)).astype(jnp.bfloat16)
            at = pl.ds(b * width, width)
            values[a, :, at] = values[a, :, at] * keep
        at = pl.ds((a % half) * width, width)
        gives.append(pltpu.make_async_copy(values.at[a], tile_ref.at[a // half, at], tile_sems.at[a]))
        gives[-1].start()
    for move in gives:
        move.wait()


def prepare(base, g0_values, g0_pattern, sigma_values, sigma_pairs):
    rows, cols = g0_values.shape
    block_rows = g0_pattern.shape[0]
    slots, width = sigma_values.shape[1], sigma_values.shape[2]
    return pl.pallas_call(
        functools.partial(prepare_kernel, slots, width),
        out_shape=(
            jax.ShapeDtypeStruct((slots * width + TAIL, width), jnp.bfloat16),
            jax.ShapeDtypeStruct((2, rows // 2, cols), jnp.bfloat16),
        ),
        in_specs=[SMEM] + [HBM] * 4,
        out_specs=(HBM, HBM),
        scratch_shapes=[
            pltpu.VMEM((g0_pattern.shape[1], block_rows), jnp.int32),
            pltpu.VMEM((block_rows, width, cols), jnp.bfloat16),
            pltpu.VMEM((slots + 1, width, width), jnp.bfloat16),
            pltpu.VMEM((2, slots), jnp.int32),
            pltpu.VMEM((TAIL, width), jnp.int32),
            pltpu.SemaphoreType.DMA((2,)),
            pltpu.SemaphoreType.DMA,
            pltpu.SemaphoreType.DMA((block_rows,)),
            pltpu.SemaphoreType.DMA((block_rows,)),
            pltpu.SemaphoreType.DMA((slots + 1,)),
        ],
        compiler_params=pltpu.CompilerParams(vmem_limit_bytes=FIRST_VMEM_BYTES),
        cost_estimate=NO_COST,
        name="prepare",
    )(base, g0_values, g0_pattern.T, sigma_values, sigma_pairs[0].T)


def place_slots(slots, width, row_ref, col_ref, parts, dense_ref, spare, sem):
    for i, part in enumerate(parts):
        for s in range(slots):
            source = part.at[pl.ds(s * width, width)]
            row, col = row_ref[i, s], col_ref[i, s]

            @pl.when(row >= 0)
            def _():
                target = dense_ref.at[pl.ds(pl.multiple_of(row, width), width), pl.ds(pl.multiple_of(col, width), width)]
                pltpu.make_async_copy(source, target, sem.at[i]).start()

            @pl.when(row < 0)
            def _():
                pltpu.make_async_copy(source, spare.at[pl.ds(s * width, width)], sem.at[i]).start()
    for i, part in enumerate(parts):
        pltpu.make_async_copy(part.at[pl.ds(0, slots * width)], spare, sem.at[i]).wait()


def spread_kernel(count, slots, width, row_ref, col_ref, *refs):
    parts, (dense_ref, spare, sem) = refs[:count], refs[count:]
    dense_ref[...] = jnp.zeros_like(dense_ref)
    place_slots(slots, width, row_ref, col_ref, parts, dense_ref, spare, sem)


def spread(row_at, col_at, parts, slots, rows, depth):
    width = parts[0].shape[1]
    return pl.pallas_call(
        functools.partial(spread_kernel, len(parts), slots, width),
        out_shape=jax.ShapeDtypeStruct((rows, depth), jnp.bfloat16),
        in_specs=[SMEM, SMEM] + [ANY] * len(parts),
        out_specs=VMEM,
        scratch_shapes=[pltpu.VMEM((slots * width, width), jnp.bfloat16), pltpu.SemaphoreType.DMA((len(parts),))],
        compiler_params=kernel_params(),
        cost_estimate=NO_COST,
        name="spread",
    )(row_at, col_at, *parts)


def fill_kernel(count, slots, width, row_ref, col_ref, *refs):
    parts, (_, dense_ref, spare, sem) = refs[:count], refs[count:]
    place_slots(slots, width, row_ref, col_ref, parts, dense_ref, spare, sem)


def fill(row_at, col_at, parts, dense, slots):
    width = parts[0].shape[1]
    return pl.pallas_call(
        functools.partial(fill_kernel, len(parts), slots, width),
        out_shape=jax.ShapeDtypeStruct(dense.shape, dense.dtype),
        in_specs=[SMEM, SMEM] + [ANY] * (len(parts) + 1),
        out_specs=ANY,
        scratch_shapes=[pltpu.VMEM((slots * width, width), jnp.bfloat16), pltpu.SemaphoreType.DMA((len(parts),))],
        input_output_aliases={2 + len(parts): 0},
        compiler_params=kernel_params(),
        cost_estimate=NO_COST,
        name="fill",
    )(row_at, col_at, *parts, dense)


def half_refs(refs):
    found = []
    for ref in refs:
        found += [ref.at[0], ref.at[1]] if len(ref.shape) == 3 else [ref]
    return found


def turn_kernel(source_ref, dense_ref, *refs):
    parts, out_ref = half_refs(refs[:-1]), refs[-1]
    _, half, cols = out_ref.shape
    tile = min(256, half)
    for side in range(2):
        @pl.loop(0, half // tile)
        def _(t):
            at = pl.multiple_of(t * tile, tile)
            total = jnp.zeros((tile, cols), jnp.float32)
            for i, part in enumerate(parts):
                start = pl.multiple_of(source_ref[i // 2] * (2 * half) + (i % 2) * half, half)
                total += jnp.dot(
                    dense_ref[pl.ds(side * half + at, tile), pl.ds(start, half)], part[...],
                    preferred_element_type=jnp.float32,
                )
            out_ref[side, pl.ds(at, tile), :] = total.astype(jnp.bfloat16)


def turn(sources, dense, parts):
    _, half, cols = parts[0].shape
    return pl.pallas_call(
        turn_kernel,
        out_shape=jax.ShapeDtypeStruct((2, half, cols), jnp.bfloat16),
        in_specs=[SMEM] + [VMEM] * (1 + len(parts)),
        out_specs=VMEM,
        compiler_params=kernel_params(),
        cost_estimate=NO_COST,
        name="turn",
    )(sources, dense, *parts)


def add_products(total, owner_ref, lead, parts, column_ref):
    cols = parts[0].shape[-1]
    for i, part in enumerate(parts):
        start = pl.multiple_of(owner_ref[lead + i] * cols, cols)
        total += jnp.dot(part, column_ref[pl.ds(start, cols), :], preferred_element_type=jnp.float32)
    return total


def close_kernel(n_col, groups, source_ref, owner_ref, *refs):
    col_refs, row_refs = half_refs(refs[:n_col]), refs[n_col:-3]
    total_ref, column_ref, sem = refs[-3:]
    _, half, _ = row_refs[0].shape

    def column_copy(i):
        start = pl.multiple_of(source_ref[i // 2] * (2 * half) + (i % 2) * half, half)
        return pltpu.make_async_copy(col_refs[i], column_ref.at[pl.ds(start, half)], sem.at[i])

    for i in range(len(col_refs)):
        column_copy(i).start()
    for i in range(len(col_refs)):
        column_copy(i).wait()
    tile = min(256, half)

    def add_group(lead, size):
        for side in range(2):
            @pl.loop(0, half // tile)
            def _(t):
                at = pl.ds(pl.multiple_of(t * tile, tile), tile)
                if lead == 0:
                    total = row_refs[0][side, at, :].astype(jnp.float32)
                else:
                    total = total_ref[side, at, :]
                parts = [part[side, at, :] for part in row_refs[lead:lead + size]]
                total_ref[side, at, :] = add_products(total, owner_ref, lead, parts, column_ref)

    lead = 0
    for size in groups:
        if lead == 0:
            add_group(lead, size)
        else:
            pl.when(owner_ref[lead] >= 0)(functools.partial(add_group, lead, size))
        lead += size


def close(sources, owners, col_parts, groups):
    row_parts = [part for group in groups for part in group]
    _, half, cols = row_parts[0].shape
    n_col = len(col_parts)
    n_half = sum(part.ndim - 1 for part in col_parts)
    return pl.pallas_call(
        functools.partial(close_kernel, n_col, [len(group) for group in groups]),
        out_shape=(
            jax.ShapeDtypeStruct((2, half, cols), jnp.float32),
            jax.ShapeDtypeStruct((n_half * half, cols), jnp.bfloat16),
        ),
        in_specs=[SMEM, SMEM] + [ANY] * n_col + [VMEM] * len(row_parts),
        out_specs=(VMEM, VMEM),
        scratch_shapes=[pltpu.SemaphoreType.DMA((n_half,))],
        compiler_params=kernel_params(),
        cost_estimate=NO_COST,
        name="close",
    )(sources, owners, *col_parts, *row_parts)


def last_kernel(n_row, owner_ref, total_ref, column_ref, *refs):
    row_refs, out_ref, result, sem = refs[:n_row], refs[-3], refs[-2], refs[-1]
    _, half, _ = row_refs[0].shape
    tile = min(256, half)
    moves = []
    for side in range(2):
        for t in range(half // tile):
            at = pl.ds(t * tile, tile)

            @pl.when(owner_ref[0] >= 0)
            def _():
                parts = [part[side, at, :] for part in row_refs]
                total = add_products(total_ref[side, at, :], owner_ref, 0, parts, column_ref)
                result[side, at, :] = total.astype(jnp.bfloat16)

            @pl.when(owner_ref[0] < 0)
            def _():
                result[side, at, :] = total_ref[side, at, :].astype(jnp.bfloat16)

            target = out_ref.at[pl.ds(side * half + t * tile, tile)]
            moves.append(pltpu.make_async_copy(result.at[side, at], target, sem.at[len(moves)]))
            moves[-1].start()
    for move in moves:
        move.wait()


def last(owners, total, column, row_parts):
    _, half, cols = row_parts[0].shape
    n_row = len(row_parts)
    return pl.pallas_call(
        functools.partial(last_kernel, n_row),
        out_shape=jax.ShapeDtypeStruct((2 * half, cols), jnp.bfloat16),
        in_specs=[SMEM] + [VMEM] * (2 + n_row),
        out_specs=HBM,
        scratch_shapes=[
            pltpu.VMEM((2, half, cols), jnp.bfloat16),
            pltpu.SemaphoreType.DMA((2 * half // min(256, half),)),
        ],
        compiler_params=kernel_params(),
        cost_estimate=NO_COST,
        name="last",
    )(owners, total, column, *row_parts)


class Grid:
    def __init__(self, n_row, n_col):
        side = math.isqrt(n_row)
        self.nx = side if side * side == n_row else n_row
        self.ny = n_row // self.nx
        self.nz, self.nc = n_col // 2, 2
        row, col = lax.axis_index("row"), lax.axis_index("col")
        self.y, self.x = row // self.nx, row % self.nx
        self.z, self.core = col // self.nc, col % self.nc

    def shift(self, value, axis):
        pairs = []
        for y in range(self.ny):
            for x in range(self.nx):
                to = (y, (x + 1) % self.nx) if axis == "x" else ((y + 1) % self.ny, x)
                pairs.append((y * self.nx + x, to[0] * self.nx + to[1]))
        return lax.ppermute(value, "row", pairs)

    def along_z(self, value, route):
        return lax.ppermute(
            value, "col", [(z * self.nc + c, to * self.nc + c) for z, to in route.items() for c in range(self.nc)]
        )

    def twin(self, value):
        return lax.ppermute(
            value, "col", [(z * self.nc + c, z * self.nc + 1 - c) for z in range(self.nz) for c in range(self.nc)]
        )

    def plane(self, tile):
        found = []
        for dy in range(self.ny):
            along = tile
            for dx in range(self.nx):
                found.append(along)
                along = self.shift(along, "x") if dx + 1 < self.nx else along
            tile = self.shift(tile, "y") if dy + 1 < self.ny else tile
        return found

    def plane_sources(self):
        found = [
            ((self.y - dy) % self.ny) * self.nx + (self.x - dx) % self.nx
            for dy in range(self.ny) for dx in range(self.nx)
        ]
        return jnp.stack(found).astype(jnp.int32)

    def around(self, value):
        found = [value]
        for _ in range(self.nz - 1):
            found.append(self.along_z(found[-1], {z: (z + 1) % self.nz for z in range(self.nz)}))
        return found

    def col_owners(self, *held):
        found = []
        for z in held:
            found += [jnp.where(z >= 0, z * self.nc + core, -1) for core in (self.core, 1 - self.core)]
        return jnp.stack(found).astype(jnp.int32)


NEAR = {0: 1, 1: 0, 2: 3, 3: 2}
MIRROR = {0: 3, 1: 2, 2: 1, 3: 0}
MIDDLE = {0: 0, 1: 2, 2: 1, 3: 3}


def per_device(n_row, n_col, g0_values, g0_pattern, sigma_values, sigma_pairs, sigma_count):
    block_rows, block_cols = g0_pattern.shape
    rows, cols = g0_values.shape
    slots, width = sigma_values.shape[1], sigma_values.shape[2]
    depth = rows * n_row
    grid = Grid(n_row, n_col)
    sources = grid.plane_sources()
    z = grid.z
    base = jnp.stack([lax.axis_index("row") * block_rows, lax.axis_index("col") * block_cols, sigma_count[0, 0]])
    message, tile = prepare(base.astype(jnp.int32), g0_values, g0_pattern, sigma_values, sigma_pairs)

    def names(parts, held_by):
        found = jnp.stack([part[slots * width:slots * width + 2, :slots] for part in parts]).astype(jnp.int32)
        row_at = jnp.where(found[:, 0] >= 0, found[:, 0] * width, -1)
        return row_at, held_by[:, None] * cols + found[:, 1] * width

    def dense_rows(owners, parts):
        first = spread(*names(parts[:-2], owners[:-2]), parts[:-2], slots, rows, depth)
        return fill(*names(parts[-2:], owners[-2:]), parts[-2:], first, slots)

    if (grid.ny, grid.nx, grid.nz) != (2, 2, 4):
        owners = grid.col_owners(*[(z - s) % grid.nz for s in range(grid.nz)])
        sigma_parts = []
        for value in grid.around(message):
            sigma_parts += [value, grid.twin(value)]
        turned = turn(sources, dense_rows(owners, sigma_parts), grid.plane(tile))
        row_parts = []
        for value in grid.around(tile):
            row_parts += [value, grid.twin(value)]
        total, column = close(sources, owners[:-2], grid.plane(turned), [row_parts[:-2]])
        return last(owners[-2:], total, column, row_parts[-2:])

    with jax.named_scope("slots_far"):
        s_far = grid.along_z(message, MIRROR)
    with jax.named_scope("slots_near"):
        s_near = grid.along_z(message, NEAR)
    with jax.named_scope("g0_x"):
        by_x = grid.shift(tile, "x")
    with jax.named_scope("g0_y"):
        by_y = grid.shift(tile, "y")
    with jax.named_scope("slots_twin"):
        s_twin = grid.twin(message)
    with jax.named_scope("slots_cross"):
        s_cross = grid.along_z(after(s_far, s_near), NEAR)
    with jax.named_scope("slots_far_twin"):
        s_far_twin = grid.twin(after(s_far, s_near))
    with jax.named_scope("slots_near_twin"):
        s_near_twin = grid.twin(after(s_near, s_far_twin))
    with jax.named_scope("g0_near"):
        near = grid.along_z(after(tile, s_far_twin, s_near_twin), NEAR)
    with jax.named_scope("g0_middle"):
        middle = grid.along_z(after(tile, s_far_twin, s_near_twin), MIDDLE)
    with jax.named_scope("g0_xy_upper"):
        far_upper = grid.shift(by_x[0], "y")
    with jax.named_scope("g0_xy_lower"):
        far_lower = grid.shift(by_y[1], "x")
    with jax.named_scope("slots_cross_twin"):
        s_cross_twin = grid.twin(after(s_cross, s_near_twin))
    slot_owners = grid.col_owners(z, z ^ 1, 3 - z, 3 - (z ^ 1))
    dense = dense_rows(slot_owners, [message, s_twin, s_near, s_near_twin, s_far, s_far_twin, s_cross, s_cross_twin])
    turned = turn(sources, dense, [tile, by_x, by_y, far_upper, far_lower])

    with jax.named_scope("turned_x"):
        by_x = grid.shift(turned, "x")
    with jax.named_scope("turned_y"):
        by_y = grid.shift(turned, "y")
    with jax.named_scope("g0_near_2"):
        near_2 = grid.along_z(after(middle, near), NEAR)
    with jax.named_scope("g0_middle_2"):
        middle_2 = grid.along_z(after(near, middle), MIDDLE)
    with jax.named_scope("g0_twin"):
        tile_twin = grid.twin(after(tile, turned))
    with jax.named_scope("g0_near_twin"):
        near_twin = grid.twin(after(near, tile_twin))
    with jax.named_scope("g0_middle_twin"):
        middle_twin = grid.twin(after(middle, near_twin))
    with jax.named_scope("g0_near_3"):
        near_3 = grid.along_z(after(middle_2, near_2, by_x, by_y), NEAR)
    with jax.named_scope("turned_xy_upper"):
        far_upper = grid.shift(by_x[0], "y")
    with jax.named_scope("turned_xy_lower"):
        far_lower = grid.shift(by_y[1], "x")
    with jax.named_scope("g0_near_2_twin"):
        near_2_twin = grid.twin(near_2)
    with jax.named_scope("g0_middle_2_twin"):
        middle_2_twin = grid.twin(after(middle_2, near_2_twin))
    at_end = (z == 0) | (z == 3)
    owners = grid.col_owners(
        z, z ^ 1, jnp.where(at_end, 2 - z // 3, -1), jnp.where(at_end, -1, 3 - z), jnp.where(at_end, -1, 3 * (2 - z))
    )
    last_owners = grid.col_owners(jnp.where(at_end, 3 - z, -1))
    groups = [[tile, tile_twin, near, near_twin], [near_2, near_2_twin], [middle, middle_twin, middle_2, middle_2_twin]]
    total, column = close(sources, owners, [turned, by_x, by_y, far_upper, far_lower], groups)
    with jax.named_scope("g0_near_3_twin"):
        near_3_twin = grid.twin(after(near_3, column))
    return last(last_owners, total, column, [near_3, near_3_twin])


def solution(mesh):
    placed = (
        P("row", "col"),
        P("row", "col"),
        P("row", "col", None, None),
        P("row", "col", None),
        P("row", "col"),
    )
    return jax.shard_map(
        functools.partial(per_device, mesh.shape["row"], mesh.shape["col"]),
        mesh=mesh, in_specs=placed, out_specs=P("row", "col"), check_vma=False,
    )
```

time: 153 us -> 145 us (0.948)
  waiting for transfers between devices: 83 us -> 56.7 us
  local copies, waits for them, and re-layouts: 1.89 us -> 23.2 us
  starting transfers between devices: 41.8 us -> 36.1 us
  Pallas kernels: 23.8 us -> 26.2 us
    unnamed x14 -> x46, local copies, waits for them, and re-layouts: 1.73 us -> 21.2 us
    ppermute x12 -> x8, waiting for transfers between devices: 29.3 us -> 12.5 us  [shift(): return lax.ppermute(value, 'row', pairs)]
    ppermute x7 -> x8, waiting for transfers between devices: 53.7 us -> 39.5 us  [along_z(): lax.ppermute(value, 'col', [(z * self.nc + c, to * self.nc + c) for z, to...]
    ppermute x9 -> x10, waiting for transfers between devices: 0.02 us -> 4.62 us  [twin(): lax.ppermute(value, 'col', [(z * self.nc + c, z * self.nc + 1 - c) for z...]
    ppermute x12 -> x8, starting transfers between devices: 14.2 us -> 10.2 us  [shift(): return lax.ppermute(value, 'row', pairs)]
    ppermute x7 -> x8, starting transfers between devices: 27.6 us -> 24.7 us  [along_z(): lax.ppermute(value, 'col', [(z * self.nc + c, to * self.nc + c) for z, to...]
    pallas_call x5 -> x3, Pallas kernels: 15 us -> 17.6 us  [the longest x1 8.29 us: close(): pl.pallas_call(functools.partial(close_kernel, n_col, [len(group) for gro...]
    squeeze x1 -> x4, local copies, waits for them, and re-layouts: 0.07 us -> 1.77 us  [the longest x2 0.91 us: per_device(): far_lower = grid.shift(by_y[1], 'x')]
  transfers between devices with their start and end apart: 28 -> 26, of which waited for: 14 -> 12; matrix products, arithmetic and copies ran while one was open for 1% -> 2% of each run, Pallas kernels for 11% -> 13%
where the time goes in v4:
time: 145 us; the launch traced here: 144 us
  waiting for transfers between devices  56.7 us (39%)
  starting transfers between devices  36.1 us (25%)
  Pallas kernels  26.2 us (18%)
  local copies, waits for them, and re-layouts  23.2 us (16%)
    ppermute x8, waiting for transfers between devices, along_z(): lax.ppermute(value, 'col', [(z * self.nc + c, to * self.nc + c) for z, to...  39.5 us
    ppermute x8, starting transfers between devices, along_z(): lax.ppermute(value, 'col', [(z * self.nc + c, to * self.nc + c) for z, to...  24.7 us
    unnamed x46, local copies, waits for them, and re-layouts  21.2 us
    ppermute x8, waiting for transfers between devices, shift(): return lax.ppermute(value, 'row', pairs)  12.5 us
    ppermute x8, starting transfers between devices, shift(): return lax.ppermute(value, 'row', pairs)  10.2 us
    pallas_call x1, Pallas kernels, close(): pl.pallas_call(functools.partial(close_kernel, n_col, [len(group) for gro...  8.29 us
    pallas_call x1, Pallas kernels, turn(): pl.pallas_call(turn_kernel, out_shape=jax.ShapeDtypeStruct((2, half, cols...  5.58 us
    ppermute x10, waiting for transfers between devices, twin(): lax.ppermute(value, 'col', [(z * self.nc + c, z * self.nc + 1 - c) for z...  4.62 us
  transfers between devices with their start and end apart: 26, of which 12 were waited for; matrix products, arithmetic and copies ran while one was open for 2% of the time, Pallas kernels for 13%

profile of v4, /device:TPU:0, one launch (start us, length us, event | category | flops | bytes accessed | tf_op | source)
XLA Modules:
  0.0 144.0 jit_solution(7127092548698708001)
XLA Ops:
  1.3 3.9 %prepare.1 = (bf16[1552,128]{1,0:T(8,128)(2,1)}, bf16[2,512,512]{2,1,0:T(8,128)(2,1)}) custom-call(s32[3]{0:T(128)} %pad_add_fusion.2.base_ref, bf16[1024,512]{1,0:T(8,128)(2,1)} %values_ref.1, s32[4,8]{1,0:T(4,128)} %bitcast.72, bf16[1,12,128,128]{3,2,1,0:T(8,128)(2,1)} %slots_ref.1, s32[2,12]{1,0:T(2,128)} %bitcast.73), custom_call_target="tpu_custom_call" | custom-call | tf_op jit(solution)/shard_map/prepare/pallas_call | solution.py:85
  5.2 5.1 %collective-permute-start = (bf16[1552,128]{1,0:T(8,128)(2,1)}, bf16[1552,128]{1,0:T(8,128)(2,1)S(1)}, u32[]{:S(2)}, u32[]{:S(2)}) collective-permute-start(bf16[1552,128]{1,0:T(8,128)(2,1)} %get-tuple-element.21.refs_0_), channel_id=1, source_target_pairs={{0,6},{1,7},{2,4},{3,5},{4,2},{5,3},{6,0},{7,1},{8,14},{9,15},{10,... | collective-permute-start | bytes 1191944 | tf_op jit(solution)/shard_map/slots_far/ppermute | solution.py:334
  14.2 6.4 %collective-permute-done.refs_4_ = bf16[1552,128]{1,0:T(8,128)(2,1)S(1)} collective-permute-done((bf16[1552,128]{1,0:T(8,128)(2,1)}, bf16[1552,128]{1,0:T(8,128)(2,1)S(1)}, u32[]{:S(2)}, u32[]{:S(2)}) %collective-permute-start) | collective-permute-done | bytes 397344 | tf_op jit(solution)/shard_map/slots_far/ppermute | solution.py:334
  20.6 7.7 %collective-permute-done.1.refs_2_ = bf16[1552,128]{1,0:T(8,128)(2,1)S(1)} collective-permute-done((bf16[1552,128]{1,0:T(8,128)(2,1)}, bf16[1552,128]{1,0:T(8,128)(2,1)S(1)}, u32[]{:S(2)}, u32[]{:S(2)}) %collective-permute-start.1) | collective-permute-done | bytes 397344 | tf_op jit(solution)/shard_map/slots_near/ppermute | solution.py:334
  28.3 1.7 %collective-permute-start.2 = (bf16[1552,128]{1,0:T(8,128)(2,1)S(1)}, bf16[1552,128]{1,0:T(8,128)(2,1)S(1)}, u32[]{:S(2)}, u32[]{:S(2)}) collective-permute-start(bf16[1552,128]{1,0:T(8,128)(2,1)S(1)} %collective-permute-done.refs_4_), channel_id=1, source_target_pairs={{0,2},{1,3},{2,0},{3,1},{4,6},{5,7},{6,4},{7,5},{8,10},{9,11},{10,... | collective-permute-start | bytes 1191944 | tf_op jit(solution)/shard_map/slots_cross/ppermute | solution.py:334
  30.0 1.7 %collective-permute-done.3.refs_5_ = bf16[1552,128]{1,0:T(8,128)(2,1)S(1)} collective-permute-done((bf16[1552,128]{1,0:T(8,128)(2,1)S(1)}, bf16[1552,128]{1,0:T(8,128)(2,1)S(1)}, u32[]{:S(2)}, u32[]{:S(2)}) %collective-permute-start.3) | collective-permute-done | bytes 397344 | tf_op jit(solution)/shard_map/slots_far_twin/ppermute | solution.py:339
  31.9 7.6 %collective-permute-done.2.refs_0_ = bf16[1552,128]{1,0:T(8,128)(2,1)S(1)} collective-permute-done((bf16[1552,128]{1,0:T(8,128)(2,1)S(1)}, bf16[1552,128]{1,0:T(8,128)(2,1)S(1)}, u32[]{:S(2)}, u32[]{:S(2)}) %collective-permute-start.2) | collective-permute-done | bytes 397344 | tf_op jit(solution)/shard_map/slots_cross/ppermute | solution.py:334
  39.5 1.6 %collective-permute-start.9 = (bf16[512,512]{1,0:T(8,128)(2,1)S(1)}, bf16[512,512]{1,0:T(8,128)(2,1)S(1)}, u32[]{:S(2)}, u32[]{:S(2)}) collective-permute-start(bf16[512,512]{1,0:T(8,128)(2,1)S(1)} %slice_bitcast_fusion.3), channel_id=1, source_target_pairs={{0,16},{8,24},{16,0},{24,8},{1,17},{9,25},{17,1},{25,9},{2,18},{10... | collective-permute-start | bytes 1572872 | tf_op jit(solution)/shard_map/g0_xy_upper/ppermute | solution.py:331
  41.1 1.6 %collective-permute-start.10 = (bf16[512,512]{1,0:T(8,128)(2,1)S(1)}, bf16[512,512]{1,0:T(8,128)(2,1)S(1)}, u32[]{:S(2)}, u32[]{:S(2)}) collective-permute-start(bf16[512,512]{1,0:T(8,128)(2,1)S(1)} %slice_bitcast_fusion.2), channel_id=1, source_target_pairs={{0,8},{8,0},{16,24},{24,16},{1,9},{9,1},{17,25},{25,17},{2,10},{10... | collective-permute-start | bytes 1572872 | tf_op jit(solution)/shard_map/g0_xy_lower/ppermute | solution.py:331
  43.4 9.4 %collective-permute-start.18 = (bf16[2,512,512]{2,1,0:T(8,128)(2,1)}, bf16[2,512,512]{2,1,0:T(8,128)(2,1)}, u32[]{:S(2)}, u32[]{:S(2)}) collective-permute-start(bf16[2,512,512]{2,1,0:T(8,128)(2,1)} %get-tuple-element.27.refs_0_.refs_5_), channel_id=1, source_target_pairs={{0,0},{1,1},{2,4},{3,5},{4,2},{5,3},{6,6},{7,7},{8,8},{9,9},{10,12... | collective-permute-start | bytes 3145736 | tf_op jit(solution)/shard_map/g0_middle/ppermute | solution.py:334
  53.9 3.3 %spread.1.refs_2_ = bf16[1024,4096]{1,0:T(8,128)(2,1)S(1)} custom-call(s32[6,12]{1,0:T(8,128)S(1)} %bitcast.69, s32[6,12]{1,0:T(8,128)S(1)} %bitcast_add_fusion.col_ref, bf16[1552,128]{1,0:T(8,128)(2,1)S(1)} %copy-done.19, bf16[1552,128]{1,0:T(8,128)(2,1)S(1)} %collective-permute-done.6.refs_1_, bf16[1552,128]{1,0:T(8,128)(2,1)S(1)} %collective-permute-done.1.refs_2_, ...), custom_call_target="tpu_custom_call" | custom-call | tf_op jit(solution)/shard_map/spread/pallas_call | solution.py:137
  58.9 5.6 %turn.1.refs_0_ = bf16[2,512,512]{2,1,0:T(8,128)(2,1)S(1)} custom-call(s32[4]{0:T(128)S(1)} %pad_add_fusion.1.source_ref, bf16[1024,4096]{1,0:T(8,128)(2,1)S(1)} %fill.1.dense_ref, bf16[2,512,512]{2,1,0:T(8,128)(2,1)S(1)} %copy-done.2, bf16[2,512,512]{2,1,0:T(8,128)(2,1)S(1)} %collective-permute-done.7.refs_1_, bf16[2,512,512]{2,1,0:T(8,128)(2,1)S(1)} %copy-done.4, ...), custom_call_target="tpu_custom_call" | custom-call | tf_op jit(solution)/shard_map/turn/pallas_call | solution.py:196
  66.6 3.7 %collective-permute-start.19 = (bf16[2,512,512]{2,1,0:T(8,128)(2,1)}, bf16[2,512,512]{2,1,0:T(8,128)(2,1)S(1)}, u32[]{:S(2)}, u32[]{:S(2)}) collective-permute-start(bf16[2,512,512]{2,1,0:T(8,128)(2,1)} %collective-permute-done.18.refs_11_), channel_id=1, source_target_pairs={{0,2},{1,3},{2,0},{3,1},{4,6},{5,7},{6,4},{7,5},{8,10},{9,11},{10,... | collective-permute-start | bytes 3145736 | tf_op jit(solution)/shard_map/g0_near_2/ppermute | solution.py:334
  71.4 1.6 %collective-permute-start.22 = (bf16[2,512,512]{2,1,0:T(8,128)(2,1)S(1)}, bf16[2,512,512]{2,1,0:T(8,128)(2,1)}, u32[]{:S(2)}, u32[]{:S(2)}) collective-permute-start(bf16[2,512,512]{2,1,0:T(8,128)(2,1)S(1)} %collective-permute-done.16.refs_7_), channel_id=1, source_target_pairs={{0,0},{1,1},{2,4},{3,5},{4,2},{5,3},{6,6},{7,7},{8,8},{9,9},{10,12... | collective-permute-start | bytes 3145736 | tf_op jit(solution)/shard_map/g0_middle_2/ppermute | solution.py:334
  74.9 16.3 %collective-permute-done.19.refs_9_ = bf16[2,512,512]{2,1,0:T(8,128)(2,1)S(1)} collective-permute-done((bf16[2,512,512]{2,1,0:T(8,128)(2,1)}, bf16[2,512,512]{2,1,0:T(8,128)(2,1)S(1)}, u32[]{:S(2)}, u32[]{:S(2)}) %collective-permute-start.19) | collective-permute-done | bytes 1048608 | tf_op jit(solution)/shard_map/g0_near_2/ppermute | solution.py:334
  95.3 2.5 %collective-permute-start.24 = (bf16[2,512,512]{2,1,0:T(8,128)(2,1)}, bf16[2,512,512]{2,1,0:T(8,128)(2,1)}, u32[]{:S(2)}, u32[]{:S(2)}) collective-permute-start(bf16[2,512,512]{2,1,0:T(8,128)(2,1)} %collective-permute-done.22.refs_13_), channel_id=1, source_target_pairs={{0,2},{1,3},{2,0},{3,1},{4,6},{5,7},{6,4},{7,5},{8,10},{9,11},{10,... | collective-permute-start | bytes 3145736 | tf_op jit(solution)/shard_map/g0_near_3/ppermute | solution.py:334
  102.6 9.9 %collective-permute-done.13.refs_3_ = bf16[512,512]{1,0:T(8,128)(2,1)} collective-permute-done((bf16[512,512]{1,0:T(8,128)(2,1)}, bf16[512,512]{1,0:T(8,128)(2,1)}, u32[]{:S(2)}, u32[]{:S(2)}) %collective-permute-start.13) | collective-permute-done | bytes 524320 | tf_op jit(solution)/shard_map/turned_xy_upper/ppermute | solution.py:331
  112.5 2.1 %collective-permute-done.14.refs_4_ = bf16[512,512]{1,0:T(8,128)(2,1)} collective-permute-done((bf16[512,512]{1,0:T(8,128)(2,1)}, bf16[512,512]{1,0:T(8,128)(2,1)}, u32[]{:S(2)}, u32[]{:S(2)}) %collective-permute-start.14) | collective-permute-done | bytes 524320 | tf_op jit(solution)/shard_map/turned_xy_lower/ppermute | solution.py:331
  121.9 8.3 %close.1 = (f32[2,512,512]{2,1,0:T(8,128)S(1)}, bf16[4096,512]{1,0:T(8,128)(2,1)S(1)}) custom-call(s32[4]{0:T(128)S(1)} %pad_add_fusion.1.source_ref, s32[10]{0:T(128)S(1)} %stack.135.owner_ref, bf16[2,512,512]{2,1,0:T(8,128)(2,1)S(1)} %turn.1.refs_0_, bf16[2,512,512]{2,1,0:T(8,128)(2,1)S(1)} %collective-permute-done.11.refs_1_, ...), custom_call_target="tpu_custom_call" | custom-call | tf_op jit(solution)/shard_map/close/pallas_call | solution.py:256
  130.2 1.9 %copy-done = bf16[4096,512]{1,0:T(8,128)(2,1)} copy-done((bf16[4096,512]{1,0:T(8,128)(2,1)}, bf16[4096,512]{1,0:T(8,128)(2,1)S(1)}, u32[]{:S(2)}) %copy-start) | copy-done | bytes 4194328
  133.6 2.8 %collective-permute-done.25.refs_1_ = bf16[2,512,512]{2,1,0:T(8,128)(2,1)S(1)} collective-permute-done((bf16[2,512,512]{2,1,0:T(8,128)(2,1)}, bf16[2,512,512]{2,1,0:T(8,128)(2,1)S(1)}, u32[]{:S(2)}, u32[]{:S(2)}) %collective-permute-start.25) | collective-permute-done | bytes 1048608 | tf_op jit(solution)/shard_map/g0_near_3_twin/ppermute | solution.py:339
  136.4 2.2 %copy-done.1 = bf16[4096,512]{1,0:T(8,128)(2,1)S(1)} copy-done((bf16[4096,512]{1,0:T(8,128)(2,1)S(1)}, bf16[4096,512]{1,0:T(8,128)(2,1)}, u32[]{:S(2)}) %copy-start.1) | copy-done | bytes 4194328
  138.6 1.6 %copy-done.8 = f32[2,512,512]{2,1,0:T(8,128)S(1)} copy-done((f32[2,512,512]{2,1,0:T(8,128)S(1)}, f32[2,512,512]{2,1,0:T(8,128)}, u32[]{:S(2)}) %copy-start.8) | copy-done | bytes 2097176
  140.2 3.8 %last.1 = bf16[1024,512]{1,0:T(8,128)(2,1)} custom-call(s32[2]{0:T(128)S(1)} %pad_add_fusion.owner_ref, f32[2,512,512]{2,1,0:T(8,128)S(1)} %copy-done.8, bf16[4096,512]{1,0:T(8,128)(2,1)S(1)} %copy-done.1, bf16[2,512,512]{2,1,0:T(8,128)(2,1)} %collective-permute-done.24.refs_0_, bf16[2,512,512]{2,1,0:T(8,128)(2,1)S(1)} %collective-permute-done.25.refs_1_), custom_call_target="tpu_custom_call" | custom-call | tf_op jit(solution)/shard_map/last/pallas_call | solution.py:300
  (100 shorter events, 30.8 us)
Async XLA Ops:
  5.2 15.4 %collective-permute-start = (bf16[1552,128]{1,0:T(8,128)(2,1)}, bf16[1552,128]{1,0:T(8,128)(2,1)S(1)}, u32[]{:S(2)}, u32[]{:S(2)}) collective-permute-start(bf16[1552,128]{1,0:T(8,128)(2,1)} %get-tuple-element.21.refs_0_), channel_id=1, source_target_pairs={{0,6},{1,7},{2,4},{3,5},{4,2},{5,3},{6,0},{7,1},{8,14},{9,15},{10,... | collective-permute-start | bytes 1191944 | tf_op jit(solution)/shard_map/slots_far/ppermute | solution.py:334
  10.3 18.0 %collective-permute-start.1 = (bf16[1552,128]{1,0:T(8,128)(2,1)}, bf16[1552,128]{1,0:T(8,128)(2,1)S(1)}, u32[]{:S(2)}, u32[]{:S(2)}) collective-permute-start(bf16[1552,128]{1,0:T(8,128)(2,1)} %get-tuple-element.21.refs_0_), channel_id=1, source_target_pairs={{0,2},{1,3},{2,0},{3,1},{4,6},{5,7},{6,4},{7,5},{8,10},{9,11},{10,... | collective-permute-start | bytes 1191944 | tf_op jit(solution)/shard_map/slots_near/ppermute | solution.py:334
  10.3 19.7 %collective-permute-start.6 = (bf16[1552,128]{1,0:T(8,128)(2,1)}, bf16[1552,128]{1,0:T(8,128)(2,1)S(1)}, u32[]{:S(2)}, u32[]{:S(2)}) collective-permute-start(bf16[1552,128]{1,0:T(8,128)(2,1)} %get-tuple-element.21.refs_0_), channel_id=1, source_target_pairs={{0,1},{1,0},{2,3},{3,2},{4,5},{5,4},{6,7},{7,6},{8,9},{9,8},{10,11... | collective-permute-start | bytes 1191944 | tf_op jit(solution)/shard_map/slots_twin/ppermute | solution.py:339
  10.3 29.2 %collective-permute-start.7 = (bf16[2,512,512]{2,1,0:T(8,128)(2,1)}, bf16[2,512,512]{2,1,0:T(8,128)(2,1)S(1)}, u32[]{:S(2)}, u32[]{:S(2)}) collective-permute-start(bf16[2,512,512]{2,1,0:T(8,128)(2,1)} %get-tuple-element.27.refs_0_.refs_5_), channel_id=1, source_target_pairs={{0,8},{8,0},{16,24},{24,16},{1,9},{9,1},{17,25},{25,17},{2,10},{10... | collective-permute-start | bytes 3145736 | tf_op jit(solution)/shard_map/g0_x/ppermute | solution.py:331
  11.8 29.3 %collective-permute-start.8 = (bf16[2,512,512]{2,1,0:T(8,128)(2,1)}, bf16[2,512,512]{2,1,0:T(8,128)(2,1)S(1)}, u32[]{:S(2)}, u32[]{:S(2)}) collective-permute-start(bf16[2,512,512]{2,1,0:T(8,128)(2,1)} %get-tuple-element.27.refs_0_.refs_5_), channel_id=1, source_target_pairs={{0,16},{8,24},{16,0},{24,8},{1,17},{9,25},{17,1},{25,9},{2,18},{10... | collective-permute-start | bytes 3145736 | tf_op jit(solution)/shard_map/g0_y/ppermute | solution.py:331
  28.3 11.1 %collective-permute-start.2 = (bf16[1552,128]{1,0:T(8,128)(2,1)S(1)}, bf16[1552,128]{1,0:T(8,128)(2,1)S(1)}, u32[]{:S(2)}, u32[]{:S(2)}) collective-permute-start(bf16[1552,128]{1,0:T(8,128)(2,1)S(1)} %collective-permute-done.refs_4_), channel_id=1, source_target_pairs={{0,2},{1,3},{2,0},{3,1},{4,6},{5,7},{6,4},{7,5},{8,10},{9,11},{10,... | collective-permute-start | bytes 1191944 | tf_op jit(solution)/shard_map/slots_cross/ppermute | solution.py:334
  31.8 10.9 %collective-permute-start.4 = (bf16[1552,128]{1,0:T(8,128)(2,1)S(1)}, bf16[1552,128]{1,0:T(8,128)(2,1)S(1)}, u32[]{:S(2)}, u32[]{:S(2)}) collective-permute-start(bf16[1552,128]{1,0:T(8,128)(2,1)S(1)} %collective-permute-done.1.refs_2_), channel_id=1, source_target_pairs={{0,1},{1,0},{2,3},{3,2},{4,5},{5,4},{6,7},{7,6},{8,9},{9,8},{10,11... | collective-permute-start | bytes 1191944 | tf_op jit(solution)/shard_map/slots_near_twin/ppermute | solution.py:339
  39.5 19.2 %collective-permute-start.9 = (bf16[512,512]{1,0:T(8,128)(2,1)S(1)}, bf16[512,512]{1,0:T(8,128)(2,1)S(1)}, u32[]{:S(2)}, u32[]{:S(2)}) collective-permute-start(bf16[512,512]{1,0:T(8,128)(2,1)S(1)} %slice_bitcast_fusion.3), channel_id=1, source_target_pairs={{0,16},{8,24},{16,0},{24,8},{1,17},{9,25},{17,1},{25,9},{2,18},{10... | collective-permute-start | bytes 1572872 | tf_op jit(solution)/shard_map/g0_xy_upper/ppermute | solution.py:331
  41.1 17.6 %collective-permute-start.10 = (bf16[512,512]{1,0:T(8,128)(2,1)S(1)}, bf16[512,512]{1,0:T(8,128)(2,1)S(1)}, u32[]{:S(2)}, u32[]{:S(2)}) collective-permute-start(bf16[512,512]{1,0:T(8,128)(2,1)S(1)} %slice_bitcast_fusion.2), channel_id=1, source_target_pairs={{0,8},{8,0},{16,24},{24,16},{1,9},{9,1},{17,25},{25,17},{2,10},{10... | collective-permute-start | bytes 1572872 | tf_op jit(solution)/shard_map/g0_xy_lower/ppermute | solution.py:331
  42.7 23.9 %collective-permute-start.16 = (bf16[2,512,512]{2,1,0:T(8,128)(2,1)}, bf16[2,512,512]{2,1,0:T(8,128)(2,1)S(1)}, u32[]{:S(2)}, u32[]{:S(2)}) collective-permute-start(bf16[2,512,512]{2,1,0:T(8,128)(2,1)} %get-tuple-element.27.refs_0_.refs_5_), channel_id=1, source_target_pairs={{0,2},{1,3},{2,0},{3,1},{4,6},{5,7},{6,4},{7,5},{8,10},{9,11},{10,... | collective-permute-start | bytes 3145736 | tf_op jit(solution)/shard_map/g0_near/ppermute | solution.py:334
  43.4 23.2 %collective-permute-start.18 = (bf16[2,512,512]{2,1,0:T(8,128)(2,1)}, bf16[2,512,512]{2,1,0:T(8,128)(2,1)}, u32[]{:S(2)}, u32[]{:S(2)}) collective-permute-start(bf16[2,512,512]{2,1,0:T(8,128)(2,1)} %get-tuple-element.27.refs_0_.refs_5_), channel_id=1, source_target_pairs={{0,0},{1,1},{2,4},{3,5},{4,2},{5,3},{6,6},{7,7},{8,8},{9,9},{10,12... | collective-permute-start | bytes 3145736 | tf_op jit(solution)/shard_map/g0_middle/ppermute | solution.py:334
  52.8 4.4 %collective-permute-start.5 = (bf16[1552,128]{1,0:T(8,128)(2,1)S(1)}, bf16[1552,128]{1,0:T(8,128)(2,1)S(1)}, u32[]{:S(2)}, u32[]{:S(2)}) collective-permute-start(bf16[1552,128]{1,0:T(8,128)(2,1)S(1)} %collective-permute-done.2.refs_0_), channel_id=1, source_target_pairs={{0,1},{1,0},{2,3},{3,2},{4,5},{5,4},{6,7},{7,6},{8,9},{9,8},{10,11... | collective-permute-start | bytes 1191944 | tf_op jit(solution)/shard_map/slots_cross_twin/ppermute | solution.py:339
  64.5 8.5 %collective-permute-start.15 = (bf16[2,512,512]{2,1,0:T(8,128)(2,1)S(1)}, bf16[2,512,512]{2,1,0:T(8,128)(2,1)S(1)}, u32[]{:S(2)}, u32[]{:S(2)}) collective-permute-start(bf16[2,512,512]{2,1,0:T(8,128)(2,1)S(1)} %copy-done.2), channel_id=1, source_target_pairs={{0,1},{1,0},{2,3},{3,2},{4,5},{5,4},{6,7},{7,6},{8,9},{9,8},{10,11... | collective-permute-start | bytes 3145736 | tf_op jit(solution)/shard_map/g0_twin/ppermute | solution.py:339
  66.6 24.7 %collective-permute-start.19 = (bf16[2,512,512]{2,1,0:T(8,128)(2,1)}, bf16[2,512,512]{2,1,0:T(8,128)(2,1)S(1)}, u32[]{:S(2)}, u32[]{:S(2)}) collective-permute-start(bf16[2,512,512]{2,1,0:T(8,128)(2,1)} %collective-permute-done.18.refs_11_), channel_id=1, source_target_pairs={{0,2},{1,3},{2,0},{3,1},{4,6},{5,7},{6,4},{7,5},{8,10},{9,11},{10,... | collective-permute-start | bytes 3145736 | tf_op jit(solution)/shard_map/g0_near_2/ppermute | solution.py:334
  70.3 22.2 %collective-permute-start.11 = (bf16[2,512,512]{2,1,0:T(8,128)(2,1)S(1)}, bf16[2,512,512]{2,1,0:T(8,128)(2,1)S(1)}, u32[]{:S(2)}, u32[]{:S(2)}) collective-permute-start(bf16[2,512,512]{2,1,0:T(8,128)(2,1)S(1)} %turn.1.refs_0_), channel_id=1, source_target_pairs={{0,8},{8,0},{16,24},{24,16},{1,9},{9,1},{17,25},{25,17},{2,10},{10... | collective-permute-start | bytes 3145736 | tf_op jit(solution)/shard_map/turned_x/ppermute | solution.py:331
  70.9 21.9 %collective-permute-start.12 = (bf16[2,512,512]{2,1,0:T(8,128)(2,1)S(1)}, bf16[2,512,512]{2,1,0:T(8,128)(2,1)S(1)}, u32[]{:S(2)}, u32[]{:S(2)}) collective-permute-start(bf16[2,512,512]{2,1,0:T(8,128)(2,1)S(1)} %turn.1.refs_0_), channel_id=1, source_target_pairs={{0,16},{8,24},{16,0},{24,8},{1,17},{9,25},{17,1},{25,9},{2,18},{10... | collective-permute-start | bytes 3145736 | tf_op jit(solution)/shard_map/turned_y/ppermute | solution.py:331
  71.4 21.4 %collective-permute-start.22 = (bf16[2,512,512]{2,1,0:T(8,128)(2,1)S(1)}, bf16[2,512,512]{2,1,0:T(8,128)(2,1)}, u32[]{:S(2)}, u32[]{:S(2)}) collective-permute-start(bf16[2,512,512]{2,1,0:T(8,128)(2,1)S(1)} %collective-permute-done.16.refs_7_), channel_id=1, source_target_pairs={{0,0},{1,1},{2,4},{3,5},{4,2},{5,3},{6,6},{7,7},{8,8},{9,9},{10,12... | collective-permute-start | bytes 3145736 | tf_op jit(solution)/shard_map/g0_middle_2/ppermute | solution.py:334
  74.0 18.8 %collective-permute-start.17 = (bf16[2,512,512]{2,1,0:T(8,128)(2,1)S(1)}, bf16[2,512,512]{2,1,0:T(8,128)(2,1)S(1)}, u32[]{:S(2)}, u32[]{:S(2)}) collective-permute-start(bf16[2,512,512]{2,1,0:T(8,128)(2,1)S(1)} %collective-permute-done.16.refs_7_), channel_id=1, source_target_pairs={{0,1},{1,0},{2,3},{3,2},{4,5},{5,4},{6,7},{7,6},{8,9},{9,8},{10,11... | collective-permute-start | bytes 3145736 | tf_op jit(solution)/shard_map/g0_near_twin/ppermute | solution.py:339
  93.8 20.7 %collective-permute-start.21 = (bf16[2,512,512]{2,1,0:T(8,128)(2,1)}, bf16[2,512,512]{2,1,0:T(8,128)(2,1)}, u32[]{:S(2)}, u32[]{:S(2)}) collective-permute-start(bf16[2,512,512]{2,1,0:T(8,128)(2,1)} %collective-permute-done.18.refs_11_), channel_id=1, source_target_pairs={{0,1},{1,0},{2,3},{3,2},{4,5},{5,4},{6,7},{7,6},{8,9},{9,8},{10,11... | collective-permute-start | bytes 3145736 | tf_op jit(solution)/shard_map/g0_middle_twin/ppermute | solution.py:339
  94.9 19.7 %collective-permute-start.23 = (bf16[2,512,512]{2,1,0:T(8,128)(2,1)}, bf16[2,512,512]{2,1,0:T(8,128)(2,1)}, u32[]{:S(2)}, u32[]{:S(2)}) collective-permute-start(bf16[2,512,512]{2,1,0:T(8,128)(2,1)} %collective-permute-done.22.refs_13_), channel_id=1, source_target_pairs={{0,1},{1,0},{2,3},{3,2},{4,5},{5,4},{6,7},{7,6},{8,9},{9,8},{10,11... | collective-permute-start | bytes 3145736 | tf_op jit(solution)/shard_map/g0_middle_2_twin/ppermute | solution.py:339
  95.3 38.2 %collective-permute-start.24 = (bf16[2,512,512]{2,1,0:T(8,128)(2,1)}, bf16[2,512,512]{2,1,0:T(8,128)(2,1)}, u32[]{:S(2)}, u32[]{:S(2)}) collective-permute-start(bf16[2,512,512]{2,1,0:T(8,128)(2,1)} %collective-permute-done.22.refs_13_), channel_id=1, source_target_pairs={{0,2},{1,3},{2,0},{3,1},{4,6},{5,7},{6,4},{7,5},{8,10},{9,11},{10,... | collective-permute-start | bytes 3145736 | tf_op jit(solution)/shard_map/g0_near_3/ppermute | solution.py:334
  98.6 13.9 %collective-permute-start.13 = (bf16[512,512]{1,0:T(8,128)(2,1)}, bf16[512,512]{1,0:T(8,128)(2,1)}, u32[]{:S(2)}, u32[]{:S(2)}) collective-permute-start(bf16[512,512]{1,0:T(8,128)(2,1)} %slice_bitcast_fusion.1), channel_id=1, source_target_pairs={{0,16},{8,24},{16,0},{24,8},{1,17},{9,25},{17,1},{25,9},{2,18},{10... | collective-permute-start | bytes 1572872 | tf_op jit(solution)/shard_map/turned_xy_upper/ppermute | solution.py:331
  101.0 13.6 %collective-permute-start.14 = (bf16[512,512]{1,0:T(8,128)(2,1)}, bf16[512,512]{1,0:T(8,128)(2,1)}, u32[]{:S(2)}, u32[]{:S(2)}) collective-permute-start(bf16[512,512]{1,0:T(8,128)(2,1)} %slice_bitcast_fusion), channel_id=1, source_target_pairs={{0,8},{8,0},{16,24},{24,16},{1,9},{9,1},{17,25},{25,17},{2,10},{10... | collective-permute-start | bytes 1572872 | tf_op jit(solution)/shard_map/turned_xy_lower/ppermute | solution.py:331
  133.5 2.9 %collective-permute-start.25 = (bf16[2,512,512]{2,1,0:T(8,128)(2,1)}, bf16[2,512,512]{2,1,0:T(8,128)(2,1)S(1)}, u32[]{:S(2)}, u32[]{:S(2)}) collective-permute-start(bf16[2,512,512]{2,1,0:T(8,128)(2,1)} %collective-permute-done.24.refs_0_), channel_id=1, source_target_pairs={{0,1},{1,0},{2,3},{3,2},{4,5},{5,4},{6,7},{7,6},{8,9},{9,8},{10,11... | collective-permute-start | bytes 3145736 | tf_op jit(solution)/shard_map/g0_near_3_twin/ppermute | solution.py:339
  (22 other events, 51.3 us)

commit v5 on v4

v5 whole, which is shorter than its diff:
```python
import functools
import math

import jax
import jax.numpy as jnp
from jax import lax
from jax.experimental import pallas as pl
from jax.experimental.pallas import tpu as pltpu
from jax.sharding import PartitionSpec as P

VMEM_BYTES = 6 * 1024 * 1024
FIRST_VMEM_BYTES = 60 * 1024 * 1024
ANY = pl.BlockSpec(memory_space=pl.ANY)
HBM = pl.BlockSpec(memory_space=pltpu.HBM)
SMEM = pl.BlockSpec(memory_space=pltpu.SMEM)
VMEM = pl.BlockSpec(memory_space=pltpu.VMEM)
TAIL = 16
NO_COST = pl.CostEstimate(flops=0, bytes_accessed=0, transcendentals=0)


def kernel_params():
    return pltpu.CompilerParams(vmem_limit_bytes=VMEM_BYTES)


def after(value, *earlier):
    return lax.optimization_barrier((value, *earlier))[0]


def pack_kernel(slots, width, base_ref, slots_ref, pairs_ref, message_ref, pairs, names, tail, sems, tail_sem):
    fetch = pltpu.make_async_copy(pairs_ref, pairs, tail_sem)
    fetch.start()
    moves = [
        pltpu.make_async_copy(slots_ref.at[0, s], message_ref.at[pl.ds(s * width, width)], sems.at[s])
        for s in range(slots)
    ]
    for move in moves:
        move.start()
    names[...] = jnp.full(names.shape, -1, jnp.int32)
    fetch.wait()
    shape = pairs.shape
    first = lax.broadcasted_iota(jnp.int32, shape, 0) == 0
    local = pairs[...] - jnp.where(first, base_ref[0], base_ref[1])
    live = lax.broadcasted_iota(jnp.int32, shape, 1) < base_ref[2]
    names[pl.ds(0, shape[0]), pl.ds(0, shape[1])] = jnp.where(live, local, -1)
    tail[...] = names[...].astype(jnp.float32).astype(jnp.bfloat16)
    give = pltpu.make_async_copy(tail, message_ref.at[pl.ds(slots * width, TAIL)], tail_sem)
    give.start()
    for move in moves:
        move.wait()
    give.wait()


def pack(base, sigma_values, sigma_pairs):
    slots, width = sigma_values.shape[1], sigma_values.shape[2]
    return pl.pallas_call(
        functools.partial(pack_kernel, slots, width),
        out_shape=jax.ShapeDtypeStruct((slots * width + TAIL, width), jnp.bfloat16),
        in_specs=[SMEM, HBM, HBM],
        out_specs=HBM,
        scratch_shapes=[
            pltpu.VMEM((2, slots), jnp.int32),
            pltpu.VMEM((TAIL, width), jnp.int32),
            pltpu.VMEM((TAIL, width), jnp.bfloat16),
            pltpu.SemaphoreType.DMA((slots,)),
            pltpu.SemaphoreType.DMA,
        ],
        compiler_params=pltpu.CompilerParams(vmem_limit_bytes=FIRST_VMEM_BYTES),
        cost_estimate=NO_COST,
        name="pack",
    )(base, sigma_values, sigma_pairs[0].T)


def mask_kernel(
    width, pattern_ref, values_ref, tile_ref, upper_ref, lower_ref, pattern, values, pattern_sem, in_sems, tile_sems, half_sems
):
    block_cols, block_rows = pattern_ref.shape
    half = block_rows // 2
    fetch = pltpu.make_async_copy(pattern_ref, pattern, pattern_sem)
    fetch.start()
    fetches = [
        pltpu.make_async_copy(values_ref.at[pl.ds(a * width, width)], values.at[a], in_sems.at[a])
        for a in range(block_rows)
    ]
    for move in fetches:
        move.start()
    fetch.wait()
    gives = []
    for a in range(block_rows):
        fetches[a].wait()
        for b in range(block_cols):
            keep = pattern[b:b + 1, a:a + 1].astype(jnp.float32)
            keep = jnp.broadcast_to(keep, (width, width)).astype(jnp.bfloat16)
            at = pl.ds(b * width, width)
            values[a, :, at] = values[a, :, at] * keep
        at = pl.ds((a % half) * width, width)
        gives.append(pltpu.make_async_copy(values.at[a], tile_ref.at[a // half, at], tile_sems.at[a]))
        gives[-1].start()
        target = upper_ref if a < half else lower_ref
        gives.append(pltpu.make_async_copy(values.at[a], target.at[at], half_sems.at[a]))
        gives[-1].start()
    for move in gives:
        move.wait()


def masked(g0_values, g0_pattern):
    rows, cols = g0_values.shape
    block_rows, block_cols = g0_pattern.shape
    width = rows // block_rows
    half = jax.ShapeDtypeStruct((rows // 2, cols), jnp.bfloat16)
    return pl.pallas_call(
        functools.partial(mask_kernel, width),
        out_shape=(jax.ShapeDtypeStruct((2, rows // 2, cols), jnp.bfloat16), half, half),
        in_specs=[HBM, HBM],
        out_specs=(HBM, HBM, HBM),
        scratch_shapes=[
            pltpu.VMEM((block_cols, block_rows), jnp.int32),
            pltpu.VMEM((block_rows, width, cols), jnp.bfloat16),
            pltpu.SemaphoreType.DMA,
            pltpu.SemaphoreType.DMA((block_rows,)),
            pltpu.SemaphoreType.DMA((block_rows,)),
            pltpu.SemaphoreType.DMA((block_rows,)),
        ],
        compiler_params=pltpu.CompilerParams(vmem_limit_bytes=FIRST_VMEM_BYTES),
        cost_estimate=NO_COST,
        name="mask",
    )(g0_pattern.T, g0_values)


def place_slots(slots, width, row_ref, col_ref, parts, dense_ref, spare, sem):
    for i, part in enumerate(parts):
        for s in range(slots):
            source = part.at[pl.ds(s * width, width)]
            row, col = row_ref[i, s], col_ref[i, s]

            @pl.when(row >= 0)
            def _():
                target = dense_ref.at[pl.ds(pl.multiple_of(row, width), width), pl.ds(pl.multiple_of(col, width), width)]
                pltpu.make_async_copy(source, target, sem.at[i]).start()

            @pl.when(row < 0)
            def _():
                pltpu.make_async_copy(source, spare.at[pl.ds(s * width, width)], sem.at[i]).start()
    for i, part in enumerate(parts):
        pltpu.make_async_copy(part.at[pl.ds(0, slots * width)], spare, sem.at[i]).wait()


def spread_kernel(count, slots, width, row_ref, col_ref, *refs):
    parts, (dense_ref, spare, sem) = refs[:count], refs[count:]
    dense_ref[...] = jnp.zeros_like(dense_ref)
    place_slots(slots, width, row_ref, col_ref, parts, dense_ref, spare, sem)


def spread(row_at, col_at, parts, slots, rows, depth):
    width = parts[0].shape[1]
    return pl.pallas_call(
        functools.partial(spread_kernel, len(parts), slots, width),
        out_shape=jax.ShapeDtypeStruct((rows, depth), jnp.bfloat16),
        in_specs=[SMEM, SMEM] + [ANY] * len(parts),
        out_specs=VMEM,
        scratch_shapes=[pltpu.VMEM((slots * width, width), jnp.bfloat16), pltpu.SemaphoreType.DMA((len(parts),))],
        compiler_params=kernel_params(),
        cost_estimate=NO_COST,
        name="spread",
    )(row_at, col_at, *parts)


def fill_kernel(count, slots, width, row_ref, col_ref, *refs):
    parts, (_, dense_ref, spare, sem) = refs[:count], refs[count:]
    place_slots(slots, width, row_ref, col_ref, parts, dense_ref, spare, sem)


def fill(row_at, col_at, parts, dense, slots):
    width = parts[0].shape[1]
    return pl.pallas_call(
        functools.partial(fill_kernel, len(parts), slots, width),
        out_shape=jax.ShapeDtypeStruct(dense.shape, dense.dtype),
        in_specs=[SMEM, SMEM] + [ANY] * (len(parts) + 1),
        out_specs=ANY,
        scratch_shapes=[pltpu.VMEM((slots * width, width), jnp.bfloat16), pltpu.SemaphoreType.DMA((len(parts),))],
        input_output_aliases={2 + len(parts): 0},
        compiler_params=kernel_params(),
        cost_estimate=NO_COST,
        name="fill",
    )(row_at, col_at, *parts, dense)


def half_refs(refs):
    found = []
    for ref in refs:
        found += [ref.at[0], ref.at[1]] if len(ref.shape) == 3 else [ref]
    return found


def turn_kernel(source_ref, dense_ref, own_ref, *refs):
    out_ref, own, sem = refs[-3:]
    parts = half_refs([own, *refs[:-3]])
    _, half, cols = out_ref.shape
    fetch = pltpu.make_async_copy(own_ref, own, sem)
    fetch.start()
    fetch.wait()
    tile = min(256, half)
    for side in range(2):
        @pl.loop(0, half // tile)
        def _(t):
            at = pl.multiple_of(t * tile, tile)
            total = jnp.zeros((tile, cols), jnp.float32)
            for i, part in enumerate(parts):
                start = pl.multiple_of(source_ref[i // 2] * (2 * half) + (i % 2) * half, half)
                total += jnp.dot(
                    dense_ref[pl.ds(side * half + at, tile), pl.ds(start, half)], part[...],
                    preferred_element_type=jnp.float32,
                )
            out_ref[side, pl.ds(at, tile), :] = total.astype(jnp.bfloat16)


def turn(sources, dense, parts):
    _, half, cols = parts[0].shape
    return pl.pallas_call(
        turn_kernel,
        out_shape=jax.ShapeDtypeStruct((2, half, cols), jnp.bfloat16),
        in_specs=[SMEM, VMEM, ANY] + [VMEM] * (len(parts) - 1),
        out_specs=VMEM,
        scratch_shapes=[pltpu.VMEM((2, half, cols), jnp.bfloat16), pltpu.SemaphoreType.DMA],
        compiler_params=kernel_params(),
        cost_estimate=NO_COST,
        name="turn",
    )(sources, dense, *parts)


def add_products(total, owner_ref, parts, column_ref):
    cols = parts[0].shape[-1]
    for i, part in enumerate(parts):
        start = pl.multiple_of(owner_ref[i] * cols, cols)
        total += jnp.dot(part, column_ref[pl.ds(start, cols), :], preferred_element_type=jnp.float32)
    return total


def close_kernel(n_col, source_ref, owner_ref, *refs):
    total_ref, column_ref, own, sem, own_sem = refs[-5:]
    col_refs, row_refs = half_refs(refs[:n_col]), half_refs([own, *refs[n_col + 1:-5]])
    half, _ = row_refs[0].shape
    fetch = pltpu.make_async_copy(refs[n_col], own, own_sem)
    fetch.start()

    def column_copy(i):
        start = pl.multiple_of(source_ref[i // 2] * (2 * half) + (i % 2) * half, half)
        return pltpu.make_async_copy(col_refs[i], column_ref.at[pl.ds(start, half)], sem.at[i])

    for i in range(len(col_refs)):
        column_copy(i).start()
    for i in range(len(col_refs)):
        column_copy(i).wait()
    fetch.wait()
    tile = min(256, half)
    for side in range(2):
        @pl.loop(0, half // tile)
        def _(t):
            at = pl.ds(pl.multiple_of(t * tile, tile), tile)
            parts = [part[at, :] for part in row_refs[side::2]]
            total_ref[side, at, :] = add_products(parts[0].astype(jnp.float32), owner_ref, parts, column_ref)


def close(sources, owners, col_parts, row_parts):
    half, cols = row_parts[0].shape[-2:]
    n_col = len(col_parts)
    n_half = sum(part.ndim - 1 for part in col_parts)
    return pl.pallas_call(
        functools.partial(close_kernel, n_col),
        out_shape=(
            jax.ShapeDtypeStruct((2, half, cols), jnp.float32),
            jax.ShapeDtypeStruct((n_half * half, cols), jnp.bfloat16),
        ),
        in_specs=[SMEM, SMEM] + [ANY] * (n_col + 1) + [VMEM] * (len(row_parts) - 1),
        out_specs=(VMEM, VMEM),
        scratch_shapes=[
            pltpu.VMEM((2, half, cols), jnp.bfloat16),
            pltpu.SemaphoreType.DMA((n_half,)),
            pltpu.SemaphoreType.DMA,
        ],
        compiler_params=kernel_params(),
        cost_estimate=NO_COST,
        name="close",
    )(sources, owners, *col_parts, *row_parts)


def last_kernel(side, n_row, owner_ref, total_ref, column_ref, *refs):
    row_refs, out_ref, result, sem = refs[:n_row], refs[-3], refs[-2], refs[-1]
    half, _ = row_refs[0].shape
    tile = min(256, half)
    moves = []
    for t in range(half // tile):
        at = pl.ds(t * tile, tile)
        parts = [part[at, :] for part in row_refs]
        result[at, :] = add_products(total_ref[side, at, :], owner_ref, parts, column_ref).astype(jnp.bfloat16)
        target = out_ref.at[pl.ds(side * half + t * tile, tile)]
        moves.append(pltpu.make_async_copy(result.at[at], target, sem.at[t]))
        moves[-1].start()
    for move in moves:
        move.wait()


def last(side, owners, total, column, row_parts, earlier=None):
    half, cols = row_parts[0].shape
    n_row = len(row_parts)
    operands = [owners, total, column, *row_parts]
    specs = [SMEM] + [VMEM] * (2 + n_row)
    aliases = {}
    if earlier is not None:
        aliases = {len(operands): 0}
        operands.append(earlier)
        specs.append(HBM)
    return pl.pallas_call(
        functools.partial(last_kernel, side, n_row),
        out_shape=jax.ShapeDtypeStruct((2 * half, cols), jnp.bfloat16),
        in_specs=specs,
        out_specs=HBM,
        scratch_shapes=[
            pltpu.VMEM((half, cols), jnp.bfloat16),
            pltpu.SemaphoreType.DMA((half // min(256, half),)),
        ],
        input_output_aliases=aliases,
        compiler_params=kernel_params(),
        cost_estimate=NO_COST,
        name="last",
    )(*operands)


class Grid:
    def __init__(self, n_row, n_col):
        side = math.isqrt(n_row)
        self.nx = side if side * side == n_row else n_row
        self.ny = n_row // self.nx
        self.nz, self.nc = n_col // 2, 2
        row, col = lax.axis_index("row"), lax.axis_index("col")
        self.y, self.x = row // self.nx, row % self.nx
        self.z, self.core = col // self.nc, col % self.nc

    def shift(self, value, axis):
        pairs = []
        for y in range(self.ny):
            for x in range(self.nx):
                to = (y, (x + 1) % self.nx) if axis == "x" else ((y + 1) % self.ny, x)
                pairs.append((y * self.nx + x, to[0] * self.nx + to[1]))
        return lax.ppermute(value, "row", pairs)

    def along_z(self, value, route):
        return lax.ppermute(
            value, "col", [(z * self.nc + c, to * self.nc + c) for z, to in route.items() for c in range(self.nc)]
        )

    def twin(self, value):
        return lax.ppermute(
            value, "col", [(z * self.nc + c, z * self.nc + 1 - c) for z in range(self.nz) for c in range(self.nc)]
        )

    def plane(self, tile):
        found = []
        for dy in range(self.ny):
            along = tile
            for dx in range(self.nx):
                found.append(along)
                along = self.shift(along, "x") if dx + 1 < self.nx else along
            tile = self.shift(tile, "y") if dy + 1 < self.ny else tile
        return found

    def plane_sources(self):
        found = [
            ((self.y - dy) % self.ny) * self.nx + (self.x - dx) % self.nx
            for dy in range(self.ny) for dx in range(self.nx)
        ]
        return jnp.stack(found).astype(jnp.int32)

    def around(self, value):
        found = [value]
        for _ in range(self.nz - 1):
            found.append(self.along_z(found[-1], {z: (z + 1) % self.nz for z in range(self.nz)}))
        return found

    def col_owners(self, *held):
        found = []
        for z in held:
            found += [z * self.nc + core for core in (self.core, 1 - self.core)]
        return jnp.stack(found).astype(jnp.int32)


NEAR = {0: 1, 1: 0, 2: 3, 3: 2}
MIRROR = {0: 3, 1: 2, 2: 1, 3: 0}


def per_device(n_row, n_col, g0_values, g0_pattern, sigma_values, sigma_pairs, sigma_count):
    block_rows, block_cols = g0_pattern.shape
    rows, cols = g0_values.shape
    slots, width = sigma_values.shape[1], sigma_values.shape[2]
    depth = rows * n_row
    grid = Grid(n_row, n_col)
    sources = grid.plane_sources()
    z = grid.z
    base = jnp.stack([lax.axis_index("row") * block_rows, lax.axis_index("col") * block_cols, sigma_count[0, 0]])
    message = pack(base.astype(jnp.int32), sigma_values, sigma_pairs)
    tile, upper, lower = masked(after(g0_values, message), g0_pattern)

    def names(parts, held_by):
        found = jnp.stack([part[slots * width:slots * width + 2, :slots] for part in parts]).astype(jnp.int32)
        row_at = jnp.where(found[:, 0] >= 0, found[:, 0] * width, -1)
        return row_at, held_by[:, None] * cols + found[:, 1] * width

    def dense_rows(owners, parts):
        return spread(*names(parts, owners), parts, slots, rows, depth)

    def dense_fill(owners, parts, first):
        return fill(*names(parts, owners), parts, first, slots)

    if (grid.ny, grid.nx, grid.nz) != (2, 2, 4):
        owners = grid.col_owners(*[(z - s) % grid.nz for s in range(grid.nz)])
        sigma_parts = []
        for value in grid.around(message):
            sigma_parts += [value, grid.twin(value)]
        dense = dense_fill(owners[-2:], sigma_parts[-2:], dense_rows(owners[:-2], sigma_parts[:-2]))
        turned = turn(sources, dense, grid.plane(tile))
        row_parts = []
        for value in grid.around(tile):
            row_parts += [value, grid.twin(value)]
        total, column = close(sources, owners[:-2], grid.plane(turned), row_parts[:-2])
        result = None
        for side in range(2):
            result = last(side, owners[-2:], total, column, [part[side] for part in row_parts[-2:]], result)
        return result

    with jax.named_scope("slots_far"):
        s_far = grid.along_z(message, MIRROR)
    with jax.named_scope("slots_near"):
        s_near = grid.along_z(message, NEAR)
    with jax.named_scope("g0_x"):
        by_x = grid.shift(tile, "x")
    with jax.named_scope("g0_y"):
        by_y = grid.shift(tile, "y")
    with jax.named_scope("slots_twin"):
        s_twin = grid.twin(message)
    slot_owners = grid.col_owners(z, z ^ 1, 3 - z, 3 - (z ^ 1))
    with jax.named_scope("slots_cross"):
        s_cross = grid.along_z(after(s_far, s_near), NEAR)
    with jax.named_scope("slots_far_twin"):
        s_far_twin = grid.twin(after(s_far, s_near))
    with jax.named_scope("slots_near_twin"):
        s_near_twin = grid.twin(after(s_near, s_far_twin))
    with jax.named_scope("g0_xy_upper"):
        far_upper = grid.shift(by_x[0], "y")
    with jax.named_scope("g0_xy_lower"):
        far_lower = grid.shift(by_y[1], "x")
    dense = dense_rows(slot_owners[:-2], [message, s_twin, s_near, s_near_twin, s_far, s_far_twin])
    with jax.named_scope("g0_near_upper"):
        near_u = grid.along_z(after(upper, s_cross), NEAR)
    with jax.named_scope("g0_far_upper"):
        far_u = grid.along_z(after(upper, s_cross), MIRROR)
    with jax.named_scope("slots_cross_twin"):
        s_cross_twin = grid.twin(after(s_cross, s_near_twin))
    dense = dense_fill(slot_owners[-2:], [s_cross, s_cross_twin], dense)
    turned = turn(sources, dense, [tile, by_x, by_y, far_upper, far_lower])

    with jax.named_scope("turned_x"):
        by_x = grid.shift(turned, "x")
    with jax.named_scope("turned_y"):
        by_y = grid.shift(turned, "y")
    with jax.named_scope("g0_near_lower"):
        near_l = grid.along_z(after(lower, near_u, far_u), NEAR)
    with jax.named_scope("g0_far_lower"):
        far_l = grid.along_z(after(lower, near_u, far_u), MIRROR)
    with jax.named_scope("g0_twin"):
        tile_twin = grid.twin(after(tile, turned))
    with jax.named_scope("g0_near_upper_twin"):
        near_u_twin = grid.twin(after(near_u, tile_twin))
    with jax.named_scope("g0_far_upper_twin"):
        far_u_twin = grid.twin(after(far_u, near_u_twin))
    with jax.named_scope("turned_xy_upper"):
        far_upper = grid.shift(by_x[0], "y")
    with jax.named_scope("turned_xy_lower"):
        far_lower = grid.shift(by_y[1], "x")
    with jax.named_scope("g0_cross_upper"):
        cross_u = grid.along_z(after(far_u, near_l, by_x, by_y), NEAR)
    with jax.named_scope("g0_near_lower_twin"):
        near_l_twin = grid.twin(near_l)
    with jax.named_scope("g0_far_lower_twin"):
        far_l_twin = grid.twin(after(far_l, near_l_twin))
    with jax.named_scope("g0_cross_lower"):
        cross_l = grid.along_z(after(far_l, near_l), NEAR)
    row_parts = [tile, tile_twin, near_u, near_l, near_u_twin, near_l_twin, far_u, far_l, far_u_twin, far_l_twin]
    total, column = close(sources, slot_owners[:-2], [turned, by_x, by_y, far_upper, far_lower], row_parts)
    with jax.named_scope("g0_cross_upper_twin"):
        cross_u_twin = grid.twin(after(cross_u, column))
    with jax.named_scope("g0_cross_lower_twin"):
        cross_l_twin = grid.twin(after(cross_l, column))
    result = last(0, slot_owners[-2:], total, column, [cross_u, cross_u_twin])
    return last(1, slot_owners[-2:], total, column, [cross_l, cross_l_twin], result)


def solution(mesh):
    placed = (
        P("row", "col"),
        P("row", "col"),
        P("row", "col", None, None),
        P("row", "col", None),
        P("row", "col"),
    )
    return jax.shard_map(
        functools.partial(per_device, mesh.shape["row"], mesh.shape["col"]),
        mesh=mesh, in_specs=placed, out_specs=P("row", "col"), check_vma=False,
    )
```

time: 145 us -> 132 us (0.910)
  local copies, waits for them, and re-layouts: 23.2 us -> 1.95 us
  starting transfers between devices: 36.1 us -> 25 us
  waiting for transfers between devices: 56.7 us -> 66.9 us
  Pallas kernels: 26.2 us -> 36.1 us
    unnamed x46 -> x12, local copies, waits for them, and re-layouts: 21.2 us -> 1.71 us
    ppermute x8 -> x9, starting transfers between devices: 24.7 us -> 13.2 us  [along_z(): lax.ppermute(value, 'col', [(z * self.nc + c, to * self.nc + c) for z, to...]
    ppermute x8 -> x9, waiting for transfers between devices: 39.5 us -> 50 us  [along_z(): lax.ppermute(value, 'col', [(z * self.nc + c, to * self.nc + c) for z, to...]
    pallas_call x3 -> x5, Pallas kernels: 16 us -> 25.6 us  [the longest x1 13.8 us: pack(): pl.pallas_call(functools.partial(pack_kernel, slots, width), out_shape=ja...]
    ppermute x10 -> x11, waiting for transfers between devices: 4.62 us -> 0.03 us  [twin(): lax.ppermute(value, 'col', [(z * self.nc + c, z * self.nc + 1 - c) for z...]
    ppermute x8, waiting for transfers between devices: 12.5 us -> 16.9 us  [shift(): return lax.ppermute(value, 'row', pairs)]
  transfers between devices with their start and end apart: 26 -> 28, of which waited for: 12 -> 11; matrix products, arithmetic and copies ran while one was open for 2% -> 1% of each run, Pallas kernels for 13% -> 15%
where the time goes in v5:
time: 132 us
  waiting for transfers between devices  66.9 us (51%)
  Pallas kernels  36.1 us (27%)
  starting transfers between devices  25 us (19%)
  local copies, waits for them, and re-layouts  1.95 us (1%)
    ppermute x9, waiting for transfers between devices, along_z(): lax.ppermute(value, 'col', [(z * self.nc + c, to * self.nc + c) for z, to...  50 us
    ppermute x8, waiting for transfers between devices, shift(): return lax.ppermute(value, 'row', pairs)  16.9 us
    pallas_call x1, Pallas kernels, pack(): pl.pallas_call(functools.partial(pack_kernel, slots, width), out_shape=ja...  13.8 us
    ppermute x9, starting transfers between devices, along_z(): lax.ppermute(value, 'col', [(z * self.nc + c, to * self.nc + c) for z, to...  13.2 us
    ppermute x8, starting transfers between devices, shift(): return lax.ppermute(value, 'row', pairs)  11.2 us
    pallas_call x1, Pallas kernels, turn(): pl.pallas_call(turn_kernel, out_shape=jax.ShapeDtypeStruct((2, half, cols...  5.72 us
    pallas_call x1, Pallas kernels, close(): pl.pallas_call(functools.partial(close_kernel, n_col), out_shape=(jax.Sha...  4.95 us
    pallas_call x2, Pallas kernels, last(): pl.pallas_call(functools.partial(last_kernel, side, n_row), out_shape=jax...  3.95 us
  transfers between devices with their start and end apart: 28, of which 11 were waited for; matrix products, arithmetic and copies ran while one was open for 1% of the time, Pallas kernels for 15%

profile of v5, /device:TPU:0, one launch (start us, length us, event | category | flops | bytes accessed | tf_op | source)
XLA Modules:
  0.0 131.7 jit_solution(392046738751568171)
XLA Ops:
  1.2 13.8 %pack.1.refs_0_ = bf16[1552,128]{1,0:T(8,128)(2,1)} custom-call(s32[3]{0:T(128)} %pad_add_fusion.2.base_ref, bf16[1,12,128,128]{3,2,1,0:T(8,128)(2,1)} %slots_ref.1, s32[2,12]{1,0:T(2,128)} %bitcast.67), custom_call_target="tpu_custom_call" | custom-call | tf_op jit(solution)/shard_map/pack/pallas_call | solution.py:55
  15.0 5.1 %collective-permute-start = (bf16[1552,128]{1,0:T(8,128)(2,1)}, bf16[1552,128]{1,0:T(8,128)(2,1)S(1)}, u32[]{:S(2)}, u32[]{:S(2)}) collective-permute-start(bf16[1552,128]{1,0:T(8,128)(2,1)} %pack.1.refs_0_), channel_id=1, source_target_pairs={{0,6},{1,7},{2,4},{3,5},{4,2},{5,3},{6,0},{7,1},{8,14},{9,15},{10,... | collective-permute-start | bytes 1191944 | tf_op jit(solution)/shard_map/slots_far/ppermute | solution.py:347
  20.2 2.9 %mask.1 = (bf16[2,512,512]{2,1,0:T(8,128)(2,1)}, bf16[512,512]{1,0:T(8,128)(2,1)}, bf16[512,512]{1,0:T(8,128)(2,1)}) custom-call(s32[4,8]{1,0:T(4,128)} %bitcast.66, bf16[1024,512]{1,0:T(8,128)(2,1)} %values_ref), custom_call_target="tpu_custom_call" | custom-call | tf_op jit(solution)/shard_map/mask/pallas_call | solution.py:110
  23.0 1.6 %collective-permute-start.7 = (bf16[2,512,512]{2,1,0:T(8,128)(2,1)}, bf16[2,512,512]{2,1,0:T(8,128)(2,1)S(1)}, u32[]{:S(2)}, u32[]{:S(2)}) collective-permute-start(bf16[2,512,512]{2,1,0:T(8,128)(2,1)} %get-tuple-element.29.own_ref.refs_5_), channel_id=1, source_target_pairs={{0,8},{8,0},{16,24},{24,16},{1,9},{9,1},{17,25},{25,17},{2,10},{10... | collective-permute-start | bytes 3145736 | tf_op jit(solution)/shard_map/g0_x/ppermute | solution.py:344
  24.6 1.5 %collective-permute-start.8 = (bf16[2,512,512]{2,1,0:T(8,128)(2,1)}, bf16[2,512,512]{2,1,0:T(8,128)(2,1)S(1)}, u32[]{:S(2)}, u32[]{:S(2)}) collective-permute-start(bf16[2,512,512]{2,1,0:T(8,128)(2,1)} %get-tuple-element.29.own_ref.refs_5_), channel_id=1, source_target_pairs={{0,16},{8,24},{16,0},{24,8},{1,17},{9,25},{17,1},{25,9},{2,18},{10... | collective-permute-start | bytes 3145736 | tf_op jit(solution)/shard_map/g0_y/ppermute | solution.py:344
  27.0 3.4 %collective-permute-done.refs_4_ = bf16[1552,128]{1,0:T(8,128)(2,1)S(1)} collective-permute-done((bf16[1552,128]{1,0:T(8,128)(2,1)}, bf16[1552,128]{1,0:T(8,128)(2,1)S(1)}, u32[]{:S(2)}, u32[]{:S(2)}) %collective-permute-start) | collective-permute-done | bytes 397344 | tf_op jit(solution)/shard_map/slots_far/ppermute | solution.py:347
  30.5 7.7 %collective-permute-done.1.refs_2_ = bf16[1552,128]{1,0:T(8,128)(2,1)S(1)} collective-permute-done((bf16[1552,128]{1,0:T(8,128)(2,1)}, bf16[1552,128]{1,0:T(8,128)(2,1)S(1)}, u32[]{:S(2)}, u32[]{:S(2)}) %collective-permute-start.1) | collective-permute-done | bytes 397344 | tf_op jit(solution)/shard_map/slots_near/ppermute | solution.py:347
  38.2 1.7 %collective-permute-start.2 = (bf16[1552,128]{1,0:T(8,128)(2,1)S(1)}, bf16[1552,128]{1,0:T(8,128)(2,1)S(1)}, u32[]{:S(2)}, u32[]{:S(2)}) collective-permute-start(bf16[1552,128]{1,0:T(8,128)(2,1)S(1)} %collective-permute-done.refs_4_), channel_id=1, source_target_pairs={{0,2},{1,3},{2,0},{3,1},{4,6},{5,7},{6,4},{7,5},{8,10},{9,11},{10,... | collective-permute-start | bytes 1191944 | tf_op jit(solution)/shard_map/slots_cross/ppermute | solution.py:347
  39.9 9.4 %collective-permute-done.2.refs_0_ = bf16[1552,128]{1,0:T(8,128)(2,1)S(1)} collective-permute-done((bf16[1552,128]{1,0:T(8,128)(2,1)S(1)}, bf16[1552,128]{1,0:T(8,128)(2,1)S(1)}, u32[]{:S(2)}, u32[]{:S(2)}) %collective-permute-start.2) | collective-permute-done | bytes 397344 | tf_op jit(solution)/shard_map/slots_cross/ppermute | solution.py:347
  52.1 1.6 %collective-permute-start.10 = (bf16[512,512]{1,0:T(8,128)(2,1)S(1)}, bf16[512,512]{1,0:T(8,128)(2,1)S(1)}, u32[]{:S(2)}, u32[]{:S(2)}) collective-permute-start(bf16[512,512]{1,0:T(8,128)(2,1)S(1)} %slice_bitcast_fusion.2), channel_id=1, source_target_pairs={{0,8},{8,0},{16,24},{24,16},{1,9},{9,1},{17,25},{25,17},{2,10},{10... | collective-permute-start | bytes 1572872 | tf_op jit(solution)/shard_map/g0_xy_lower/ppermute | solution.py:344
  54.8 3.6 %spread.1.refs_2_ = bf16[1024,4096]{1,0:T(8,128)(2,1)S(1)} custom-call(s32[6,12]{1,0:T(8,128)S(1)} %bitcast.63, s32[6,12]{1,0:T(8,128)S(1)} %bitcast_add_fusion.col_ref, bf16[1552,128]{1,0:T(8,128)(2,1)S(1)} %copy-done.1, bf16[1552,128]{1,0:T(8,128)(2,1)S(1)} %collective-permute-done.6.refs_1_, bf16[1552,128]{1,0:T(8,128)(2,1)S(1)} %collective-permute-done.1.refs_2_, ...), custom_call_target="tpu_custom_call" | custom-call | tf_op jit(solution)/shard_map/spread/pallas_call | solution.py:155
  59.7 5.3 %collective-permute-done.9.refs_2_ = bf16[512,512]{1,0:T(8,128)(2,1)S(1)} collective-permute-done((bf16[512,512]{1,0:T(8,128)(2,1)S(1)}, bf16[512,512]{1,0:T(8,128)(2,1)S(1)}, u32[]{:S(2)}, u32[]{:S(2)}) %collective-permute-start.9) | collective-permute-done | bytes 524320 | tf_op jit(solution)/shard_map/g0_xy_upper/ppermute | solution.py:344
  66.2 5.7 %turn.1.refs_0_ = bf16[2,512,512]{2,1,0:T(8,128)(2,1)S(1)} custom-call(s32[4]{0:T(128)S(1)} %pad_add_fusion.1.source_ref, bf16[1024,4096]{1,0:T(8,128)(2,1)S(1)} %fill.1.dense_ref, bf16[2,512,512]{2,1,0:T(8,128)(2,1)S(1)} %copy-done, bf16[2,512,512]{2,1,0:T(8,128)(2,1)S(1)} %collective-permute-done.7.refs_0_, ...), custom_call_target="tpu_custom_call" | custom-call | tf_op jit(solution)/shard_map/turn/pallas_call | solution.py:218
  72.0 1.8 %collective-permute-done.16.refs_7_ = bf16[512,512]{1,0:T(8,128)(2,1)S(1)} collective-permute-done((bf16[512,512]{1,0:T(8,128)(2,1)}, bf16[512,512]{1,0:T(8,128)(2,1)S(1)}, u32[]{:S(2)}, u32[]{:S(2)}) %collective-permute-start.16) | collective-permute-done | bytes 524320 | tf_op jit(solution)/shard_map/g0_near_upper/ppermute | solution.py:347
  73.8 1.7 %collective-permute-start.18 = (bf16[512,512]{1,0:T(8,128)(2,1)S(1)}, bf16[512,512]{1,0:T(8,128)(2,1)S(1)}, u32[]{:S(2)}, u32[]{:S(2)}) collective-permute-start(bf16[512,512]{1,0:T(8,128)(2,1)S(1)} %copy-done.2), channel_id=1, source_target_pairs={{0,2},{1,3},{2,0},{3,1},{4,6},{5,7},{6,4},{7,5},{8,10},{9,11},{10,... | collective-permute-start | bytes 1572872 | tf_op jit(solution)/shard_map/g0_near_lower/ppermute | solution.py:347
  79.7 8.2 %collective-permute-done.18.refs_8_ = bf16[512,512]{1,0:T(8,128)(2,1)S(1)} collective-permute-done((bf16[512,512]{1,0:T(8,128)(2,1)S(1)}, bf16[512,512]{1,0:T(8,128)(2,1)S(1)}, u32[]{:S(2)}, u32[]{:S(2)}) %collective-permute-start.18) | collective-permute-done | bytes 524320 | tf_op jit(solution)/shard_map/g0_near_lower/ppermute | solution.py:347
  88.4 11.2 %collective-permute-done.21.refs_12_ = bf16[512,512]{1,0:T(8,128)(2,1)S(1)} collective-permute-done((bf16[512,512]{1,0:T(8,128)(2,1)S(1)}, bf16[512,512]{1,0:T(8,128)(2,1)S(1)}, u32[]{:S(2)}, u32[]{:S(2)}) %collective-permute-start.21) | collective-permute-done | bytes 524320 | tf_op jit(solution)/shard_map/g0_far_lower/ppermute | solution.py:347
  100.3 1.6 %collective-permute-start.14 = (bf16[512,512]{1,0:T(8,128)(2,1)S(1)}, bf16[512,512]{1,0:T(8,128)(2,1)S(1)}, u32[]{:S(2)}, u32[]{:S(2)}) collective-permute-start(bf16[512,512]{1,0:T(8,128)(2,1)S(1)} %slice_bitcast_fusion), channel_id=1, source_target_pairs={{0,8},{8,0},{16,24},{24,16},{1,9},{9,1},{17,25},{25,17},{2,10},{10... | collective-permute-start | bytes 1572872 | tf_op jit(solution)/shard_map/turned_xy_lower/ppermute | solution.py:344
  101.8 2.1 %collective-permute-start.26 = (bf16[512,512]{1,0:T(8,128)(2,1)S(1)}, bf16[512,512]{1,0:T(8,128)(2,1)S(1)}, u32[]{:S(2)}, u32[]{:S(2)}) collective-permute-start(bf16[512,512]{1,0:T(8,128)(2,1)S(1)} %collective-permute-done.17.refs_11_), channel_id=1, source_target_pairs={{0,2},{1,3},{2,0},{3,1},{4,6},{5,7},{6,4},{7,5},{8,10},{9,11},{10,... | collective-permute-start | bytes 1572872 | tf_op jit(solution)/shard_map/g0_cross_upper/ppermute | solution.py:347
  104.0 10.1 %collective-permute-done.13.refs_3_ = bf16[512,512]{1,0:T(8,128)(2,1)S(1)} collective-permute-done((bf16[512,512]{1,0:T(8,128)(2,1)S(1)}, bf16[512,512]{1,0:T(8,128)(2,1)S(1)}, u32[]{:S(2)}, u32[]{:S(2)}) %collective-permute-start.13) | collective-permute-done | bytes 524320 | tf_op jit(solution)/shard_map/turned_xy_upper/ppermute | solution.py:344
  114.4 4.9 %close.1 = (f32[2,512,512]{2,1,0:T(8,128)S(1)}, bf16[4096,512]{1,0:T(8,128)(2,1)S(1)}) custom-call(s32[4]{0:T(128)S(1)} %pad_add_fusion.1.source_ref, s32[6]{0:T(128)S(1)} %stack.97.owner_ref, bf16[2,512,512]{2,1,0:T(8,128)(2,1)S(1)} %turn.1.refs_0_, bf16[2,512,512]{2,1,0:T(8,128)(2,1)S(1)} %collective-permute-done.11.refs_1_, ...), custom_call_target="tpu_custom_call" | custom-call | tf_op jit(solution)/shard_map/close/pallas_call | solution.py:267
  119.4 8.3 %collective-permute-done.24.refs_0_ = bf16[512,512]{1,0:T(8,128)(2,1)S(1)} collective-permute-done((bf16[512,512]{1,0:T(8,128)(2,1)S(1)}, bf16[512,512]{1,0:T(8,128)(2,1)S(1)}, u32[]{:S(2)}, u32[]{:S(2)}) %collective-permute-start.24) | collective-permute-done | bytes 524320 | tf_op jit(solution)/shard_map/g0_cross_lower/ppermute | solution.py:347
  127.7 2.0 %last.2.refs_2_ = bf16[1024,512]{1,0:T(8,128)(2,1)} custom-call(s32[2]{0:T(128)S(1)} %get-tuple-element.44.owner_ref, f32[2,512,512]{2,1,0:T(8,128)S(1)} %get-tuple-element.37.total_ref, bf16[4096,512]{1,0:T(8,128)(2,1)S(1)} %get-tuple-element.38.column_ref, bf16[512,512]{1,0:T(8,128)(2,1)S(1)} %collective-permute-done.26.refs_0_, ...), custom_call_target="tpu_custom_call" | custom-call | tf_op jit(solution)/shard_map/last/pallas_call | solution.py:312
  129.7 2.0 %last.3 = bf16[1024,512]{1,0:T(8,128)(2,1)} custom-call(s32[2]{0:T(128)S(1)} %get-tuple-element.44.owner_ref, f32[2,512,512]{2,1,0:T(8,128)S(1)} %get-tuple-element.37.total_ref, bf16[4096,512]{1,0:T(8,128)(2,1)S(1)} %get-tuple-element.38.column_ref, bf16[512,512]{1,0:T(8,128)(2,1)S(1)} %collective-permute-done.24.refs_0_, ...), custom_call_target="tpu_custom_call", output_to_operand_aliasing={{}: (5, {})} | custom-call | tf_op jit(solution)/shard_map/last/pallas_call | solution.py:312
  (70 shorter events, 13.8 us)
Async XLA Ops:
  15.0 15.4 %collective-permute-start = (bf16[1552,128]{1,0:T(8,128)(2,1)}, bf16[1552,128]{1,0:T(8,128)(2,1)S(1)}, u32[]{:S(2)}, u32[]{:S(2)}) collective-permute-start(bf16[1552,128]{1,0:T(8,128)(2,1)} %pack.1.refs_0_), channel_id=1, source_target_pairs={{0,6},{1,7},{2,4},{3,5},{4,2},{5,3},{6,0},{7,1},{8,14},{9,15},{10,... | collective-permute-start | bytes 1191944 | tf_op jit(solution)/shard_map/slots_far/ppermute | solution.py:347
  20.1 18.0 %collective-permute-start.1 = (bf16[1552,128]{1,0:T(8,128)(2,1)}, bf16[1552,128]{1,0:T(8,128)(2,1)S(1)}, u32[]{:S(2)}, u32[]{:S(2)}) collective-permute-start(bf16[1552,128]{1,0:T(8,128)(2,1)} %pack.1.refs_0_), channel_id=1, source_target_pairs={{0,2},{1,3},{2,0},{3,1},{4,6},{5,7},{6,4},{7,5},{8,10},{9,11},{10,... | collective-permute-start | bytes 1191944 | tf_op jit(solution)/shard_map/slots_near/ppermute | solution.py:347
  20.2 19.7 %collective-permute-start.6 = (bf16[1552,128]{1,0:T(8,128)(2,1)}, bf16[1552,128]{1,0:T(8,128)(2,1)S(1)}, u32[]{:S(2)}, u32[]{:S(2)}) collective-permute-start(bf16[1552,128]{1,0:T(8,128)(2,1)} %pack.1.refs_0_), channel_id=1, source_target_pairs={{0,1},{1,0},{2,3},{3,2},{4,5},{5,4},{6,7},{7,6},{8,9},{9,8},{10,11... | collective-permute-start | bytes 1191944 | tf_op jit(solution)/shard_map/slots_twin/ppermute | solution.py:352
  23.0 27.5 %collective-permute-start.7 = (bf16[2,512,512]{2,1,0:T(8,128)(2,1)}, bf16[2,512,512]{2,1,0:T(8,128)(2,1)S(1)}, u32[]{:S(2)}, u32[]{:S(2)}) collective-permute-start(bf16[2,512,512]{2,1,0:T(8,128)(2,1)} %get-tuple-element.29.own_ref.refs_5_), channel_id=1, source_target_pairs={{0,8},{8,0},{16,24},{24,16},{1,9},{9,1},{17,25},{25,17},{2,10},{10... | collective-permute-start | bytes 3145736 | tf_op jit(solution)/shard_map/g0_x/ppermute | solution.py:344
  24.6 27.4 %collective-permute-start.8 = (bf16[2,512,512]{2,1,0:T(8,128)(2,1)}, bf16[2,512,512]{2,1,0:T(8,128)(2,1)S(1)}, u32[]{:S(2)}, u32[]{:S(2)}) collective-permute-start(bf16[2,512,512]{2,1,0:T(8,128)(2,1)} %get-tuple-element.29.own_ref.refs_5_), channel_id=1, source_target_pairs={{0,16},{8,24},{16,0},{24,8},{1,17},{9,25},{17,1},{25,9},{2,18},{10... | collective-permute-start | bytes 3145736 | tf_op jit(solution)/shard_map/g0_y/ppermute | solution.py:344
  38.2 11.1 %collective-permute-start.2 = (bf16[1552,128]{1,0:T(8,128)(2,1)S(1)}, bf16[1552,128]{1,0:T(8,128)(2,1)S(1)}, u32[]{:S(2)}, u32[]{:S(2)}) collective-permute-start(bf16[1552,128]{1,0:T(8,128)(2,1)S(1)} %collective-permute-done.refs_4_), channel_id=1, source_target_pairs={{0,2},{1,3},{2,0},{3,1},{4,6},{5,7},{6,4},{7,5},{8,10},{9,11},{10,... | collective-permute-start | bytes 1191944 | tf_op jit(solution)/shard_map/slots_cross/ppermute | solution.py:347
  39.9 10.7 %collective-permute-start.3 = (bf16[1552,128]{1,0:T(8,128)(2,1)S(1)}, bf16[1552,128]{1,0:T(8,128)(2,1)S(1)}, u32[]{:S(2)}, u32[]{:S(2)}) collective-permute-start(bf16[1552,128]{1,0:T(8,128)(2,1)S(1)} %collective-permute-done.refs_4_), channel_id=1, source_target_pairs={{0,1},{1,0},{2,3},{3,2},{4,5},{5,4},{6,7},{7,6},{8,9},{9,8},{10,11... | collective-permute-start | bytes 1191944 | tf_op jit(solution)/shard_map/slots_far_twin/ppermute | solution.py:352
  49.3 24.4 %collective-permute-start.16 = (bf16[512,512]{1,0:T(8,128)(2,1)}, bf16[512,512]{1,0:T(8,128)(2,1)S(1)}, u32[]{:S(2)}, u32[]{:S(2)}) collective-permute-start(bf16[512,512]{1,0:T(8,128)(2,1)} %get-tuple-element.31), channel_id=1, source_target_pairs={{0,2},{1,3},{2,0},{3,1},{4,6},{5,7},{6,4},{7,5},{8,10},{9,11},{10,... | collective-permute-start | bytes 1572872 | tf_op jit(solution)/shard_map/g0_near_upper/ppermute | solution.py:347
  50.0 23.8 %collective-permute-start.17 = (bf16[512,512]{1,0:T(8,128)(2,1)}, bf16[512,512]{1,0:T(8,128)(2,1)S(1)}, u32[]{:S(2)}, u32[]{:S(2)}) collective-permute-start(bf16[512,512]{1,0:T(8,128)(2,1)} %get-tuple-element.31), channel_id=1, source_target_pairs={{0,6},{1,7},{2,4},{3,5},{4,2},{5,3},{6,0},{7,1},{8,14},{9,15},{10,... | collective-permute-start | bytes 1572872 | tf_op jit(solution)/shard_map/g0_far_upper/ppermute | solution.py:347
  50.6 14.4 %collective-permute-start.9 = (bf16[512,512]{1,0:T(8,128)(2,1)S(1)}, bf16[512,512]{1,0:T(8,128)(2,1)S(1)}, u32[]{:S(2)}, u32[]{:S(2)}) collective-permute-start(bf16[512,512]{1,0:T(8,128)(2,1)S(1)} %slice_bitcast_fusion.3), channel_id=1, source_target_pairs={{0,16},{8,24},{16,0},{24,8},{1,17},{9,25},{17,1},{25,9},{2,18},{10... | collective-permute-start | bytes 1572872 | tf_op jit(solution)/shard_map/g0_xy_upper/ppermute | solution.py:344
  52.1 14.1 %collective-permute-start.10 = (bf16[512,512]{1,0:T(8,128)(2,1)S(1)}, bf16[512,512]{1,0:T(8,128)(2,1)S(1)}, u32[]{:S(2)}, u32[]{:S(2)}) collective-permute-start(bf16[512,512]{1,0:T(8,128)(2,1)S(1)} %slice_bitcast_fusion.2), channel_id=1, source_target_pairs={{0,8},{8,0},{16,24},{24,16},{1,9},{9,1},{17,25},{25,17},{2,10},{10... | collective-permute-start | bytes 1572872 | tf_op jit(solution)/shard_map/g0_xy_lower/ppermute | solution.py:344
  71.9 16.0 %collective-permute-start.15 = (bf16[2,512,512]{2,1,0:T(8,128)(2,1)S(1)}, bf16[2,512,512]{2,1,0:T(8,128)(2,1)S(1)}, u32[]{:S(2)}, u32[]{:S(2)}) collective-permute-start(bf16[2,512,512]{2,1,0:T(8,128)(2,1)S(1)} %copy-done), channel_id=1, source_target_pairs={{0,1},{1,0},{2,3},{3,2},{4,5},{5,4},{6,7},{7,6},{8,9},{9,8},{10,11... | collective-permute-start | bytes 3145736 | tf_op jit(solution)/shard_map/g0_twin/ppermute | solution.py:352
  73.8 14.1 %collective-permute-start.18 = (bf16[512,512]{1,0:T(8,128)(2,1)S(1)}, bf16[512,512]{1,0:T(8,128)(2,1)S(1)}, u32[]{:S(2)}, u32[]{:S(2)}) collective-permute-start(bf16[512,512]{1,0:T(8,128)(2,1)S(1)} %copy-done.2), channel_id=1, source_target_pairs={{0,2},{1,3},{2,0},{3,1},{4,6},{5,7},{6,4},{7,5},{8,10},{9,11},{10,... | collective-permute-start | bytes 1572872 | tf_op jit(solution)/shard_map/g0_near_lower/ppermute | solution.py:347
  75.5 24.1 %collective-permute-start.11 = (bf16[2,512,512]{2,1,0:T(8,128)(2,1)S(1)}, bf16[2,512,512]{2,1,0:T(8,128)(2,1)S(1)}, u32[]{:S(2)}, u32[]{:S(2)}) collective-permute-start(bf16[2,512,512]{2,1,0:T(8,128)(2,1)S(1)} %turn.1.refs_0_), channel_id=1, source_target_pairs={{0,8},{8,0},{16,24},{24,16},{1,9},{9,1},{17,25},{25,17},{2,10},{10... | collective-permute-start | bytes 3145736 | tf_op jit(solution)/shard_map/turned_x/ppermute | solution.py:344
  77.0 23.2 %collective-permute-start.12 = (bf16[2,512,512]{2,1,0:T(8,128)(2,1)S(1)}, bf16[2,512,512]{2,1,0:T(8,128)(2,1)S(1)}, u32[]{:S(2)}, u32[]{:S(2)}) collective-permute-start(bf16[2,512,512]{2,1,0:T(8,128)(2,1)S(1)} %turn.1.refs_0_), channel_id=1, source_target_pairs={{0,16},{8,24},{16,0},{24,8},{1,17},{9,25},{17,1},{25,9},{2,18},{10... | collective-permute-start | bytes 3145736 | tf_op jit(solution)/shard_map/turned_y/ppermute | solution.py:344
  78.5 21.1 %collective-permute-start.21 = (bf16[512,512]{1,0:T(8,128)(2,1)S(1)}, bf16[512,512]{1,0:T(8,128)(2,1)S(1)}, u32[]{:S(2)}, u32[]{:S(2)}) collective-permute-start(bf16[512,512]{1,0:T(8,128)(2,1)S(1)} %copy-done.2), channel_id=1, source_target_pairs={{0,6},{1,7},{2,4},{3,5},{4,2},{5,3},{6,0},{7,1},{8,14},{9,15},{10,... | collective-permute-start | bytes 1572872 | tf_op jit(solution)/shard_map/g0_far_lower/ppermute | solution.py:347
  87.9 11.7 %collective-permute-start.20 = (bf16[512,512]{1,0:T(8,128)(2,1)S(1)}, bf16[512,512]{1,0:T(8,128)(2,1)S(1)}, u32[]{:S(2)}, u32[]{:S(2)}) collective-permute-start(bf16[512,512]{1,0:T(8,128)(2,1)S(1)} %collective-permute-done.18.refs_8_), channel_id=1, source_target_pairs={{0,1},{1,0},{2,3},{3,2},{4,5},{5,4},{6,7},{7,6},{8,9},{9,8},{10,11... | collective-permute-start | bytes 1572872 | tf_op jit(solution)/shard_map/g0_near_lower_twin/ppermute | solution.py:352
  87.9 13.9 %collective-permute-start.19 = (bf16[512,512]{1,0:T(8,128)(2,1)S(1)}, bf16[512,512]{1,0:T(8,128)(2,1)S(1)}, u32[]{:S(2)}, u32[]{:S(2)}) collective-permute-start(bf16[512,512]{1,0:T(8,128)(2,1)S(1)} %collective-permute-done.16.refs_7_), channel_id=1, source_target_pairs={{0,1},{1,0},{2,3},{3,2},{4,5},{5,4},{6,7},{7,6},{8,9},{9,8},{10,11... | collective-permute-start | bytes 1572872 | tf_op jit(solution)/shard_map/g0_near_upper_twin/ppermute | solution.py:352
  99.6 14.4 %collective-permute-start.13 = (bf16[512,512]{1,0:T(8,128)(2,1)S(1)}, bf16[512,512]{1,0:T(8,128)(2,1)S(1)}, u32[]{:S(2)}, u32[]{:S(2)}) collective-permute-start(bf16[512,512]{1,0:T(8,128)(2,1)S(1)} %slice_bitcast_fusion.1), channel_id=1, source_target_pairs={{0,16},{8,24},{16,0},{24,8},{1,17},{9,25},{17,1},{25,9},{2,18},{10... | collective-permute-start | bytes 1572872 | tf_op jit(solution)/shard_map/turned_xy_upper/ppermute | solution.py:344
  100.3 14.1 %collective-permute-start.14 = (bf16[512,512]{1,0:T(8,128)(2,1)S(1)}, bf16[512,512]{1,0:T(8,128)(2,1)S(1)}, u32[]{:S(2)}, u32[]{:S(2)}) collective-permute-start(bf16[512,512]{1,0:T(8,128)(2,1)S(1)} %slice_bitcast_fusion), channel_id=1, source_target_pairs={{0,8},{8,0},{16,24},{24,16},{1,9},{9,1},{17,25},{25,17},{2,10},{10... | collective-permute-start | bytes 1572872 | tf_op jit(solution)/shard_map/turned_xy_lower/ppermute | solution.py:344
  101.8 12.6 %collective-permute-start.22 = (bf16[512,512]{1,0:T(8,128)(2,1)S(1)}, bf16[512,512]{1,0:T(8,128)(2,1)S(1)}, u32[]{:S(2)}, u32[]{:S(2)}) collective-permute-start(bf16[512,512]{1,0:T(8,128)(2,1)S(1)} %collective-permute-done.17.refs_11_), channel_id=1, source_target_pairs={{0,1},{1,0},{2,3},{3,2},{4,5},{5,4},{6,7},{7,6},{8,9},{9,8},{10,11... | collective-permute-start | bytes 1572872 | tf_op jit(solution)/shard_map/g0_far_upper_twin/ppermute | solution.py:352
  101.8 17.5 %collective-permute-start.26 = (bf16[512,512]{1,0:T(8,128)(2,1)S(1)}, bf16[512,512]{1,0:T(8,128)(2,1)S(1)}, u32[]{:S(2)}, u32[]{:S(2)}) collective-permute-start(bf16[512,512]{1,0:T(8,128)(2,1)S(1)} %collective-permute-done.17.refs_11_), channel_id=1, source_target_pairs={{0,2},{1,3},{2,0},{3,1},{4,6},{5,7},{6,4},{7,5},{8,10},{9,11},{10,... | collective-permute-start | bytes 1572872 | tf_op jit(solution)/shard_map/g0_cross_upper/ppermute | solution.py:347
  103.9 23.8 %collective-permute-start.24 = (bf16[512,512]{1,0:T(8,128)(2,1)S(1)}, bf16[512,512]{1,0:T(8,128)(2,1)S(1)}, u32[]{:S(2)}, u32[]{:S(2)}) collective-permute-start(bf16[512,512]{1,0:T(8,128)(2,1)S(1)} %collective-permute-done.21.refs_12_), channel_id=1, source_target_pairs={{0,2},{1,3},{2,0},{3,1},{4,6},{5,7},{6,4},{7,5},{8,10},{9,11},{10,... | collective-permute-start | bytes 1572872 | tf_op jit(solution)/shard_map/g0_cross_lower/ppermute | solution.py:347
  119.3 8.4 %collective-permute-start.27 = (bf16[512,512]{1,0:T(8,128)(2,1)S(1)}, bf16[512,512]{1,0:T(8,128)(2,1)S(1)}, u32[]{:S(2)}, u32[]{:S(2)}) collective-permute-start(bf16[512,512]{1,0:T(8,128)(2,1)S(1)} %collective-permute-done.26.refs_0_), channel_id=1, source_target_pairs={{0,1},{1,0},{2,3},{3,2},{4,5},{5,4},{6,7},{7,6},{8,9},{9,8},{10,11... | collective-permute-start | bytes 1572872 | tf_op jit(solution)/shard_map/g0_cross_upper_twin/ppermute | solution.py:352
  (7 other events, 36.8 us)

commit v6 on v5

--- a/solution.py
+++ b/solution.py
@@ -26,15 +26,11 @@
     return lax.optimization_barrier((value, *earlier))[0]
 
 
-def pack_kernel(slots, width, base_ref, slots_ref, pairs_ref, message_ref, pairs, names, tail, sems, tail_sem):
-    fetch = pltpu.make_async_copy(pairs_ref, pairs, tail_sem)
+def pack_kernel(slots, width, base_ref, slots_ref, pairs_ref, message_ref, pairs, names, message, pair_sem, in_sem, out_sem):
+    fetch = pltpu.make_async_copy(pairs_ref, pairs, pair_sem)
     fetch.start()
-    moves = [
-        pltpu.make_async_copy(slots_ref.at[0, s], message_ref.at[pl.ds(s * width, width)], sems.at[s])
-        for s in range(slots)
-    ]
-    for move in moves:
-        move.start()
+    take = pltpu.make_async_copy(slots_ref.at[0], message.at[pl.ds(0, slots)], in_sem)
+    take.start()
     names[...] = jnp.full(names.shape, -1, jnp.int32)
     fetch.wait()
     shape = pairs.shape
@@ -42,12 +38,20 @@
     local = pairs[...] - jnp.where(first, base_ref[0], base_ref[1])
     live = lax.broadcasted_iota(jnp.int32, shape, 1) < base_ref[2]
     names[pl.ds(0, shape[0]), pl.ds(0, shape[1])] = jnp.where(live, local, -1)
-    tail[...] = names[...].astype(jnp.float32).astype(jnp.bfloat16)
-    give = pltpu.make_async_copy(tail, message_ref.at[pl.ds(slots * width, TAIL)], tail_sem)
-    give.start()
-    for move in moves:
-        move.wait()
-    give.wait()
+    message[slots, pl.ds(0, TAIL), :] = names[...].astype(jnp.float32).astype(jnp.bfloat16)
+    take.wait()
+    gives = [
+        pltpu.make_async_copy(message.at[s], message_ref.at[pl.ds(s * width, width)], out_sem.at[s]) for s in range(slots)
+    ]
+    gives.append(
+        pltpu.make_async_copy(
+            message.at[slots, pl.ds(0, TAIL)], message_ref.at[pl.ds(slots * width, TAIL)], out_sem.at[slots]
+        )
+    )
+    for give in gives:
+        give.start()
+    for give in gives:
+        give.wait()
 
 
 def pack(base, sigma_values, sigma_pairs):
@@ -60,9 +64,10 @@
         scratch_shapes=[
             pltpu.VMEM((2, slots), jnp.int32),
             pltpu.VMEM((TAIL, width), jnp.int32),
-            pltpu.VMEM((TAIL, width), jnp.bfloat16),
-            pltpu.SemaphoreType.DMA((slots,)),
+            pltpu.VMEM((slots + 1, width, width), jnp.bfloat16),
             pltpu.SemaphoreType.DMA,
+            pltpu.SemaphoreType.DMA,
+            pltpu.SemaphoreType.DMA((slots + 1,)),
         ],
         compiler_params=pltpu.CompilerParams(vmem_limit_bytes=FIRST_VMEM_BYTES),
         cost_estimate=NO_COST,
@@ -451,26 +456,26 @@
     with jax.named_scope("g0_near_upper"):
         near_u = grid.along_z(after(upper, s_cross), NEAR)
     with jax.named_scope("g0_far_upper"):
-        far_u = grid.along_z(after(upper, s_cross), MIRROR)
+        far_u = grid.along_z(after(upper, s_far, s_near), MIRROR)
     with jax.named_scope("slots_cross_twin"):
         s_cross_twin = grid.twin(after(s_cross, s_near_twin))
     dense = dense_fill(slot_owners[-2:], [s_cross, s_cross_twin], dense)
     turned = turn(sources, dense, [tile, by_x, by_y, far_upper, far_lower])
 
+    with jax.named_scope("g0_far_upper_twin"):
+        far_u_twin = grid.twin(after(far_u, far_upper, far_lower))
     with jax.named_scope("turned_x"):
         by_x = grid.shift(turned, "x")
     with jax.named_scope("turned_y"):
         by_y = grid.shift(turned, "y")
-    with jax.named_scope("g0_near_lower"):
-        near_l = grid.along_z(after(lower, near_u, far_u), NEAR)
     with jax.named_scope("g0_far_lower"):
-        far_l = grid.along_z(after(lower, near_u, far_u), MIRROR)
+        far_l = grid.along_z(after(lower, far_u_twin), MIRROR)
     with jax.named_scope("g0_twin"):
         tile_twin = grid.twin(after(tile, turned))
     with jax.named_scope("g0_near_upper_twin"):
         near_u_twin = grid.twin(after(near_u, tile_twin))
-    with jax.named_scope("g0_far_upper_twin"):
-        far_u_twin = grid.twin(after(far_u, near_u_twin))
+    with jax.named_scope("g0_near_lower"):
+        near_l = grid.along_z(after(lower, near_u, far_u_twin), NEAR)
     with jax.named_scope("turned_xy_upper"):
         far_upper = grid.shift(by_x[0], "y")
     with jax.named_scope("turned_xy_lower"):

time: 132 us -> 128 us (0.970)
  Pallas kernels: 36.1 us -> 25 us
  waiting for transfers between devices: 66.9 us -> 77.3 us
  starting transfers between devices: 25 us -> 21.3 us
    pallas_call x1, Pallas kernels: 13.8 us -> 2.56 us  [pack(): pl.pallas_call(functools.partial(pack_kernel, slots, width), out_shape=ja...]
    ppermute x9, waiting for transfers between devices: 50 us -> 60.4 us  [along_z(): lax.ppermute(value, 'col', [(z * self.nc + c, to * self.nc + c) for z, to...]
    ppermute x9, starting transfers between devices: 13.2 us -> 9.05 us  [along_z(): lax.ppermute(value, 'col', [(z * self.nc + c, to * self.nc + c) for z, to...]
    ppermute x8, waiting for transfers between devices: 16.9 us -> 15.5 us  [shift(): return lax.ppermute(value, 'row', pairs)]
  transfers between devices with their start and end apart: 28 -> 28, of which waited for: 11 -> 10; matrix products, arithmetic and copies ran while one was open for 1% -> 1% of each run, Pallas kernels for 15% -> 16%
where the time goes in v6:
time: 128 us; the launch traced here: 127 us
  waiting for transfers between devices  77.3 us (60%)
  Pallas kernels  25 us (20%)
  starting transfers between devices  21.3 us (17%)
  local copies, waits for them, and re-layouts  1.97 us (2%)
    ppermute x9, waiting for transfers between devices, along_z(): lax.ppermute(value, 'col', [(z * self.nc + c, to * self.nc + c) for z, to...  60.4 us
    ppermute x8, waiting for transfers between devices, shift(): return lax.ppermute(value, 'row', pairs)  15.5 us
    ppermute x8, starting transfers between devices, shift(): return lax.ppermute(value, 'row', pairs)  11.5 us
    ppermute x9, starting transfers between devices, along_z(): lax.ppermute(value, 'col', [(z * self.nc + c, to * self.nc + c) for z, to...  9.05 us
    pallas_call x1, Pallas kernels, turn(): pl.pallas_call(turn_kernel, out_shape=jax.ShapeDtypeStruct((2, half, cols...  5.73 us
    pallas_call x1, Pallas kernels, close(): pl.pallas_call(functools.partial(close_kernel, n_col), out_shape=(jax.Sha...  4.95 us
    pallas_call x2, Pallas kernels, last(): pl.pallas_call(functools.partial(last_kernel, side, n_row), out_shape=jax...  3.95 us
    pallas_call x1, Pallas kernels, spread(): pl.pallas_call(functools.partial(spread_kernel, len(parts), slots, width)...  3.77 us
  transfers between devices with their start and end apart: 28, of which 10 were waited for; matrix products, arithmetic and copies ran while one was open for 1% of the time, Pallas kernels for 16%

profile of v6, /device:TPU:0, one launch (start us, length us, event | category | flops | bytes accessed | tf_op | source)
XLA Modules:
  0.0 127.3 jit_solution(9101758932336195727)
XLA Ops:
  1.2 2.6 %pack.1.refs_0_ = bf16[1552,128]{1,0:T(8,128)(2,1)} custom-call(s32[3]{0:T(128)} %pad_add_fusion.2.base_ref, bf16[1,12,128,128]{3,2,1,0:T(8,128)(2,1)} %slots_ref.1, s32[2,12]{1,0:T(2,128)} %bitcast.67), custom_call_target="tpu_custom_call" | custom-call | tf_op jit(solution)/shard_map/pack/pallas_call | solution.py:59
  3.8 5.1 %collective-permute-start = (bf16[1552,128]{1,0:T(8,128)(2,1)}, bf16[1552,128]{1,0:T(8,128)(2,1)S(1)}, u32[]{:S(2)}, u32[]{:S(2)}) collective-permute-start(bf16[1552,128]{1,0:T(8,128)(2,1)} %pack.1.refs_0_), channel_id=1, source_target_pairs={{0,6},{1,7},{2,4},{3,5},{4,2},{5,3},{6,0},{7,1},{8,14},{9,15},{10,... | collective-permute-start | bytes 1191944 | tf_op jit(solution)/shard_map/slots_far/ppermute | solution.py:352
  8.9 2.9 %mask.1 = (bf16[2,512,512]{2,1,0:T(8,128)(2,1)}, bf16[512,512]{1,0:T(8,128)(2,1)}, bf16[512,512]{1,0:T(8,128)(2,1)}) custom-call(s32[4,8]{1,0:T(4,128)} %bitcast.66, bf16[1024,512]{1,0:T(8,128)(2,1)} %values_ref), custom_call_target="tpu_custom_call" | custom-call | tf_op jit(solution)/shard_map/mask/pallas_call | solution.py:115
  11.8 1.6 %collective-permute-start.7 = (bf16[2,512,512]{2,1,0:T(8,128)(2,1)}, bf16[2,512,512]{2,1,0:T(8,128)(2,1)S(1)}, u32[]{:S(2)}, u32[]{:S(2)}) collective-permute-start(bf16[2,512,512]{2,1,0:T(8,128)(2,1)} %get-tuple-element.31.own_ref.refs_5_), channel_id=1, source_target_pairs={{0,8},{8,0},{16,24},{24,16},{1,9},{9,1},{17,25},{25,17},{2,10},{10... | collective-permute-start | bytes 3145736 | tf_op jit(solution)/shard_map/g0_x/ppermute | solution.py:349
  13.4 1.5 %collective-permute-start.8 = (bf16[2,512,512]{2,1,0:T(8,128)(2,1)}, bf16[2,512,512]{2,1,0:T(8,128)(2,1)S(1)}, u32[]{:S(2)}, u32[]{:S(2)}) collective-permute-start(bf16[2,512,512]{2,1,0:T(8,128)(2,1)} %get-tuple-element.31.own_ref.refs_5_), channel_id=1, source_target_pairs={{0,16},{8,24},{16,0},{24,8},{1,17},{9,25},{17,1},{25,9},{2,18},{10... | collective-permute-start | bytes 3145736 | tf_op jit(solution)/shard_map/g0_y/ppermute | solution.py:349
  15.8 3.4 %collective-permute-done.refs_4_ = bf16[1552,128]{1,0:T(8,128)(2,1)S(1)} collective-permute-done((bf16[1552,128]{1,0:T(8,128)(2,1)}, bf16[1552,128]{1,0:T(8,128)(2,1)S(1)}, u32[]{:S(2)}, u32[]{:S(2)}) %collective-permute-start) | collective-permute-done | bytes 397344 | tf_op jit(solution)/shard_map/slots_far/ppermute | solution.py:352
  19.2 7.7 %collective-permute-done.1.refs_2_ = bf16[1552,128]{1,0:T(8,128)(2,1)S(1)} collective-permute-done((bf16[1552,128]{1,0:T(8,128)(2,1)}, bf16[1552,128]{1,0:T(8,128)(2,1)S(1)}, u32[]{:S(2)}, u32[]{:S(2)}) %collective-permute-start.1) | collective-permute-done | bytes 397344 | tf_op jit(solution)/shard_map/slots_near/ppermute | solution.py:352
  26.9 1.7 %collective-permute-start.2 = (bf16[1552,128]{1,0:T(8,128)(2,1)S(1)}, bf16[1552,128]{1,0:T(8,128)(2,1)S(1)}, u32[]{:S(2)}, u32[]{:S(2)}) collective-permute-start(bf16[1552,128]{1,0:T(8,128)(2,1)S(1)} %collective-permute-done.refs_4_), channel_id=1, source_target_pairs={{0,2},{1,3},{2,0},{3,1},{4,6},{5,7},{6,4},{7,5},{8,10},{9,11},{10,... | collective-permute-start | bytes 1191944 | tf_op jit(solution)/shard_map/slots_cross/ppermute | solution.py:352
  29.1 1.3 %collective-permute-done.3.refs_5_ = bf16[1552,128]{1,0:T(8,128)(2,1)S(1)} collective-permute-done((bf16[1552,128]{1,0:T(8,128)(2,1)S(1)}, bf16[1552,128]{1,0:T(8,128)(2,1)S(1)}, u32[]{:S(2)}, u32[]{:S(2)}) %collective-permute-start.3) | collective-permute-done | bytes 397344 | tf_op jit(solution)/shard_map/slots_far_twin/ppermute | solution.py:357
  30.5 18.7 %collective-permute-done.2.refs_0_ = bf16[1552,128]{1,0:T(8,128)(2,1)S(1)} collective-permute-done((bf16[1552,128]{1,0:T(8,128)(2,1)S(1)}, bf16[1552,128]{1,0:T(8,128)(2,1)S(1)}, u32[]{:S(2)}, u32[]{:S(2)}) %collective-permute-start.2) | collective-permute-done | bytes 397344 | tf_op jit(solution)/shard_map/slots_cross/ppermute | solution.py:352
  49.3 2.0 %collective-permute-start.9 = (bf16[512,512]{1,0:T(8,128)(2,1)S(1)}, bf16[512,512]{1,0:T(8,128)(2,1)S(1)}, u32[]{:S(2)}, u32[]{:S(2)}) collective-permute-start(bf16[512,512]{1,0:T(8,128)(2,1)S(1)} %slice_bitcast_fusion.3), channel_id=1, source_target_pairs={{0,16},{8,24},{16,0},{24,8},{1,17},{9,25},{17,1},{25,9},{2,18},{10... | collective-permute-start | bytes 1572872 | tf_op jit(solution)/shard_map/g0_xy_upper/ppermute | solution.py:349
  51.3 1.6 %collective-permute-start.10 = (bf16[512,512]{1,0:T(8,128)(2,1)S(1)}, bf16[512,512]{1,0:T(8,128)(2,1)S(1)}, u32[]{:S(2)}, u32[]{:S(2)}) collective-permute-start(bf16[512,512]{1,0:T(8,128)(2,1)S(1)} %slice_bitcast_fusion.2), channel_id=1, source_target_pairs={{0,8},{8,0},{16,24},{24,16},{1,9},{9,1},{17,25},{25,17},{2,10},{10... | collective-permute-start | bytes 1572872 | tf_op jit(solution)/shard_map/g0_xy_lower/ppermute | solution.py:349
  54.0 3.8 %spread.1.refs_2_ = bf16[1024,4096]{1,0:T(8,128)(2,1)S(1)} custom-call(s32[6,12]{1,0:T(8,128)S(1)} %bitcast.63, s32[6,12]{1,0:T(8,128)S(1)} %bitcast_add_fusion.col_ref, bf16[1552,128]{1,0:T(8,128)(2,1)S(1)} %copy-done.1, bf16[1552,128]{1,0:T(8,128)(2,1)S(1)} %collective-permute-done.6.refs_1_, bf16[1552,128]{1,0:T(8,128)(2,1)S(1)} %collective-permute-done.1.refs_2_, ...), custom_call_target="tpu_custom_call" | custom-call | tf_op jit(solution)/shard_map/spread/pallas_call | solution.py:160
  58.5 2.0 %collective-permute-done.10.refs_3_ = bf16[512,512]{1,0:T(8,128)(2,1)S(1)} collective-permute-done((bf16[512,512]{1,0:T(8,128)(2,1)S(1)}, bf16[512,512]{1,0:T(8,128)(2,1)S(1)}, u32[]{:S(2)}, u32[]{:S(2)}) %collective-permute-start.10) | collective-permute-done | bytes 524320 | tf_op jit(solution)/shard_map/g0_xy_lower/ppermute | solution.py:349
  61.9 5.7 %turn.1.refs_0_ = bf16[2,512,512]{2,1,0:T(8,128)(2,1)S(1)} custom-call(s32[4]{0:T(128)S(1)} %pad_add_fusion.1.source_ref, bf16[1024,4096]{1,0:T(8,128)(2,1)S(1)} %fill.1.dense_ref, bf16[2,512,512]{2,1,0:T(8,128)(2,1)S(1)} %copy-done, bf16[2,512,512]{2,1,0:T(8,128)(2,1)S(1)} %collective-permute-done.7.refs_0_, ...), custom_call_target="tpu_custom_call" | custom-call | tf_op jit(solution)/shard_map/turn/pallas_call | solution.py:223
  67.6 1.7 %collective-permute-start.11 = (bf16[2,512,512]{2,1,0:T(8,128)(2,1)S(1)}, bf16[2,512,512]{2,1,0:T(8,128)(2,1)S(1)}, u32[]{:S(2)}, u32[]{:S(2)}) collective-permute-start(bf16[2,512,512]{2,1,0:T(8,128)(2,1)S(1)} %turn.1.refs_0_), channel_id=1, source_target_pairs={{0,8},{8,0},{16,24},{24,16},{1,9},{9,1},{17,25},{25,17},{2,10},{10... | collective-permute-start | bytes 3145736 | tf_op jit(solution)/shard_map/turned_x/ppermute | solution.py:349
  70.2 1.8 %collective-permute-start.19 = (bf16[512,512]{1,0:T(8,128)(2,1)S(1)}, bf16[512,512]{1,0:T(8,128)(2,1)S(1)}, u32[]{:S(2)}, u32[]{:S(2)}) collective-permute-start(bf16[512,512]{1,0:T(8,128)(2,1)S(1)} %copy-done.2), channel_id=1, source_target_pairs={{0,2},{1,3},{2,0},{3,1},{4,6},{5,7},{6,4},{7,5},{8,10},{9,11},{10,... | collective-permute-start | bytes 1572872 | tf_op jit(solution)/shard_map/g0_near_lower/ppermute | solution.py:352
  72.0 23.3 %collective-permute-done.19.refs_8_ = bf16[512,512]{1,0:T(8,128)(2,1)S(1)} collective-permute-done((bf16[512,512]{1,0:T(8,128)(2,1)S(1)}, bf16[512,512]{1,0:T(8,128)(2,1)S(1)}, u32[]{:S(2)}, u32[]{:S(2)}) %collective-permute-start.19) | collective-permute-done | bytes 524320 | tf_op jit(solution)/shard_map/g0_near_lower/ppermute | solution.py:352
  95.3 1.5 %collective-permute-start.13 = (bf16[512,512]{1,0:T(8,128)(2,1)S(1)}, bf16[512,512]{1,0:T(8,128)(2,1)S(1)}, u32[]{:S(2)}, u32[]{:S(2)}) collective-permute-start(bf16[512,512]{1,0:T(8,128)(2,1)S(1)} %slice_bitcast_fusion.1), channel_id=1, source_target_pairs={{0,16},{8,24},{16,0},{24,8},{1,17},{9,25},{17,1},{25,9},{2,18},{10... | collective-permute-start | bytes 1572872 | tf_op jit(solution)/shard_map/turned_xy_upper/ppermute | solution.py:349
  98.2 11.5 %collective-permute-done.13.refs_3_ = bf16[512,512]{1,0:T(8,128)(2,1)S(1)} collective-permute-done((bf16[512,512]{1,0:T(8,128)(2,1)S(1)}, bf16[512,512]{1,0:T(8,128)(2,1)S(1)}, u32[]{:S(2)}, u32[]{:S(2)}) %collective-permute-start.13) | collective-permute-done | bytes 524320 | tf_op jit(solution)/shard_map/turned_xy_upper/ppermute | solution.py:349
  111.0 4.9 %close.1 = (f32[2,512,512]{2,1,0:T(8,128)S(1)}, bf16[4096,512]{1,0:T(8,128)(2,1)S(1)}) custom-call(s32[4]{0:T(128)S(1)} %pad_add_fusion.1.source_ref, s32[6]{0:T(128)S(1)} %stack.97.owner_ref, bf16[2,512,512]{2,1,0:T(8,128)(2,1)S(1)} %turn.1.refs_0_, bf16[2,512,512]{2,1,0:T(8,128)(2,1)S(1)} %collective-permute-done.11.refs_1_, ...), custom_call_target="tpu_custom_call" | custom-call | tf_op jit(solution)/shard_map/close/pallas_call | solution.py:272
  116.0 7.3 %collective-permute-done.24.refs_0_ = bf16[512,512]{1,0:T(8,128)(2,1)S(1)} collective-permute-done((bf16[512,512]{1,0:T(8,128)(2,1)S(1)}, bf16[512,512]{1,0:T(8,128)(2,1)S(1)}, u32[]{:S(2)}, u32[]{:S(2)}) %collective-permute-start.24) | collective-permute-done | bytes 524320 | tf_op jit(solution)/shard_map/g0_cross_lower/ppermute | solution.py:352
  123.4 2.0 %last.2.refs_2_ = bf16[1024,512]{1,0:T(8,128)(2,1)} custom-call(s32[2]{0:T(128)S(1)} %get-tuple-element.48.owner_ref, f32[2,512,512]{2,1,0:T(8,128)S(1)} %get-tuple-element.41.total_ref, bf16[4096,512]{1,0:T(8,128)(2,1)S(1)} %get-tuple-element.42.column_ref, bf16[512,512]{1,0:T(8,128)(2,1)S(1)} %collective-permute-done.26.refs_0_, ...), custom_call_target="tpu_custom_call" | custom-call | tf_op jit(solution)/shard_map/last/pallas_call | solution.py:317
  125.3 2.0 %last.3 = bf16[1024,512]{1,0:T(8,128)(2,1)} custom-call(s32[2]{0:T(128)S(1)} %get-tuple-element.48.owner_ref, f32[2,512,512]{2,1,0:T(8,128)S(1)} %get-tuple-element.41.total_ref, bf16[4096,512]{1,0:T(8,128)(2,1)S(1)} %get-tuple-element.42.column_ref, bf16[512,512]{1,0:T(8,128)(2,1)S(1)} %collective-permute-done.24.refs_0_, ...), custom_call_target="tpu_custom_call", output_to_operand_aliasing={{}: (5, {})} | custom-call | tf_op jit(solution)/shard_map/last/pallas_call | solution.py:317
  (70 shorter events, 8.9 us)
Async XLA Ops:
  3.8 15.4 %collective-permute-start = (bf16[1552,128]{1,0:T(8,128)(2,1)}, bf16[1552,128]{1,0:T(8,128)(2,1)S(1)}, u32[]{:S(2)}, u32[]{:S(2)}) collective-permute-start(bf16[1552,128]{1,0:T(8,128)(2,1)} %pack.1.refs_0_), channel_id=1, source_target_pairs={{0,6},{1,7},{2,4},{3,5},{4,2},{5,3},{6,0},{7,1},{8,14},{9,15},{10,... | collective-permute-start | bytes 1191944 | tf_op jit(solution)/shard_map/slots_far/ppermute | solution.py:352
  8.9 18.0 %collective-permute-start.1 = (bf16[1552,128]{1,0:T(8,128)(2,1)}, bf16[1552,128]{1,0:T(8,128)(2,1)S(1)}, u32[]{:S(2)}, u32[]{:S(2)}) collective-permute-start(bf16[1552,128]{1,0:T(8,128)(2,1)} %pack.1.refs_0_), channel_id=1, source_target_pairs={{0,2},{1,3},{2,0},{3,1},{4,6},{5,7},{6,4},{7,5},{8,10},{9,11},{10,... | collective-permute-start | bytes 1191944 | tf_op jit(solution)/shard_map/slots_near/ppermute | solution.py:352
  8.9 19.7 %collective-permute-start.6 = (bf16[1552,128]{1,0:T(8,128)(2,1)}, bf16[1552,128]{1,0:T(8,128)(2,1)S(1)}, u32[]{:S(2)}, u32[]{:S(2)}) collective-permute-start(bf16[1552,128]{1,0:T(8,128)(2,1)} %pack.1.refs_0_), channel_id=1, source_target_pairs={{0,1},{1,0},{2,3},{3,2},{4,5},{5,4},{6,7},{7,6},{8,9},{9,8},{10,11... | collective-permute-start | bytes 1191944 | tf_op jit(solution)/shard_map/slots_twin/ppermute | solution.py:357
  11.8 37.4 %collective-permute-start.7 = (bf16[2,512,512]{2,1,0:T(8,128)(2,1)}, bf16[2,512,512]{2,1,0:T(8,128)(2,1)S(1)}, u32[]{:S(2)}, u32[]{:S(2)}) collective-permute-start(bf16[2,512,512]{2,1,0:T(8,128)(2,1)} %get-tuple-element.31.own_ref.refs_5_), channel_id=1, source_target_pairs={{0,8},{8,0},{16,24},{24,16},{1,9},{9,1},{17,25},{25,17},{2,10},{10... | collective-permute-start | bytes 3145736 | tf_op jit(solution)/shard_map/g0_x/ppermute | solution.py:349
  13.4 37.9 %collective-permute-start.8 = (bf16[2,512,512]{2,1,0:T(8,128)(2,1)}, bf16[2,512,512]{2,1,0:T(8,128)(2,1)S(1)}, u32[]{:S(2)}, u32[]{:S(2)}) collective-permute-start(bf16[2,512,512]{2,1,0:T(8,128)(2,1)} %get-tuple-element.31.own_ref.refs_5_), channel_id=1, source_target_pairs={{0,16},{8,24},{16,0},{24,8},{1,17},{9,25},{17,1},{25,9},{2,18},{10... | collective-permute-start | bytes 3145736 | tf_op jit(solution)/shard_map/g0_y/ppermute | solution.py:349
  26.9 22.3 %collective-permute-start.2 = (bf16[1552,128]{1,0:T(8,128)(2,1)S(1)}, bf16[1552,128]{1,0:T(8,128)(2,1)S(1)}, u32[]{:S(2)}, u32[]{:S(2)}) collective-permute-start(bf16[1552,128]{1,0:T(8,128)(2,1)S(1)} %collective-permute-done.refs_4_), channel_id=1, source_target_pairs={{0,2},{1,3},{2,0},{3,1},{4,6},{5,7},{6,4},{7,5},{8,10},{9,11},{10,... | collective-permute-start | bytes 1191944 | tf_op jit(solution)/shard_map/slots_cross/ppermute | solution.py:352
  28.6 29.2 %collective-permute-start.17 = (bf16[512,512]{1,0:T(8,128)(2,1)}, bf16[512,512]{1,0:T(8,128)(2,1)S(1)}, u32[]{:S(2)}, u32[]{:S(2)}) collective-permute-start(bf16[512,512]{1,0:T(8,128)(2,1)} %get-tuple-element.35), channel_id=1, source_target_pairs={{0,6},{1,7},{2,4},{3,5},{4,2},{5,3},{6,0},{7,1},{8,14},{9,15},{10,... | collective-permute-start | bytes 1572872 | tf_op jit(solution)/shard_map/g0_far_upper/ppermute | solution.py:352
  30.4 22.5 %collective-permute-start.4 = (bf16[1552,128]{1,0:T(8,128)(2,1)S(1)}, bf16[1552,128]{1,0:T(8,128)(2,1)S(1)}, u32[]{:S(2)}, u32[]{:S(2)}) collective-permute-start(bf16[1552,128]{1,0:T(8,128)(2,1)S(1)} %collective-permute-done.1.refs_2_), channel_id=1, source_target_pairs={{0,1},{1,0},{2,3},{3,2},{4,5},{5,4},{6,7},{7,6},{8,9},{9,8},{10,11... | collective-permute-start | bytes 1191944 | tf_op jit(solution)/shard_map/slots_near_twin/ppermute | solution.py:357
  49.2 21.0 %collective-permute-start.16 = (bf16[512,512]{1,0:T(8,128)(2,1)}, bf16[512,512]{1,0:T(8,128)(2,1)S(1)}, u32[]{:S(2)}, u32[]{:S(2)}) collective-permute-start(bf16[512,512]{1,0:T(8,128)(2,1)} %get-tuple-element.35), channel_id=1, source_target_pairs={{0,2},{1,3},{2,0},{3,1},{4,6},{5,7},{6,4},{7,5},{8,10},{9,11},{10,... | collective-permute-start | bytes 1572872 | tf_op jit(solution)/shard_map/g0_near_upper/ppermute | solution.py:352
  49.3 9.2 %collective-permute-start.9 = (bf16[512,512]{1,0:T(8,128)(2,1)S(1)}, bf16[512,512]{1,0:T(8,128)(2,1)S(1)}, u32[]{:S(2)}, u32[]{:S(2)}) collective-permute-start(bf16[512,512]{1,0:T(8,128)(2,1)S(1)} %slice_bitcast_fusion.3), channel_id=1, source_target_pairs={{0,16},{8,24},{16,0},{24,8},{1,17},{9,25},{17,1},{25,9},{2,18},{10... | collective-permute-start | bytes 1572872 | tf_op jit(solution)/shard_map/g0_xy_upper/ppermute | solution.py:349
  51.3 9.2 %collective-permute-start.10 = (bf16[512,512]{1,0:T(8,128)(2,1)S(1)}, bf16[512,512]{1,0:T(8,128)(2,1)S(1)}, u32[]{:S(2)}, u32[]{:S(2)}) collective-permute-start(bf16[512,512]{1,0:T(8,128)(2,1)S(1)} %slice_bitcast_fusion.2), channel_id=1, source_target_pairs={{0,8},{8,0},{16,24},{24,16},{1,9},{9,1},{17,25},{25,17},{2,10},{10... | collective-permute-start | bytes 1572872 | tf_op jit(solution)/shard_map/g0_xy_lower/ppermute | solution.py:349
  52.9 7.7 %collective-permute-start.5 = (bf16[1552,128]{1,0:T(8,128)(2,1)S(1)}, bf16[1552,128]{1,0:T(8,128)(2,1)S(1)}, u32[]{:S(2)}, u32[]{:S(2)}) collective-permute-start(bf16[1552,128]{1,0:T(8,128)(2,1)S(1)} %collective-permute-done.2.refs_0_), channel_id=1, source_target_pairs={{0,1},{1,0},{2,3},{3,2},{4,5},{5,4},{6,7},{7,6},{8,9},{9,8},{10,11... | collective-permute-start | bytes 1191944 | tf_op jit(solution)/shard_map/slots_cross_twin/ppermute | solution.py:357
  60.5 9.7 %collective-permute-start.18 = (bf16[512,512]{1,0:T(8,128)(2,1)S(1)}, bf16[512,512]{1,0:T(8,128)(2,1)S(1)}, u32[]{:S(2)}, u32[]{:S(2)}) collective-permute-start(bf16[512,512]{1,0:T(8,128)(2,1)S(1)} %collective-permute-done.17.refs_11_), channel_id=1, source_target_pairs={{0,1},{1,0},{2,3},{3,2},{4,5},{5,4},{6,7},{7,6},{8,9},{9,8},{10,11... | collective-permute-start | bytes 1572872 | tf_op jit(solution)/shard_map/g0_far_upper_twin/ppermute | solution.py:357
  67.6 27.7 %collective-permute-start.11 = (bf16[2,512,512]{2,1,0:T(8,128)(2,1)S(1)}, bf16[2,512,512]{2,1,0:T(8,128)(2,1)S(1)}, u32[]{:S(2)}, u32[]{:S(2)}) collective-permute-start(bf16[2,512,512]{2,1,0:T(8,128)(2,1)S(1)} %turn.1.refs_0_), channel_id=1, source_target_pairs={{0,8},{8,0},{16,24},{24,16},{1,9},{9,1},{17,25},{25,17},{2,10},{10... | collective-permute-start | bytes 3145736 | tf_op jit(solution)/shard_map/turned_x/ppermute | solution.py:349
  69.3 27.5 %collective-permute-start.12 = (bf16[2,512,512]{2,1,0:T(8,128)(2,1)S(1)}, bf16[2,512,512]{2,1,0:T(8,128)(2,1)S(1)}, u32[]{:S(2)}, u32[]{:S(2)}) collective-permute-start(bf16[2,512,512]{2,1,0:T(8,128)(2,1)S(1)} %turn.1.refs_0_), channel_id=1, source_target_pairs={{0,16},{8,24},{16,0},{24,8},{1,17},{9,25},{17,1},{25,9},{2,18},{10... | collective-permute-start | bytes 3145736 | tf_op jit(solution)/shard_map/turned_y/ppermute | solution.py:349
  70.2 25.1 %collective-permute-start.19 = (bf16[512,512]{1,0:T(8,128)(2,1)S(1)}, bf16[512,512]{1,0:T(8,128)(2,1)S(1)}, u32[]{:S(2)}, u32[]{:S(2)}) collective-permute-start(bf16[512,512]{1,0:T(8,128)(2,1)S(1)} %copy-done.2), channel_id=1, source_target_pairs={{0,2},{1,3},{2,0},{3,1},{4,6},{5,7},{6,4},{7,5},{8,10},{9,11},{10,... | collective-permute-start | bytes 1572872 | tf_op jit(solution)/shard_map/g0_near_lower/ppermute | solution.py:352
  72.0 25.7 %collective-permute-start.15 = (bf16[2,512,512]{2,1,0:T(8,128)(2,1)S(1)}, bf16[2,512,512]{2,1,0:T(8,128)(2,1)S(1)}, u32[]{:S(2)}, u32[]{:S(2)}) collective-permute-start(bf16[2,512,512]{2,1,0:T(8,128)(2,1)S(1)} %copy-done), channel_id=1, source_target_pairs={{0,1},{1,0},{2,3},{3,2},{4,5},{5,4},{6,7},{7,6},{8,9},{9,8},{10,11... | collective-permute-start | bytes 3145736 | tf_op jit(solution)/shard_map/g0_twin/ppermute | solution.py:357
  72.0 25.7 %collective-permute-start.22 = (bf16[512,512]{1,0:T(8,128)(2,1)S(1)}, bf16[512,512]{1,0:T(8,128)(2,1)S(1)}, u32[]{:S(2)}, u32[]{:S(2)}) collective-permute-start(bf16[512,512]{1,0:T(8,128)(2,1)S(1)} %copy-done.2), channel_id=1, source_target_pairs={{0,6},{1,7},{2,4},{3,5},{4,2},{5,3},{6,0},{7,1},{8,14},{9,15},{10,... | collective-permute-start | bytes 1572872 | tf_op jit(solution)/shard_map/g0_far_lower/ppermute | solution.py:352
  95.3 14.4 %collective-permute-start.13 = (bf16[512,512]{1,0:T(8,128)(2,1)S(1)}, bf16[512,512]{1,0:T(8,128)(2,1)S(1)}, u32[]{:S(2)}, u32[]{:S(2)}) collective-permute-start(bf16[512,512]{1,0:T(8,128)(2,1)S(1)} %slice_bitcast_fusion.1), channel_id=1, source_target_pairs={{0,16},{8,24},{16,0},{24,8},{1,17},{9,25},{17,1},{25,9},{2,18},{10... | collective-permute-start | bytes 1572872 | tf_op jit(solution)/shard_map/turned_xy_upper/ppermute | solution.py:349
  96.9 14.1 %collective-permute-start.14 = (bf16[512,512]{1,0:T(8,128)(2,1)S(1)}, bf16[512,512]{1,0:T(8,128)(2,1)S(1)}, u32[]{:S(2)}, u32[]{:S(2)}) collective-permute-start(bf16[512,512]{1,0:T(8,128)(2,1)S(1)} %slice_bitcast_fusion), channel_id=1, source_target_pairs={{0,8},{8,0},{16,24},{24,16},{1,9},{9,1},{17,25},{25,17},{2,10},{10... | collective-permute-start | bytes 1572872 | tf_op jit(solution)/shard_map/turned_xy_lower/ppermute | solution.py:349
  97.7 13.3 %collective-permute-start.20 = (bf16[512,512]{1,0:T(8,128)(2,1)S(1)}, bf16[512,512]{1,0:T(8,128)(2,1)S(1)}, u32[]{:S(2)}, u32[]{:S(2)}) collective-permute-start(bf16[512,512]{1,0:T(8,128)(2,1)S(1)} %collective-permute-done.16.refs_7_), channel_id=1, source_target_pairs={{0,1},{1,0},{2,3},{3,2},{4,5},{5,4},{6,7},{7,6},{8,9},{9,8},{10,11... | collective-permute-start | bytes 1572872 | tf_op jit(solution)/shard_map/g0_near_upper_twin/ppermute | solution.py:357
  97.7 13.3 %collective-permute-start.23 = (bf16[512,512]{1,0:T(8,128)(2,1)S(1)}, bf16[512,512]{1,0:T(8,128)(2,1)S(1)}, u32[]{:S(2)}, u32[]{:S(2)}) collective-permute-start(bf16[512,512]{1,0:T(8,128)(2,1)S(1)} %collective-permute-done.22.refs_12_), channel_id=1, source_target_pairs={{0,1},{1,0},{2,3},{3,2},{4,5},{5,4},{6,7},{7,6},{8,9},{9,8},{10,11... | collective-permute-start | bytes 1572872 | tf_op jit(solution)/shard_map/g0_far_lower_twin/ppermute | solution.py:357
  98.2 17.8 %collective-permute-start.26 = (bf16[512,512]{1,0:T(8,128)(2,1)S(1)}, bf16[512,512]{1,0:T(8,128)(2,1)S(1)}, u32[]{:S(2)}, u32[]{:S(2)}) collective-permute-start(bf16[512,512]{1,0:T(8,128)(2,1)S(1)} %collective-permute-done.17.refs_11_), channel_id=1, source_target_pairs={{0,2},{1,3},{2,0},{3,1},{4,6},{5,7},{6,4},{7,5},{8,10},{9,11},{10,... | collective-permute-start | bytes 1572872 | tf_op jit(solution)/shard_map/g0_cross_upper/ppermute | solution.py:352
  109.7 13.6 %collective-permute-start.24 = (bf16[512,512]{1,0:T(8,128)(2,1)S(1)}, bf16[512,512]{1,0:T(8,128)(2,1)S(1)}, u32[]{:S(2)}, u32[]{:S(2)}) collective-permute-start(bf16[512,512]{1,0:T(8,128)(2,1)S(1)} %collective-permute-done.22.refs_12_), channel_id=1, source_target_pairs={{0,2},{1,3},{2,0},{3,1},{4,6},{5,7},{6,4},{7,5},{8,10},{9,11},{10,... | collective-permute-start | bytes 1572872 | tf_op jit(solution)/shard_map/g0_cross_lower/ppermute | solution.py:352
  (7 other events, 24.1 us)

commit v7 on v5

--- a/solution.py
+++ b/solution.py
@@ -26,48 +26,14 @@
     return lax.optimization_barrier((value, *earlier))[0]
 
 
-def pack_kernel(slots, width, base_ref, slots_ref, pairs_ref, message_ref, pairs, names, tail, sems, tail_sem):
-    fetch = pltpu.make_async_copy(pairs_ref, pairs, tail_sem)
-    fetch.start()
-    moves = [
-        pltpu.make_async_copy(slots_ref.at[0, s], message_ref.at[pl.ds(s * width, width)], sems.at[s])
-        for s in range(slots)
-    ]
-    for move in moves:
-        move.start()
-    names[...] = jnp.full(names.shape, -1, jnp.int32)
-    fetch.wait()
-    shape = pairs.shape
-    first = lax.broadcasted_iota(jnp.int32, shape, 0) == 0
-    local = pairs[...] - jnp.where(first, base_ref[0], base_ref[1])
-    live = lax.broadcasted_iota(jnp.int32, shape, 1) < base_ref[2]
-    names[pl.ds(0, shape[0]), pl.ds(0, shape[1])] = jnp.where(live, local, -1)
-    tail[...] = names[...].astype(jnp.float32).astype(jnp.bfloat16)
-    give = pltpu.make_async_copy(tail, message_ref.at[pl.ds(slots * width, TAIL)], tail_sem)
-    give.start()
-    for move in moves:
-        move.wait()
-    give.wait()
-
-
-def pack(base, sigma_values, sigma_pairs):
+def pack(sigma_values, sigma_pairs, sigma_count, row_base, col_base):
     slots, width = sigma_values.shape[1], sigma_values.shape[2]
-    return pl.pallas_call(
-        functools.partial(pack_kernel, slots, width),
-        out_shape=jax.ShapeDtypeStruct((slots * width + TAIL, width), jnp.bfloat16),
-        in_specs=[SMEM, HBM, HBM],
-        out_specs=HBM,
-        scratch_shapes=[
-            pltpu.VMEM((2, slots), jnp.int32),
-            pltpu.VMEM((TAIL, width), jnp.int32),
-            pltpu.VMEM((TAIL, width), jnp.bfloat16),
-            pltpu.SemaphoreType.DMA((slots,)),
-            pltpu.SemaphoreType.DMA,
-        ],
-        compiler_params=pltpu.CompilerParams(vmem_limit_bytes=FIRST_VMEM_BYTES),
-        cost_estimate=NO_COST,
-        name="pack",
-    )(base, sigma_values, sigma_pairs[0].T)
+    first = lax.broadcasted_iota(jnp.int32, (2, slots), 0) == 0
+    slot = lax.broadcasted_iota(jnp.int32, (2, slots), 1)
+    local = sigma_pairs[0].T - jnp.where(first, row_base, col_base)
+    names = jnp.where(slot < sigma_count, local, -1).astype(jnp.bfloat16)
+    names = jnp.pad(names, ((0, TAIL - 2), (0, width - slots)))
+    return jnp.concatenate([sigma_values[0].reshape(slots * width, width), names])
 
 
 def mask_kernel(
@@ -395,8 +361,9 @@
     grid = Grid(n_row, n_col)
     sources = grid.plane_sources()
     z = grid.z
-    base = jnp.stack([lax.axis_index("row") * block_rows, lax.axis_index("col") * block_cols, sigma_count[0, 0]])
-    message = pack(base.astype(jnp.int32), sigma_values, sigma_pairs)
+    message = pack(
+        sigma_values, sigma_pairs, sigma_count, lax.axis_index("row") * block_rows, lax.axis_index("col") * block_cols
+    )
     tile, upper, lower = masked(after(g0_values, message), g0_pattern)
 
     def names(parts, held_by):
@@ -426,71 +393,70 @@
             result = last(side, owners[-2:], total, column, [part[side] for part in row_parts[-2:]], result)
         return result
 
+    slot_owners = grid.col_owners(z, z ^ 1, 3 - z, 3 - (z ^ 1))
     with jax.named_scope("slots_far"):
         s_far = grid.along_z(message, MIRROR)
     with jax.named_scope("slots_near"):
         s_near = grid.along_z(message, NEAR)
+    with jax.named_scope("slots_twin"):
+        s_tw = grid.twin(message)
     with jax.named_scope("g0_x"):
-        by_x = grid.shift(tile, "x")
+        g_x = grid.shift(tile, "x")
     with jax.named_scope("g0_y"):
-        by_y = grid.shift(tile, "y")
-    with jax.named_scope("slots_twin"):
-        s_twin = grid.twin(message)
-    slot_owners = grid.col_owners(z, z ^ 1, 3 - z, 3 - (z ^ 1))
+        g_y = grid.shift(tile, "y")
+    with jax.named_scope("slots_far_twin"):
+        s_far_tw = grid.twin(after(s_far, s_near))
     with jax.named_scope("slots_cross"):
         s_cross = grid.along_z(after(s_far, s_near), NEAR)
-    with jax.named_scope("slots_far_twin"):
-        s_far_twin = grid.twin(after(s_far, s_near))
     with jax.named_scope("slots_near_twin"):
-        s_near_twin = grid.twin(after(s_near, s_far_twin))
+        s_near_tw = grid.twin(after(s_near, s_far_tw))
     with jax.named_scope("g0_xy_upper"):
-        far_upper = grid.shift(by_x[0], "y")
+        g_xyu = grid.shift(g_x[0], "y")
     with jax.named_scope("g0_xy_lower"):
-        far_lower = grid.shift(by_y[1], "x")
-    dense = dense_rows(slot_owners[:-2], [message, s_twin, s_near, s_near_twin, s_far, s_far_twin])
-    with jax.named_scope("g0_near_upper"):
-        near_u = grid.along_z(after(upper, s_cross), NEAR)
+        g_xyl = grid.shift(after(g_y, s_far)[1], "x")
+    dense1 = dense_rows(slot_owners[:-2], [message, s_tw, s_near, s_near_tw, s_far, s_far_tw])
     with jax.named_scope("g0_far_upper"):
         far_u = grid.along_z(after(upper, s_cross), MIRROR)
+    with jax.named_scope("g0_near_upper"):
+        near_u = grid.along_z(after(upper, s_cross, s_near), NEAR)
     with jax.named_scope("slots_cross_twin"):
-        s_cross_twin = grid.twin(after(s_cross, s_near_twin))
-    dense = dense_fill(slot_owners[-2:], [s_cross, s_cross_twin], dense)
-    turned = turn(sources, dense, [tile, by_x, by_y, far_upper, far_lower])
-
+        s_cross_tw = grid.twin(after(s_cross, s_near_tw))
+    dense2 = dense_fill(slot_owners[-2:], [s_cross, s_cross_tw], dense1)
+    turned = turn(sources, dense2, [tile, g_x, g_y, g_xyu, g_xyl])
     with jax.named_scope("turned_x"):
-        by_x = grid.shift(turned, "x")
+        t_x = grid.shift(turned, "x")
     with jax.named_scope("turned_y"):
-        by_y = grid.shift(turned, "y")
+        t_y = grid.shift(turned, "y")
+    with jax.named_scope("g0_twin"):
+        tile_tw = grid.twin(after(tile, turned))
+    with jax.named_scope("g0_near_upper_twin"):
+        near_u_tw = grid.twin(after(near_u, tile_tw))
+    with jax.named_scope("g0_far_upper_twin"):
+        far_u_tw = grid.twin(far_u)
+    with jax.named_scope("g0_far_lower"):
+        far_l = grid.along_z(after(lower, near_u, far_u, turned), MIRROR)
     with jax.named_scope("g0_near_lower"):
         near_l = grid.along_z(after(lower, near_u, far_u), NEAR)
-    with jax.named_scope("g0_far_lower"):
-        far_l = grid.along_z(after(lower, near_u, far_u), MIRROR)
-    with jax.named_scope("g0_twin"):
-        tile_twin = grid.twin(after(tile, turned))
-    with jax.named_scope("g0_near_upper_twin"):
-        near_u_twin = grid.twin(after(near_u, tile_twin))
-    with jax.named_scope("g0_far_upper_twin"):
-        far_u_twin = grid.twin(after(far_u, near_u_twin))
     with jax.named_scope("turned_xy_upper"):
-        far_upper = grid.shift(by_x[0], "y")
+        t_xyu = grid.shift(after(t_x, far_u)[0], "y")
     with jax.named_scope("turned_xy_lower"):
-        far_lower = grid.shift(by_y[1], "x")
+        t_xyl = grid.shift(t_y[1], "x")
+    with jax.named_scope("g0_near_lower_twin"):
+        near_l_tw = grid.twin(after(near_l, near_u))
+    with jax.named_scope("g0_far_lower_twin"):
+        far_l_tw = grid.twin(after(far_l, near_l_tw))
     with jax.named_scope("g0_cross_upper"):
-        cross_u = grid.along_z(after(far_u, near_l, by_x, by_y), NEAR)
-    with jax.named_scope("g0_near_lower_twin"):
-        near_l_twin = grid.twin(near_l)
-    with jax.named_scope("g0_far_lower_twin"):
-        far_l_twin = grid.twin(after(far_l, near_l_twin))
+        cross_u = grid.along_z(after(far_u, t_x, t_y), NEAR)
     with jax.named_scope("g0_cross_lower"):
-        cross_l = grid.along_z(after(far_l, near_l), NEAR)
-    row_parts = [tile, tile_twin, near_u, near_l, near_u_twin, near_l_twin, far_u, far_l, far_u_twin, far_l_twin]
-    total, column = close(sources, slot_owners[:-2], [turned, by_x, by_y, far_upper, far_lower], row_parts)
+        cross_l = grid.along_z(far_l, NEAR)
+    row_parts = [tile, tile_tw, near_u, near_l, near_u_tw, near_l_tw, far_u, far_l, far_u_tw, far_l_tw]
+    total, column = close(sources, slot_owners[:-2], [turned, t_x, t_y, t_xyu, t_xyl], row_parts)
     with jax.named_scope("g0_cross_upper_twin"):
-        cross_u_twin = grid.twin(after(cross_u, column))
+        cross_u_tw = grid.twin(after(cross_u, cross_u))
+    last0 = last(0, slot_owners[-2:], total, column, [cross_u, cross_u_tw])
     with jax.named_scope("g0_cross_lower_twin"):
-        cross_l_twin = grid.twin(after(cross_l, column))
-    result = last(0, slot_owners[-2:], total, column, [cross_u, cross_u_twin])
-    return last(1, slot_owners[-2:], total, column, [cross_l, cross_l_twin], result)
+        cross_l_tw = grid.twin(after(cross_l, column))
+    return last(1, slot_owners[-2:], total, column, [cross_l, cross_l_tw], last0)
 
 
 def solution(mesh):

time: 132 us -> 116 us (0.88)
  Pallas kernels: 36.1 us -> 22.3 us
  waiting for transfers between devices: 66.9 us -> 64.3 us
    pallas_call x1 -> x0, Pallas kernels: 13.8 us -> none  [pack(): pl.pallas_call(functools.partial(pack_kernel, slots, width), out_shape=ja...]
    ppermute x9, waiting for transfers between devices: 50 us -> 45.4 us  [along_z(): lax.ppermute(value, 'col', [(z * self.nc + c, to * self.nc + c) for z, to...]
  transfers between devices with their start and end apart: 28 -> 28, of which waited for: 11 -> 15; matrix products, arithmetic and copies ran while one was open for 1% -> 1% of each run, Pallas kernels for 15% -> 18%
where the time goes in v7:
time: 116 us
  waiting for transfers between devices  64.3 us (55%)
  starting transfers between devices  25.2 us (22%)
  Pallas kernels  22.3 us (19%)
  other arithmetic  2.12 us (2%)
    ppermute x9, waiting for transfers between devices, along_z(): lax.ppermute(value, 'col', [(z * self.nc + c, to * self.nc + c) for z, to...  45.4 us
    ppermute x8, waiting for transfers between devices, shift(): return lax.ppermute(value, 'row', pairs)  17.8 us
    ppermute x9, starting transfers between devices, along_z(): lax.ppermute(value, 'col', [(z * self.nc + c, to * self.nc + c) for z, to...  13.6 us
    ppermute x8, starting transfers between devices, shift(): return lax.ppermute(value, 'row', pairs)  11.4 us
    pallas_call x1, Pallas kernels, turn(): pl.pallas_call(turn_kernel, out_shape=jax.ShapeDtypeStruct((2, half, cols...  5.74 us
    pallas_call x1, Pallas kernels, close(): pl.pallas_call(functools.partial(close_kernel, n_col), out_shape=(jax.Sha...  4.95 us
    pallas_call x2, Pallas kernels, last(): pl.pallas_call(functools.partial(last_kernel, side, n_row), out_shape=jax...  3.95 us
    pallas_call x1, Pallas kernels, spread(): pl.pallas_call(functools.partial(spread_kernel, len(parts), slots, width)...  3.11 us
  transfers between devices with their start and end apart: 28, of which 15 were waited for; matrix products, arithmetic and copies ran while one was open for 1% of the time, Pallas kernels for 18%

profile of v7, /device:TPU:0, one launch (start us, length us, event | category | flops | bytes accessed | tf_op | source)
XLA Modules:
  0.0 115.7 jit_solution(7123271286758380735)
XLA Ops:
  2.5 5.1 %collective-permute-start = (bf16[1552,128]{1,0:T(8,128)(2,1)S(1)}, bf16[1552,128]{1,0:T(8,128)(2,1)S(1)}, u32[]{:S(2)}, u32[]{:S(2)}) collective-permute-start(bf16[1552,128]{1,0:T(8,128)(2,1)S(1)} %fusion.1.refs_0_), channel_id=1, source_target_pairs={{0,6},{1,7},{2,4},{3,5},{4,2},{5,3},{6,0},{7,1},{8,14},{9,15},{10,... | collective-permute-start | bytes 1191944 | tf_op jit(solution)/shard_map/slots_far/ppermute | solution.py:313
  7.6 2.9 %mask.1 = (bf16[2,512,512]{2,1,0:T(8,128)(2,1)}, bf16[512,512]{1,0:T(8,128)(2,1)}, bf16[512,512]{1,0:T(8,128)(2,1)}) custom-call(s32[4,8]{1,0:T(4,128)} %bitcast.70, bf16[1024,512]{1,0:T(8,128)(2,1)} %values_ref), custom_call_target="tpu_custom_call" | custom-call | tf_op jit(solution)/shard_map/mask/pallas_call | solution.py:76
  13.8 3.9 %collective-permute-done.refs_4_ = bf16[1552,128]{1,0:T(8,128)(2,1)S(1)} collective-permute-done((bf16[1552,128]{1,0:T(8,128)(2,1)S(1)}, bf16[1552,128]{1,0:T(8,128)(2,1)S(1)}, u32[]{:S(2)}, u32[]{:S(2)}) %collective-permute-start) | collective-permute-done | bytes 397344 | tf_op jit(solution)/shard_map/slots_far/ppermute | solution.py:313
  17.7 7.7 %collective-permute-done.1.refs_2_ = bf16[1552,128]{1,0:T(8,128)(2,1)S(1)} collective-permute-done((bf16[1552,128]{1,0:T(8,128)(2,1)S(1)}, bf16[1552,128]{1,0:T(8,128)(2,1)S(1)}, u32[]{:S(2)}, u32[]{:S(2)}) %collective-permute-start.1) | collective-permute-done | bytes 397344 | tf_op jit(solution)/shard_map/slots_near/ppermute | solution.py:313
  25.4 1.7 %collective-permute-start.2 = (bf16[1552,128]{1,0:T(8,128)(2,1)S(1)}, bf16[1552,128]{1,0:T(8,128)(2,1)S(1)}, u32[]{:S(2)}, u32[]{:S(2)}) collective-permute-start(bf16[1552,128]{1,0:T(8,128)(2,1)S(1)} %collective-permute-done.refs_4_), channel_id=1, source_target_pairs={{0,2},{1,3},{2,0},{3,1},{4,6},{5,7},{6,4},{7,5},{8,10},{9,11},{10,... | collective-permute-start | bytes 1191944 | tf_op jit(solution)/shard_map/slots_cross/ppermute | solution.py:313
  28.9 7.6 %collective-permute-done.2.refs_0_ = bf16[1552,128]{1,0:T(8,128)(2,1)S(1)} collective-permute-done((bf16[1552,128]{1,0:T(8,128)(2,1)S(1)}, bf16[1552,128]{1,0:T(8,128)(2,1)S(1)}, u32[]{:S(2)}, u32[]{:S(2)}) %collective-permute-start.2) | collective-permute-done | bytes 397344 | tf_op jit(solution)/shard_map/slots_cross/ppermute | solution.py:313
  37.2 1.6 %collective-permute-start.9 = (bf16[512,512]{1,0:T(8,128)(2,1)S(1)}, bf16[512,512]{1,0:T(8,128)(2,1)S(1)}, u32[]{:S(2)}, u32[]{:S(2)}) collective-permute-start(bf16[512,512]{1,0:T(8,128)(2,1)S(1)} %slice_bitcast_fusion.1), channel_id=1, source_target_pairs={{0,16},{8,24},{16,0},{24,8},{1,17},{9,25},{17,1},{25,9},{2,18},{10... | collective-permute-start | bytes 1572872 | tf_op jit(solution)/shard_map/g0_xy_upper/ppermute | solution.py:310
  40.6 3.1 %spread.1.refs_2_ = bf16[1024,4096]{1,0:T(8,128)(2,1)S(1)} custom-call(s32[6,12]{1,0:T(8,128)S(1)} %bitcast.66, s32[6,12]{1,0:T(8,128)S(1)} %bitcast_add_fusion.col_ref, bf16[1552,128]{1,0:T(8,128)(2,1)S(1)} %fusion.1.refs_0_, bf16[1552,128]{1,0:T(8,128)(2,1)} %collective-permute-done.6.refs_1_, bf16[1552,128]{1,0:T(8,128)(2,1)S(1)} %collective-permute-done.1.refs_2_, ...), custom_call_target="tpu_custom_call" | custom-call | tf_op jit(solution)/shard_map/spread/pallas_call | solution.py:121
  43.8 1.7 %fill.1.dense_ref = bf16[1024,4096]{1,0:T(8,128)(2,1)S(1)} custom-call(s32[2,12]{1,0:T(2,128)S(1)} %bitcast.67, s32[2,12]{1,0:T(2,128)S(1)} %broadcast_add_fusion.col_ref, bf16[1552,128]{1,0:T(8,128)(2,1)S(1)} %collective-permute-done.2.refs_0_, bf16[1552,128]{1,0:T(8,128)(2,1)S(1)} %collective-permute-done.5.refs_1_, ...), custom_call_target="tpu_custom_call", output_to_operand_aliasing={{}: (4, {})} | custom-call | tf_op jit(solution)/shard_map/fill/pallas_call | solution.py:140
  45.5 4.5 %collective-permute-done.9.refs_2_ = bf16[512,512]{1,0:T(8,128)(2,1)S(1)} collective-permute-done((bf16[512,512]{1,0:T(8,128)(2,1)S(1)}, bf16[512,512]{1,0:T(8,128)(2,1)S(1)}, u32[]{:S(2)}, u32[]{:S(2)}) %collective-permute-start.9) | collective-permute-done | bytes 524320 | tf_op jit(solution)/shard_map/g0_xy_upper/ppermute | solution.py:310
  51.3 5.7 %turn.1.refs_0_ = bf16[2,512,512]{2,1,0:T(8,128)(2,1)S(1)} custom-call(s32[4]{0:T(128)S(1)} %pad_add_fusion.1.source_ref, bf16[1024,4096]{1,0:T(8,128)(2,1)S(1)} %fill.1.dense_ref, bf16[2,512,512]{2,1,0:T(8,128)(2,1)S(1)} %copy-done, bf16[2,512,512]{2,1,0:T(8,128)(2,1)S(1)} %collective-permute-done.7.refs_0_, ...), custom_call_target="tpu_custom_call" | custom-call | tf_op jit(solution)/shard_map/turn/pallas_call | solution.py:184
  59.2 1.8 %collective-permute-done.17.refs_7_ = bf16[512,512]{1,0:T(8,128)(2,1)S(1)} collective-permute-done((bf16[512,512]{1,0:T(8,128)(2,1)}, bf16[512,512]{1,0:T(8,128)(2,1)S(1)}, u32[]{:S(2)}, u32[]{:S(2)}) %collective-permute-start.17) | collective-permute-done | bytes 524320 | tf_op jit(solution)/shard_map/g0_near_upper/ppermute | solution.py:313
  61.3 3.5 %collective-permute-start.21 = (bf16[512,512]{1,0:T(8,128)(2,1)S(1)}, bf16[512,512]{1,0:T(8,128)(2,1)S(1)}, u32[]{:S(2)}, u32[]{:S(2)}) collective-permute-start(bf16[512,512]{1,0:T(8,128)(2,1)S(1)} %copy-done.1), channel_id=1, source_target_pairs={{0,6},{1,7},{2,4},{3,5},{4,2},{5,3},{6,0},{7,1},{8,14},{9,15},{10,... | collective-permute-start | bytes 1572872 | tf_op jit(solution)/shard_map/g0_far_lower/ppermute | solution.py:313
  64.8 8.9 %collective-permute-done.18.refs_8_ = bf16[512,512]{1,0:T(8,128)(2,1)S(1)} collective-permute-done((bf16[512,512]{1,0:T(8,128)(2,1)S(1)}, bf16[512,512]{1,0:T(8,128)(2,1)S(1)}, u32[]{:S(2)}, u32[]{:S(2)}) %collective-permute-start.18) | collective-permute-done | bytes 524320 | tf_op jit(solution)/shard_map/g0_near_lower/ppermute | solution.py:313
  73.7 6.1 %collective-permute-done.11.refs_1_ = bf16[2,512,512]{2,1,0:T(8,128)(2,1)S(1)} collective-permute-done((bf16[2,512,512]{2,1,0:T(8,128)(2,1)S(1)}, bf16[2,512,512]{2,1,0:T(8,128)(2,1)S(1)}, u32[]{:S(2)}, u32[]{:S(2)}) %collective-permute-start.11) | collective-permute-done | bytes 1048608 | tf_op jit(solution)/shard_map/turned_x/ppermute | solution.py:310
  81.1 2.2 %collective-permute-start.26 = (bf16[512,512]{1,0:T(8,128)(2,1)S(1)}, bf16[512,512]{1,0:T(8,128)(2,1)S(1)}, u32[]{:S(2)}, u32[]{:S(2)}) collective-permute-start(bf16[512,512]{1,0:T(8,128)(2,1)S(1)} %collective-permute-done.13.refs_11_), channel_id=1, source_target_pairs={{0,2},{1,3},{2,0},{3,1},{4,6},{5,7},{6,4},{7,5},{8,10},{9,11},{10,... | collective-permute-start | bytes 1572872 | tf_op jit(solution)/shard_map/g0_cross_upper/ppermute | solution.py:313
  83.3 3.4 %collective-permute-done.21.refs_12_ = bf16[512,512]{1,0:T(8,128)(2,1)S(1)} collective-permute-done((bf16[512,512]{1,0:T(8,128)(2,1)S(1)}, bf16[512,512]{1,0:T(8,128)(2,1)S(1)}, u32[]{:S(2)}, u32[]{:S(2)}) %collective-permute-start.21) | collective-permute-done | bytes 524320 | tf_op jit(solution)/shard_map/g0_far_lower/ppermute | solution.py:313
  86.7 1.6 %collective-permute-start.14 = (bf16[512,512]{1,0:T(8,128)(2,1)S(1)}, bf16[512,512]{1,0:T(8,128)(2,1)S(1)}, u32[]{:S(2)}, u32[]{:S(2)}) collective-permute-start(bf16[512,512]{1,0:T(8,128)(2,1)S(1)} %slice_bitcast_fusion.2), channel_id=1, source_target_pairs={{0,16},{8,24},{16,0},{24,8},{1,17},{9,25},{17,1},{25,9},{2,18},{10... | collective-permute-start | bytes 1572872 | tf_op jit(solution)/shard_map/turned_xy_upper/ppermute | solution.py:310
  89.9 7.9 %collective-permute-done.26.refs_0_ = bf16[512,512]{1,0:T(8,128)(2,1)S(1)} collective-permute-done((bf16[512,512]{1,0:T(8,128)(2,1)S(1)}, bf16[512,512]{1,0:T(8,128)(2,1)S(1)}, u32[]{:S(2)}, u32[]{:S(2)}) %collective-permute-start.26) | collective-permute-done | bytes 524320 | tf_op jit(solution)/shard_map/g0_cross_upper/ppermute | solution.py:313
  97.9 3.3 %collective-permute-done.14.refs_3_ = bf16[512,512]{1,0:T(8,128)(2,1)S(1)} collective-permute-done((bf16[512,512]{1,0:T(8,128)(2,1)S(1)}, bf16[512,512]{1,0:T(8,128)(2,1)S(1)}, u32[]{:S(2)}, u32[]{:S(2)}) %collective-permute-start.14) | collective-permute-done | bytes 524320 | tf_op jit(solution)/shard_map/turned_xy_upper/ppermute | solution.py:310
  102.5 4.9 %close.1 = (f32[2,512,512]{2,1,0:T(8,128)S(1)}, bf16[4096,512]{1,0:T(8,128)(2,1)S(1)}) custom-call(s32[4]{0:T(128)S(1)} %pad_add_fusion.1.source_ref, s32[6]{0:T(128)S(1)} %stack.88.owner_ref, bf16[2,512,512]{2,1,0:T(8,128)(2,1)S(1)} %turn.1.refs_0_, bf16[2,512,512]{2,1,0:T(8,128)(2,1)S(1)} %collective-permute-done.11.refs_1_, ...), custom_call_target="tpu_custom_call" | custom-call | tf_op jit(solution)/shard_map/close/pallas_call | solution.py:233
  107.5 4.2 %collective-permute-done.24.refs_0_ = bf16[512,512]{1,0:T(8,128)(2,1)S(1)} collective-permute-done((bf16[512,512]{1,0:T(8,128)(2,1)S(1)}, bf16[512,512]{1,0:T(8,128)(2,1)S(1)}, u32[]{:S(2)}, u32[]{:S(2)}) %collective-permute-start.24) | collective-permute-done | bytes 524320 | tf_op jit(solution)/shard_map/g0_cross_lower/ppermute | solution.py:313
  111.7 2.0 %last.2.refs_2_ = bf16[1024,512]{1,0:T(8,128)(2,1)} custom-call(s32[2]{0:T(128)S(1)} %get-tuple-element.52.owner_ref, f32[2,512,512]{2,1,0:T(8,128)S(1)} %get-tuple-element.44.total_ref, bf16[4096,512]{1,0:T(8,128)(2,1)S(1)} %get-tuple-element.45.column_ref, bf16[512,512]{1,0:T(8,128)(2,1)S(1)} %collective-permute-done.26.refs_0_, ...), custom_call_target="tpu_custom_call" | custom-call | tf_op jit(solution)/shard_map/last/pallas_call | solution.py:278
  113.7 2.0 %last.3 = bf16[1024,512]{1,0:T(8,128)(2,1)} custom-call(s32[2]{0:T(128)S(1)} %get-tuple-element.52.owner_ref, f32[2,512,512]{2,1,0:T(8,128)S(1)} %get-tuple-element.44.total_ref, bf16[4096,512]{1,0:T(8,128)(2,1)S(1)} %get-tuple-element.45.column_ref, bf16[512,512]{1,0:T(8,128)(2,1)S(1)} %collective-permute-done.24.refs_0_, ...), custom_call_target="tpu_custom_call", output_to_operand_aliasing={{}: (5, {})} | custom-call | tf_op jit(solution)/shard_map/last/pallas_call | solution.py:278
  (69 shorter events, 17.5 us)
Async XLA Ops:
  2.5 15.2 %collective-permute-start = (bf16[1552,128]{1,0:T(8,128)(2,1)S(1)}, bf16[1552,128]{1,0:T(8,128)(2,1)S(1)}, u32[]{:S(2)}, u32[]{:S(2)}) collective-permute-start(bf16[1552,128]{1,0:T(8,128)(2,1)S(1)} %fusion.1.refs_0_), channel_id=1, source_target_pairs={{0,6},{1,7},{2,4},{3,5},{4,2},{5,3},{6,0},{7,1},{8,14},{9,15},{10,... | collective-permute-start | bytes 1191944 | tf_op jit(solution)/shard_map/slots_far/ppermute | solution.py:313
  7.6 17.8 %collective-permute-start.1 = (bf16[1552,128]{1,0:T(8,128)(2,1)S(1)}, bf16[1552,128]{1,0:T(8,128)(2,1)S(1)}, u32[]{:S(2)}, u32[]{:S(2)}) collective-permute-start(bf16[1552,128]{1,0:T(8,128)(2,1)S(1)} %fusion.1.refs_0_), channel_id=1, source_target_pairs={{0,2},{1,3},{2,0},{3,1},{4,6},{5,7},{6,4},{7,5},{8,10},{9,11},{10,... | collective-permute-start | bytes 1191944 | tf_op jit(solution)/shard_map/slots_near/ppermute | solution.py:313
  7.6 19.5 %collective-permute-start.6 = (bf16[1552,128]{1,0:T(8,128)(2,1)S(1)}, bf16[1552,128]{1,0:T(8,128)(2,1)}, u32[]{:S(2)}, u32[]{:S(2)}) collective-permute-start(bf16[1552,128]{1,0:T(8,128)(2,1)S(1)} %fusion.1.refs_0_), channel_id=1, source_target_pairs={{0,1},{1,0},{2,3},{3,2},{4,5},{5,4},{6,7},{7,6},{8,9},{9,8},{10,11... | collective-permute-start | bytes 1191944 | tf_op jit(solution)/shard_map/slots_twin/ppermute | solution.py:318
  10.5 26.7 %collective-permute-start.7 = (bf16[2,512,512]{2,1,0:T(8,128)(2,1)}, bf16[2,512,512]{2,1,0:T(8,128)(2,1)S(1)}, u32[]{:S(2)}, u32[]{:S(2)}) collective-permute-start(bf16[2,512,512]{2,1,0:T(8,128)(2,1)} %get-tuple-element.36.own_ref.refs_5_), channel_id=1, source_target_pairs={{0,8},{8,0},{16,24},{24,16},{1,9},{9,1},{17,25},{25,17},{2,10},{10... | collective-permute-start | bytes 3145736 | tf_op jit(solution)/shard_map/g0_x/ppermute | solution.py:310
  12.0 26.8 %collective-permute-start.8 = (bf16[2,512,512]{2,1,0:T(8,128)(2,1)}, bf16[2,512,512]{2,1,0:T(8,128)(2,1)S(1)}, u32[]{:S(2)}, u32[]{:S(2)}) collective-permute-start(bf16[2,512,512]{2,1,0:T(8,128)(2,1)} %get-tuple-element.36.own_ref.refs_5_), channel_id=1, source_target_pairs={{0,16},{8,24},{16,0},{24,8},{1,17},{9,25},{17,1},{25,9},{2,18},{10... | collective-permute-start | bytes 3145736 | tf_op jit(solution)/shard_map/g0_y/ppermute | solution.py:310
  25.4 11.1 %collective-permute-start.2 = (bf16[1552,128]{1,0:T(8,128)(2,1)S(1)}, bf16[1552,128]{1,0:T(8,128)(2,1)S(1)}, u32[]{:S(2)}, u32[]{:S(2)}) collective-permute-start(bf16[1552,128]{1,0:T(8,128)(2,1)S(1)} %collective-permute-done.refs_4_), channel_id=1, source_target_pairs={{0,2},{1,3},{2,0},{3,1},{4,6},{5,7},{6,4},{7,5},{8,10},{9,11},{10,... | collective-permute-start | bytes 1191944 | tf_op jit(solution)/shard_map/slots_cross/ppermute | solution.py:313
  28.8 11.6 %collective-permute-start.4 = (bf16[1552,128]{1,0:T(8,128)(2,1)S(1)}, bf16[1552,128]{1,0:T(8,128)(2,1)S(1)}, u32[]{:S(2)}, u32[]{:S(2)}) collective-permute-start(bf16[1552,128]{1,0:T(8,128)(2,1)S(1)} %collective-permute-done.1.refs_2_), channel_id=1, source_target_pairs={{0,1},{1,0},{2,3},{3,2},{4,5},{5,4},{6,7},{7,6},{8,9},{9,8},{10,11... | collective-permute-start | bytes 1191944 | tf_op jit(solution)/shard_map/slots_near_twin/ppermute | solution.py:318
  36.5 22.6 %collective-permute-start.13 = (bf16[512,512]{1,0:T(8,128)(2,1)}, bf16[512,512]{1,0:T(8,128)(2,1)S(1)}, u32[]{:S(2)}, u32[]{:S(2)}) collective-permute-start(bf16[512,512]{1,0:T(8,128)(2,1)} %get-tuple-element.37), channel_id=1, source_target_pairs={{0,6},{1,7},{2,4},{3,5},{4,2},{5,3},{6,0},{7,1},{8,14},{9,15},{10,... | collective-permute-start | bytes 1572872 | tf_op jit(solution)/shard_map/g0_far_upper/ppermute | solution.py:313
  37.2 23.8 %collective-permute-start.17 = (bf16[512,512]{1,0:T(8,128)(2,1)}, bf16[512,512]{1,0:T(8,128)(2,1)S(1)}, u32[]{:S(2)}, u32[]{:S(2)}) collective-permute-start(bf16[512,512]{1,0:T(8,128)(2,1)} %get-tuple-element.37), channel_id=1, source_target_pairs={{0,2},{1,3},{2,0},{3,1},{4,6},{5,7},{6,4},{7,5},{8,10},{9,11},{10,... | collective-permute-start | bytes 1572872 | tf_op jit(solution)/shard_map/g0_near_upper/ppermute | solution.py:313
  37.2 12.7 %collective-permute-start.9 = (bf16[512,512]{1,0:T(8,128)(2,1)S(1)}, bf16[512,512]{1,0:T(8,128)(2,1)S(1)}, u32[]{:S(2)}, u32[]{:S(2)}) collective-permute-start(bf16[512,512]{1,0:T(8,128)(2,1)S(1)} %slice_bitcast_fusion.1), channel_id=1, source_target_pairs={{0,16},{8,24},{16,0},{24,8},{1,17},{9,25},{17,1},{25,9},{2,18},{10... | collective-permute-start | bytes 1572872 | tf_op jit(solution)/shard_map/g0_xy_upper/ppermute | solution.py:310
  38.9 12.5 %collective-permute-start.10 = (bf16[512,512]{1,0:T(8,128)(2,1)S(1)}, bf16[512,512]{1,0:T(8,128)(2,1)S(1)}, u32[]{:S(2)}, u32[]{:S(2)}) collective-permute-start(bf16[512,512]{1,0:T(8,128)(2,1)S(1)} %slice_bitcast_fusion.3), channel_id=1, source_target_pairs={{0,8},{8,0},{16,24},{24,16},{1,9},{9,1},{17,25},{25,17},{2,10},{10... | collective-permute-start | bytes 1572872 | tf_op jit(solution)/shard_map/g0_xy_lower/ppermute | solution.py:310
  57.1 22.8 %collective-permute-start.11 = (bf16[2,512,512]{2,1,0:T(8,128)(2,1)S(1)}, bf16[2,512,512]{2,1,0:T(8,128)(2,1)S(1)}, u32[]{:S(2)}, u32[]{:S(2)}) collective-permute-start(bf16[2,512,512]{2,1,0:T(8,128)(2,1)S(1)} %turn.1.refs_0_), channel_id=1, source_target_pairs={{0,8},{8,0},{16,24},{24,16},{1,9},{9,1},{17,25},{25,17},{2,10},{10... | collective-permute-start | bytes 3145736 | tf_op jit(solution)/shard_map/turned_x/ppermute | solution.py:310
  58.6 22.4 %collective-permute-start.12 = (bf16[2,512,512]{2,1,0:T(8,128)(2,1)S(1)}, bf16[2,512,512]{2,1,0:T(8,128)(2,1)S(1)}, u32[]{:S(2)}, u32[]{:S(2)}) collective-permute-start(bf16[2,512,512]{2,1,0:T(8,128)(2,1)S(1)} %turn.1.refs_0_), channel_id=1, source_target_pairs={{0,16},{8,24},{16,0},{24,8},{1,17},{9,25},{17,1},{25,9},{2,18},{10... | collective-permute-start | bytes 3145736 | tf_op jit(solution)/shard_map/turned_y/ppermute | solution.py:310
  61.0 12.8 %collective-permute-start.18 = (bf16[512,512]{1,0:T(8,128)(2,1)S(1)}, bf16[512,512]{1,0:T(8,128)(2,1)S(1)}, u32[]{:S(2)}, u32[]{:S(2)}) collective-permute-start(bf16[512,512]{1,0:T(8,128)(2,1)S(1)} %copy-done.1), channel_id=1, source_target_pairs={{0,2},{1,3},{2,0},{3,1},{4,6},{5,7},{6,4},{7,5},{8,10},{9,11},{10,... | collective-permute-start | bytes 1572872 | tf_op jit(solution)/shard_map/g0_near_lower/ppermute | solution.py:313
  61.3 27.0 %collective-permute-start.16 = (bf16[2,512,512]{2,1,0:T(8,128)(2,1)S(1)}, bf16[2,512,512]{2,1,0:T(8,128)(2,1)S(1)}, u32[]{:S(2)}, u32[]{:S(2)}) collective-permute-start(bf16[2,512,512]{2,1,0:T(8,128)(2,1)S(1)} %copy-done), channel_id=1, source_target_pairs={{0,1},{1,0},{2,3},{3,2},{4,5},{5,4},{6,7},{7,6},{8,9},{9,8},{10,11... | collective-permute-start | bytes 3145736 | tf_op jit(solution)/shard_map/g0_twin/ppermute | solution.py:318
  61.3 25.4 %collective-permute-start.21 = (bf16[512,512]{1,0:T(8,128)(2,1)S(1)}, bf16[512,512]{1,0:T(8,128)(2,1)S(1)}, u32[]{:S(2)}, u32[]{:S(2)}) collective-permute-start(bf16[512,512]{1,0:T(8,128)(2,1)S(1)} %copy-done.1), channel_id=1, source_target_pairs={{0,6},{1,7},{2,4},{3,5},{4,2},{5,3},{6,0},{7,1},{8,14},{9,15},{10,... | collective-permute-start | bytes 1572872 | tf_op jit(solution)/shard_map/g0_far_lower/ppermute | solution.py:313
  73.7 13.0 %collective-permute-start.20 = (bf16[512,512]{1,0:T(8,128)(2,1)S(1)}, bf16[512,512]{1,0:T(8,128)(2,1)S(1)}, u32[]{:S(2)}, u32[]{:S(2)}) collective-permute-start(bf16[512,512]{1,0:T(8,128)(2,1)S(1)} %collective-permute-done.18.refs_8_), channel_id=1, source_target_pairs={{0,1},{1,0},{2,3},{3,2},{4,5},{5,4},{6,7},{7,6},{8,9},{9,8},{10,11... | collective-permute-start | bytes 1572872 | tf_op jit(solution)/shard_map/g0_near_lower_twin/ppermute | solution.py:318
  81.1 16.8 %collective-permute-start.26 = (bf16[512,512]{1,0:T(8,128)(2,1)S(1)}, bf16[512,512]{1,0:T(8,128)(2,1)S(1)}, u32[]{:S(2)}, u32[]{:S(2)}) collective-permute-start(bf16[512,512]{1,0:T(8,128)(2,1)S(1)} %collective-permute-done.13.refs_11_), channel_id=1, source_target_pairs={{0,2},{1,3},{2,0},{3,1},{4,6},{5,7},{6,4},{7,5},{8,10},{9,11},{10,... | collective-permute-start | bytes 1572872 | tf_op jit(solution)/shard_map/g0_cross_upper/ppermute | solution.py:313
  86.7 11.1 %collective-permute-start.23 = (bf16[512,512]{1,0:T(8,128)(2,1)S(1)}, bf16[512,512]{1,0:T(8,128)(2,1)S(1)}, u32[]{:S(2)}, u32[]{:S(2)}) collective-permute-start(bf16[512,512]{1,0:T(8,128)(2,1)S(1)} %collective-permute-done.21.refs_12_), channel_id=1, source_target_pairs={{0,1},{1,0},{2,3},{3,2},{4,5},{5,4},{6,7},{7,6},{8,9},{9,8},{10,11... | collective-permute-start | bytes 1572872 | tf_op jit(solution)/shard_map/g0_far_lower_twin/ppermute | solution.py:318
  86.7 14.4 %collective-permute-start.14 = (bf16[512,512]{1,0:T(8,128)(2,1)S(1)}, bf16[512,512]{1,0:T(8,128)(2,1)S(1)}, u32[]{:S(2)}, u32[]{:S(2)}) collective-permute-start(bf16[512,512]{1,0:T(8,128)(2,1)S(1)} %slice_bitcast_fusion.2), channel_id=1, source_target_pairs={{0,16},{8,24},{16,0},{24,8},{1,17},{9,25},{17,1},{25,9},{2,18},{10... | collective-permute-start | bytes 1572872 | tf_op jit(solution)/shard_map/turned_xy_upper/ppermute | solution.py:310
  88.4 14.1 %collective-permute-start.15 = (bf16[512,512]{1,0:T(8,128)(2,1)S(1)}, bf16[512,512]{1,0:T(8,128)(2,1)S(1)}, u32[]{:S(2)}, u32[]{:S(2)}) collective-permute-start(bf16[512,512]{1,0:T(8,128)(2,1)S(1)} %slice_bitcast_fusion), channel_id=1, source_target_pairs={{0,8},{8,0},{16,24},{24,16},{1,9},{9,1},{17,25},{25,17},{2,10},{10... | collective-permute-start | bytes 1572872 | tf_op jit(solution)/shard_map/turned_xy_lower/ppermute | solution.py:310
  89.9 12.6 %collective-permute-start.19 = (bf16[512,512]{1,0:T(8,128)(2,1)S(1)}, bf16[512,512]{1,0:T(8,128)(2,1)S(1)}, u32[]{:S(2)}, u32[]{:S(2)}) collective-permute-start(bf16[512,512]{1,0:T(8,128)(2,1)S(1)} %collective-permute-done.17.refs_7_), channel_id=1, source_target_pairs={{0,1},{1,0},{2,3},{3,2},{4,5},{5,4},{6,7},{7,6},{8,9},{9,8},{10,11... | collective-permute-start | bytes 1572872 | tf_op jit(solution)/shard_map/g0_near_upper_twin/ppermute | solution.py:318
  97.8 13.8 %collective-permute-start.24 = (bf16[512,512]{1,0:T(8,128)(2,1)S(1)}, bf16[512,512]{1,0:T(8,128)(2,1)S(1)}, u32[]{:S(2)}, u32[]{:S(2)}) collective-permute-start(bf16[512,512]{1,0:T(8,128)(2,1)S(1)} %collective-permute-done.21.refs_12_), channel_id=1, source_target_pairs={{0,2},{1,3},{2,0},{3,1},{4,6},{5,7},{6,4},{7,5},{8,10},{9,11},{10,... | collective-permute-start | bytes 1572872 | tf_op jit(solution)/shard_map/g0_cross_lower/ppermute | solution.py:313
  97.8 13.8 %collective-permute-start.27 = (bf16[512,512]{1,0:T(8,128)(2,1)S(1)}, bf16[512,512]{1,0:T(8,128)(2,1)S(1)}, u32[]{:S(2)}, u32[]{:S(2)}) collective-permute-start(bf16[512,512]{1,0:T(8,128)(2,1)S(1)} %collective-permute-done.26.refs_0_), channel_id=1, source_target_pairs={{0,1},{1,0},{2,3},{3,2},{4,5},{5,4},{6,7},{7,6},{8,9},{9,8},{10,11... | collective-permute-start | bytes 1572872 | tf_op jit(solution)/shard_map/g0_cross_upper_twin/ppermute | solution.py:318
  (6 other events, 40.1 us)

commit v8 on v7

--- a/solution.py
+++ b/solution.py
@@ -157,76 +157,91 @@
     return found
 
 
-def turn_kernel(source_ref, dense_ref, own_ref, *refs):
-    out_ref, own, sem = refs[-3:]
-    parts = half_refs([own, *refs[:-3]])
-    _, half, cols = out_ref.shape
-    fetch = pltpu.make_async_copy(own_ref, own, sem)
-    fetch.start()
-    fetch.wait()
-    tile = min(256, half)
-    for side in range(2):
-        @pl.loop(0, half // tile)
-        def _(t):
-            at = pl.multiple_of(t * tile, tile)
-            total = jnp.zeros((tile, cols), jnp.float32)
-            for i, part in enumerate(parts):
-                start = pl.multiple_of(source_ref[i // 2] * (2 * half) + (i % 2) * half, half)
-                total += jnp.dot(
-                    dense_ref[pl.ds(side * half + at, tile), pl.ds(start, half)], part[...],
-                    preferred_element_type=jnp.float32,
-                )
-            out_ref[side, pl.ds(at, tile), :] = total.astype(jnp.bfloat16)
-
-
-def turn(sources, dense, parts):
-    _, half, cols = parts[0].shape
-    return pl.pallas_call(
-        turn_kernel,
-        out_shape=jax.ShapeDtypeStruct((2, half, cols), jnp.bfloat16),
-        in_specs=[SMEM, VMEM, ANY] + [VMEM] * (len(parts) - 1),
-        out_specs=VMEM,
-        scratch_shapes=[pltpu.VMEM((2, half, cols), jnp.bfloat16), pltpu.SemaphoreType.DMA],
-        compiler_params=kernel_params(),
-        cost_estimate=NO_COST,
-        name="turn",
-    )(sources, dense, *parts)
-
-
-def add_products(total, owner_ref, parts, column_ref):
-    cols = parts[0].shape[-1]
-    for i, part in enumerate(parts):
-        start = pl.multiple_of(owner_ref[i] * cols, cols)
-        total += jnp.dot(part, column_ref[pl.ds(start, cols), :], preferred_element_type=jnp.float32)
-    return total
-
-
-def close_kernel(n_col, source_ref, owner_ref, *refs):
-    total_ref, column_ref, own, sem, own_sem = refs[-5:]
-    col_refs, row_refs = half_refs(refs[:n_col]), half_refs([own, *refs[n_col + 1:-5]])
-    half, _ = row_refs[0].shape
-    fetch = pltpu.make_async_copy(refs[n_col], own, own_sem)
-    fetch.start()
-
-    def column_copy(i):
-        start = pl.multiple_of(source_ref[i // 2] * (2 * half) + (i % 2) * half, half)
-        return pltpu.make_async_copy(col_refs[i], column_ref.at[pl.ds(start, half)], sem.at[i])
-
-    for i in range(len(col_refs)):
-        column_copy(i).start()
-    for i in range(len(col_refs)):
-        column_copy(i).wait()
-    fetch.wait()
+def column_start(source_ref, i, half):
+    return pl.multiple_of(source_ref[i // 2] * (2 * half) + (i % 2) * half, half)
+
+
+def turn_kernel(first, source_ref, dense_ref, own_ref, *refs):
+    if first == 0:
+        out_ref, own, sem = refs[-3:]
+        parts = half_refs([own, *refs[:-3]])
+        fetch = pltpu.make_async_copy(own_ref, own, sem)
+        fetch.start()
+        fetch.wait()
+    else:
+        out_ref, own, parts = refs[-1], own_ref, refs[:-1]
+    half, cols = parts[0].shape
     tile = min(256, half)
     for side in range(2):
         @pl.loop(0, half // tile)
         def _(t):
             at = pl.ds(pl.multiple_of(t * tile, tile), tile)
-            parts = [part[at, :] for part in row_refs[side::2]]
-            total_ref[side, at, :] = add_products(parts[0].astype(jnp.float32), owner_ref, parts, column_ref)
-
-
-def close(sources, owners, col_parts, row_parts):
+            rows = pl.ds(pl.multiple_of(side * half + t * tile, tile), tile)
+            total = jnp.zeros((tile, cols), jnp.float32) if first == 0 else own[side, at, :]
+            for i, part in enumerate(parts):
+                start = column_start(source_ref, first + i, half)
+                total += jnp.dot(dense_ref[rows, pl.ds(start, half)], part[...], preferred_element_type=jnp.float32)
+            out_ref[side, at, :] = total.astype(out_ref.dtype)
+
+
+def turn(first, sources, dense, start, parts, dtype):
+    _, half, cols = start.shape
+    return pl.pallas_call(
+        functools.partial(turn_kernel, first),
+        out_shape=jax.ShapeDtypeStruct((2, half, cols), dtype),
+        in_specs=[SMEM, VMEM, VMEM if first else ANY] + [VMEM] * len(parts),
+        out_specs=VMEM,
+        scratch_shapes=[] if first else [pltpu.VMEM((2, half, cols), start.dtype), pltpu.SemaphoreType.DMA],
+        compiler_params=kernel_params(),
+        cost_estimate=NO_COST,
+        name="turn" if first == 0 else "turn_rest",
+    )(sources, dense, start, *parts)
+
+
+def add_products(total, owner_ref, lead, parts, column_ref):
+    cols = parts[0].shape[-1]
+    for i, part in enumerate(parts):
+        start = pl.multiple_of(owner_ref[lead + i] * cols, cols)
+        total += jnp.dot(part, column_ref[pl.ds(start, cols), :], preferred_element_type=jnp.float32)
+    return total
+
+
+def add_blocks(late, late_ref, owner_ref, total_ref, column_ref, row_refs):
+    half = row_refs[0].shape[0]
+    tile = min(256, half)
+    for block in range(len(row_refs) // 4):
+        @pl.when(late_ref[block] == late)
+        def _():
+            for side in range(2):
+                refs = row_refs[4 * block + side:4 * block + 4:2]
+
+                @pl.loop(0, half // tile)
+                def _(t):
+                    at = pl.ds(pl.multiple_of(t * tile, tile), tile)
+                    parts = [ref[at, :] for ref in refs]
+                    total_ref[side, at, :] = add_products(total_ref[side, at, :], owner_ref, 2 * block, parts, column_ref)
+
+
+def close_kernel(n_col, source_ref, owner_ref, late_ref, *refs):
+    total_ref, column_ref, own, sem, own_sem = refs[-5:]
+    col_refs, row_refs = half_refs(refs[:n_col]), half_refs([own, *refs[n_col + 1:-5]])
+    half = row_refs[0].shape[0]
+    fetch = pltpu.make_async_copy(refs[n_col], own, own_sem)
+    fetch.start()
+    moves = [
+        pltpu.make_async_copy(ref, column_ref.at[pl.ds(column_start(source_ref, i, half), half)], sem.at[i])
+        for i, ref in enumerate(col_refs)
+    ]
+    for move in moves:
+        move.start()
+    fetch.wait()
+    total_ref[...] = own[...].astype(jnp.float32)
+    for move in moves:
+        move.wait()
+    add_blocks(0, late_ref, owner_ref, total_ref, column_ref, row_refs)
+
+
+def close(sources, owners, late, col_parts, row_parts, depth):
     half, cols = row_parts[0].shape[-2:]
     n_col = len(col_parts)
     n_half = sum(part.ndim - 1 for part in col_parts)
@@ -234,9 +249,9 @@
         functools.partial(close_kernel, n_col),
         out_shape=(
             jax.ShapeDtypeStruct((2, half, cols), jnp.float32),
-            jax.ShapeDtypeStruct((n_half * half, cols), jnp.bfloat16),
+            jax.ShapeDtypeStruct((depth, cols), jnp.bfloat16),
         ),
-        in_specs=[SMEM, SMEM] + [ANY] * (n_col + 1) + [VMEM] * (len(row_parts) - 1),
+        in_specs=[SMEM, SMEM, SMEM] + [ANY] * (n_col + 1) + [VMEM] * (len(row_parts) - 1),
         out_specs=(VMEM, VMEM),
         scratch_shapes=[
             pltpu.VMEM((2, half, cols), jnp.bfloat16),
@@ -246,7 +261,45 @@
         compiler_params=kernel_params(),
         cost_estimate=NO_COST,
         name="close",
-    )(sources, owners, *col_parts, *row_parts)
+    )(sources, owners, late, *col_parts, *row_parts)
+
+
+def close_rest_kernel(first, n_col, source_ref, owner_ref, late_ref, _, __, *refs):
+    total_ref, column_ref, own, sem, own_sem = refs[-5:]
+    col_refs, row_refs = refs[:n_col], half_refs([own, *refs[n_col + 1:-5]])
+    half = row_refs[0].shape[0]
+    fetch = pltpu.make_async_copy(refs[n_col], own, own_sem)
+    fetch.start()
+    moves = [
+        pltpu.make_async_copy(ref, column_ref.at[pl.ds(column_start(source_ref, first + i, half), half)], sem.at[i])
+        for i, ref in enumerate(col_refs)
+    ]
+    for move in moves:
+        move.start()
+    fetch.wait()
+    for move in moves:
+        move.wait()
+    add_blocks(1, late_ref, owner_ref, total_ref, column_ref, row_refs)
+
+
+def close_rest(first, sources, owners, late, total, column, col_parts, row_parts):
+    half, cols = row_parts[0].shape[-2:]
+    n_col = len(col_parts)
+    return pl.pallas_call(
+        functools.partial(close_rest_kernel, first, n_col),
+        out_shape=(jax.ShapeDtypeStruct(total.shape, total.dtype), jax.ShapeDtypeStruct(column.shape, column.dtype)),
+        in_specs=[SMEM] * 3 + [VMEM, VMEM] + [ANY] * (n_col + 1) + [VMEM] * (len(row_parts) - 1),
+        out_specs=(VMEM, VMEM),
+        scratch_shapes=[
+            pltpu.VMEM((2, half, cols), jnp.bfloat16),
+            pltpu.SemaphoreType.DMA((n_col,)),
+            pltpu.SemaphoreType.DMA,
+        ],
+        input_output_aliases={3: 0, 4: 1},
+        compiler_params=kernel_params(),
+        cost_estimate=NO_COST,
+        name="close_rest",
+    )(sources, owners, late, total, column, *col_parts, *row_parts)
 
 
 def last_kernel(side, n_row, owner_ref, total_ref, column_ref, *refs):
@@ -257,7 +310,7 @@
     for t in range(half // tile):
         at = pl.ds(t * tile, tile)
         parts = [part[at, :] for part in row_refs]
-        result[at, :] = add_products(total_ref[side, at, :], owner_ref, parts, column_ref).astype(jnp.bfloat16)
+        result[at, :] = add_products(total_ref[side, at, :], owner_ref, 0, parts, column_ref).astype(jnp.bfloat16)
         target = out_ref.at[pl.ds(side * half + t * tile, tile)]
         moves.append(pltpu.make_async_copy(result.at[at], target, sem.at[t]))
         moves[-1].start()
@@ -383,17 +436,20 @@
         for value in grid.around(message):
             sigma_parts += [value, grid.twin(value)]
         dense = dense_fill(owners[-2:], sigma_parts[-2:], dense_rows(owners[:-2], sigma_parts[:-2]))
-        turned = turn(sources, dense, grid.plane(tile))
+        found = grid.plane(tile)
+        turned = turn(0, sources, dense, found[0], found[1:], jnp.bfloat16)
         row_parts = []
         for value in grid.around(tile):
             row_parts += [value, grid.twin(value)]
-        total, column = close(sources, owners[:-2], grid.plane(turned), row_parts[:-2])
+        late = jnp.zeros((grid.nz - 1,), jnp.int32)
+        total, column = close(sources, owners[:-2], late, grid.plane(turned), row_parts[:-2], depth)
         result = None
         for side in range(2):
             result = last(side, owners[-2:], total, column, [part[side] for part in row_parts[-2:]], result)
         return result
 
     slot_owners = grid.col_owners(z, z ^ 1, 3 - z, 3 - (z ^ 1))
+    small = message[slots * width:]
     with jax.named_scope("slots_far"):
         s_far = grid.along_z(message, MIRROR)
     with jax.named_scope("slots_near"):
@@ -405,54 +461,61 @@
     with jax.named_scope("g0_y"):
         g_y = grid.shift(tile, "y")
     with jax.named_scope("slots_far_twin"):
-        s_far_tw = grid.twin(after(s_far, s_near))
+        s_far_tw = grid.twin(s_far)
     with jax.named_scope("slots_cross"):
-        s_cross = grid.along_z(after(s_far, s_near), NEAR)
+        s_cross = grid.along_z(after(s_far, s_far), NEAR)
     with jax.named_scope("slots_near_twin"):
         s_near_tw = grid.twin(after(s_near, s_far_tw))
     with jax.named_scope("g0_xy_upper"):
         g_xyu = grid.shift(g_x[0], "y")
     with jax.named_scope("g0_xy_lower"):
-        g_xyl = grid.shift(after(g_y, s_far)[1], "x")
+        g_xyl = grid.shift(g_y[1], "x")
     dense1 = dense_rows(slot_owners[:-2], [message, s_tw, s_near, s_near_tw, s_far, s_far_tw])
     with jax.named_scope("g0_far_upper"):
-        far_u = grid.along_z(after(upper, s_cross), MIRROR)
+        far_u = grid.along_z(after(upper, s_cross, s_near, s_far), MIRROR)
     with jax.named_scope("g0_near_upper"):
-        near_u = grid.along_z(after(upper, s_cross, s_near), NEAR)
+        near_u = grid.along_z(after(upper, s_cross), NEAR)
     with jax.named_scope("slots_cross_twin"):
-        s_cross_tw = grid.twin(after(s_cross, s_near_tw))
+        s_cross_tw = grid.twin(after(s_cross, s_near_tw, s_far_tw))
+    with jax.named_scope("small_2"):
+        d2 = grid.twin(small)
     dense2 = dense_fill(slot_owners[-2:], [s_cross, s_cross_tw], dense1)
-    turned = turn(sources, dense2, [tile, g_x, g_y, g_xyu, g_xyl])
+    turn_a = turn(0, sources, dense2, tile, [g_x, g_y], jnp.float32)
+    turned = turn(6, sources, dense2, after(turn_a, dense2, g_xyl), [g_xyu, g_xyl], jnp.bfloat16)
     with jax.named_scope("turned_x"):
         t_x = grid.shift(turned, "x")
     with jax.named_scope("turned_y"):
-        t_y = grid.shift(turned, "y")
+        t_y = grid.shift(after(turned, near_u, dense2), "y")
     with jax.named_scope("g0_twin"):
-        tile_tw = grid.twin(after(tile, turned))
+        tile_tw = grid.twin(after(tile, dense1))
     with jax.named_scope("g0_near_upper_twin"):
-        near_u_tw = grid.twin(after(near_u, tile_tw))
+        near_u_tw = grid.twin(after(near_u, turned))
     with jax.named_scope("g0_far_upper_twin"):
-        far_u_tw = grid.twin(far_u)
+        far_u_tw = grid.twin(after(far_u, turned, d2))
     with jax.named_scope("g0_far_lower"):
-        far_l = grid.along_z(after(lower, near_u, far_u, turned), MIRROR)
+        far_l = grid.along_z(after(lower, far_u), MIRROR)
     with jax.named_scope("g0_near_lower"):
-        near_l = grid.along_z(after(lower, near_u, far_u), NEAR)
+        near_l = grid.along_z(after(lower, near_u_tw), NEAR)
+    with jax.named_scope("small_4"):
+        d4 = grid.twin(after(small, t_x))
     with jax.named_scope("turned_xy_upper"):
-        t_xyu = grid.shift(after(t_x, far_u)[0], "y")
+        t_xyu = grid.shift(after(t_x, t_x)[0], "y")
     with jax.named_scope("turned_xy_lower"):
         t_xyl = grid.shift(t_y[1], "x")
     with jax.named_scope("g0_near_lower_twin"):
-        near_l_tw = grid.twin(after(near_l, near_u))
+        near_l_tw = grid.twin(near_l)
     with jax.named_scope("g0_far_lower_twin"):
-        far_l_tw = grid.twin(after(far_l, near_l_tw))
+        far_l_tw = grid.twin(after(far_l, near_l))
+    row_parts = [tile, tile_tw, near_u, near_l, near_u_tw, near_l_tw, far_u, far_l, far_u_tw, far_l_tw]
+    late = (jnp.stack([z, z ^ 1, 3 - z]) == sources[3]).astype(jnp.int32)
+    total_a, column_a = close(sources, slot_owners[:-2], late, [after(turned, t_xyu), t_x, t_y], row_parts, depth)
     with jax.named_scope("g0_cross_upper"):
-        cross_u = grid.along_z(after(far_u, t_x, t_y), NEAR)
+        cross_u = grid.along_z(after(far_u, far_l, t_x, t_y), NEAR)
     with jax.named_scope("g0_cross_lower"):
-        cross_l = grid.along_z(far_l, NEAR)
-    row_parts = [tile, tile_tw, near_u, near_l, near_u_tw, near_l_tw, far_u, far_l, far_u_tw, far_l_tw]
-    total, column = close(sources, slot_owners[:-2], [turned, t_x, t_y, t_xyu, t_xyl], row_parts)
+        cross_l = grid.along_z(after(far_l, far_l_tw, d4, tile_tw), NEAR)
+    total, column = close_rest(6, sources, slot_owners[:-2], late, total_a, column_a, [t_xyu, t_xyl], row_parts)
     with jax.named_scope("g0_cross_upper_twin"):
-        cross_u_tw = grid.twin(after(cross_u, cross_u))
+        cross_u_tw = grid.twin(after(cross_u, near_l_tw))
     last0 = last(0, slot_owners[-2:], total, column, [cross_u, cross_u_tw])
     with jax.named_scope("g0_cross_lower_twin"):
         cross_l_tw = grid.twin(after(cross_l, column))

time: 116 us -> 118 us (1.017)
  Pallas kernels: 22.3 us -> 26.3 us
  starting transfers between devices: 25.2 us -> 23.5 us
    ppermute x8, waiting for transfers between devices: 17.8 us -> 0.02 us  [shift(): return lax.ppermute(value, 'row', pairs)]
    ppermute x9, waiting for transfers between devices: 45.4 us -> 61.9 us  [along_z(): lax.ppermute(value, 'col', [(z * self.nc + c, to * self.nc + c) for z, to...]
    pallas_call x1 -> x3, Pallas kernels: 5.74 us -> 9.44 us  [the longest x2 6.92 us: turn(): pl.pallas_call(functools.partial(turn_kernel, first), out_shape=jax.Shape...]
    ppermute x9, starting transfers between devices: 13.6 us -> 11.1 us  [along_z(): lax.ppermute(value, 'col', [(z * self.nc + c, to * self.nc + c) for z, to...]
    ppermute x11, starting transfers between devices: 0.18 us -> 1.87 us  [twin(): lax.ppermute(value, 'col', [(z * self.nc + c, z * self.nc + 1 - c) for z...]
  transfers between devices with their start and end apart: 28 -> 28, of which waited for: 15 -> 8; matrix products, arithmetic and copies ran while one was open for 1% -> 1% of each run, Pallas kernels for 18% -> 21%
where the time goes in v8:
time: 118 us
  waiting for transfers between devices  63.9 us (54%)
  Pallas kernels  26.3 us (22%)
  starting transfers between devices  23.5 us (20%)
  other arithmetic  2.2 us (2%)
    ppermute x9, waiting for transfers between devices, along_z(): lax.ppermute(value, 'col', [(z * self.nc + c, to * self.nc + c) for z, to...  61.9 us
    ppermute x9, starting transfers between devices, along_z(): lax.ppermute(value, 'col', [(z * self.nc + c, to * self.nc + c) for z, to...  11.1 us
    ppermute x8, starting transfers between devices, shift(): return lax.ppermute(value, 'row', pairs)  10.6 us
    pallas_call x2, Pallas kernels, turn(): pl.pallas_call(functools.partial(turn_kernel, first), out_shape=jax.Shape...  6.92 us
    pallas_call x1, Pallas kernels, close(): pl.pallas_call(functools.partial(close_kernel, n_col), out_shape=(jax.Sha...  4.59 us
    pallas_call x1, Pallas kernels, spread(): pl.pallas_call(functools.partial(spread_kernel, len(parts), slots, width)...  4.07 us
    pallas_call x2, Pallas kernels, last(): pl.pallas_call(functools.partial(last_kernel, side, n_row), out_shape=jax...  3.96 us
    pallas_call x1, Pallas kernels, masked(): pl.pallas_call(functools.partial(mask_kernel, width), out_shape=(jax.Shap...  2.88 us
  transfers between devices with their start and end apart: 28, of which 8 were waited for; matrix products, arithmetic and copies ran while one was open for 1% of the time, Pallas kernels for 21%

profile of v8, /device:TPU:0, one launch (start us, length us, event | category | flops | bytes accessed | tf_op | source)
XLA Modules:
  0.0 117.7 jit_solution(1998966772605050287)
XLA Ops:
  3.0 2.6 %collective-permute-start.2 = (bf16[1552,128]{1,0:T(8,128)(2,1)S(1)}, bf16[1552,128]{1,0:T(8,128)(2,1)S(1)}, u32[]{:S(2)}, u32[]{:S(2)}) collective-permute-start(bf16[1552,128]{1,0:T(8,128)(2,1)S(1)} %fusion.1.refs_0_), channel_id=1, source_target_pairs={{0,2},{1,3},{2,0},{3,1},{4,6},{5,7},{6,4},{7,5},{8,10},{9,11},{10,... | collective-permute-start | bytes 1191944 | tf_op jit(solution)/shard_map/slots_near/ppermute | solution.py:366
  5.6 2.5 %collective-permute-start = (bf16[1552,128]{1,0:T(8,128)(2,1)S(1)}, bf16[1552,128]{1,0:T(8,128)(2,1)}, u32[]{:S(2)}, u32[]{:S(2)}) collective-permute-start(bf16[1552,128]{1,0:T(8,128)(2,1)S(1)} %fusion.1.refs_0_), channel_id=1, source_target_pairs={{0,6},{1,7},{2,4},{3,5},{4,2},{5,3},{6,0},{7,1},{8,14},{9,15},{10,... | collective-permute-start | bytes 1191944 | tf_op jit(solution)/shard_map/slots_far/ppermute | solution.py:366
  8.1 2.9 %mask.1 = (bf16[2,512,512]{2,1,0:T(8,128)(2,1)}, bf16[512,512]{1,0:T(8,128)(2,1)}, bf16[512,512]{1,0:T(8,128)(2,1)}) custom-call(s32[4,8]{1,0:T(4,128)} %bitcast.73, bf16[1024,512]{1,0:T(8,128)(2,1)} %values_ref), custom_call_target="tpu_custom_call" | custom-call | tf_op jit(solution)/shard_map/mask/pallas_call | solution.py:76
  11.0 1.6 %collective-permute-start.7 = (bf16[2,512,512]{2,1,0:T(8,128)(2,1)}, bf16[2,512,512]{2,1,0:T(8,128)(2,1)S(1)}, u32[]{:S(2)}, u32[]{:S(2)}) collective-permute-start(bf16[2,512,512]{2,1,0:T(8,128)(2,1)} %get-tuple-element.43.own_ref.refs_3_.refs_2_), channel_id=1, source_target_pairs={{0,8},{8,0},{16,24},{24,16},{1,9},{9,1},{17,25},{25,17},{2,10},{10... | collective-permute-start | bytes 3145736 | tf_op jit(solution)/shard_map/g0_x/ppermute | solution.py:363
  12.6 1.5 %collective-permute-start.8 = (bf16[2,512,512]{2,1,0:T(8,128)(2,1)}, bf16[2,512,512]{2,1,0:T(8,128)(2,1)S(1)}, u32[]{:S(2)}, u32[]{:S(2)}) collective-permute-start(bf16[2,512,512]{2,1,0:T(8,128)(2,1)} %get-tuple-element.43.own_ref.refs_3_.refs_2_), channel_id=1, source_target_pairs={{0,16},{8,24},{16,0},{24,8},{1,17},{9,25},{17,1},{25,9},{2,18},{10... | collective-permute-start | bytes 3145736 | tf_op jit(solution)/shard_map/g0_y/ppermute | solution.py:363
  14.3 12.0 %collective-permute-done.refs_4_ = bf16[1552,128]{1,0:T(8,128)(2,1)} collective-permute-done((bf16[1552,128]{1,0:T(8,128)(2,1)S(1)}, bf16[1552,128]{1,0:T(8,128)(2,1)}, u32[]{:S(2)}, u32[]{:S(2)}) %collective-permute-start) | collective-permute-done | bytes 397344 | tf_op jit(solution)/shard_map/slots_far/ppermute | solution.py:366
  27.0 1.9 %collective-permute-done.3.refs_5_ = bf16[1552,128]{1,0:T(8,128)(2,1)S(1)} collective-permute-done((bf16[1552,128]{1,0:T(8,128)(2,1)}, bf16[1552,128]{1,0:T(8,128)(2,1)S(1)}, u32[]{:S(2)}, u32[]{:S(2)}) %collective-permute-start.3) | collective-permute-done | bytes 397344 | tf_op jit(solution)/shard_map/slots_far_twin/ppermute | solution.py:371
  29.0 8.3 %collective-permute-done.1.refs_0_ = bf16[1552,128]{1,0:T(8,128)(2,1)S(1)} collective-permute-done((bf16[1552,128]{1,0:T(8,128)(2,1)}, bf16[1552,128]{1,0:T(8,128)(2,1)S(1)}, u32[]{:S(2)}, u32[]{:S(2)}) %collective-permute-start.1) | collective-permute-done | bytes 397344 | tf_op jit(solution)/shard_map/slots_cross/ppermute | solution.py:366
  37.6 2.7 %collective-permute-start.19 = (bf16[512,512]{1,0:T(8,128)(2,1)}, bf16[512,512]{1,0:T(8,128)(2,1)S(1)}, u32[]{:S(2)}, u32[]{:S(2)}) collective-permute-start(bf16[512,512]{1,0:T(8,128)(2,1)} %get-tuple-element.47), channel_id=1, source_target_pairs={{0,6},{1,7},{2,4},{3,5},{4,2},{5,3},{6,0},{7,1},{8,14},{9,15},{10,... | collective-permute-start | bytes 1572872 | tf_op jit(solution)/shard_map/g0_far_upper/ppermute | solution.py:366
  40.3 1.6 %collective-permute-start.9 = (bf16[512,512]{1,0:T(8,128)(2,1)S(1)}, bf16[512,512]{1,0:T(8,128)(2,1)S(1)}, u32[]{:S(2)}, u32[]{:S(2)}) collective-permute-start(bf16[512,512]{1,0:T(8,128)(2,1)S(1)} %slice_bitcast_fusion.2), channel_id=1, source_target_pairs={{0,8},{8,0},{16,24},{24,16},{1,9},{9,1},{17,25},{25,17},{2,10},{10... | collective-permute-start | bytes 1572872 | tf_op jit(solution)/shard_map/g0_xy_lower/ppermute | solution.py:363
  41.9 1.6 %collective-permute-start.10 = (bf16[512,512]{1,0:T(8,128)(2,1)S(1)}, bf16[512,512]{1,0:T(8,128)(2,1)S(1)}, u32[]{:S(2)}, u32[]{:S(2)}) collective-permute-start(bf16[512,512]{1,0:T(8,128)(2,1)S(1)} %slice_bitcast_fusion.1), channel_id=1, source_target_pairs={{0,16},{8,24},{16,0},{24,8},{1,17},{9,25},{17,1},{25,9},{2,18},{10... | collective-permute-start | bytes 1572872 | tf_op jit(solution)/shard_map/g0_xy_upper/ppermute | solution.py:363
  44.3 4.1 %spread.1.refs_2_ = bf16[1024,4096]{1,0:T(8,128)(2,1)S(1)} custom-call(s32[6,12]{1,0:T(8,128)S(1)} %bitcast.69, s32[6,12]{1,0:T(8,128)S(1)} %bitcast_add_fusion.col_ref, bf16[1552,128]{1,0:T(8,128)(2,1)S(1)} %fusion.1.refs_0_, bf16[1552,128]{1,0:T(8,128)(2,1)S(1)} %collective-permute-done.6.refs_1_, bf16[1552,128]{1,0:T(8,128)(2,1)S(1)} %collective-permute-done.2.refs_2_, ...), custom_call_target="tpu_custom_call" | custom-call | tf_op jit(solution)/shard_map/spread/pallas_call | solution.py:121
  49.9 4.6 %turn.1.own_ref = f32[2,512,512]{2,1,0:T(8,128)S(1)} custom-call(s32[4]{0:T(128)S(1)} %pad_add_fusion.1.source_ref, bf16[1024,4096]{1,0:T(8,128)(2,1)S(1)} %fill.1.dense_ref, bf16[2,512,512]{2,1,0:T(8,128)(2,1)S(1)} %copy-done, bf16[2,512,512]{2,1,0:T(8,128)(2,1)S(1)} %collective-permute-done.7.refs_0_, bf16[2,512,512]{2,1,0:T(8,128)(2,1)S(1)} %collective-permute-done.8.refs_1_), custom_call_target="tpu_custom_call" | custom-call | tf_op jit(solution)/shard_map/turn/pallas_call | solution.py:189
  54.6 2.3 %turn_rest.1.refs_0_ = bf16[2,512,512]{2,1,0:T(8,128)(2,1)S(1)} custom-call(s32[4]{0:T(128)S(1)} %pad_add_fusion.1.source_ref, bf16[1024,4096]{1,0:T(8,128)(2,1)S(1)} %fill.1.dense_ref, f32[2,512,512]{2,1,0:T(8,128)S(1)} %turn.1.own_ref, bf16[512,512]{1,0:T(8,128)(2,1)S(1)} %collective-permute-done.10.refs_0_, ...), custom_call_target="tpu_custom_call" | custom-call | tf_op jit(solution)/shard_map/turn_rest/pallas_call | solution.py:189
  58.7 3.3 %collective-permute-done.19.refs_9_.refs_8_ = bf16[512,512]{1,0:T(8,128)(2,1)S(1)} collective-permute-done((bf16[512,512]{1,0:T(8,128)(2,1)}, bf16[512,512]{1,0:T(8,128)(2,1)S(1)}, u32[]{:S(2)}, u32[]{:S(2)}) %collective-permute-start.19) | collective-permute-done | bytes 524320 | tf_op jit(solution)/shard_map/g0_far_upper/ppermute | solution.py:366
  63.6 15.1 %collective-permute-done.20.refs_10_.refs_9_ = bf16[512,512]{1,0:T(8,128)(2,1)S(1)} collective-permute-done((bf16[512,512]{1,0:T(8,128)(2,1)S(1)}, bf16[512,512]{1,0:T(8,128)(2,1)S(1)}, u32[]{:S(2)}, u32[]{:S(2)}) %collective-permute-start.20) | collective-permute-done | bytes 524320 | tf_op jit(solution)/shard_map/g0_far_lower/ppermute | solution.py:366
  78.7 7.3 %collective-permute-done.17.refs_6_.refs_5_ = bf16[512,512]{1,0:T(8,128)(2,1)S(1)} collective-permute-done((bf16[512,512]{1,0:T(8,128)(2,1)S(1)}, bf16[512,512]{1,0:T(8,128)(2,1)S(1)}, u32[]{:S(2)}, u32[]{:S(2)}) %collective-permute-start.17) | collective-permute-done | bytes 524320 | tf_op jit(solution)/shard_map/g0_near_lower/ppermute | solution.py:366
  86.4 1.6 %collective-permute-start.12 = (bf16[512,512]{1,0:T(8,128)(2,1)S(1)}, bf16[512,512]{1,0:T(8,128)(2,1)S(1)}, u32[]{:S(2)}, u32[]{:S(2)}) collective-permute-start(bf16[512,512]{1,0:T(8,128)(2,1)S(1)} %slice_bitcast_fusion.3), channel_id=1, source_target_pairs={{0,16},{8,24},{16,0},{24,8},{1,17},{9,25},{17,1},{25,9},{2,18},{10... | collective-permute-start | bytes 1572872 | tf_op jit(solution)/shard_map/turned_xy_upper/ppermute | solution.py:363
  90.1 10.2 %collective-permute-done.26.refs_0_ = bf16[512,512]{1,0:T(8,128)(2,1)S(1)} collective-permute-done((bf16[512,512]{1,0:T(8,128)(2,1)S(1)}, bf16[512,512]{1,0:T(8,128)(2,1)S(1)}, u32[]{:S(2)}, u32[]{:S(2)}) %collective-permute-start.26) | collective-permute-done | bytes 524320 | tf_op jit(solution)/shard_map/g0_cross_upper/ppermute | solution.py:366
  100.8 4.6 %close.1 = (f32[2,512,512]{2,1,0:T(8,128)S(1)}, bf16[4096,512]{1,0:T(8,128)(2,1)S(1)}) custom-call(s32[4]{0:T(128)S(1)} %pad_add_fusion.1.source_ref, s32[6]{0:T(128)S(1)} %stack.100.owner_ref, s32[3]{0:T(128)S(1)} %compare_convert_fusion.late_ref, bf16[2,512,512]{2,1,0:T(8,128)(2,1)S(1)} %turn_rest.1.refs_0_, ...), custom_call_target="tpu_custom_call" | custom-call | tf_op jit(solution)/shard_map/close/pallas_call | solution.py:248
  105.4 2.5 %close_rest.1 = (f32[2,512,512]{2,1,0:T(8,128)S(1)}, bf16[4096,512]{1,0:T(8,128)(2,1)S(1)}) custom-call(s32[4]{0:T(128)S(1)} %pad_add_fusion.1.source_ref, s32[6]{0:T(128)S(1)} %stack.100.owner_ref, s32[3]{0:T(128)S(1)} %compare_convert_fusion.late_ref, f32[2,512,512]{2,1,0:T(8,128)S(1)} %get-tuple-element.51._, ...), custom_call_target="tpu_custom_call", output_to_operand_aliasing={{0}: (3, {}), {1}: (4, {})} | custom-call | tf_op jit(solution)/shard_map/close_rest/pallas_call | solution.py:288
  107.9 5.8 %collective-permute-done.24.refs_0_ = bf16[512,512]{1,0:T(8,128)(2,1)S(1)} collective-permute-done((bf16[512,512]{1,0:T(8,128)(2,1)S(1)}, bf16[512,512]{1,0:T(8,128)(2,1)S(1)}, u32[]{:S(2)}, u32[]{:S(2)}) %collective-permute-start.24) | collective-permute-done | bytes 524320 | tf_op jit(solution)/shard_map/g0_cross_lower/ppermute | solution.py:366
  113.8 2.0 %last.2.refs_2_ = bf16[1024,512]{1,0:T(8,128)(2,1)} custom-call(s32[2]{0:T(128)S(1)} %get-tuple-element.62.owner_ref, f32[2,512,512]{2,1,0:T(8,128)S(1)} %get-tuple-element.53.total_ref, bf16[4096,512]{1,0:T(8,128)(2,1)S(1)} %get-tuple-element.54.column_ref, bf16[512,512]{1,0:T(8,128)(2,1)S(1)} %collective-permute-done.26.refs_0_, ...), custom_call_target="tpu_custom_call" | custom-call | tf_op jit(solution)/shard_map/last/pallas_call | solution.py:331
  115.8 2.0 %last.3 = bf16[1024,512]{1,0:T(8,128)(2,1)} custom-call(s32[2]{0:T(128)S(1)} %get-tuple-element.62.owner_ref, f32[2,512,512]{2,1,0:T(8,128)S(1)} %get-tuple-element.53.total_ref, bf16[4096,512]{1,0:T(8,128)(2,1)S(1)} %get-tuple-element.54.column_ref, bf16[512,512]{1,0:T(8,128)(2,1)S(1)} %collective-permute-done.24.refs_0_, ...), custom_call_target="tpu_custom_call", output_to_operand_aliasing={{}: (5, {})} | custom-call | tf_op jit(solution)/shard_map/last/pallas_call | solution.py:331
  (72 shorter events, 12.4 us)
Async XLA Ops:
  2.5 24.5 %collective-permute-start.6 = (bf16[1552,128]{1,0:T(8,128)(2,1)S(1)}, bf16[1552,128]{1,0:T(8,128)(2,1)S(1)}, u32[]{:S(2)}, u32[]{:S(2)}) collective-permute-start(bf16[1552,128]{1,0:T(8,128)(2,1)S(1)} %fusion.1.refs_0_), channel_id=1, source_target_pairs={{0,1},{1,0},{2,3},{3,2},{4,5},{5,4},{6,7},{7,6},{8,9},{9,8},{10,11... | collective-permute-start | bytes 1191944 | tf_op jit(solution)/shard_map/slots_twin/ppermute | solution.py:371
  3.0 24.0 %collective-permute-start.2 = (bf16[1552,128]{1,0:T(8,128)(2,1)S(1)}, bf16[1552,128]{1,0:T(8,128)(2,1)S(1)}, u32[]{:S(2)}, u32[]{:S(2)}) collective-permute-start(bf16[1552,128]{1,0:T(8,128)(2,1)S(1)} %fusion.1.refs_0_), channel_id=1, source_target_pairs={{0,2},{1,3},{2,0},{3,1},{4,6},{5,7},{6,4},{7,5},{8,10},{9,11},{10,... | collective-permute-start | bytes 1191944 | tf_op jit(solution)/shard_map/slots_near/ppermute | solution.py:366
  5.6 20.7 %collective-permute-start = (bf16[1552,128]{1,0:T(8,128)(2,1)S(1)}, bf16[1552,128]{1,0:T(8,128)(2,1)}, u32[]{:S(2)}, u32[]{:S(2)}) collective-permute-start(bf16[1552,128]{1,0:T(8,128)(2,1)S(1)} %fusion.1.refs_0_), channel_id=1, source_target_pairs={{0,6},{1,7},{2,4},{3,5},{4,2},{5,3},{6,0},{7,1},{8,14},{9,15},{10,... | collective-permute-start | bytes 1191944 | tf_op jit(solution)/shard_map/slots_far/ppermute | solution.py:366
  11.0 30.8 %collective-permute-start.7 = (bf16[2,512,512]{2,1,0:T(8,128)(2,1)}, bf16[2,512,512]{2,1,0:T(8,128)(2,1)S(1)}, u32[]{:S(2)}, u32[]{:S(2)}) collective-permute-start(bf16[2,512,512]{2,1,0:T(8,128)(2,1)} %get-tuple-element.43.own_ref.refs_3_.refs_2_), channel_id=1, source_target_pairs={{0,8},{8,0},{16,24},{24,16},{1,9},{9,1},{17,25},{25,17},{2,10},{10... | collective-permute-start | bytes 3145736 | tf_op jit(solution)/shard_map/g0_x/ppermute | solution.py:363
  12.6 27.7 %collective-permute-start.8 = (bf16[2,512,512]{2,1,0:T(8,128)(2,1)}, bf16[2,512,512]{2,1,0:T(8,128)(2,1)S(1)}, u32[]{:S(2)}, u32[]{:S(2)}) collective-permute-start(bf16[2,512,512]{2,1,0:T(8,128)(2,1)} %get-tuple-element.43.own_ref.refs_3_.refs_2_), channel_id=1, source_target_pairs={{0,16},{8,24},{16,0},{24,8},{1,17},{9,25},{17,1},{25,9},{2,18},{10... | collective-permute-start | bytes 3145736 | tf_op jit(solution)/shard_map/g0_y/ppermute | solution.py:363
  26.4 10.9 %collective-permute-start.1 = (bf16[1552,128]{1,0:T(8,128)(2,1)}, bf16[1552,128]{1,0:T(8,128)(2,1)S(1)}, u32[]{:S(2)}, u32[]{:S(2)}) collective-permute-start(bf16[1552,128]{1,0:T(8,128)(2,1)} %collective-permute-done.refs_4_), channel_id=1, source_target_pairs={{0,2},{1,3},{2,0},{3,1},{4,6},{5,7},{6,4},{7,5},{8,10},{9,11},{10,... | collective-permute-start | bytes 1191944 | tf_op jit(solution)/shard_map/slots_cross/ppermute | solution.py:366
  28.9 14.6 %collective-permute-start.4 = (bf16[1552,128]{1,0:T(8,128)(2,1)S(1)}, bf16[1552,128]{1,0:T(8,128)(2,1)S(1)}, u32[]{:S(2)}, u32[]{:S(2)}) collective-permute-start(bf16[1552,128]{1,0:T(8,128)(2,1)S(1)} %collective-permute-done.2.refs_2_), channel_id=1, source_target_pairs={{0,1},{1,0},{2,3},{3,2},{4,5},{5,4},{6,7},{7,6},{8,9},{9,8},{10,11... | collective-permute-start | bytes 1191944 | tf_op jit(solution)/shard_map/slots_near_twin/ppermute | solution.py:371
  37.3 19.6 %collective-permute-start.13 = (bf16[512,512]{1,0:T(8,128)(2,1)}, bf16[512,512]{1,0:T(8,128)(2,1)S(1)}, u32[]{:S(2)}, u32[]{:S(2)}) collective-permute-start(bf16[512,512]{1,0:T(8,128)(2,1)} %get-tuple-element.47), channel_id=1, source_target_pairs={{0,2},{1,3},{2,0},{3,1},{4,6},{5,7},{6,4},{7,5},{8,10},{9,11},{10,... | collective-permute-start | bytes 1572872 | tf_op jit(solution)/shard_map/g0_near_upper/ppermute | solution.py:366
  37.6 24.4 %collective-permute-start.19 = (bf16[512,512]{1,0:T(8,128)(2,1)}, bf16[512,512]{1,0:T(8,128)(2,1)S(1)}, u32[]{:S(2)}, u32[]{:S(2)}) collective-permute-start(bf16[512,512]{1,0:T(8,128)(2,1)} %get-tuple-element.47), channel_id=1, source_target_pairs={{0,6},{1,7},{2,4},{3,5},{4,2},{5,3},{6,0},{7,1},{8,14},{9,15},{10,... | collective-permute-start | bytes 1572872 | tf_op jit(solution)/shard_map/g0_far_upper/ppermute | solution.py:366
  40.3 14.3 %collective-permute-start.9 = (bf16[512,512]{1,0:T(8,128)(2,1)S(1)}, bf16[512,512]{1,0:T(8,128)(2,1)S(1)}, u32[]{:S(2)}, u32[]{:S(2)}) collective-permute-start(bf16[512,512]{1,0:T(8,128)(2,1)S(1)} %slice_bitcast_fusion.2), channel_id=1, source_target_pairs={{0,8},{8,0},{16,24},{24,16},{1,9},{9,1},{17,25},{25,17},{2,10},{10... | collective-permute-start | bytes 1572872 | tf_op jit(solution)/shard_map/g0_xy_lower/ppermute | solution.py:363
  41.9 12.7 %collective-permute-start.10 = (bf16[512,512]{1,0:T(8,128)(2,1)S(1)}, bf16[512,512]{1,0:T(8,128)(2,1)S(1)}, u32[]{:S(2)}, u32[]{:S(2)}) collective-permute-start(bf16[512,512]{1,0:T(8,128)(2,1)S(1)} %slice_bitcast_fusion.1), channel_id=1, source_target_pairs={{0,16},{8,24},{16,0},{24,8},{1,17},{9,25},{17,1},{25,9},{2,18},{10... | collective-permute-start | bytes 1572872 | tf_op jit(solution)/shard_map/g0_xy_upper/ppermute | solution.py:363
  56.9 6.6 %collective-permute-start.16 = (bf16[512,512]{1,0:T(8,128)(2,1)S(1)}, bf16[512,512]{1,0:T(8,128)(2,1)S(1)}, u32[]{:S(2)}, u32[]{:S(2)}) collective-permute-start(bf16[512,512]{1,0:T(8,128)(2,1)S(1)} %collective-permute-done.13.refs_5_.refs_4_), channel_id=1, source_target_pairs={{0,1},{1,0},{2,3},{3,2},{4,5},{5,4},{6,7},{7,6},{8,9},{9,8},{10,11... | collective-permute-start | bytes 1572872 | tf_op jit(solution)/shard_map/g0_near_upper_twin/ppermute | solution.py:371
  57.4 28.5 %collective-permute-start.14 = (bf16[2,512,512]{2,1,0:T(8,128)(2,1)S(1)}, bf16[2,512,512]{2,1,0:T(8,128)(2,1)S(1)}, u32[]{:S(2)}, u32[]{:S(2)}) collective-permute-start(bf16[2,512,512]{2,1,0:T(8,128)(2,1)S(1)} %turn_rest.1.refs_0_), channel_id=1, source_target_pairs={{0,16},{8,24},{16,0},{24,8},{1,17},{9,25},{17,1},{25,9},{2,18},{10... | collective-permute-start | bytes 3145736 | tf_op jit(solution)/shard_map/turned_y/ppermute | solution.py:363
  57.7 28.3 %collective-permute-start.11 = (bf16[2,512,512]{2,1,0:T(8,128)(2,1)S(1)}, bf16[2,512,512]{2,1,0:T(8,128)(2,1)S(1)}, u32[]{:S(2)}, u32[]{:S(2)}) collective-permute-start(bf16[2,512,512]{2,1,0:T(8,128)(2,1)S(1)} %turn_rest.1.refs_0_), channel_id=1, source_target_pairs={{0,8},{8,0},{16,24},{24,16},{1,9},{9,1},{17,25},{25,17},{2,10},{10... | collective-permute-start | bytes 3145736 | tf_op jit(solution)/shard_map/turned_x/ppermute | solution.py:363
  62.0 16.7 %collective-permute-start.20 = (bf16[512,512]{1,0:T(8,128)(2,1)S(1)}, bf16[512,512]{1,0:T(8,128)(2,1)S(1)}, u32[]{:S(2)}, u32[]{:S(2)}) collective-permute-start(bf16[512,512]{1,0:T(8,128)(2,1)S(1)} %copy-done.1), channel_id=1, source_target_pairs={{0,6},{1,7},{2,4},{3,5},{4,2},{5,3},{6,0},{7,1},{8,14},{9,15},{10,... | collective-permute-start | bytes 1572872 | tf_op jit(solution)/shard_map/g0_far_lower/ppermute | solution.py:366
  63.4 22.5 %collective-permute-start.17 = (bf16[512,512]{1,0:T(8,128)(2,1)S(1)}, bf16[512,512]{1,0:T(8,128)(2,1)S(1)}, u32[]{:S(2)}, u32[]{:S(2)}) collective-permute-start(bf16[512,512]{1,0:T(8,128)(2,1)S(1)} %copy-done.1), channel_id=1, source_target_pairs={{0,2},{1,3},{2,0},{3,1},{4,6},{5,7},{6,4},{7,5},{8,10},{9,11},{10,... | collective-permute-start | bytes 1572872 | tf_op jit(solution)/shard_map/g0_near_lower/ppermute | solution.py:366
  63.6 24.4 %collective-permute-start.15 = (bf16[2,512,512]{2,1,0:T(8,128)(2,1)S(1)}, bf16[2,512,512]{2,1,0:T(8,128)(2,1)S(1)}, u32[]{:S(2)}, u32[]{:S(2)}) collective-permute-start(bf16[2,512,512]{2,1,0:T(8,128)(2,1)S(1)} %copy-done), channel_id=1, source_target_pairs={{0,1},{1,0},{2,3},{3,2},{4,5},{5,4},{6,7},{7,6},{8,9},{9,8},{10,11... | collective-permute-start | bytes 3145736 | tf_op jit(solution)/shard_map/g0_twin/ppermute | solution.py:371
  86.0 14.3 %collective-permute-start.26 = (bf16[512,512]{1,0:T(8,128)(2,1)S(1)}, bf16[512,512]{1,0:T(8,128)(2,1)S(1)}, u32[]{:S(2)}, u32[]{:S(2)}) collective-permute-start(bf16[512,512]{1,0:T(8,128)(2,1)S(1)} %collective-permute-done.19.refs_9_.refs_8_), channel_id=1, source_target_pairs={{0,2},{1,3},{2,0},{3,1},{4,6},{5,7},{6,4},{7,5},{8,10},{9,11},{10,... | collective-permute-start | bytes 1572872 | tf_op jit(solution)/shard_map/g0_cross_upper/ppermute | solution.py:366
  86.4 14.3 %collective-permute-start.12 = (bf16[512,512]{1,0:T(8,128)(2,1)S(1)}, bf16[512,512]{1,0:T(8,128)(2,1)S(1)}, u32[]{:S(2)}, u32[]{:S(2)}) collective-permute-start(bf16[512,512]{1,0:T(8,128)(2,1)S(1)} %slice_bitcast_fusion.3), channel_id=1, source_target_pairs={{0,16},{8,24},{16,0},{24,8},{1,17},{9,25},{17,1},{25,9},{2,18},{10... | collective-permute-start | bytes 1572872 | tf_op jit(solution)/shard_map/turned_xy_upper/ppermute | solution.py:363
  88.0 12.7 %collective-permute-start.18 = (bf16[512,512]{1,0:T(8,128)(2,1)S(1)}, bf16[512,512]{1,0:T(8,128)(2,1)S(1)}, u32[]{:S(2)}, u32[]{:S(2)}) collective-permute-start(bf16[512,512]{1,0:T(8,128)(2,1)S(1)} %collective-permute-done.17.refs_6_.refs_5_), channel_id=1, source_target_pairs={{0,1},{1,0},{2,3},{3,2},{4,5},{5,4},{6,7},{7,6},{8,9},{9,8},{10,11... | collective-permute-start | bytes 1572872 | tf_op jit(solution)/shard_map/g0_near_lower_twin/ppermute | solution.py:371
  88.1 12.7 %collective-permute-start.21 = (bf16[512,512]{1,0:T(8,128)(2,1)S(1)}, bf16[512,512]{1,0:T(8,128)(2,1)S(1)}, u32[]{:S(2)}, u32[]{:S(2)}) collective-permute-start(bf16[512,512]{1,0:T(8,128)(2,1)S(1)} %collective-permute-done.19.refs_9_.refs_8_), channel_id=1, source_target_pairs={{0,1},{1,0},{2,3},{3,2},{4,5},{5,4},{6,7},{7,6},{8,9},{9,8},{10,11... | collective-permute-start | bytes 1572872 | tf_op jit(solution)/shard_map/g0_far_upper_twin/ppermute | solution.py:371
  88.6 16.7 %collective-permute-start.23 = (bf16[512,512]{1,0:T(8,128)(2,1)S(1)}, bf16[512,512]{1,0:T(8,128)(2,1)S(1)}, u32[]{:S(2)}, u32[]{:S(2)}) collective-permute-start(bf16[512,512]{1,0:T(8,128)(2,1)S(1)} %slice_bitcast_fusion), channel_id=1, source_target_pairs={{0,8},{8,0},{16,24},{24,16},{1,9},{9,1},{17,25},{25,17},{2,10},{10... | collective-permute-start | bytes 1572872 | tf_op jit(solution)/shard_map/turned_xy_lower/ppermute | solution.py:363
  100.3 13.5 %collective-permute-start.24 = (bf16[512,512]{1,0:T(8,128)(2,1)S(1)}, bf16[512,512]{1,0:T(8,128)(2,1)S(1)}, u32[]{:S(2)}, u32[]{:S(2)}) collective-permute-start(bf16[512,512]{1,0:T(8,128)(2,1)S(1)} %collective-permute-done.20.refs_10_.refs_9_), channel_id=1, source_target_pairs={{0,2},{1,3},{2,0},{3,1},{4,6},{5,7},{6,4},{7,5},{8,10},{9,11},{10,... | collective-permute-start | bytes 1572872 | tf_op jit(solution)/shard_map/g0_cross_lower/ppermute | solution.py:366
  100.7 13.0 %collective-permute-start.27 = (bf16[512,512]{1,0:T(8,128)(2,1)S(1)}, bf16[512,512]{1,0:T(8,128)(2,1)S(1)}, u32[]{:S(2)}, u32[]{:S(2)}) collective-permute-start(bf16[512,512]{1,0:T(8,128)(2,1)S(1)} %collective-permute-done.26.refs_0_), channel_id=1, source_target_pairs={{0,1},{1,0},{2,3},{3,2},{4,5},{5,4},{6,7},{7,6},{8,9},{9,8},{10,11... | collective-permute-start | bytes 1572872 | tf_op jit(solution)/shard_map/g0_cross_upper_twin/ppermute | solution.py:371
  (6 other events, 19.7 us)

commit v9 on v8

--- a/solution.py
+++ b/solution.py
@@ -448,78 +448,74 @@
             result = last(side, owners[-2:], total, column, [part[side] for part in row_parts[-2:]], result)
         return result
 
-    slot_owners = grid.col_owners(z, z ^ 1, 3 - z, 3 - (z ^ 1))
+    slot_owners = grid.col_owners(z, z ^ 1, 3 - z, z ^ 2)
     small = message[slots * width:]
     with jax.named_scope("slots_far"):
         s_far = grid.along_z(message, MIRROR)
     with jax.named_scope("slots_near"):
         s_near = grid.along_z(message, NEAR)
-    with jax.named_scope("slots_twin"):
-        s_tw = grid.twin(message)
     with jax.named_scope("g0_x"):
         g_x = grid.shift(tile, "x")
     with jax.named_scope("g0_y"):
         g_y = grid.shift(tile, "y")
+    with jax.named_scope("slots_twin"):
+        s_tw = grid.twin(message)
+    with jax.named_scope("slots_cross"):
+        s_cross = grid.along_z(after(s_far, s_near), NEAR)
+    with jax.named_scope("g0_far_upper"):
+        far_u = grid.along_z(after(upper, s_far, s_tw), MIRROR)
+    with jax.named_scope("slots_near_twin"):
+        s_near_tw = grid.twin(s_near)
     with jax.named_scope("slots_far_twin"):
-        s_far_tw = grid.twin(s_far)
-    with jax.named_scope("slots_cross"):
-        s_cross = grid.along_z(after(s_far, s_far), NEAR)
-    with jax.named_scope("slots_near_twin"):
-        s_near_tw = grid.twin(after(s_near, s_far_tw))
+        s_far_tw = grid.twin(after(s_far, s_near_tw, g_x))
     with jax.named_scope("g0_xy_upper"):
-        g_xyu = grid.shift(g_x[0], "y")
+        g_xyu = grid.shift(after(g_x, g_x, s_near_tw)[0], "y")
     with jax.named_scope("g0_xy_lower"):
         g_xyl = grid.shift(g_y[1], "x")
     dense1 = dense_rows(slot_owners[:-2], [message, s_tw, s_near, s_near_tw, s_far, s_far_tw])
-    with jax.named_scope("g0_far_upper"):
-        far_u = grid.along_z(after(upper, s_cross, s_near, s_far), MIRROR)
-    with jax.named_scope("g0_near_upper"):
-        near_u = grid.along_z(after(upper, s_cross), NEAR)
+    with jax.named_scope("g0_near"):
+        near = grid.along_z(after(tile, s_cross, s_far), NEAR)
     with jax.named_scope("slots_cross_twin"):
-        s_cross_tw = grid.twin(after(s_cross, s_near_tw, s_far_tw))
+        s_cross_tw = grid.twin(s_cross)
     with jax.named_scope("small_2"):
-        d2 = grid.twin(small)
+        d2 = grid.twin(after(small, s_far_tw))
     dense2 = dense_fill(slot_owners[-2:], [s_cross, s_cross_tw], dense1)
-    turn_a = turn(0, sources, dense2, tile, [g_x, g_y], jnp.float32)
-    turned = turn(6, sources, dense2, after(turn_a, dense2, g_xyl), [g_xyu, g_xyl], jnp.bfloat16)
+    turn_a = turn(0, sources, dense2, after(tile, s_near_tw), [g_x, g_y], jnp.float32)
+    turned = turn(6, sources, dense2, after(turn_a, d2, far_u), [g_xyu, g_xyl], jnp.bfloat16)
+    with jax.named_scope("g0_far_lower"):
+        far_l = grid.along_z(after(lower, g_xyl, s_cross_tw), MIRROR)
     with jax.named_scope("turned_x"):
         t_x = grid.shift(turned, "x")
     with jax.named_scope("turned_y"):
-        t_y = grid.shift(after(turned, near_u, dense2), "y")
+        t_y = grid.shift(after(turned, g_xyu), "y")
+    with jax.named_scope("small_5"):
+        d5 = grid.twin(small)
     with jax.named_scope("g0_twin"):
-        tile_tw = grid.twin(after(tile, dense1))
-    with jax.named_scope("g0_near_upper_twin"):
-        near_u_tw = grid.twin(after(near_u, turned))
+        tile_tw = grid.twin(tile)
     with jax.named_scope("g0_far_upper_twin"):
-        far_u_tw = grid.twin(after(far_u, turned, d2))
-    with jax.named_scope("g0_far_lower"):
-        far_l = grid.along_z(after(lower, far_u), MIRROR)
-    with jax.named_scope("g0_near_lower"):
-        near_l = grid.along_z(after(lower, near_u_tw), NEAR)
-    with jax.named_scope("small_4"):
-        d4 = grid.twin(after(small, t_x))
+        far_u_tw = grid.twin(after(far_u, tile_tw))
+    with jax.named_scope("g0_near_twin"):
+        near_tw = grid.twin(after(near, far_u_tw))
+    with jax.named_scope("g0_cross_upper"):
+        cross_u = grid.along_z(after(far_u, near), NEAR)
+    with jax.named_scope("g0_cross_lower"):
+        cross_l = grid.along_z(far_l, NEAR)
     with jax.named_scope("turned_xy_upper"):
-        t_xyu = grid.shift(after(t_x, t_x)[0], "y")
+        t_xyu = grid.shift(t_x[0], "y")
     with jax.named_scope("turned_xy_lower"):
-        t_xyl = grid.shift(t_y[1], "x")
-    with jax.named_scope("g0_near_lower_twin"):
-        near_l_tw = grid.twin(near_l)
+        t_xyl = grid.shift(after(t_y, t_y)[1], "x")
     with jax.named_scope("g0_far_lower_twin"):
-        far_l_tw = grid.twin(after(far_l, near_l))
-    row_parts = [tile, tile_tw, near_u, near_l, near_u_tw, near_l_tw, far_u, far_l, far_u_tw, far_l_tw]
+        far_l_tw = grid.twin(far_l)
+    row_parts = [tile, tile_tw, near, near_tw, far_u, far_l, far_u_tw, far_l_tw]
     late = (jnp.stack([z, z ^ 1, 3 - z]) == sources[3]).astype(jnp.int32)
-    total_a, column_a = close(sources, slot_owners[:-2], late, [after(turned, t_xyu), t_x, t_y], row_parts, depth)
-    with jax.named_scope("g0_cross_upper"):
-        cross_u = grid.along_z(after(far_u, far_l, t_x, t_y), NEAR)
-    with jax.named_scope("g0_cross_lower"):
-        cross_l = grid.along_z(after(far_l, far_l_tw, d4, tile_tw), NEAR)
+    total_a, column_a = close(sources, slot_owners[:-2], late, [after(turned, tile_tw, d5), t_x, t_y], row_parts, depth)
     total, column = close_rest(6, sources, slot_owners[:-2], late, total_a, column_a, [t_xyu, t_xyl], row_parts)
     with jax.named_scope("g0_cross_upper_twin"):
-        cross_u_tw = grid.twin(after(cross_u, near_l_tw))
+        cross_u_tw = grid.twin(after(cross_u, column_a, t_xyl))
     last0 = last(0, slot_owners[-2:], total, column, [cross_u, cross_u_tw])
     with jax.named_scope("g0_cross_lower_twin"):
-        cross_l_tw = grid.twin(after(cross_l, column))
-    return last(1, slot_owners[-2:], total, column, [cross_l, cross_l_tw], last0)
+        cross_l_tw = grid.twin(after(cross_l, far_l_tw))
+    return last(1, slot_owners[-2:], after(total, cross_u_tw), column, [cross_l, cross_l_tw], last0)
 
 
 def solution(mesh):

time: 118 us -> 117 us (level)
  waiting for transfers between devices: 63.9 us -> 44.1 us
  starting transfers between devices: 23.5 us -> 43.1 us
    ppermute x9 -> x8, waiting for transfers between devices: 61.9 us -> 36.5 us  [along_z(): lax.ppermute(value, 'col', [(z * self.nc + c, to * self.nc + c) for z, to...]
    ppermute x9 -> x8, starting transfers between devices: 11.1 us -> 31.5 us  [along_z(): lax.ppermute(value, 'col', [(z * self.nc + c, to * self.nc + c) for z, to...]
    ppermute x8, waiting for transfers between devices: 0.02 us -> 4.84 us  [shift(): return lax.ppermute(value, 'row', pairs)]
    ppermute x11 -> x10, waiting for transfers between devices: 1.93 us -> 2.8 us  [twin(): lax.ppermute(value, 'col', [(z * self.nc + c, z * self.nc + 1 - c) for z...]
  transfers between devices with their start and end apart: 28 -> 26, of which waited for: 8 -> 11; matrix products, arithmetic and copies ran while one was open for 1% -> 1% of each run, Pallas kernels for 21% -> 20%
where the time goes in v9:
time: 117 us
  waiting for transfers between devices  44.1 us (38%)
  starting transfers between devices  43.1 us (37%)
  Pallas kernels  25.8 us (22%)
  other arithmetic  2.2 us (2%)
    ppermute x8, waiting for transfers between devices, along_z(): lax.ppermute(value, 'col', [(z * self.nc + c, to * self.nc + c) for z, to...  36.5 us
    ppermute x8, starting transfers between devices, along_z(): lax.ppermute(value, 'col', [(z * self.nc + c, to * self.nc + c) for z, to...  31.5 us
    ppermute x8, starting transfers between devices, shift(): return lax.ppermute(value, 'row', pairs)  10.5 us
    pallas_call x2, Pallas kernels, turn(): pl.pallas_call(functools.partial(turn_kernel, first), out_shape=jax.Shape...  6.87 us
    ppermute x8, waiting for transfers between devices, shift(): return lax.ppermute(value, 'row', pairs)  4.84 us
    pallas_call x1, Pallas kernels, close(): pl.pallas_call(functools.partial(close_kernel, n_col), out_shape=(jax.Sha...  4.58 us
    pallas_call x2, Pallas kernels, last(): pl.pallas_call(functools.partial(last_kernel, side, n_row), out_shape=jax...  3.96 us
    pallas_call x1, Pallas kernels, spread(): pl.pallas_call(functools.partial(spread_kernel, len(parts), slots, width)...  3.65 us
  transfers between devices with their start and end apart: 26, of which 11 were waited for; matrix products, arithmetic and copies ran while one was open for 1% of the time, Pallas kernels for 20%

profile of v9, /device:TPU:0, one launch (start us, length us, event | category | flops | bytes accessed | tf_op | source)
XLA Modules:
  0.0 117.1 jit_solution(11807658461878815421)
XLA Ops:
  3.0 2.6 %collective-permute-start.1 = (bf16[1552,128]{1,0:T(8,128)(2,1)S(1)}, bf16[1552,128]{1,0:T(8,128)(2,1)S(1)}, u32[]{:S(2)}, u32[]{:S(2)}) collective-permute-start(bf16[1552,128]{1,0:T(8,128)(2,1)S(1)} %fusion.1.refs_0_), channel_id=1, source_target_pairs={{0,2},{1,3},{2,0},{3,1},{4,6},{5,7},{6,4},{7,5},{8,10},{9,11},{10,... | collective-permute-start | bytes 1191944 | tf_op jit(solution)/shard_map/slots_near/ppermute | solution.py:366
  5.6 2.5 %collective-permute-start = (bf16[1552,128]{1,0:T(8,128)(2,1)S(1)}, bf16[1552,128]{1,0:T(8,128)(2,1)}, u32[]{:S(2)}, u32[]{:S(2)}) collective-permute-start(bf16[1552,128]{1,0:T(8,128)(2,1)S(1)} %fusion.1.refs_0_), channel_id=1, source_target_pairs={{0,6},{1,7},{2,4},{3,5},{4,2},{5,3},{6,0},{7,1},{8,14},{9,15},{10,... | collective-permute-start | bytes 1191944 | tf_op jit(solution)/shard_map/slots_far/ppermute | solution.py:366
  8.1 2.9 %mask.1 = (bf16[2,512,512]{2,1,0:T(8,128)(2,1)}, bf16[512,512]{1,0:T(8,128)(2,1)}, bf16[512,512]{1,0:T(8,128)(2,1)}) custom-call(s32[4,8]{1,0:T(4,128)} %bitcast.73, bf16[1024,512]{1,0:T(8,128)(2,1)} %values_ref), custom_call_target="tpu_custom_call" | custom-call | tf_op jit(solution)/shard_map/mask/pallas_call | solution.py:76
  11.0 1.6 %collective-permute-start.6 = (bf16[2,512,512]{2,1,0:T(8,128)(2,1)}, bf16[2,512,512]{2,1,0:T(8,128)(2,1)S(1)}, u32[]{:S(2)}, u32[]{:S(2)}) collective-permute-start(bf16[2,512,512]{2,1,0:T(8,128)(2,1)} %get-tuple-element.34.own_ref.refs_3_.refs_2_), channel_id=1, source_target_pairs={{0,8},{8,0},{16,24},{24,16},{1,9},{9,1},{17,25},{25,17},{2,10},{10... | collective-permute-start | bytes 3145736 | tf_op jit(solution)/shard_map/g0_x/ppermute | solution.py:363
  12.5 1.5 %collective-permute-start.8 = (bf16[2,512,512]{2,1,0:T(8,128)(2,1)}, bf16[2,512,512]{2,1,0:T(8,128)(2,1)S(1)}, u32[]{:S(2)}, u32[]{:S(2)}) collective-permute-start(bf16[2,512,512]{2,1,0:T(8,128)(2,1)} %get-tuple-element.34.own_ref.refs_3_.refs_2_), channel_id=1, source_target_pairs={{0,16},{8,24},{16,0},{24,8},{1,17},{9,25},{17,1},{25,9},{2,18},{10... | collective-permute-start | bytes 3145736 | tf_op jit(solution)/shard_map/g0_y/ppermute | solution.py:363
  15.4 10.9 %collective-permute-done.refs_4_ = bf16[1552,128]{1,0:T(8,128)(2,1)} collective-permute-done((bf16[1552,128]{1,0:T(8,128)(2,1)S(1)}, bf16[1552,128]{1,0:T(8,128)(2,1)}, u32[]{:S(2)}, u32[]{:S(2)}) %collective-permute-start) | collective-permute-done | bytes 397344 | tf_op jit(solution)/shard_map/slots_far/ppermute | solution.py:366
  27.0 1.7 %collective-permute-done.5.refs_3_ = bf16[1552,128]{1,0:T(8,128)(2,1)S(1)} collective-permute-done((bf16[1552,128]{1,0:T(8,128)(2,1)S(1)}, bf16[1552,128]{1,0:T(8,128)(2,1)S(1)}, u32[]{:S(2)}, u32[]{:S(2)}) %collective-permute-start.5) | collective-permute-done | bytes 397344 | tf_op jit(solution)/shard_map/slots_near_twin/ppermute | solution.py:371
  28.7 2.6 %collective-permute-start.9 = (bf16[512,512]{1,0:T(8,128)(2,1)}, bf16[512,512]{1,0:T(8,128)(2,1)S(1)}, u32[]{:S(2)}, u32[]{:S(2)}) collective-permute-start(bf16[512,512]{1,0:T(8,128)(2,1)} %get-tuple-element.36), channel_id=1, source_target_pairs={{0,6},{1,7},{2,4},{3,5},{4,2},{5,3},{6,0},{7,1},{8,14},{9,15},{10,... | collective-permute-start | bytes 1572872 | tf_op jit(solution)/shard_map/g0_far_upper/ppermute | solution.py:366
  31.3 6.7 %collective-permute-done.2.refs_0_ = bf16[1552,128]{1,0:T(8,128)(2,1)S(1)} collective-permute-done((bf16[1552,128]{1,0:T(8,128)(2,1)}, bf16[1552,128]{1,0:T(8,128)(2,1)S(1)}, u32[]{:S(2)}, u32[]{:S(2)}) %collective-permute-start.2) | collective-permute-done | bytes 397344 | tf_op jit(solution)/shard_map/slots_cross/ppermute | solution.py:366
  41.7 1.5 %collective-permute-start.10 = (bf16[512,512]{1,0:T(8,128)(2,1)S(1)}, bf16[512,512]{1,0:T(8,128)(2,1)S(1)}, u32[]{:S(2)}, u32[]{:S(2)}) collective-permute-start(bf16[512,512]{1,0:T(8,128)(2,1)S(1)} %slice_bitcast_fusion.3), channel_id=1, source_target_pairs={{0,16},{8,24},{16,0},{24,8},{1,17},{9,25},{17,1},{25,9},{2,18},{10... | collective-permute-start | bytes 1572872 | tf_op jit(solution)/shard_map/g0_xy_upper/ppermute | solution.py:363
  43.3 1.5 %collective-permute-start.11 = (bf16[512,512]{1,0:T(8,128)(2,1)S(1)}, bf16[512,512]{1,0:T(8,128)(2,1)S(1)}, u32[]{:S(2)}, u32[]{:S(2)}) collective-permute-start(bf16[512,512]{1,0:T(8,128)(2,1)S(1)} %slice_bitcast_fusion.1), channel_id=1, source_target_pairs={{0,8},{8,0},{16,24},{24,16},{1,9},{9,1},{17,25},{25,17},{2,10},{10... | collective-permute-start | bytes 1572872 | tf_op jit(solution)/shard_map/g0_xy_lower/ppermute | solution.py:363
  44.9 3.7 %spread.1.refs_2_ = bf16[1024,4096]{1,0:T(8,128)(2,1)S(1)} custom-call(s32[6,12]{1,0:T(8,128)S(1)} %bitcast.69, s32[6,12]{1,0:T(8,128)S(1)} %bitcast_add_fusion.col_ref, bf16[1552,128]{1,0:T(8,128)(2,1)S(1)} %fusion.1.refs_0_, bf16[1552,128]{1,0:T(8,128)(2,1)S(1)} %collective-permute-done.4.refs_1_, bf16[1552,128]{1,0:T(8,128)(2,1)S(1)} %collective-permute-done.1.refs_2_, ...), custom_call_target="tpu_custom_call" | custom-call | tf_op jit(solution)/shard_map/spread/pallas_call | solution.py:121
  50.0 4.6 %turn.1.own_ref = f32[2,512,512]{2,1,0:T(8,128)S(1)} custom-call(s32[4]{0:T(128)S(1)} %pad_add_fusion.1.source_ref, bf16[1024,4096]{1,0:T(8,128)(2,1)S(1)} %fill.1.dense_ref, bf16[2,512,512]{2,1,0:T(8,128)(2,1)S(1)} %copy-done, bf16[2,512,512]{2,1,0:T(8,128)(2,1)S(1)} %collective-permute-done.6.refs_0_, bf16[2,512,512]{2,1,0:T(8,128)(2,1)S(1)} %collective-permute-done.8.refs_1_), custom_call_target="tpu_custom_call" | custom-call | tf_op jit(solution)/shard_map/turn/pallas_call | solution.py:189
  57.0 2.3 %turn_rest.1.refs_0_ = bf16[2,512,512]{2,1,0:T(8,128)(2,1)S(1)} custom-call(s32[4]{0:T(128)S(1)} %pad_add_fusion.1.source_ref, bf16[1024,4096]{1,0:T(8,128)(2,1)S(1)} %fill.1.dense_ref, f32[2,512,512]{2,1,0:T(8,128)S(1)} %turn.1.own_ref, bf16[512,512]{1,0:T(8,128)(2,1)S(1)} %collective-permute-done.10.refs_0_, ...), custom_call_target="tpu_custom_call" | custom-call | tf_op jit(solution)/shard_map/turn_rest/pallas_call | solution.py:189
  60.3 1.5 %collective-permute-start.13 = (bf16[2,512,512]{2,1,0:T(8,128)(2,1)S(1)}, bf16[2,512,512]{2,1,0:T(8,128)(2,1)S(1)}, u32[]{:S(2)}, u32[]{:S(2)}) collective-permute-start(bf16[2,512,512]{2,1,0:T(8,128)(2,1)S(1)} %turn_rest.1.refs_0_), channel_id=1, source_target_pairs={{0,8},{8,0},{16,24},{24,16},{1,9},{9,1},{17,25},{25,17},{2,10},{10... | collective-permute-start | bytes 3145736 | tf_op jit(solution)/shard_map/turned_x/ppermute | solution.py:363
  61.8 9.9 %collective-permute-start.18 = (bf16[512,512]{1,0:T(8,128)(2,1)S(1)}, bf16[512,512]{1,0:T(8,128)(2,1)S(1)}, u32[]{:S(2)}, u32[]{:S(2)}) collective-permute-start(bf16[512,512]{1,0:T(8,128)(2,1)S(1)} %copy-done.1), channel_id=1, source_target_pairs={{0,6},{1,7},{2,4},{3,5},{4,2},{5,3},{6,0},{7,1},{8,14},{9,15},{10,... | collective-permute-start | bytes 1572872 | tf_op jit(solution)/shard_map/g0_far_lower/ppermute | solution.py:366
  73.0 11.6 %collective-permute-done.18.refs_8_.refs_7_ = bf16[512,512]{1,0:T(8,128)(2,1)S(1)} collective-permute-done((bf16[512,512]{1,0:T(8,128)(2,1)S(1)}, bf16[512,512]{1,0:T(8,128)(2,1)S(1)}, u32[]{:S(2)}, u32[]{:S(2)}) %collective-permute-start.18) | collective-permute-done | bytes 524320 | tf_op jit(solution)/shard_map/g0_far_lower/ppermute | solution.py:366
  85.9 10.8 %collective-permute-start.24 = (bf16[512,512]{1,0:T(8,128)(2,1)S(1)}, bf16[512,512]{1,0:T(8,128)(2,1)S(1)}, u32[]{:S(2)}, u32[]{:S(2)}) collective-permute-start(bf16[512,512]{1,0:T(8,128)(2,1)S(1)} %collective-permute-done.18.refs_8_.refs_7_), channel_id=1, source_target_pairs={{0,2},{1,3},{2,0},{3,1},{4,6},{5,7},{6,4},{7,5},{8,10},{9,11},{10,... | collective-permute-start | bytes 1572872 | tf_op jit(solution)/shard_map/g0_cross_lower/ppermute | solution.py:366
  98.1 4.6 %close.1 = (f32[2,512,512]{2,1,0:T(8,128)S(1)}, bf16[4096,512]{1,0:T(8,128)(2,1)S(1)}) custom-call(s32[4]{0:T(128)S(1)} %pad_add_fusion.1.source_ref, s32[6]{0:T(128)S(1)} %stack.100.owner_ref, s32[3]{0:T(128)S(1)} %compare_convert_fusion.late_ref, bf16[2,512,512]{2,1,0:T(8,128)(2,1)S(1)} %turn_rest.1.refs_0_, ...), custom_call_target="tpu_custom_call" | custom-call | tf_op jit(solution)/shard_map/close/pallas_call | solution.py:248
  102.8 6.1 %collective-permute-done.24.refs_0_ = bf16[512,512]{1,0:T(8,128)(2,1)S(1)} collective-permute-done((bf16[512,512]{1,0:T(8,128)(2,1)S(1)}, bf16[512,512]{1,0:T(8,128)(2,1)S(1)}, u32[]{:S(2)}, u32[]{:S(2)}) %collective-permute-start.24) | collective-permute-done | bytes 524320 | tf_op jit(solution)/shard_map/g0_cross_lower/ppermute | solution.py:366
  108.9 1.7 %collective-permute-done.20.refs_0_ = bf16[512,512]{1,0:T(8,128)(2,1)S(1)} collective-permute-done((bf16[512,512]{1,0:T(8,128)(2,1)S(1)}, bf16[512,512]{1,0:T(8,128)(2,1)S(1)}, u32[]{:S(2)}, u32[]{:S(2)}) %collective-permute-start.20) | collective-permute-done | bytes 524320 | tf_op jit(solution)/shard_map/turned_xy_upper/ppermute | solution.py:363
  110.6 2.5 %close_rest.1 = (f32[2,512,512]{2,1,0:T(8,128)S(1)}, bf16[4096,512]{1,0:T(8,128)(2,1)S(1)}) custom-call(s32[4]{0:T(128)S(1)} %pad_add_fusion.1.source_ref, s32[6]{0:T(128)S(1)} %stack.100.owner_ref, s32[3]{0:T(128)S(1)} %compare_convert_fusion.late_ref, f32[2,512,512]{2,1,0:T(8,128)S(1)} %get-tuple-element.46._, ...), custom_call_target="tpu_custom_call", output_to_operand_aliasing={{0}: (3, {}), {1}: (4, {})} | custom-call | tf_op jit(solution)/shard_map/close_rest/pallas_call | solution.py:288
  113.1 2.0 %last.2.refs_2_ = bf16[1024,512]{1,0:T(8,128)(2,1)} custom-call(s32[2]{0:T(128)S(1)} %get-tuple-element.58.owner_ref, f32[2,512,512]{2,1,0:T(8,128)S(1)} %get-tuple-element.52.total_ref, bf16[4096,512]{1,0:T(8,128)(2,1)S(1)} %get-tuple-element.53.column_ref, bf16[512,512]{1,0:T(8,128)(2,1)S(1)} %collective-permute-done.22.refs_0_, ...), custom_call_target="tpu_custom_call" | custom-call | tf_op jit(solution)/shard_map/last/pallas_call | solution.py:331
  115.1 2.0 %last.3 = bf16[1024,512]{1,0:T(8,128)(2,1)} custom-call(s32[2]{0:T(128)S(1)} %get-tuple-element.58.owner_ref, f32[2,512,512]{2,1,0:T(8,128)S(1)} %get-tuple-element.52.total_ref, bf16[4096,512]{1,0:T(8,128)(2,1)S(1)} %get-tuple-element.53.column_ref, bf16[512,512]{1,0:T(8,128)(2,1)S(1)} %collective-permute-done.24.refs_0_, ...), custom_call_target="tpu_custom_call", output_to_operand_aliasing={{}: (5, {})} | custom-call | tf_op jit(solution)/shard_map/last/pallas_call | solution.py:331
  (68 shorter events, 17.0 us)
Async XLA Ops:
  2.5 24.5 %collective-permute-start.4 = (bf16[1552,128]{1,0:T(8,128)(2,1)S(1)}, bf16[1552,128]{1,0:T(8,128)(2,1)S(1)}, u32[]{:S(2)}, u32[]{:S(2)}) collective-permute-start(bf16[1552,128]{1,0:T(8,128)(2,1)S(1)} %fusion.1.refs_0_), channel_id=1, source_target_pairs={{0,1},{1,0},{2,3},{3,2},{4,5},{5,4},{6,7},{7,6},{8,9},{9,8},{10,11... | collective-permute-start | bytes 1191944 | tf_op jit(solution)/shard_map/slots_twin/ppermute | solution.py:371
  3.0 12.4 %collective-permute-start.1 = (bf16[1552,128]{1,0:T(8,128)(2,1)S(1)}, bf16[1552,128]{1,0:T(8,128)(2,1)S(1)}, u32[]{:S(2)}, u32[]{:S(2)}) collective-permute-start(bf16[1552,128]{1,0:T(8,128)(2,1)S(1)} %fusion.1.refs_0_), channel_id=1, source_target_pairs={{0,2},{1,3},{2,0},{3,1},{4,6},{5,7},{6,4},{7,5},{8,10},{9,11},{10,... | collective-permute-start | bytes 1191944 | tf_op jit(solution)/shard_map/slots_near/ppermute | solution.py:366
  5.6 20.7 %collective-permute-start = (bf16[1552,128]{1,0:T(8,128)(2,1)S(1)}, bf16[1552,128]{1,0:T(8,128)(2,1)}, u32[]{:S(2)}, u32[]{:S(2)}) collective-permute-start(bf16[1552,128]{1,0:T(8,128)(2,1)S(1)} %fusion.1.refs_0_), channel_id=1, source_target_pairs={{0,6},{1,7},{2,4},{3,5},{4,2},{5,3},{6,0},{7,1},{8,14},{9,15},{10,... | collective-permute-start | bytes 1191944 | tf_op jit(solution)/shard_map/slots_far/ppermute | solution.py:366
  11.0 29.0 %collective-permute-start.6 = (bf16[2,512,512]{2,1,0:T(8,128)(2,1)}, bf16[2,512,512]{2,1,0:T(8,128)(2,1)S(1)}, u32[]{:S(2)}, u32[]{:S(2)}) collective-permute-start(bf16[2,512,512]{2,1,0:T(8,128)(2,1)} %get-tuple-element.34.own_ref.refs_3_.refs_2_), channel_id=1, source_target_pairs={{0,8},{8,0},{16,24},{24,16},{1,9},{9,1},{17,25},{25,17},{2,10},{10... | collective-permute-start | bytes 3145736 | tf_op jit(solution)/shard_map/g0_x/ppermute | solution.py:363
  12.5 27.5 %collective-permute-start.8 = (bf16[2,512,512]{2,1,0:T(8,128)(2,1)}, bf16[2,512,512]{2,1,0:T(8,128)(2,1)S(1)}, u32[]{:S(2)}, u32[]{:S(2)}) collective-permute-start(bf16[2,512,512]{2,1,0:T(8,128)(2,1)} %get-tuple-element.34.own_ref.refs_3_.refs_2_), channel_id=1, source_target_pairs={{0,16},{8,24},{16,0},{24,8},{1,17},{9,25},{17,1},{25,9},{2,18},{10... | collective-permute-start | bytes 3145736 | tf_op jit(solution)/shard_map/g0_y/ppermute | solution.py:363
  15.4 44.9 %collective-permute-start.12 = (bf16[2,512,512]{2,1,0:T(8,128)(2,1)}, bf16[2,512,512]{2,1,0:T(8,128)(2,1)S(1)}, u32[]{:S(2)}, u32[]{:S(2)}) collective-permute-start(bf16[2,512,512]{2,1,0:T(8,128)(2,1)} %get-tuple-element.34.own_ref.refs_3_.refs_2_), channel_id=1, source_target_pairs={{0,1},{1,0},{2,3},{3,2},{4,5},{5,4},{6,7},{7,6},{8,9},{9,8},{10,11... | collective-permute-start | bytes 3145736 | tf_op jit(solution)/shard_map/g0_twin/ppermute | solution.py:371
  26.4 11.7 %collective-permute-start.2 = (bf16[1552,128]{1,0:T(8,128)(2,1)}, bf16[1552,128]{1,0:T(8,128)(2,1)S(1)}, u32[]{:S(2)}, u32[]{:S(2)}) collective-permute-start(bf16[1552,128]{1,0:T(8,128)(2,1)} %collective-permute-done.refs_4_), channel_id=1, source_target_pairs={{0,2},{1,3},{2,0},{3,1},{4,6},{5,7},{6,4},{7,5},{8,10},{9,11},{10,... | collective-permute-start | bytes 1191944 | tf_op jit(solution)/shard_map/slots_cross/ppermute | solution.py:366
  28.7 25.9 %collective-permute-start.9 = (bf16[512,512]{1,0:T(8,128)(2,1)}, bf16[512,512]{1,0:T(8,128)(2,1)S(1)}, u32[]{:S(2)}, u32[]{:S(2)}) collective-permute-start(bf16[512,512]{1,0:T(8,128)(2,1)} %get-tuple-element.36), channel_id=1, source_target_pairs={{0,6},{1,7},{2,4},{3,5},{4,2},{5,3},{6,0},{7,1},{8,14},{9,15},{10,... | collective-permute-start | bytes 1572872 | tf_op jit(solution)/shard_map/g0_far_upper/ppermute | solution.py:366
  38.0 33.7 %collective-permute-start.15 = (bf16[2,512,512]{2,1,0:T(8,128)(2,1)}, bf16[2,512,512]{2,1,0:T(8,128)(2,1)S(1)}, u32[]{:S(2)}, u32[]{:S(2)}) collective-permute-start(bf16[2,512,512]{2,1,0:T(8,128)(2,1)} %get-tuple-element.34.own_ref.refs_3_.refs_2_), channel_id=1, source_target_pairs={{0,2},{1,3},{2,0},{3,1},{4,6},{5,7},{6,4},{7,5},{8,10},{9,11},{10,... | collective-permute-start | bytes 3145736 | tf_op jit(solution)/shard_map/g0_near/ppermute | solution.py:366
  40.0 3.3 %collective-permute-start.7 = (bf16[1552,128]{1,0:T(8,128)(2,1)}, bf16[1552,128]{1,0:T(8,128)(2,1)S(1)}, u32[]{:S(2)}, u32[]{:S(2)}) collective-permute-start(bf16[1552,128]{1,0:T(8,128)(2,1)} %collective-permute-done.refs_4_), channel_id=1, source_target_pairs={{0,1},{1,0},{2,3},{3,2},{4,5},{5,4},{6,7},{7,6},{8,9},{9,8},{10,11... | collective-permute-start | bytes 1191944 | tf_op jit(solution)/shard_map/slots_far_twin/ppermute | solution.py:371
  41.7 14.0 %collective-permute-start.10 = (bf16[512,512]{1,0:T(8,128)(2,1)S(1)}, bf16[512,512]{1,0:T(8,128)(2,1)S(1)}, u32[]{:S(2)}, u32[]{:S(2)}) collective-permute-start(bf16[512,512]{1,0:T(8,128)(2,1)S(1)} %slice_bitcast_fusion.3), channel_id=1, source_target_pairs={{0,16},{8,24},{16,0},{24,8},{1,17},{9,25},{17,1},{25,9},{2,18},{10... | collective-permute-start | bytes 1572872 | tf_op jit(solution)/shard_map/g0_xy_upper/ppermute | solution.py:363
  43.3 13.7 %collective-permute-start.11 = (bf16[512,512]{1,0:T(8,128)(2,1)S(1)}, bf16[512,512]{1,0:T(8,128)(2,1)S(1)}, u32[]{:S(2)}, u32[]{:S(2)}) collective-permute-start(bf16[512,512]{1,0:T(8,128)(2,1)S(1)} %slice_bitcast_fusion.1), channel_id=1, source_target_pairs={{0,8},{8,0},{16,24},{24,16},{1,9},{9,1},{17,25},{25,17},{2,10},{10... | collective-permute-start | bytes 1572872 | tf_op jit(solution)/shard_map/g0_xy_lower/ppermute | solution.py:363
  59.3 25.2 %collective-permute-start.14 = (bf16[2,512,512]{2,1,0:T(8,128)(2,1)S(1)}, bf16[2,512,512]{2,1,0:T(8,128)(2,1)S(1)}, u32[]{:S(2)}, u32[]{:S(2)}) collective-permute-start(bf16[2,512,512]{2,1,0:T(8,128)(2,1)S(1)} %turn_rest.1.refs_0_), channel_id=1, source_target_pairs={{0,16},{8,24},{16,0},{24,8},{1,17},{9,25},{17,1},{25,9},{2,18},{10... | collective-permute-start | bytes 3145736 | tf_op jit(solution)/shard_map/turned_y/ppermute | solution.py:363
  60.3 11.4 %collective-permute-start.16 = (bf16[512,512]{1,0:T(8,128)(2,1)S(1)}, bf16[512,512]{1,0:T(8,128)(2,1)S(1)}, u32[]{:S(2)}, u32[]{:S(2)}) collective-permute-start(bf16[512,512]{1,0:T(8,128)(2,1)S(1)} %collective-permute-done.9.refs_7_.refs_6_), channel_id=1, source_target_pairs={{0,1},{1,0},{2,3},{3,2},{4,5},{5,4},{6,7},{7,6},{8,9},{9,8},{10,11... | collective-permute-start | bytes 1572872 | tf_op jit(solution)/shard_map/g0_far_upper_twin/ppermute | solution.py:371
  60.3 25.6 %collective-permute-start.13 = (bf16[2,512,512]{2,1,0:T(8,128)(2,1)S(1)}, bf16[2,512,512]{2,1,0:T(8,128)(2,1)S(1)}, u32[]{:S(2)}, u32[]{:S(2)}) collective-permute-start(bf16[2,512,512]{2,1,0:T(8,128)(2,1)S(1)} %turn_rest.1.refs_0_), channel_id=1, source_target_pairs={{0,8},{8,0},{16,24},{24,16},{1,9},{9,1},{17,25},{25,17},{2,10},{10... | collective-permute-start | bytes 3145736 | tf_op jit(solution)/shard_map/turned_x/ppermute | solution.py:363
  61.8 22.7 %collective-permute-start.18 = (bf16[512,512]{1,0:T(8,128)(2,1)S(1)}, bf16[512,512]{1,0:T(8,128)(2,1)S(1)}, u32[]{:S(2)}, u32[]{:S(2)}) collective-permute-start(bf16[512,512]{1,0:T(8,128)(2,1)S(1)} %copy-done.1), channel_id=1, source_target_pairs={{0,6},{1,7},{2,4},{3,5},{4,2},{5,3},{6,0},{7,1},{8,14},{9,15},{10,... | collective-permute-start | bytes 1572872 | tf_op jit(solution)/shard_map/g0_far_lower/ppermute | solution.py:366
  71.8 26.3 %collective-permute-start.17 = (bf16[2,512,512]{2,1,0:T(8,128)(2,1)S(1)}, bf16[2,512,512]{2,1,0:T(8,128)(2,1)S(1)}, u32[]{:S(2)}, u32[]{:S(2)}) collective-permute-start(bf16[2,512,512]{2,1,0:T(8,128)(2,1)S(1)} %collective-permute-done.15.refs_5_.refs_4_), channel_id=1, source_target_pairs={{0,1},{1,0},{2,3},{3,2},{4,5},{5,4},{6,7},{7,6},{8,9},{9,8},{10,11... | collective-permute-start | bytes 3145736 | tf_op jit(solution)/shard_map/g0_near_twin/ppermute | solution.py:371
  71.8 30.9 %collective-permute-start.22 = (bf16[512,512]{1,0:T(8,128)(2,1)S(1)}, bf16[512,512]{1,0:T(8,128)(2,1)S(1)}, u32[]{:S(2)}, u32[]{:S(2)}) collective-permute-start(bf16[512,512]{1,0:T(8,128)(2,1)S(1)} %collective-permute-done.9.refs_7_.refs_6_), channel_id=1, source_target_pairs={{0,2},{1,3},{2,0},{3,1},{4,6},{5,7},{6,4},{7,5},{8,10},{9,11},{10,... | collective-permute-start | bytes 1572872 | tf_op jit(solution)/shard_map/g0_cross_upper/ppermute | solution.py:366
  84.5 12.2 %collective-permute-start.19 = (bf16[512,512]{1,0:T(8,128)(2,1)S(1)}, bf16[512,512]{1,0:T(8,128)(2,1)S(1)}, u32[]{:S(2)}, u32[]{:S(2)}) collective-permute-start(bf16[512,512]{1,0:T(8,128)(2,1)S(1)} %collective-permute-done.18.refs_8_.refs_7_), channel_id=1, source_target_pairs={{0,1},{1,0},{2,3},{3,2},{4,5},{5,4},{6,7},{7,6},{8,9},{9,8},{10,11... | collective-permute-start | bytes 1572872 | tf_op jit(solution)/shard_map/g0_far_lower_twin/ppermute | solution.py:371
  84.6 18.1 %collective-permute-start.21 = (bf16[512,512]{1,0:T(8,128)(2,1)S(1)}, bf16[512,512]{1,0:T(8,128)(2,1)S(1)}, u32[]{:S(2)}, u32[]{:S(2)}) collective-permute-start(bf16[512,512]{1,0:T(8,128)(2,1)S(1)} %slice_bitcast_fusion.2), channel_id=1, source_target_pairs={{0,8},{8,0},{16,24},{24,16},{1,9},{9,1},{17,25},{25,17},{2,10},{10... | collective-permute-start | bytes 1572872 | tf_op jit(solution)/shard_map/turned_xy_lower/ppermute | solution.py:363
  85.9 23.0 %collective-permute-start.24 = (bf16[512,512]{1,0:T(8,128)(2,1)S(1)}, bf16[512,512]{1,0:T(8,128)(2,1)S(1)}, u32[]{:S(2)}, u32[]{:S(2)}) collective-permute-start(bf16[512,512]{1,0:T(8,128)(2,1)S(1)} %collective-permute-done.18.refs_8_.refs_7_), channel_id=1, source_target_pairs={{0,2},{1,3},{2,0},{3,1},{4,6},{5,7},{6,4},{7,5},{8,10},{9,11},{10,... | collective-permute-start | bytes 1572872 | tf_op jit(solution)/shard_map/g0_cross_lower/ppermute | solution.py:366
  96.8 13.8 %collective-permute-start.20 = (bf16[512,512]{1,0:T(8,128)(2,1)S(1)}, bf16[512,512]{1,0:T(8,128)(2,1)S(1)}, u32[]{:S(2)}, u32[]{:S(2)}) collective-permute-start(bf16[512,512]{1,0:T(8,128)(2,1)S(1)} %slice_bitcast_fusion), channel_id=1, source_target_pairs={{0,16},{8,24},{16,0},{24,8},{1,17},{9,25},{17,1},{25,9},{2,18},{10... | collective-permute-start | bytes 1572872 | tf_op jit(solution)/shard_map/turned_xy_upper/ppermute | solution.py:363
  102.7 10.4 %collective-permute-start.23 = (bf16[512,512]{1,0:T(8,128)(2,1)S(1)}, bf16[512,512]{1,0:T(8,128)(2,1)S(1)}, u32[]{:S(2)}, u32[]{:S(2)}) collective-permute-start(bf16[512,512]{1,0:T(8,128)(2,1)S(1)} %collective-permute-done.22.refs_0_), channel_id=1, source_target_pairs={{0,1},{1,0},{2,3},{3,2},{4,5},{5,4},{6,7},{7,6},{8,9},{9,8},{10,11... | collective-permute-start | bytes 1572872 | tf_op jit(solution)/shard_map/g0_cross_upper_twin/ppermute | solution.py:371
  108.9 6.2 %collective-permute-start.25 = (bf16[512,512]{1,0:T(8,128)(2,1)S(1)}, bf16[512,512]{1,0:T(8,128)(2,1)S(1)}, u32[]{:S(2)}, u32[]{:S(2)}) collective-permute-start(bf16[512,512]{1,0:T(8,128)(2,1)S(1)} %collective-permute-done.24.refs_0_), channel_id=1, source_target_pairs={{0,1},{1,0},{2,3},{3,2},{4,5},{5,4},{6,7},{7,6},{8,9},{9,8},{10,11... | collective-permute-start | bytes 1572872 | tf_op jit(solution)/shard_map/g0_cross_lower_twin/ppermute | solution.py:371
  (4 other events, 12.1 us)

commit v10 on v9

--- a/solution.py
+++ b/solution.py
@@ -461,31 +461,31 @@
     with jax.named_scope("slots_twin"):
         s_tw = grid.twin(message)
     with jax.named_scope("slots_cross"):
-        s_cross = grid.along_z(after(s_far, s_near), NEAR)
-    with jax.named_scope("g0_far_upper"):
-        far_u = grid.along_z(after(upper, s_far, s_tw), MIRROR)
+        s_cross = grid.along_z(s_far, NEAR)
     with jax.named_scope("slots_near_twin"):
         s_near_tw = grid.twin(s_near)
     with jax.named_scope("slots_far_twin"):
         s_far_tw = grid.twin(after(s_far, s_near_tw, g_x))
+    with jax.named_scope("g0_far_upper"):
+        far_u = grid.along_z(after(upper, s_cross), MIRROR)
     with jax.named_scope("g0_xy_upper"):
-        g_xyu = grid.shift(after(g_x, g_x, s_near_tw)[0], "y")
+        g_xyu = grid.shift(after(g_x, s_near_tw, s_near, s_cross)[0], "y")
     with jax.named_scope("g0_xy_lower"):
         g_xyl = grid.shift(g_y[1], "x")
     dense1 = dense_rows(slot_owners[:-2], [message, s_tw, s_near, s_near_tw, s_far, s_far_tw])
     with jax.named_scope("g0_near"):
-        near = grid.along_z(after(tile, s_cross, s_far), NEAR)
+        near = grid.along_z(after(tile, s_far, s_cross), NEAR)
     with jax.named_scope("slots_cross_twin"):
-        s_cross_tw = grid.twin(s_cross)
-    with jax.named_scope("small_2"):
-        d2 = grid.twin(after(small, s_far_tw))
+        s_cross_tw = grid.twin(after(s_cross, g_y))
     dense2 = dense_fill(slot_owners[-2:], [s_cross, s_cross_tw], dense1)
     turn_a = turn(0, sources, dense2, after(tile, s_near_tw), [g_x, g_y], jnp.float32)
-    turned = turn(6, sources, dense2, after(turn_a, d2, far_u), [g_xyu, g_xyl], jnp.bfloat16)
+    turned = turn(6, sources, dense2, turn_a, [g_xyu, g_xyl], jnp.bfloat16)
     with jax.named_scope("g0_far_lower"):
         far_l = grid.along_z(after(lower, g_xyl, s_cross_tw), MIRROR)
+    with jax.named_scope("small_3"):
+        d3 = grid.twin(small)
     with jax.named_scope("turned_x"):
-        t_x = grid.shift(turned, "x")
+        t_x = grid.shift(after(turned, d3), "x")
     with jax.named_scope("turned_y"):
         t_y = grid.shift(after(turned, g_xyu), "y")
     with jax.named_scope("small_5"):
@@ -497,24 +497,26 @@
     with jax.named_scope("g0_near_twin"):
         near_tw = grid.twin(after(near, far_u_tw))
     with jax.named_scope("g0_cross_upper"):
-        cross_u = grid.along_z(after(far_u, near), NEAR)
+        cross_u = grid.along_z(far_u, NEAR)
     with jax.named_scope("g0_cross_lower"):
         cross_l = grid.along_z(far_l, NEAR)
     with jax.named_scope("turned_xy_upper"):
-        t_xyu = grid.shift(t_x[0], "y")
+        t_xyu = grid.shift(after(t_x, far_l)[0], "y")
     with jax.named_scope("turned_xy_lower"):
-        t_xyl = grid.shift(after(t_y, t_y)[1], "x")
+        t_xyl = grid.shift(t_y[1], "x")
     with jax.named_scope("g0_far_lower_twin"):
         far_l_tw = grid.twin(far_l)
+    with jax.named_scope("small_6"):
+        d6 = grid.twin(after(small, d3))
     row_parts = [tile, tile_tw, near, near_tw, far_u, far_l, far_u_tw, far_l_tw]
     late = (jnp.stack([z, z ^ 1, 3 - z]) == sources[3]).astype(jnp.int32)
-    total_a, column_a = close(sources, slot_owners[:-2], late, [after(turned, tile_tw, d5), t_x, t_y], row_parts, depth)
+    total_a, column_a = close(sources, slot_owners[:-2], late, [after(turned, tile_tw, d5, d6), t_x, t_y], row_parts, depth)
     total, column = close_rest(6, sources, slot_owners[:-2], late, total_a, column_a, [t_xyu, t_xyl], row_parts)
     with jax.named_scope("g0_cross_upper_twin"):
-        cross_u_tw = grid.twin(after(cross_u, column_a, t_xyl))
+        cross_u_tw = grid.twin(after(cross_u, column_a, t_xyl, cross_u))
     last0 = last(0, slot_owners[-2:], total, column, [cross_u, cross_u_tw])
     with jax.named_scope("g0_cross_lower_twin"):
-        cross_l_tw = grid.twin(after(cross_l, far_l_tw))
+        cross_l_tw = grid.twin(cross_l)
     return last(1, slot_owners[-2:], after(total, cross_u_tw), column, [cross_l, cross_l_tw], last0)
 
 

time: 117 us -> 115 us (0.983)
  starting transfers between devices: 43.1 us -> 24 us
  waiting for transfers between devices: 44.1 us -> 60.8 us
    ppermute x8, starting transfers between devices: 31.5 us -> 11 us  [along_z(): lax.ppermute(value, 'col', [(z * self.nc + c, to * self.nc + c) for z, to...]
    ppermute x8, waiting for transfers between devices: 36.5 us -> 51.2 us  [along_z(): lax.ppermute(value, 'col', [(z * self.nc + c, to * self.nc + c) for z, to...]
    ppermute x8, waiting for transfers between devices: 4.84 us -> 7.54 us  [shift(): return lax.ppermute(value, 'row', pairs)]
    ppermute x10 -> x11, waiting for transfers between devices: 2.8 us -> 2.01 us  [twin(): lax.ppermute(value, 'col', [(z * self.nc + c, z * self.nc + 1 - c) for z...]
  transfers between devices with their start and end apart: 26 -> 27, of which waited for: 11 -> 12; matrix products, arithmetic and copies ran while one was open for 1% -> 1% of each run, Pallas kernels for 20% -> 21%
where the time goes in v10:
time: 115 us
  waiting for transfers between devices  60.8 us (53%)
  Pallas kernels  26 us (23%)
  starting transfers between devices  24 us (21%)
  other arithmetic  2.2 us (2%)
    ppermute x8, waiting for transfers between devices, along_z(): lax.ppermute(value, 'col', [(z * self.nc + c, to * self.nc + c) for z, to...  51.2 us
    ppermute x8, starting transfers between devices, shift(): return lax.ppermute(value, 'row', pairs)  11.4 us
    ppermute x8, starting transfers between devices, along_z(): lax.ppermute(value, 'col', [(z * self.nc + c, to * self.nc + c) for z, to...  11 us
    ppermute x8, waiting for transfers between devices, shift(): return lax.ppermute(value, 'row', pairs)  7.54 us
    pallas_call x2, Pallas kernels, turn(): pl.pallas_call(functools.partial(turn_kernel, first), out_shape=jax.Shape...  6.9 us
    pallas_call x1, Pallas kernels, close(): pl.pallas_call(functools.partial(close_kernel, n_col), out_shape=(jax.Sha...  4.58 us
    pallas_call x2, Pallas kernels, last(): pl.pallas_call(functools.partial(last_kernel, side, n_row), out_shape=jax...  3.96 us
    pallas_call x1, Pallas kernels, spread(): pl.pallas_call(functools.partial(spread_kernel, len(parts), slots, width)...  3.76 us
  transfers between devices with their start and end apart: 27, of which 12 were waited for; matrix products, arithmetic and copies ran while one was open for 1% of the time, Pallas kernels for 21%

profile of v10, /device:TPU:0, one launch (start us, length us, event | category | flops | bytes accessed | tf_op | source)
XLA Modules:
  0.0 114.8 jit_solution(14872539027330881271)
XLA Ops:
  3.0 2.6 %collective-permute-start.5 = (bf16[1552,128]{1,0:T(8,128)(2,1)S(1)}, bf16[1552,128]{1,0:T(8,128)(2,1)S(1)}, u32[]{:S(2)}, u32[]{:S(2)}) collective-permute-start(bf16[1552,128]{1,0:T(8,128)(2,1)S(1)} %pad_maximum_fusion.refs_0_), channel_id=1, source_target_pairs={{0,2},{1,3},{2,0},{3,1},{4,6},{5,7},{6,4},{7,5},{8,10},{9,11},{10,... | collective-permute-start | bytes 1191944 | tf_op jit(solution)/shard_map/slots_near/ppermute | solution.py:366
  5.6 2.5 %collective-permute-start = (bf16[1552,128]{1,0:T(8,128)(2,1)S(1)}, bf16[1552,128]{1,0:T(8,128)(2,1)}, u32[]{:S(2)}, u32[]{:S(2)}) collective-permute-start(bf16[1552,128]{1,0:T(8,128)(2,1)S(1)} %pad_maximum_fusion.refs_0_), channel_id=1, source_target_pairs={{0,6},{1,7},{2,4},{3,5},{4,2},{5,3},{6,0},{7,1},{8,14},{9,15},{10,... | collective-permute-start | bytes 1191944 | tf_op jit(solution)/shard_map/slots_far/ppermute | solution.py:366
  8.1 2.9 %mask.1 = (bf16[2,512,512]{2,1,0:T(8,128)(2,1)}, bf16[512,512]{1,0:T(8,128)(2,1)}, bf16[512,512]{1,0:T(8,128)(2,1)}) custom-call(s32[4,8]{1,0:T(4,128)} %bitcast.73, bf16[1024,512]{1,0:T(8,128)(2,1)} %values_ref), custom_call_target="tpu_custom_call" | custom-call | tf_op jit(solution)/shard_map/mask/pallas_call | solution.py:76
  11.0 1.6 %collective-permute-start.7 = (bf16[2,512,512]{2,1,0:T(8,128)(2,1)}, bf16[2,512,512]{2,1,0:T(8,128)(2,1)S(1)}, u32[]{:S(2)}, u32[]{:S(2)}) collective-permute-start(bf16[2,512,512]{2,1,0:T(8,128)(2,1)} %get-tuple-element.37.own_ref.refs_3_.refs_2_), channel_id=1, source_target_pairs={{0,8},{8,0},{16,24},{24,16},{1,9},{9,1},{17,25},{25,17},{2,10},{10... | collective-permute-start | bytes 3145736 | tf_op jit(solution)/shard_map/g0_x/ppermute | solution.py:363
  12.6 1.5 %collective-permute-start.2 = (bf16[2,512,512]{2,1,0:T(8,128)(2,1)}, bf16[2,512,512]{2,1,0:T(8,128)(2,1)S(1)}, u32[]{:S(2)}, u32[]{:S(2)}) collective-permute-start(bf16[2,512,512]{2,1,0:T(8,128)(2,1)} %get-tuple-element.37.own_ref.refs_3_.refs_2_), channel_id=1, source_target_pairs={{0,16},{8,24},{16,0},{24,8},{1,17},{9,25},{17,1},{25,9},{2,18},{10... | collective-permute-start | bytes 3145736 | tf_op jit(solution)/shard_map/g0_y/ppermute | solution.py:363
  15.4 10.9 %collective-permute-done.refs_4_ = bf16[1552,128]{1,0:T(8,128)(2,1)} collective-permute-done((bf16[1552,128]{1,0:T(8,128)(2,1)S(1)}, bf16[1552,128]{1,0:T(8,128)(2,1)}, u32[]{:S(2)}, u32[]{:S(2)}) %collective-permute-start) | collective-permute-done | bytes 397344 | tf_op jit(solution)/shard_map/slots_far/ppermute | solution.py:366
  27.0 10.3 %collective-permute-done.1.refs_0_ = bf16[1552,128]{1,0:T(8,128)(2,1)S(1)} collective-permute-done((bf16[1552,128]{1,0:T(8,128)(2,1)}, bf16[1552,128]{1,0:T(8,128)(2,1)S(1)}, u32[]{:S(2)}, u32[]{:S(2)}) %collective-permute-start.1) | collective-permute-done | bytes 397344 | tf_op jit(solution)/shard_map/slots_cross/ppermute | solution.py:366
  37.3 2.3 %collective-permute-start.16 = (bf16[512,512]{1,0:T(8,128)(2,1)}, bf16[512,512]{1,0:T(8,128)(2,1)S(1)}, u32[]{:S(2)}, u32[]{:S(2)}) collective-permute-start(bf16[512,512]{1,0:T(8,128)(2,1)} %get-tuple-element.39), channel_id=1, source_target_pairs={{0,6},{1,7},{2,4},{3,5},{4,2},{5,3},{6,0},{7,1},{8,14},{9,15},{10,... | collective-permute-start | bytes 1572872 | tf_op jit(solution)/shard_map/g0_far_upper/ppermute | solution.py:366
  42.2 1.5 %collective-permute-start.9 = (bf16[512,512]{1,0:T(8,128)(2,1)S(1)}, bf16[512,512]{1,0:T(8,128)(2,1)S(1)}, u32[]{:S(2)}, u32[]{:S(2)}) collective-permute-start(bf16[512,512]{1,0:T(8,128)(2,1)S(1)} %slice_bitcast_fusion.3), channel_id=1, source_target_pairs={{0,16},{8,24},{16,0},{24,8},{1,17},{9,25},{17,1},{25,9},{2,18},{10... | collective-permute-start | bytes 1572872 | tf_op jit(solution)/shard_map/g0_xy_upper/ppermute | solution.py:363
  43.8 1.6 %collective-permute-start.10 = (bf16[512,512]{1,0:T(8,128)(2,1)S(1)}, bf16[512,512]{1,0:T(8,128)(2,1)S(1)}, u32[]{:S(2)}, u32[]{:S(2)}) collective-permute-start(bf16[512,512]{1,0:T(8,128)(2,1)S(1)} %slice_bitcast_fusion.1), channel_id=1, source_target_pairs={{0,8},{8,0},{16,24},{24,16},{1,9},{9,1},{17,25},{25,17},{2,10},{10... | collective-permute-start | bytes 1572872 | tf_op jit(solution)/shard_map/g0_xy_lower/ppermute | solution.py:363
  45.4 3.8 %spread.1.refs_2_ = bf16[1024,4096]{1,0:T(8,128)(2,1)S(1)} custom-call(s32[6,12]{1,0:T(8,128)S(1)} %bitcast.69, s32[6,12]{1,0:T(8,128)S(1)} %bitcast_add_fusion.col_ref, bf16[1552,128]{1,0:T(8,128)(2,1)S(1)} %pad_maximum_fusion.refs_0_, bf16[1552,128]{1,0:T(8,128)(2,1)S(1)} %collective-permute-done.4.refs_1_, ...), custom_call_target="tpu_custom_call" | custom-call | tf_op jit(solution)/shard_map/spread/pallas_call | solution.py:121
  50.6 4.6 %turn.1.own_ref = f32[2,512,512]{2,1,0:T(8,128)S(1)} custom-call(s32[4]{0:T(128)S(1)} %pad_add_fusion.1.source_ref, bf16[1024,4096]{1,0:T(8,128)(2,1)S(1)} %fill.1.dense_ref, bf16[2,512,512]{2,1,0:T(8,128)(2,1)S(1)} %copy-done, bf16[2,512,512]{2,1,0:T(8,128)(2,1)S(1)} %collective-permute-done.7.refs_0_, bf16[2,512,512]{2,1,0:T(8,128)(2,1)S(1)} %collective-permute-done.2.refs_1_), custom_call_target="tpu_custom_call" | custom-call | tf_op jit(solution)/shard_map/turn/pallas_call | solution.py:189
  57.5 2.3 %turn_rest.1.refs_0_ = bf16[2,512,512]{2,1,0:T(8,128)(2,1)S(1)} custom-call(s32[4]{0:T(128)S(1)} %pad_add_fusion.1.source_ref, bf16[1024,4096]{1,0:T(8,128)(2,1)S(1)} %fill.1.dense_ref, f32[2,512,512]{2,1,0:T(8,128)S(1)} %turn.1.own_ref, bf16[512,512]{1,0:T(8,128)(2,1)S(1)} %collective-permute-done.9.refs_0_, ...), custom_call_target="tpu_custom_call" | custom-call | tf_op jit(solution)/shard_map/turn_rest/pallas_call | solution.py:189
  63.1 1.5 %collective-permute-start.19 = (bf16[512,512]{1,0:T(8,128)(2,1)S(1)}, bf16[512,512]{1,0:T(8,128)(2,1)S(1)}, u32[]{:S(2)}, u32[]{:S(2)}) collective-permute-start(bf16[512,512]{1,0:T(8,128)(2,1)S(1)} %copy-done.1), channel_id=1, source_target_pairs={{0,6},{1,7},{2,4},{3,5},{4,2},{5,3},{6,0},{7,1},{8,14},{9,15},{10,... | collective-permute-start | bytes 1572872 | tf_op jit(solution)/shard_map/g0_far_lower/ppermute | solution.py:366
  64.6 12.1 %collective-permute-done.15.refs_5_.refs_4_ = bf16[2,512,512]{2,1,0:T(8,128)(2,1)S(1)} collective-permute-done((bf16[2,512,512]{2,1,0:T(8,128)(2,1)}, bf16[2,512,512]{2,1,0:T(8,128)(2,1)S(1)}, u32[]{:S(2)}, u32[]{:S(2)}) %collective-permute-start.15) | collective-permute-done | bytes 1048608 | tf_op jit(solution)/shard_map/g0_near/ppermute | solution.py:366
  77.1 10.9 %collective-permute-done.19.refs_8_.refs_7_ = bf16[512,512]{1,0:T(8,128)(2,1)S(1)} collective-permute-done((bf16[512,512]{1,0:T(8,128)(2,1)S(1)}, bf16[512,512]{1,0:T(8,128)(2,1)S(1)}, u32[]{:S(2)}, u32[]{:S(2)}) %collective-permute-start.19) | collective-permute-done | bytes 524320 | tf_op jit(solution)/shard_map/g0_far_lower/ppermute | solution.py:366
  88.0 1.6 %collective-permute-start.22 = (bf16[512,512]{1,0:T(8,128)(2,1)S(1)}, bf16[512,512]{1,0:T(8,128)(2,1)S(1)}, u32[]{:S(2)}, u32[]{:S(2)}) collective-permute-start(bf16[512,512]{1,0:T(8,128)(2,1)S(1)} %slice_bitcast_fusion), channel_id=1, source_target_pairs={{0,8},{8,0},{16,24},{24,16},{1,9},{9,1},{17,25},{25,17},{2,10},{10... | collective-permute-start | bytes 1572872 | tf_op jit(solution)/shard_map/turned_xy_lower/ppermute | solution.py:363
  90.8 1.6 %collective-permute-start.21 = (bf16[512,512]{1,0:T(8,128)(2,1)S(1)}, bf16[512,512]{1,0:T(8,128)(2,1)S(1)}, u32[]{:S(2)}, u32[]{:S(2)}) collective-permute-start(bf16[512,512]{1,0:T(8,128)(2,1)S(1)} %slice_bitcast_fusion.2), channel_id=1, source_target_pairs={{0,16},{8,24},{16,0},{24,8},{1,17},{9,25},{17,1},{25,9},{2,18},{10... | collective-permute-start | bytes 1572872 | tf_op jit(solution)/shard_map/turned_xy_upper/ppermute | solution.py:363
  92.4 4.6 %close.1 = (f32[2,512,512]{2,1,0:T(8,128)S(1)}, bf16[4096,512]{1,0:T(8,128)(2,1)S(1)}) custom-call(s32[4]{0:T(128)S(1)} %pad_add_fusion.1.source_ref, s32[6]{0:T(128)S(1)} %stack.100.owner_ref, s32[3]{0:T(128)S(1)} %compare_convert_fusion.late_ref, bf16[2,512,512]{2,1,0:T(8,128)(2,1)S(1)} %turn_rest.1.refs_0_, ...), custom_call_target="tpu_custom_call" | custom-call | tf_op jit(solution)/shard_map/close/pallas_call | solution.py:248
  97.2 5.3 %collective-permute-done.22.refs_1_ = bf16[512,512]{1,0:T(8,128)(2,1)S(1)} collective-permute-done((bf16[512,512]{1,0:T(8,128)(2,1)S(1)}, bf16[512,512]{1,0:T(8,128)(2,1)S(1)}, u32[]{:S(2)}, u32[]{:S(2)}) %collective-permute-start.22) | collective-permute-done | bytes 524320 | tf_op jit(solution)/shard_map/turned_xy_lower/ppermute | solution.py:363
  102.4 5.7 %collective-permute-done.25.refs_0_ = bf16[512,512]{1,0:T(8,128)(2,1)S(1)} collective-permute-done((bf16[512,512]{1,0:T(8,128)(2,1)S(1)}, bf16[512,512]{1,0:T(8,128)(2,1)S(1)}, u32[]{:S(2)}, u32[]{:S(2)}) %collective-permute-start.25) | collective-permute-done | bytes 524320 | tf_op jit(solution)/shard_map/g0_cross_lower/ppermute | solution.py:366
  108.3 2.5 %close_rest.1 = (f32[2,512,512]{2,1,0:T(8,128)S(1)}, bf16[4096,512]{1,0:T(8,128)(2,1)S(1)}) custom-call(s32[4]{0:T(128)S(1)} %pad_add_fusion.1.source_ref, s32[6]{0:T(128)S(1)} %stack.100.owner_ref, s32[3]{0:T(128)S(1)} %compare_convert_fusion.late_ref, f32[2,512,512]{2,1,0:T(8,128)S(1)} %get-tuple-element.44._, ...), custom_call_target="tpu_custom_call", output_to_operand_aliasing={{0}: (3, {}), {1}: (4, {})} | custom-call | tf_op jit(solution)/shard_map/close_rest/pallas_call | solution.py:288
  110.8 2.0 %last.2.refs_2_ = bf16[1024,512]{1,0:T(8,128)(2,1)} custom-call(s32[2]{0:T(128)S(1)} %get-tuple-element.54.owner_ref, f32[2,512,512]{2,1,0:T(8,128)S(1)} %get-tuple-element.49.total_ref, bf16[4096,512]{1,0:T(8,128)(2,1)S(1)} %get-tuple-element.50.column_ref, bf16[512,512]{1,0:T(8,128)(2,1)S(1)} %collective-permute-done.23.refs_0_, ...), custom_call_target="tpu_custom_call" | custom-call | tf_op jit(solution)/shard_map/last/pallas_call | solution.py:331
  112.8 2.0 %last.3 = bf16[1024,512]{1,0:T(8,128)(2,1)} custom-call(s32[2]{0:T(128)S(1)} %get-tuple-element.54.owner_ref, f32[2,512,512]{2,1,0:T(8,128)S(1)} %get-tuple-element.49.total_ref, bf16[4096,512]{1,0:T(8,128)(2,1)S(1)} %get-tuple-element.50.column_ref, bf16[512,512]{1,0:T(8,128)(2,1)S(1)} %collective-permute-done.25.refs_0_, ...), custom_call_target="tpu_custom_call", output_to_operand_aliasing={{}: (5, {})} | custom-call | tf_op jit(solution)/shard_map/last/pallas_call | solution.py:331
  (71 shorter events, 15.8 us)
Async XLA Ops:
  2.5 11.9 %collective-permute-start.4 = (bf16[1552,128]{1,0:T(8,128)(2,1)S(1)}, bf16[1552,128]{1,0:T(8,128)(2,1)S(1)}, u32[]{:S(2)}, u32[]{:S(2)}) collective-permute-start(bf16[1552,128]{1,0:T(8,128)(2,1)S(1)} %pad_maximum_fusion.refs_0_), channel_id=1, source_target_pairs={{0,1},{1,0},{2,3},{3,2},{4,5},{5,4},{6,7},{7,6},{8,9},{9,8},{10,11... | collective-permute-start | bytes 1191944 | tf_op jit(solution)/shard_map/slots_twin/ppermute | solution.py:371
  3.0 12.4 %collective-permute-start.5 = (bf16[1552,128]{1,0:T(8,128)(2,1)S(1)}, bf16[1552,128]{1,0:T(8,128)(2,1)S(1)}, u32[]{:S(2)}, u32[]{:S(2)}) collective-permute-start(bf16[1552,128]{1,0:T(8,128)(2,1)S(1)} %pad_maximum_fusion.refs_0_), channel_id=1, source_target_pairs={{0,2},{1,3},{2,0},{3,1},{4,6},{5,7},{6,4},{7,5},{8,10},{9,11},{10,... | collective-permute-start | bytes 1191944 | tf_op jit(solution)/shard_map/slots_near/ppermute | solution.py:366
  5.6 20.7 %collective-permute-start = (bf16[1552,128]{1,0:T(8,128)(2,1)S(1)}, bf16[1552,128]{1,0:T(8,128)(2,1)}, u32[]{:S(2)}, u32[]{:S(2)}) collective-permute-start(bf16[1552,128]{1,0:T(8,128)(2,1)S(1)} %pad_maximum_fusion.refs_0_), channel_id=1, source_target_pairs={{0,6},{1,7},{2,4},{3,5},{4,2},{5,3},{6,0},{7,1},{8,14},{9,15},{10,... | collective-permute-start | bytes 1191944 | tf_op jit(solution)/shard_map/slots_far/ppermute | solution.py:366
  11.0 29.3 %collective-permute-start.7 = (bf16[2,512,512]{2,1,0:T(8,128)(2,1)}, bf16[2,512,512]{2,1,0:T(8,128)(2,1)S(1)}, u32[]{:S(2)}, u32[]{:S(2)}) collective-permute-start(bf16[2,512,512]{2,1,0:T(8,128)(2,1)} %get-tuple-element.37.own_ref.refs_3_.refs_2_), channel_id=1, source_target_pairs={{0,8},{8,0},{16,24},{24,16},{1,9},{9,1},{17,25},{25,17},{2,10},{10... | collective-permute-start | bytes 3145736 | tf_op jit(solution)/shard_map/g0_x/ppermute | solution.py:363
  12.6 27.7 %collective-permute-start.2 = (bf16[2,512,512]{2,1,0:T(8,128)(2,1)}, bf16[2,512,512]{2,1,0:T(8,128)(2,1)S(1)}, u32[]{:S(2)}, u32[]{:S(2)}) collective-permute-start(bf16[2,512,512]{2,1,0:T(8,128)(2,1)} %get-tuple-element.37.own_ref.refs_3_.refs_2_), channel_id=1, source_target_pairs={{0,16},{8,24},{16,0},{24,8},{1,17},{9,25},{17,1},{25,9},{2,18},{10... | collective-permute-start | bytes 3145736 | tf_op jit(solution)/shard_map/g0_y/ppermute | solution.py:363
  14.3 46.1 %collective-permute-start.11 = (bf16[2,512,512]{2,1,0:T(8,128)(2,1)}, bf16[2,512,512]{2,1,0:T(8,128)(2,1)S(1)}, u32[]{:S(2)}, u32[]{:S(2)}) collective-permute-start(bf16[2,512,512]{2,1,0:T(8,128)(2,1)} %get-tuple-element.37.own_ref.refs_3_.refs_2_), channel_id=1, source_target_pairs={{0,1},{1,0},{2,3},{3,2},{4,5},{5,4},{6,7},{7,6},{8,9},{9,8},{10,11... | collective-permute-start | bytes 3145736 | tf_op jit(solution)/shard_map/g0_twin/ppermute | solution.py:371
  15.4 11.5 %collective-permute-start.6 = (bf16[1552,128]{1,0:T(8,128)(2,1)S(1)}, bf16[1552,128]{1,0:T(8,128)(2,1)S(1)}, u32[]{:S(2)}, u32[]{:S(2)}) collective-permute-start(bf16[1552,128]{1,0:T(8,128)(2,1)S(1)} %collective-permute-done.5.refs_2_), channel_id=1, source_target_pairs={{0,1},{1,0},{2,3},{3,2},{4,5},{5,4},{6,7},{7,6},{8,9},{9,8},{10,11... | collective-permute-start | bytes 1191944 | tf_op jit(solution)/shard_map/slots_near_twin/ppermute | solution.py:371
  26.4 10.9 %collective-permute-start.1 = (bf16[1552,128]{1,0:T(8,128)(2,1)}, bf16[1552,128]{1,0:T(8,128)(2,1)S(1)}, u32[]{:S(2)}, u32[]{:S(2)}) collective-permute-start(bf16[1552,128]{1,0:T(8,128)(2,1)} %collective-permute-done.refs_4_), channel_id=1, source_target_pairs={{0,2},{1,3},{2,0},{3,1},{4,6},{5,7},{6,4},{7,5},{8,10},{9,11},{10,... | collective-permute-start | bytes 1191944 | tf_op jit(solution)/shard_map/slots_cross/ppermute | solution.py:366
  37.3 23.1 %collective-permute-start.16 = (bf16[512,512]{1,0:T(8,128)(2,1)}, bf16[512,512]{1,0:T(8,128)(2,1)S(1)}, u32[]{:S(2)}, u32[]{:S(2)}) collective-permute-start(bf16[512,512]{1,0:T(8,128)(2,1)} %get-tuple-element.39), channel_id=1, source_target_pairs={{0,6},{1,7},{2,4},{3,5},{4,2},{5,3},{6,0},{7,1},{8,14},{9,15},{10,... | collective-permute-start | bytes 1572872 | tf_op jit(solution)/shard_map/g0_far_upper/ppermute | solution.py:366
  39.6 37.1 %collective-permute-start.15 = (bf16[2,512,512]{2,1,0:T(8,128)(2,1)}, bf16[2,512,512]{2,1,0:T(8,128)(2,1)S(1)}, u32[]{:S(2)}, u32[]{:S(2)}) collective-permute-start(bf16[2,512,512]{2,1,0:T(8,128)(2,1)} %get-tuple-element.37.own_ref.refs_3_.refs_2_), channel_id=1, source_target_pairs={{0,2},{1,3},{2,0},{3,1},{4,6},{5,7},{6,4},{7,5},{8,10},{9,11},{10,... | collective-permute-start | bytes 3145736 | tf_op jit(solution)/shard_map/g0_near/ppermute | solution.py:366
  40.3 3.5 %collective-permute-start.3 = (bf16[1552,128]{1,0:T(8,128)(2,1)S(1)}, bf16[1552,128]{1,0:T(8,128)(2,1)S(1)}, u32[]{:S(2)}, u32[]{:S(2)}) collective-permute-start(bf16[1552,128]{1,0:T(8,128)(2,1)S(1)} %collective-permute-done.1.refs_0_), channel_id=1, source_target_pairs={{0,1},{1,0},{2,3},{3,2},{4,5},{5,4},{6,7},{7,6},{8,9},{9,8},{10,11... | collective-permute-start | bytes 1191944 | tf_op jit(solution)/shard_map/slots_cross_twin/ppermute | solution.py:371
  42.2 14.0 %collective-permute-start.9 = (bf16[512,512]{1,0:T(8,128)(2,1)S(1)}, bf16[512,512]{1,0:T(8,128)(2,1)S(1)}, u32[]{:S(2)}, u32[]{:S(2)}) collective-permute-start(bf16[512,512]{1,0:T(8,128)(2,1)S(1)} %slice_bitcast_fusion.3), channel_id=1, source_target_pairs={{0,16},{8,24},{16,0},{24,8},{1,17},{9,25},{17,1},{25,9},{2,18},{10... | collective-permute-start | bytes 1572872 | tf_op jit(solution)/shard_map/g0_xy_upper/ppermute | solution.py:363
  43.8 13.8 %collective-permute-start.10 = (bf16[512,512]{1,0:T(8,128)(2,1)S(1)}, bf16[512,512]{1,0:T(8,128)(2,1)S(1)}, u32[]{:S(2)}, u32[]{:S(2)}) collective-permute-start(bf16[512,512]{1,0:T(8,128)(2,1)S(1)} %slice_bitcast_fusion.1), channel_id=1, source_target_pairs={{0,8},{8,0},{16,24},{24,16},{1,9},{9,1},{17,25},{25,17},{2,10},{10... | collective-permute-start | bytes 1572872 | tf_op jit(solution)/shard_map/g0_xy_lower/ppermute | solution.py:363
  59.8 28.2 %collective-permute-start.14 = (bf16[2,512,512]{2,1,0:T(8,128)(2,1)S(1)}, bf16[2,512,512]{2,1,0:T(8,128)(2,1)S(1)}, u32[]{:S(2)}, u32[]{:S(2)}) collective-permute-start(bf16[2,512,512]{2,1,0:T(8,128)(2,1)S(1)} %turn_rest.1.refs_0_), channel_id=1, source_target_pairs={{0,16},{8,24},{16,0},{24,8},{1,17},{9,25},{17,1},{25,9},{2,18},{10... | collective-permute-start | bytes 3145736 | tf_op jit(solution)/shard_map/turned_y/ppermute | solution.py:363
  60.4 4.2 %collective-permute-start.17 = (bf16[512,512]{1,0:T(8,128)(2,1)S(1)}, bf16[512,512]{1,0:T(8,128)(2,1)S(1)}, u32[]{:S(2)}, u32[]{:S(2)}) collective-permute-start(bf16[512,512]{1,0:T(8,128)(2,1)S(1)} %collective-permute-done.16.refs_7_.refs_6_), channel_id=1, source_target_pairs={{0,1},{1,0},{2,3},{3,2},{4,5},{5,4},{6,7},{7,6},{8,9},{9,8},{10,11... | collective-permute-start | bytes 1572872 | tf_op jit(solution)/shard_map/g0_far_upper_twin/ppermute | solution.py:371
  61.6 28.0 %collective-permute-start.13 = (bf16[2,512,512]{2,1,0:T(8,128)(2,1)S(1)}, bf16[2,512,512]{2,1,0:T(8,128)(2,1)S(1)}, u32[]{:S(2)}, u32[]{:S(2)}) collective-permute-start(bf16[2,512,512]{2,1,0:T(8,128)(2,1)S(1)} %turn_rest.1.refs_0_), channel_id=1, source_target_pairs={{0,8},{8,0},{16,24},{24,16},{1,9},{9,1},{17,25},{25,17},{2,10},{10... | collective-permute-start | bytes 3145736 | tf_op jit(solution)/shard_map/turned_x/ppermute | solution.py:363
  63.1 24.9 %collective-permute-start.19 = (bf16[512,512]{1,0:T(8,128)(2,1)S(1)}, bf16[512,512]{1,0:T(8,128)(2,1)S(1)}, u32[]{:S(2)}, u32[]{:S(2)}) collective-permute-start(bf16[512,512]{1,0:T(8,128)(2,1)S(1)} %copy-done.1), channel_id=1, source_target_pairs={{0,6},{1,7},{2,4},{3,5},{4,2},{5,3},{6,0},{7,1},{8,14},{9,15},{10,... | collective-permute-start | bytes 1572872 | tf_op jit(solution)/shard_map/g0_far_lower/ppermute | solution.py:366
  76.7 15.7 %collective-permute-start.18 = (bf16[2,512,512]{2,1,0:T(8,128)(2,1)S(1)}, bf16[2,512,512]{2,1,0:T(8,128)(2,1)S(1)}, u32[]{:S(2)}, u32[]{:S(2)}) collective-permute-start(bf16[2,512,512]{2,1,0:T(8,128)(2,1)S(1)} %collective-permute-done.15.refs_5_.refs_4_), channel_id=1, source_target_pairs={{0,1},{1,0},{2,3},{3,2},{4,5},{5,4},{6,7},{7,6},{8,9},{9,8},{10,11... | collective-permute-start | bytes 3145736 | tf_op jit(solution)/shard_map/g0_near_twin/ppermute | solution.py:371
  76.7 20.5 %collective-permute-start.23 = (bf16[512,512]{1,0:T(8,128)(2,1)S(1)}, bf16[512,512]{1,0:T(8,128)(2,1)S(1)}, u32[]{:S(2)}, u32[]{:S(2)}) collective-permute-start(bf16[512,512]{1,0:T(8,128)(2,1)S(1)} %collective-permute-done.16.refs_7_.refs_6_), channel_id=1, source_target_pairs={{0,2},{1,3},{2,0},{3,1},{4,6},{5,7},{6,4},{7,5},{8,10},{9,11},{10,... | collective-permute-start | bytes 1572872 | tf_op jit(solution)/shard_map/g0_cross_upper/ppermute | solution.py:366
  88.0 14.4 %collective-permute-start.22 = (bf16[512,512]{1,0:T(8,128)(2,1)S(1)}, bf16[512,512]{1,0:T(8,128)(2,1)S(1)}, u32[]{:S(2)}, u32[]{:S(2)}) collective-permute-start(bf16[512,512]{1,0:T(8,128)(2,1)S(1)} %slice_bitcast_fusion), channel_id=1, source_target_pairs={{0,8},{8,0},{16,24},{24,16},{1,9},{9,1},{17,25},{25,17},{2,10},{10... | collective-permute-start | bytes 1572872 | tf_op jit(solution)/shard_map/turned_xy_lower/ppermute | solution.py:363
  89.6 18.6 %collective-permute-start.25 = (bf16[512,512]{1,0:T(8,128)(2,1)S(1)}, bf16[512,512]{1,0:T(8,128)(2,1)S(1)}, u32[]{:S(2)}, u32[]{:S(2)}) collective-permute-start(bf16[512,512]{1,0:T(8,128)(2,1)S(1)} %collective-permute-done.19.refs_8_.refs_7_), channel_id=1, source_target_pairs={{0,2},{1,3},{2,0},{3,1},{4,6},{5,7},{6,4},{7,5},{8,10},{9,11},{10,... | collective-permute-start | bytes 1572872 | tf_op jit(solution)/shard_map/g0_cross_lower/ppermute | solution.py:366
  90.8 17.4 %collective-permute-start.21 = (bf16[512,512]{1,0:T(8,128)(2,1)S(1)}, bf16[512,512]{1,0:T(8,128)(2,1)S(1)}, u32[]{:S(2)}, u32[]{:S(2)}) collective-permute-start(bf16[512,512]{1,0:T(8,128)(2,1)S(1)} %slice_bitcast_fusion.2), channel_id=1, source_target_pairs={{0,16},{8,24},{16,0},{24,8},{1,17},{9,25},{17,1},{25,9},{2,18},{10... | collective-permute-start | bytes 1572872 | tf_op jit(solution)/shard_map/turned_xy_upper/ppermute | solution.py:363
  102.4 8.3 %collective-permute-start.24 = (bf16[512,512]{1,0:T(8,128)(2,1)S(1)}, bf16[512,512]{1,0:T(8,128)(2,1)S(1)}, u32[]{:S(2)}, u32[]{:S(2)}) collective-permute-start(bf16[512,512]{1,0:T(8,128)(2,1)S(1)} %collective-permute-done.23.refs_0_), channel_id=1, source_target_pairs={{0,1},{1,0},{2,3},{3,2},{4,5},{5,4},{6,7},{7,6},{8,9},{9,8},{10,11... | collective-permute-start | bytes 1572872 | tf_op jit(solution)/shard_map/g0_cross_upper_twin/ppermute | solution.py:371
  108.2 4.6 %collective-permute-start.26 = (bf16[512,512]{1,0:T(8,128)(2,1)S(1)}, bf16[512,512]{1,0:T(8,128)(2,1)S(1)}, u32[]{:S(2)}, u32[]{:S(2)}) collective-permute-start(bf16[512,512]{1,0:T(8,128)(2,1)S(1)} %collective-permute-done.25.refs_0_), channel_id=1, source_target_pairs={{0,1},{1,0},{2,3},{3,2},{4,5},{5,4},{6,7},{7,6},{8,9},{9,8},{10,11... | collective-permute-start | bytes 1572872 | tf_op jit(solution)/shard_map/g0_cross_lower_twin/ppermute | solution.py:371
  (5 other events, 15.1 us)

commit v11 on v10

--- a/solution.py
+++ b/solution.py
@@ -459,11 +459,11 @@
     with jax.named_scope("g0_y"):
         g_y = grid.shift(tile, "y")
     with jax.named_scope("slots_twin"):
-        s_tw = grid.twin(message)
+        s_tw = grid.twin(after(message, s_far))
     with jax.named_scope("slots_cross"):
         s_cross = grid.along_z(s_far, NEAR)
     with jax.named_scope("slots_near_twin"):
-        s_near_tw = grid.twin(s_near)
+        s_near_tw = grid.twin(after(s_near, s_tw))
     with jax.named_scope("slots_far_twin"):
         s_far_tw = grid.twin(after(s_far, s_near_tw, g_x))
     with jax.named_scope("g0_far_upper"):

time: 115 us -> 114 us (level)
  waiting for transfers between devices: 60.8 us -> 50.2 us
  starting transfers between devices: 24 us -> 33.5 us
    ppermute x8, waiting for transfers between devices: 51.2 us -> 40 us  [along_z(): lax.ppermute(value, 'col', [(z * self.nc + c, to * self.nc + c) for z, to...]
    ppermute x8, starting transfers between devices: 11 us -> 20.8 us  [along_z(): lax.ppermute(value, 'col', [(z * self.nc + c, to * self.nc + c) for z, to...]
  transfers between devices with their start and end apart: 27 -> 27, of which waited for: 12 -> 12; matrix products, arithmetic and copies ran while one was open for 1% -> 2% of each run, Pallas kernels for 21% -> 20%
where the time goes in v11:
time: 114 us
  waiting for transfers between devices  50.2 us (44%)
  starting transfers between devices  33.5 us (29%)
  Pallas kernels  25.2 us (22%)
  other arithmetic  2.2 us (2%)
  local copies, waits for them, and re-layouts  1.64 us (1%)
    ppermute x8, waiting for transfers between devices, along_z(): lax.ppermute(value, 'col', [(z * self.nc + c, to * self.nc + c) for z, to...  40 us
    ppermute x8, starting transfers between devices, along_z(): lax.ppermute(value, 'col', [(z * self.nc + c, to * self.nc + c) for z, to...  20.8 us
    ppermute x8, starting transfers between devices, shift(): return lax.ppermute(value, 'row', pairs)  11.4 us
    ppermute x8, waiting for transfers between devices, shift(): return lax.ppermute(value, 'row', pairs)  7.76 us
    pallas_call x2, Pallas kernels, turn(): pl.pallas_call(functools.partial(turn_kernel, first), out_shape=jax.Shape...  6.83 us
    pallas_call x1, Pallas kernels, close(): pl.pallas_call(functools.partial(close_kernel, n_col), out_shape=(jax.Sha...  4.58 us
    pallas_call x2, Pallas kernels, last(): pl.pallas_call(functools.partial(last_kernel, side, n_row), out_shape=jax...  3.95 us
    pallas_call x1, Pallas kernels, spread(): pl.pallas_call(functools.partial(spread_kernel, len(parts), slots, width)...  2.94 us
  transfers between devices with their start and end apart: 27, of which 12 were waited for; matrix products, arithmetic and copies ran while one was open for 2% of the time, Pallas kernels for 20%

profile of v11, /device:TPU:0, one launch (start us, length us, event | category | flops | bytes accessed | tf_op | source)
XLA Modules:
  0.0 113.7 jit_solution(9086239871922392121)
XLA Ops:
  2.5 5.1 %collective-permute-start = (bf16[1552,128]{1,0:T(8,128)(2,1)S(1)}, bf16[1552,128]{1,0:T(8,128)(2,1)S(1)}, u32[]{:S(2)}, u32[]{:S(2)}) collective-permute-start(bf16[1552,128]{1,0:T(8,128)(2,1)S(1)} %pad_maximum_fusion.refs_0_), channel_id=1, source_target_pairs={{0,6},{1,7},{2,4},{3,5},{4,2},{5,3},{6,0},{7,1},{8,14},{9,15},{10,... | collective-permute-start | bytes 1191944 | tf_op jit(solution)/shard_map/slots_far/ppermute | solution.py:366
  7.6 2.9 %mask.1 = (bf16[2,512,512]{2,1,0:T(8,128)(2,1)}, bf16[512,512]{1,0:T(8,128)(2,1)}, bf16[512,512]{1,0:T(8,128)(2,1)}) custom-call(s32[4,8]{1,0:T(4,128)} %bitcast.73, bf16[1024,512]{1,0:T(8,128)(2,1)} %values_ref), custom_call_target="tpu_custom_call" | custom-call | tf_op jit(solution)/shard_map/mask/pallas_call | solution.py:76
  10.5 1.6 %collective-permute-start.7 = (bf16[2,512,512]{2,1,0:T(8,128)(2,1)}, bf16[2,512,512]{2,1,0:T(8,128)(2,1)S(1)}, u32[]{:S(2)}, u32[]{:S(2)}) collective-permute-start(bf16[2,512,512]{2,1,0:T(8,128)(2,1)} %get-tuple-element.41.own_ref.refs_3_.refs_2_), channel_id=1, source_target_pairs={{0,8},{8,0},{16,24},{24,16},{1,9},{9,1},{17,25},{25,17},{2,10},{10... | collective-permute-start | bytes 3145736 | tf_op jit(solution)/shard_map/g0_x/ppermute | solution.py:363
  13.6 4.1 %collective-permute-done.refs_4_ = bf16[1552,128]{1,0:T(8,128)(2,1)S(1)} collective-permute-done((bf16[1552,128]{1,0:T(8,128)(2,1)S(1)}, bf16[1552,128]{1,0:T(8,128)(2,1)S(1)}, u32[]{:S(2)}, u32[]{:S(2)}) %collective-permute-start) | collective-permute-done | bytes 397344 | tf_op jit(solution)/shard_map/slots_far/ppermute | solution.py:366
  17.7 7.3 %collective-permute-start.1 = (bf16[1552,128]{1,0:T(8,128)(2,1)S(1)}, bf16[1552,128]{1,0:T(8,128)(2,1)}, u32[]{:S(2)}, u32[]{:S(2)}) collective-permute-start(bf16[1552,128]{1,0:T(8,128)(2,1)S(1)} %collective-permute-done.refs_4_), channel_id=1, source_target_pairs={{0,2},{1,3},{2,0},{3,1},{4,6},{5,7},{6,4},{7,5},{8,10},{9,11},{10,... | collective-permute-start | bytes 1191944 | tf_op jit(solution)/shard_map/slots_cross/ppermute | solution.py:366
  25.9 9.1 %collective-permute-done.1.refs_0_ = bf16[1552,128]{1,0:T(8,128)(2,1)} collective-permute-done((bf16[1552,128]{1,0:T(8,128)(2,1)S(1)}, bf16[1552,128]{1,0:T(8,128)(2,1)}, u32[]{:S(2)}, u32[]{:S(2)}) %collective-permute-start.1) | collective-permute-done | bytes 397344 | tf_op jit(solution)/shard_map/slots_cross/ppermute | solution.py:366
  35.0 2.5 %collective-permute-start.16 = (bf16[512,512]{1,0:T(8,128)(2,1)}, bf16[512,512]{1,0:T(8,128)(2,1)S(1)}, u32[]{:S(2)}, u32[]{:S(2)}) collective-permute-start(bf16[512,512]{1,0:T(8,128)(2,1)} %get-tuple-element.43), channel_id=1, source_target_pairs={{0,6},{1,7},{2,4},{3,5},{4,2},{5,3},{6,0},{7,1},{8,14},{9,15},{10,... | collective-permute-start | bytes 1572872 | tf_op jit(solution)/shard_map/g0_far_upper/ppermute | solution.py:366
  39.9 1.6 %collective-permute-start.10 = (bf16[512,512]{1,0:T(8,128)(2,1)S(1)}, bf16[512,512]{1,0:T(8,128)(2,1)S(1)}, u32[]{:S(2)}, u32[]{:S(2)}) collective-permute-start(bf16[512,512]{1,0:T(8,128)(2,1)S(1)} %slice_bitcast_fusion.1), channel_id=1, source_target_pairs={{0,8},{8,0},{16,24},{24,16},{1,9},{9,1},{17,25},{25,17},{2,10},{10... | collective-permute-start | bytes 1572872 | tf_op jit(solution)/shard_map/g0_xy_lower/ppermute | solution.py:363
  45.2 2.9 %spread.1.refs_2_ = bf16[1024,4096]{1,0:T(8,128)(2,1)S(1)} custom-call(s32[6,12]{1,0:T(8,128)S(1)} %bitcast.69, s32[6,12]{1,0:T(8,128)S(1)} %bitcast_add_fusion.col_ref, bf16[1552,128]{1,0:T(8,128)(2,1)S(1)} %pad_maximum_fusion.refs_0_, bf16[1552,128]{1,0:T(8,128)(2,1)} %collective-permute-done.4.refs_1_, ...), custom_call_target="tpu_custom_call" | custom-call | tf_op jit(solution)/shard_map/spread/pallas_call | solution.py:121
  48.1 1.5 %fill.1.dense_ref = bf16[1024,4096]{1,0:T(8,128)(2,1)S(1)} custom-call(s32[2,12]{1,0:T(2,128)S(1)} %bitcast.70, s32[2,12]{1,0:T(2,128)S(1)} %broadcast_add_fusion.col_ref, bf16[1552,128]{1,0:T(8,128)(2,1)} %collective-permute-done.1.refs_0_, bf16[1552,128]{1,0:T(8,128)(2,1)S(1)} %collective-permute-done.3.refs_1_, ...), custom_call_target="tpu_custom_call", output_to_operand_aliasing={{}: (4, {})} | custom-call | tf_op jit(solution)/shard_map/fill/pallas_call | solution.py:140
  49.7 4.5 %turn.1.own_ref = f32[2,512,512]{2,1,0:T(8,128)S(1)} custom-call(s32[4]{0:T(128)S(1)} %pad_add_fusion.1.source_ref, bf16[1024,4096]{1,0:T(8,128)(2,1)S(1)} %fill.1.dense_ref, bf16[2,512,512]{2,1,0:T(8,128)(2,1)S(1)} %copy-done, bf16[2,512,512]{2,1,0:T(8,128)(2,1)S(1)} %collective-permute-done.7.refs_0_, bf16[2,512,512]{2,1,0:T(8,128)(2,1)S(1)} %collective-permute-done.2.refs_1_), custom_call_target="tpu_custom_call" | custom-call | tf_op jit(solution)/shard_map/turn/pallas_call | solution.py:189
  54.2 3.3 %collective-permute-done.9.refs_0_ = bf16[512,512]{1,0:T(8,128)(2,1)S(1)} collective-permute-done((bf16[512,512]{1,0:T(8,128)(2,1)S(1)}, bf16[512,512]{1,0:T(8,128)(2,1)S(1)}, u32[]{:S(2)}, u32[]{:S(2)}) %collective-permute-start.9) | collective-permute-done | bytes 524320 | tf_op jit(solution)/shard_map/g0_xy_upper/ppermute | solution.py:363
  57.5 2.3 %turn_rest.1.refs_0_ = bf16[2,512,512]{2,1,0:T(8,128)(2,1)S(1)} custom-call(s32[4]{0:T(128)S(1)} %pad_add_fusion.1.source_ref, bf16[1024,4096]{1,0:T(8,128)(2,1)S(1)} %fill.1.dense_ref, f32[2,512,512]{2,1,0:T(8,128)S(1)} %turn.1.own_ref, bf16[512,512]{1,0:T(8,128)(2,1)S(1)} %collective-permute-done.9.refs_0_, ...), custom_call_target="tpu_custom_call" | custom-call | tf_op jit(solution)/shard_map/turn_rest/pallas_call | solution.py:189
  59.8 1.6 %collective-permute-start.14 = (bf16[2,512,512]{2,1,0:T(8,128)(2,1)S(1)}, bf16[2,512,512]{2,1,0:T(8,128)(2,1)S(1)}, u32[]{:S(2)}, u32[]{:S(2)}) collective-permute-start(bf16[2,512,512]{2,1,0:T(8,128)(2,1)S(1)} %turn_rest.1.refs_0_), channel_id=1, source_target_pairs={{0,16},{8,24},{16,0},{24,8},{1,17},{9,25},{17,1},{25,9},{2,18},{10... | collective-permute-start | bytes 3145736 | tf_op jit(solution)/shard_map/turned_y/ppermute | solution.py:363
  65.4 9.0 %collective-permute-done.15.refs_5_.refs_4_ = bf16[2,512,512]{2,1,0:T(8,128)(2,1)S(1)} collective-permute-done((bf16[2,512,512]{2,1,0:T(8,128)(2,1)}, bf16[2,512,512]{2,1,0:T(8,128)(2,1)S(1)}, u32[]{:S(2)}, u32[]{:S(2)}) %collective-permute-start.15) | collective-permute-done | bytes 1048608 | tf_op jit(solution)/shard_map/g0_near/ppermute | solution.py:366
  75.0 10.6 %collective-permute-done.19.refs_8_.refs_7_ = bf16[512,512]{1,0:T(8,128)(2,1)S(1)} collective-permute-done((bf16[512,512]{1,0:T(8,128)(2,1)S(1)}, bf16[512,512]{1,0:T(8,128)(2,1)S(1)}, u32[]{:S(2)}, u32[]{:S(2)}) %collective-permute-start.19) | collective-permute-done | bytes 524320 | tf_op jit(solution)/shard_map/g0_far_lower/ppermute | solution.py:366
  85.7 1.6 %collective-permute-start.22 = (bf16[512,512]{1,0:T(8,128)(2,1)S(1)}, bf16[512,512]{1,0:T(8,128)(2,1)S(1)}, u32[]{:S(2)}, u32[]{:S(2)}) collective-permute-start(bf16[512,512]{1,0:T(8,128)(2,1)S(1)} %slice_bitcast_fusion), channel_id=1, source_target_pairs={{0,8},{8,0},{16,24},{24,16},{1,9},{9,1},{17,25},{25,17},{2,10},{10... | collective-permute-start | bytes 1572872 | tf_op jit(solution)/shard_map/turned_xy_lower/ppermute | solution.py:363
  87.8 3.0 %collective-permute-start.25 = (bf16[512,512]{1,0:T(8,128)(2,1)S(1)}, bf16[512,512]{1,0:T(8,128)(2,1)S(1)}, u32[]{:S(2)}, u32[]{:S(2)}) collective-permute-start(bf16[512,512]{1,0:T(8,128)(2,1)S(1)} %collective-permute-done.19.refs_8_.refs_7_), channel_id=1, source_target_pairs={{0,2},{1,3},{2,0},{3,1},{4,6},{5,7},{6,4},{7,5},{8,10},{9,11},{10,... | collective-permute-start | bytes 1572872 | tf_op jit(solution)/shard_map/g0_cross_lower/ppermute | solution.py:366
  91.5 4.6 %close.1 = (f32[2,512,512]{2,1,0:T(8,128)S(1)}, bf16[4096,512]{1,0:T(8,128)(2,1)S(1)}) custom-call(s32[4]{0:T(128)S(1)} %pad_add_fusion.1.source_ref, s32[6]{0:T(128)S(1)} %stack.100.owner_ref, s32[3]{0:T(128)S(1)} %compare_convert_fusion.late_ref, bf16[2,512,512]{2,1,0:T(8,128)(2,1)S(1)} %turn_rest.1.refs_0_, ...), custom_call_target="tpu_custom_call" | custom-call | tf_op jit(solution)/shard_map/close/pallas_call | solution.py:248
  96.1 4.0 %collective-permute-done.22.refs_1_ = bf16[512,512]{1,0:T(8,128)(2,1)S(1)} collective-permute-done((bf16[512,512]{1,0:T(8,128)(2,1)S(1)}, bf16[512,512]{1,0:T(8,128)(2,1)S(1)}, u32[]{:S(2)}, u32[]{:S(2)}) %collective-permute-start.22) | collective-permute-done | bytes 524320 | tf_op jit(solution)/shard_map/turned_xy_lower/ppermute | solution.py:363
  100.1 7.0 %collective-permute-done.25.refs_0_ = bf16[512,512]{1,0:T(8,128)(2,1)S(1)} collective-permute-done((bf16[512,512]{1,0:T(8,128)(2,1)S(1)}, bf16[512,512]{1,0:T(8,128)(2,1)S(1)}, u32[]{:S(2)}, u32[]{:S(2)}) %collective-permute-start.25) | collective-permute-done | bytes 524320 | tf_op jit(solution)/shard_map/g0_cross_lower/ppermute | solution.py:366
  107.2 2.5 %close_rest.1 = (f32[2,512,512]{2,1,0:T(8,128)S(1)}, bf16[4096,512]{1,0:T(8,128)(2,1)S(1)}) custom-call(s32[4]{0:T(128)S(1)} %pad_add_fusion.1.source_ref, s32[6]{0:T(128)S(1)} %stack.100.owner_ref, s32[3]{0:T(128)S(1)} %compare_convert_fusion.late_ref, f32[2,512,512]{2,1,0:T(8,128)S(1)} %get-tuple-element.48._, ...), custom_call_target="tpu_custom_call", output_to_operand_aliasing={{0}: (3, {}), {1}: (4, {})} | custom-call | tf_op jit(solution)/shard_map/close_rest/pallas_call | solution.py:288
  109.7 2.0 %last.2.refs_2_ = bf16[1024,512]{1,0:T(8,128)(2,1)} custom-call(s32[2]{0:T(128)S(1)} %get-tuple-element.58.owner_ref, f32[2,512,512]{2,1,0:T(8,128)S(1)} %get-tuple-element.53.total_ref, bf16[4096,512]{1,0:T(8,128)(2,1)S(1)} %get-tuple-element.54.column_ref, bf16[512,512]{1,0:T(8,128)(2,1)S(1)} %collective-permute-done.23.refs_0_, ...), custom_call_target="tpu_custom_call" | custom-call | tf_op jit(solution)/shard_map/last/pallas_call | solution.py:331
  111.7 2.0 %last.3 = bf16[1024,512]{1,0:T(8,128)(2,1)} custom-call(s32[2]{0:T(128)S(1)} %get-tuple-element.58.owner_ref, f32[2,512,512]{2,1,0:T(8,128)S(1)} %get-tuple-element.53.total_ref, bf16[4096,512]{1,0:T(8,128)(2,1)S(1)} %get-tuple-element.54.column_ref, bf16[512,512]{1,0:T(8,128)(2,1)S(1)} %collective-permute-done.25.refs_0_, ...), custom_call_target="tpu_custom_call", output_to_operand_aliasing={{}: (5, {})} | custom-call | tf_op jit(solution)/shard_map/last/pallas_call | solution.py:331
  (71 shorter events, 16.4 us)
Async XLA Ops:
  2.5 15.2 %collective-permute-start = (bf16[1552,128]{1,0:T(8,128)(2,1)S(1)}, bf16[1552,128]{1,0:T(8,128)(2,1)S(1)}, u32[]{:S(2)}, u32[]{:S(2)}) collective-permute-start(bf16[1552,128]{1,0:T(8,128)(2,1)S(1)} %pad_maximum_fusion.refs_0_), channel_id=1, source_target_pairs={{0,6},{1,7},{2,4},{3,5},{4,2},{5,3},{6,0},{7,1},{8,14},{9,15},{10,... | collective-permute-start | bytes 1191944 | tf_op jit(solution)/shard_map/slots_far/ppermute | solution.py:366
  7.6 17.8 %collective-permute-start.5 = (bf16[1552,128]{1,0:T(8,128)(2,1)S(1)}, bf16[1552,128]{1,0:T(8,128)(2,1)S(1)}, u32[]{:S(2)}, u32[]{:S(2)}) collective-permute-start(bf16[1552,128]{1,0:T(8,128)(2,1)S(1)} %pad_maximum_fusion.refs_0_), channel_id=1, source_target_pairs={{0,2},{1,3},{2,0},{3,1},{4,6},{5,7},{6,4},{7,5},{8,10},{9,11},{10,... | collective-permute-start | bytes 1191944 | tf_op jit(solution)/shard_map/slots_near/ppermute | solution.py:366
  10.5 29.3 %collective-permute-start.7 = (bf16[2,512,512]{2,1,0:T(8,128)(2,1)}, bf16[2,512,512]{2,1,0:T(8,128)(2,1)S(1)}, u32[]{:S(2)}, u32[]{:S(2)}) collective-permute-start(bf16[2,512,512]{2,1,0:T(8,128)(2,1)} %get-tuple-element.41.own_ref.refs_3_.refs_2_), channel_id=1, source_target_pairs={{0,8},{8,0},{16,24},{24,16},{1,9},{9,1},{17,25},{25,17},{2,10},{10... | collective-permute-start | bytes 3145736 | tf_op jit(solution)/shard_map/g0_x/ppermute | solution.py:363
  12.0 26.8 %collective-permute-start.2 = (bf16[2,512,512]{2,1,0:T(8,128)(2,1)}, bf16[2,512,512]{2,1,0:T(8,128)(2,1)S(1)}, u32[]{:S(2)}, u32[]{:S(2)}) collective-permute-start(bf16[2,512,512]{2,1,0:T(8,128)(2,1)} %get-tuple-element.41.own_ref.refs_3_.refs_2_), channel_id=1, source_target_pairs={{0,16},{8,24},{16,0},{24,8},{1,17},{9,25},{17,1},{25,9},{2,18},{10... | collective-permute-start | bytes 3145736 | tf_op jit(solution)/shard_map/g0_y/ppermute | solution.py:363
  17.7 7.7 %collective-permute-start.4 = (bf16[1552,128]{1,0:T(8,128)(2,1)S(1)}, bf16[1552,128]{1,0:T(8,128)(2,1)}, u32[]{:S(2)}, u32[]{:S(2)}) collective-permute-start(bf16[1552,128]{1,0:T(8,128)(2,1)S(1)} %pad_maximum_fusion.refs_0_), channel_id=1, source_target_pairs={{0,1},{1,0},{2,3},{3,2},{4,5},{5,4},{6,7},{7,6},{8,9},{9,8},{10,11... | collective-permute-start | bytes 1191944 | tf_op jit(solution)/shard_map/slots_twin/ppermute | solution.py:371
  17.7 17.3 %collective-permute-start.1 = (bf16[1552,128]{1,0:T(8,128)(2,1)S(1)}, bf16[1552,128]{1,0:T(8,128)(2,1)}, u32[]{:S(2)}, u32[]{:S(2)}) collective-permute-start(bf16[1552,128]{1,0:T(8,128)(2,1)S(1)} %collective-permute-done.refs_4_), channel_id=1, source_target_pairs={{0,2},{1,3},{2,0},{3,1},{4,6},{5,7},{6,4},{7,5},{8,10},{9,11},{10,... | collective-permute-start | bytes 1191944 | tf_op jit(solution)/shard_map/slots_cross/ppermute | solution.py:366
  25.4 36.0 %collective-permute-start.11 = (bf16[2,512,512]{2,1,0:T(8,128)(2,1)}, bf16[2,512,512]{2,1,0:T(8,128)(2,1)S(1)}, u32[]{:S(2)}, u32[]{:S(2)}) collective-permute-start(bf16[2,512,512]{2,1,0:T(8,128)(2,1)} %get-tuple-element.41.own_ref.refs_3_.refs_2_), channel_id=1, source_target_pairs={{0,1},{1,0},{2,3},{3,2},{4,5},{5,4},{6,7},{7,6},{8,9},{9,8},{10,11... | collective-permute-start | bytes 3145736 | tf_op jit(solution)/shard_map/g0_twin/ppermute | solution.py:371
  25.4 14.4 %collective-permute-start.6 = (bf16[1552,128]{1,0:T(8,128)(2,1)S(1)}, bf16[1552,128]{1,0:T(8,128)(2,1)S(1)}, u32[]{:S(2)}, u32[]{:S(2)}) collective-permute-start(bf16[1552,128]{1,0:T(8,128)(2,1)S(1)} %collective-permute-done.5.refs_2_), channel_id=1, source_target_pairs={{0,1},{1,0},{2,3},{3,2},{4,5},{5,4},{6,7},{7,6},{8,9},{9,8},{10,11... | collective-permute-start | bytes 1191944 | tf_op jit(solution)/shard_map/slots_near_twin/ppermute | solution.py:371
  35.0 26.4 %collective-permute-start.16 = (bf16[512,512]{1,0:T(8,128)(2,1)}, bf16[512,512]{1,0:T(8,128)(2,1)S(1)}, u32[]{:S(2)}, u32[]{:S(2)}) collective-permute-start(bf16[512,512]{1,0:T(8,128)(2,1)} %get-tuple-element.43), channel_id=1, source_target_pairs={{0,6},{1,7},{2,4},{3,5},{4,2},{5,3},{6,0},{7,1},{8,14},{9,15},{10,... | collective-permute-start | bytes 1572872 | tf_op jit(solution)/shard_map/g0_far_upper/ppermute | solution.py:366
  38.8 35.5 %collective-permute-start.15 = (bf16[2,512,512]{2,1,0:T(8,128)(2,1)}, bf16[2,512,512]{2,1,0:T(8,128)(2,1)S(1)}, u32[]{:S(2)}, u32[]{:S(2)}) collective-permute-start(bf16[2,512,512]{2,1,0:T(8,128)(2,1)} %get-tuple-element.41.own_ref.refs_3_.refs_2_), channel_id=1, source_target_pairs={{0,2},{1,3},{2,0},{3,1},{4,6},{5,7},{6,4},{7,5},{8,10},{9,11},{10,... | collective-permute-start | bytes 3145736 | tf_op jit(solution)/shard_map/g0_near/ppermute | solution.py:366
  39.9 14.3 %collective-permute-start.10 = (bf16[512,512]{1,0:T(8,128)(2,1)S(1)}, bf16[512,512]{1,0:T(8,128)(2,1)S(1)}, u32[]{:S(2)}, u32[]{:S(2)}) collective-permute-start(bf16[512,512]{1,0:T(8,128)(2,1)S(1)} %slice_bitcast_fusion.1), channel_id=1, source_target_pairs={{0,8},{8,0},{16,24},{24,16},{1,9},{9,1},{17,25},{25,17},{2,10},{10... | collective-permute-start | bytes 1572872 | tf_op jit(solution)/shard_map/g0_xy_lower/ppermute | solution.py:363
  43.5 14.0 %collective-permute-start.9 = (bf16[512,512]{1,0:T(8,128)(2,1)S(1)}, bf16[512,512]{1,0:T(8,128)(2,1)S(1)}, u32[]{:S(2)}, u32[]{:S(2)}) collective-permute-start(bf16[512,512]{1,0:T(8,128)(2,1)S(1)} %slice_bitcast_fusion.3), channel_id=1, source_target_pairs={{0,16},{8,24},{16,0},{24,8},{1,17},{9,25},{17,1},{25,9},{2,18},{10... | collective-permute-start | bytes 1572872 | tf_op jit(solution)/shard_map/g0_xy_upper/ppermute | solution.py:363
  59.8 25.9 %collective-permute-start.14 = (bf16[2,512,512]{2,1,0:T(8,128)(2,1)S(1)}, bf16[2,512,512]{2,1,0:T(8,128)(2,1)S(1)}, u32[]{:S(2)}, u32[]{:S(2)}) collective-permute-start(bf16[2,512,512]{2,1,0:T(8,128)(2,1)S(1)} %turn_rest.1.refs_0_), channel_id=1, source_target_pairs={{0,16},{8,24},{16,0},{24,8},{1,17},{9,25},{17,1},{25,9},{2,18},{10... | collective-permute-start | bytes 3145736 | tf_op jit(solution)/shard_map/turned_y/ppermute | solution.py:363
  61.4 4.0 %collective-permute-start.17 = (bf16[512,512]{1,0:T(8,128)(2,1)S(1)}, bf16[512,512]{1,0:T(8,128)(2,1)S(1)}, u32[]{:S(2)}, u32[]{:S(2)}) collective-permute-start(bf16[512,512]{1,0:T(8,128)(2,1)S(1)} %collective-permute-done.16.refs_7_.refs_6_), channel_id=1, source_target_pairs={{0,1},{1,0},{2,3},{3,2},{4,5},{5,4},{6,7},{7,6},{8,9},{9,8},{10,11... | collective-permute-start | bytes 1572872 | tf_op jit(solution)/shard_map/g0_far_upper_twin/ppermute | solution.py:371
  62.5 25.2 %collective-permute-start.13 = (bf16[2,512,512]{2,1,0:T(8,128)(2,1)S(1)}, bf16[2,512,512]{2,1,0:T(8,128)(2,1)S(1)}, u32[]{:S(2)}, u32[]{:S(2)}) collective-permute-start(bf16[2,512,512]{2,1,0:T(8,128)(2,1)S(1)} %turn_rest.1.refs_0_), channel_id=1, source_target_pairs={{0,8},{8,0},{16,24},{24,16},{1,9},{9,1},{17,25},{25,17},{2,10},{10... | collective-permute-start | bytes 3145736 | tf_op jit(solution)/shard_map/turned_x/ppermute | solution.py:363
  64.0 21.6 %collective-permute-start.19 = (bf16[512,512]{1,0:T(8,128)(2,1)S(1)}, bf16[512,512]{1,0:T(8,128)(2,1)S(1)}, u32[]{:S(2)}, u32[]{:S(2)}) collective-permute-start(bf16[512,512]{1,0:T(8,128)(2,1)S(1)} %copy-done.1), channel_id=1, source_target_pairs={{0,6},{1,7},{2,4},{3,5},{4,2},{5,3},{6,0},{7,1},{8,14},{9,15},{10,... | collective-permute-start | bytes 1572872 | tf_op jit(solution)/shard_map/g0_far_lower/ppermute | solution.py:366
  74.3 17.2 %collective-permute-start.18 = (bf16[2,512,512]{2,1,0:T(8,128)(2,1)S(1)}, bf16[2,512,512]{2,1,0:T(8,128)(2,1)S(1)}, u32[]{:S(2)}, u32[]{:S(2)}) collective-permute-start(bf16[2,512,512]{2,1,0:T(8,128)(2,1)S(1)} %collective-permute-done.15.refs_5_.refs_4_), channel_id=1, source_target_pairs={{0,1},{1,0},{2,3},{3,2},{4,5},{5,4},{6,7},{7,6},{8,9},{9,8},{10,11... | collective-permute-start | bytes 3145736 | tf_op jit(solution)/shard_map/g0_near_twin/ppermute | solution.py:371
  74.3 21.8 %collective-permute-start.23 = (bf16[512,512]{1,0:T(8,128)(2,1)S(1)}, bf16[512,512]{1,0:T(8,128)(2,1)S(1)}, u32[]{:S(2)}, u32[]{:S(2)}) collective-permute-start(bf16[512,512]{1,0:T(8,128)(2,1)S(1)} %collective-permute-done.16.refs_7_.refs_6_), channel_id=1, source_target_pairs={{0,2},{1,3},{2,0},{3,1},{4,6},{5,7},{6,4},{7,5},{8,10},{9,11},{10,... | collective-permute-start | bytes 1572872 | tf_op jit(solution)/shard_map/g0_cross_upper/ppermute | solution.py:366
  85.6 5.3 %collective-permute-start.20 = (bf16[512,512]{1,0:T(8,128)(2,1)S(1)}, bf16[512,512]{1,0:T(8,128)(2,1)S(1)}, u32[]{:S(2)}, u32[]{:S(2)}) collective-permute-start(bf16[512,512]{1,0:T(8,128)(2,1)S(1)} %collective-permute-done.19.refs_8_.refs_7_), channel_id=1, source_target_pairs={{0,1},{1,0},{2,3},{3,2},{4,5},{5,4},{6,7},{7,6},{8,9},{9,8},{10,11... | collective-permute-start | bytes 1572872 | tf_op jit(solution)/shard_map/g0_far_lower_twin/ppermute | solution.py:371
  85.7 14.4 %collective-permute-start.22 = (bf16[512,512]{1,0:T(8,128)(2,1)S(1)}, bf16[512,512]{1,0:T(8,128)(2,1)S(1)}, u32[]{:S(2)}, u32[]{:S(2)}) collective-permute-start(bf16[512,512]{1,0:T(8,128)(2,1)S(1)} %slice_bitcast_fusion), channel_id=1, source_target_pairs={{0,8},{8,0},{16,24},{24,16},{1,9},{9,1},{17,25},{25,17},{2,10},{10... | collective-permute-start | bytes 1572872 | tf_op jit(solution)/shard_map/turned_xy_lower/ppermute | solution.py:363
  87.8 19.4 %collective-permute-start.25 = (bf16[512,512]{1,0:T(8,128)(2,1)S(1)}, bf16[512,512]{1,0:T(8,128)(2,1)S(1)}, u32[]{:S(2)}, u32[]{:S(2)}) collective-permute-start(bf16[512,512]{1,0:T(8,128)(2,1)S(1)} %collective-permute-done.19.refs_8_.refs_7_), channel_id=1, source_target_pairs={{0,2},{1,3},{2,0},{3,1},{4,6},{5,7},{6,4},{7,5},{8,10},{9,11},{10,... | collective-permute-start | bytes 1572872 | tf_op jit(solution)/shard_map/g0_cross_lower/ppermute | solution.py:366
  90.9 16.3 %collective-permute-start.21 = (bf16[512,512]{1,0:T(8,128)(2,1)S(1)}, bf16[512,512]{1,0:T(8,128)(2,1)S(1)}, u32[]{:S(2)}, u32[]{:S(2)}) collective-permute-start(bf16[512,512]{1,0:T(8,128)(2,1)S(1)} %slice_bitcast_fusion.2), channel_id=1, source_target_pairs={{0,16},{8,24},{16,0},{24,8},{1,17},{9,25},{17,1},{25,9},{2,18},{10... | collective-permute-start | bytes 1572872 | tf_op jit(solution)/shard_map/turned_xy_upper/ppermute | solution.py:363
  100.1 9.6 %collective-permute-start.24 = (bf16[512,512]{1,0:T(8,128)(2,1)S(1)}, bf16[512,512]{1,0:T(8,128)(2,1)S(1)}, u32[]{:S(2)}, u32[]{:S(2)}) collective-permute-start(bf16[512,512]{1,0:T(8,128)(2,1)S(1)} %collective-permute-done.23.refs_0_), channel_id=1, source_target_pairs={{0,1},{1,0},{2,3},{3,2},{4,5},{5,4},{6,7},{7,6},{8,9},{9,8},{10,11... | collective-permute-start | bytes 1572872 | tf_op jit(solution)/shard_map/g0_cross_upper_twin/ppermute | solution.py:371
  107.1 4.6 %collective-permute-start.26 = (bf16[512,512]{1,0:T(8,128)(2,1)S(1)}, bf16[512,512]{1,0:T(8,128)(2,1)S(1)}, u32[]{:S(2)}, u32[]{:S(2)}) collective-permute-start(bf16[512,512]{1,0:T(8,128)(2,1)S(1)} %collective-permute-done.25.refs_0_), channel_id=1, source_target_pairs={{0,1},{1,0},{2,3},{3,2},{4,5},{5,4},{6,7},{7,6},{8,9},{9,8},{10,11... | collective-permute-start | bytes 1572872 | tf_op jit(solution)/shard_map/g0_cross_lower_twin/ppermute | solution.py:371
  (5 other events, 16.3 us)

commit v12 on v11

--- a/solution.py
+++ b/solution.py
@@ -208,7 +208,7 @@
 
 def add_blocks(late, late_ref, owner_ref, total_ref, column_ref, row_refs):
     half = row_refs[0].shape[0]
-    tile = min(256, half)
+    tile = min(512, half)
     for block in range(len(row_refs) // 4):
         @pl.when(late_ref[block] == late)
         def _():
@@ -269,14 +269,14 @@
     col_refs, row_refs = refs[:n_col], half_refs([own, *refs[n_col + 1:-5]])
     half = row_refs[0].shape[0]
     fetch = pltpu.make_async_copy(refs[n_col], own, own_sem)
-    fetch.start()
+    pl.when(late_ref[0] == 1)(fetch.start)
     moves = [
         pltpu.make_async_copy(ref, column_ref.at[pl.ds(column_start(source_ref, first + i, half), half)], sem.at[i])
         for i, ref in enumerate(col_refs)
     ]
     for move in moves:
         move.start()
-    fetch.wait()
+    pl.when(late_ref[0] == 1)(fetch.wait)
     for move in moves:
         move.wait()
     add_blocks(1, late_ref, owner_ref, total_ref, column_ref, row_refs)
@@ -305,7 +305,7 @@
 def last_kernel(side, n_row, owner_ref, total_ref, column_ref, *refs):
     row_refs, out_ref, result, sem = refs[:n_row], refs[-3], refs[-2], refs[-1]
     half, _ = row_refs[0].shape
-    tile = min(256, half)
+    tile = min(512, half)
     moves = []
     for t in range(half // tile):
         at = pl.ds(t * tile, tile)
@@ -335,7 +335,7 @@
         out_specs=HBM,
         scratch_shapes=[
             pltpu.VMEM((half, cols), jnp.bfloat16),
-            pltpu.SemaphoreType.DMA((half // min(256, half),)),
+            pltpu.SemaphoreType.DMA((half // min(512, half),)),
         ],
         input_output_aliases=aliases,
         compiler_params=kernel_params(),

time: 114 us -> 114 us (level)
  Pallas kernels: 25.2 us -> 24 us
  transfers between devices with their start and end apart: 27 -> 27, of which waited for: 12 -> 13; matrix products, arithmetic and copies ran while one was open for 2% -> 2% of each run, Pallas kernels for 20% -> 19%
where the time goes in v12:
time: 114 us; the launch traced here: 113 us
  waiting for transfers between devices  51 us (45%)
  starting transfers between devices  33.5 us (29%)
  Pallas kernels  24 us (21%)
  other arithmetic  2.2 us (2%)
  local copies, waits for them, and re-layouts  1.64 us (1%)
    ppermute x8, waiting for transfers between devices, along_z(): lax.ppermute(value, 'col', [(z * self.nc + c, to * self.nc + c) for z, to...  40.8 us
    ppermute x8, starting transfers between devices, along_z(): lax.ppermute(value, 'col', [(z * self.nc + c, to * self.nc + c) for z, to...  20.8 us
    ppermute x8, starting transfers between devices, shift(): return lax.ppermute(value, 'row', pairs)  11.4 us
    ppermute x8, waiting for transfers between devices, shift(): return lax.ppermute(value, 'row', pairs)  7.71 us
    pallas_call x2, Pallas kernels, turn(): pl.pallas_call(functools.partial(turn_kernel, first), out_shape=jax.Shape...  6.82 us
    pallas_call x2, Pallas kernels, last(): pl.pallas_call(functools.partial(last_kernel, side, n_row), out_shape=jax...  4.12 us
    pallas_call x1, Pallas kernels, close(): pl.pallas_call(functools.partial(close_kernel, n_col), out_shape=(jax.Sha...  3.58 us
    pallas_call x1, Pallas kernels, spread(): pl.pallas_call(functools.partial(spread_kernel, len(parts), slots, width)...  3.18 us
  transfers between devices with their start and end apart: 27, of which 13 were waited for; matrix products, arithmetic and copies ran while one was open for 2% of the time, Pallas kernels for 19%

profile of v12, /device:TPU:0, one launch (start us, length us, event | category | flops | bytes accessed | tf_op | source)
XLA Modules:
  0.0 113.3 jit_solution(3976598538209227830)
XLA Ops:
  2.5 5.1 %collective-permute-start = (bf16[1552,128]{1,0:T(8,128)(2,1)S(1)}, bf16[1552,128]{1,0:T(8,128)(2,1)S(1)}, u32[]{:S(2)}, u32[]{:S(2)}) collective-permute-start(bf16[1552,128]{1,0:T(8,128)(2,1)S(1)} %pad_maximum_fusion.refs_0_), channel_id=1, source_target_pairs={{0,6},{1,7},{2,4},{3,5},{4,2},{5,3},{6,0},{7,1},{8,14},{9,15},{10,... | collective-permute-start | bytes 1191944 | tf_op jit(solution)/shard_map/slots_far/ppermute | solution.py:366
  7.6 2.9 %mask.1 = (bf16[2,512,512]{2,1,0:T(8,128)(2,1)}, bf16[512,512]{1,0:T(8,128)(2,1)}, bf16[512,512]{1,0:T(8,128)(2,1)}) custom-call(s32[4,8]{1,0:T(4,128)} %bitcast.73, bf16[1024,512]{1,0:T(8,128)(2,1)} %values_ref), custom_call_target="tpu_custom_call" | custom-call | tf_op jit(solution)/shard_map/mask/pallas_call | solution.py:76
  10.5 1.6 %collective-permute-start.7 = (bf16[2,512,512]{2,1,0:T(8,128)(2,1)}, bf16[2,512,512]{2,1,0:T(8,128)(2,1)S(1)}, u32[]{:S(2)}, u32[]{:S(2)}) collective-permute-start(bf16[2,512,512]{2,1,0:T(8,128)(2,1)} %get-tuple-element.41.own_ref.refs_3_.refs_2_), channel_id=1, source_target_pairs={{0,8},{8,0},{16,24},{24,16},{1,9},{9,1},{17,25},{25,17},{2,10},{10... | collective-permute-start | bytes 3145736 | tf_op jit(solution)/shard_map/g0_x/ppermute | solution.py:363
  13.6 4.1 %collective-permute-done.refs_4_ = bf16[1552,128]{1,0:T(8,128)(2,1)S(1)} collective-permute-done((bf16[1552,128]{1,0:T(8,128)(2,1)S(1)}, bf16[1552,128]{1,0:T(8,128)(2,1)S(1)}, u32[]{:S(2)}, u32[]{:S(2)}) %collective-permute-start) | collective-permute-done | bytes 397344 | tf_op jit(solution)/shard_map/slots_far/ppermute | solution.py:366
  17.7 7.3 %collective-permute-start.1 = (bf16[1552,128]{1,0:T(8,128)(2,1)S(1)}, bf16[1552,128]{1,0:T(8,128)(2,1)}, u32[]{:S(2)}, u32[]{:S(2)}) collective-permute-start(bf16[1552,128]{1,0:T(8,128)(2,1)S(1)} %collective-permute-done.refs_4_), channel_id=1, source_target_pairs={{0,2},{1,3},{2,0},{3,1},{4,6},{5,7},{6,4},{7,5},{8,10},{9,11},{10,... | collective-permute-start | bytes 1191944 | tf_op jit(solution)/shard_map/slots_cross/ppermute | solution.py:366
  25.9 9.1 %collective-permute-done.1.refs_0_ = bf16[1552,128]{1,0:T(8,128)(2,1)} collective-permute-done((bf16[1552,128]{1,0:T(8,128)(2,1)S(1)}, bf16[1552,128]{1,0:T(8,128)(2,1)}, u32[]{:S(2)}, u32[]{:S(2)}) %collective-permute-start.1) | collective-permute-done | bytes 397344 | tf_op jit(solution)/shard_map/slots_cross/ppermute | solution.py:366
  35.0 2.5 %collective-permute-start.16 = (bf16[512,512]{1,0:T(8,128)(2,1)}, bf16[512,512]{1,0:T(8,128)(2,1)S(1)}, u32[]{:S(2)}, u32[]{:S(2)}) collective-permute-start(bf16[512,512]{1,0:T(8,128)(2,1)} %get-tuple-element.43), channel_id=1, source_target_pairs={{0,6},{1,7},{2,4},{3,5},{4,2},{5,3},{6,0},{7,1},{8,14},{9,15},{10,... | collective-permute-start | bytes 1572872 | tf_op jit(solution)/shard_map/g0_far_upper/ppermute | solution.py:366
  39.9 1.6 %collective-permute-start.10 = (bf16[512,512]{1,0:T(8,128)(2,1)S(1)}, bf16[512,512]{1,0:T(8,128)(2,1)S(1)}, u32[]{:S(2)}, u32[]{:S(2)}) collective-permute-start(bf16[512,512]{1,0:T(8,128)(2,1)S(1)} %slice_bitcast_fusion.1), channel_id=1, source_target_pairs={{0,8},{8,0},{16,24},{24,16},{1,9},{9,1},{17,25},{25,17},{2,10},{10... | collective-permute-start | bytes 1572872 | tf_op jit(solution)/shard_map/g0_xy_lower/ppermute | solution.py:363
  45.2 3.2 %spread.1.refs_2_ = bf16[1024,4096]{1,0:T(8,128)(2,1)S(1)} custom-call(s32[6,12]{1,0:T(8,128)S(1)} %bitcast.69, s32[6,12]{1,0:T(8,128)S(1)} %bitcast_add_fusion.col_ref, bf16[1552,128]{1,0:T(8,128)(2,1)S(1)} %pad_maximum_fusion.refs_0_, bf16[1552,128]{1,0:T(8,128)(2,1)} %collective-permute-done.4.refs_1_, ...), custom_call_target="tpu_custom_call" | custom-call | tf_op jit(solution)/shard_map/spread/pallas_call | solution.py:121
  48.4 1.5 %fill.1.dense_ref = bf16[1024,4096]{1,0:T(8,128)(2,1)S(1)} custom-call(s32[2,12]{1,0:T(2,128)S(1)} %bitcast.70, s32[2,12]{1,0:T(2,128)S(1)} %broadcast_add_fusion.col_ref, bf16[1552,128]{1,0:T(8,128)(2,1)} %collective-permute-done.1.refs_0_, bf16[1552,128]{1,0:T(8,128)(2,1)S(1)} %collective-permute-done.3.refs_1_, ...), custom_call_target="tpu_custom_call", output_to_operand_aliasing={{}: (4, {})} | custom-call | tf_op jit(solution)/shard_map/fill/pallas_call | solution.py:140
  49.9 4.5 %turn.1.own_ref = f32[2,512,512]{2,1,0:T(8,128)S(1)} custom-call(s32[4]{0:T(128)S(1)} %pad_add_fusion.1.source_ref, bf16[1024,4096]{1,0:T(8,128)(2,1)S(1)} %fill.1.dense_ref, bf16[2,512,512]{2,1,0:T(8,128)(2,1)S(1)} %copy-done, bf16[2,512,512]{2,1,0:T(8,128)(2,1)S(1)} %collective-permute-done.7.refs_0_, bf16[2,512,512]{2,1,0:T(8,128)(2,1)S(1)} %collective-permute-done.2.refs_1_), custom_call_target="tpu_custom_call" | custom-call | tf_op jit(solution)/shard_map/turn/pallas_call | solution.py:189
  54.5 3.0 %collective-permute-done.9.refs_0_ = bf16[512,512]{1,0:T(8,128)(2,1)S(1)} collective-permute-done((bf16[512,512]{1,0:T(8,128)(2,1)S(1)}, bf16[512,512]{1,0:T(8,128)(2,1)S(1)}, u32[]{:S(2)}, u32[]{:S(2)}) %collective-permute-start.9) | collective-permute-done | bytes 524320 | tf_op jit(solution)/shard_map/g0_xy_upper/ppermute | solution.py:363
  57.5 2.3 %turn_rest.1.refs_0_ = bf16[2,512,512]{2,1,0:T(8,128)(2,1)S(1)} custom-call(s32[4]{0:T(128)S(1)} %pad_add_fusion.1.source_ref, bf16[1024,4096]{1,0:T(8,128)(2,1)S(1)} %fill.1.dense_ref, f32[2,512,512]{2,1,0:T(8,128)S(1)} %turn.1.own_ref, bf16[512,512]{1,0:T(8,128)(2,1)S(1)} %collective-permute-done.9.refs_0_, ...), custom_call_target="tpu_custom_call" | custom-call | tf_op jit(solution)/shard_map/turn_rest/pallas_call | solution.py:189
  59.8 1.6 %collective-permute-start.14 = (bf16[2,512,512]{2,1,0:T(8,128)(2,1)S(1)}, bf16[2,512,512]{2,1,0:T(8,128)(2,1)S(1)}, u32[]{:S(2)}, u32[]{:S(2)}) collective-permute-start(bf16[2,512,512]{2,1,0:T(8,128)(2,1)S(1)} %turn_rest.1.refs_0_), channel_id=1, source_target_pairs={{0,16},{8,24},{16,0},{24,8},{1,17},{9,25},{17,1},{25,9},{2,18},{10... | collective-permute-start | bytes 3145736 | tf_op jit(solution)/shard_map/turned_y/ppermute | solution.py:363
  65.4 9.0 %collective-permute-done.15.refs_5_.refs_4_ = bf16[2,512,512]{2,1,0:T(8,128)(2,1)S(1)} collective-permute-done((bf16[2,512,512]{2,1,0:T(8,128)(2,1)}, bf16[2,512,512]{2,1,0:T(8,128)(2,1)S(1)}, u32[]{:S(2)}, u32[]{:S(2)}) %collective-permute-start.15) | collective-permute-done | bytes 1048608 | tf_op jit(solution)/shard_map/g0_near/ppermute | solution.py:366
  75.0 10.6 %collective-permute-done.19.refs_8_.refs_7_ = bf16[512,512]{1,0:T(8,128)(2,1)S(1)} collective-permute-done((bf16[512,512]{1,0:T(8,128)(2,1)S(1)}, bf16[512,512]{1,0:T(8,128)(2,1)S(1)}, u32[]{:S(2)}, u32[]{:S(2)}) %collective-permute-start.19) | collective-permute-done | bytes 524320 | tf_op jit(solution)/shard_map/g0_far_lower/ppermute | solution.py:366
  85.7 1.6 %collective-permute-start.22 = (bf16[512,512]{1,0:T(8,128)(2,1)S(1)}, bf16[512,512]{1,0:T(8,128)(2,1)S(1)}, u32[]{:S(2)}, u32[]{:S(2)}) collective-permute-start(bf16[512,512]{1,0:T(8,128)(2,1)S(1)} %slice_bitcast_fusion), channel_id=1, source_target_pairs={{0,8},{8,0},{16,24},{24,16},{1,9},{9,1},{17,25},{25,17},{2,10},{10... | collective-permute-start | bytes 1572872 | tf_op jit(solution)/shard_map/turned_xy_lower/ppermute | solution.py:363
  87.8 3.0 %collective-permute-start.25 = (bf16[512,512]{1,0:T(8,128)(2,1)S(1)}, bf16[512,512]{1,0:T(8,128)(2,1)S(1)}, u32[]{:S(2)}, u32[]{:S(2)}) collective-permute-start(bf16[512,512]{1,0:T(8,128)(2,1)S(1)} %collective-permute-done.19.refs_8_.refs_7_), channel_id=1, source_target_pairs={{0,2},{1,3},{2,0},{3,1},{4,6},{5,7},{6,4},{7,5},{8,10},{9,11},{10,... | collective-permute-start | bytes 1572872 | tf_op jit(solution)/shard_map/g0_cross_lower/ppermute | solution.py:366
  91.5 3.6 %close.1 = (f32[2,512,512]{2,1,0:T(8,128)S(1)}, bf16[4096,512]{1,0:T(8,128)(2,1)S(1)}) custom-call(s32[4]{0:T(128)S(1)} %pad_add_fusion.1.source_ref, s32[6]{0:T(128)S(1)} %stack.100.owner_ref, s32[3]{0:T(128)S(1)} %compare_convert_fusion.late_ref, bf16[2,512,512]{2,1,0:T(8,128)(2,1)S(1)} %turn_rest.1.refs_0_, ...), custom_call_target="tpu_custom_call" | custom-call | tf_op jit(solution)/shard_map/close/pallas_call | solution.py:248
  95.9 4.1 %collective-permute-done.22.refs_1_ = bf16[512,512]{1,0:T(8,128)(2,1)S(1)} collective-permute-done((bf16[512,512]{1,0:T(8,128)(2,1)S(1)}, bf16[512,512]{1,0:T(8,128)(2,1)S(1)}, u32[]{:S(2)}, u32[]{:S(2)}) %collective-permute-start.22) | collective-permute-done | bytes 524320 | tf_op jit(solution)/shard_map/turned_xy_lower/ppermute | solution.py:363
  100.1 7.0 %collective-permute-done.25.refs_0_ = bf16[512,512]{1,0:T(8,128)(2,1)S(1)} collective-permute-done((bf16[512,512]{1,0:T(8,128)(2,1)S(1)}, bf16[512,512]{1,0:T(8,128)(2,1)S(1)}, u32[]{:S(2)}, u32[]{:S(2)}) %collective-permute-start.25) | collective-permute-done | bytes 524320 | tf_op jit(solution)/shard_map/g0_cross_lower/ppermute | solution.py:366
  107.2 1.9 %close_rest.1 = (f32[2,512,512]{2,1,0:T(8,128)S(1)}, bf16[4096,512]{1,0:T(8,128)(2,1)S(1)}) custom-call(s32[4]{0:T(128)S(1)} %pad_add_fusion.1.source_ref, s32[6]{0:T(128)S(1)} %stack.100.owner_ref, s32[3]{0:T(128)S(1)} %compare_convert_fusion.late_ref, f32[2,512,512]{2,1,0:T(8,128)S(1)} %get-tuple-element.48._, ...), custom_call_target="tpu_custom_call", output_to_operand_aliasing={{0}: (3, {}), {1}: (4, {})} | custom-call | tf_op jit(solution)/shard_map/close_rest/pallas_call | solution.py:288
  109.2 2.1 %last.2.refs_2_ = bf16[1024,512]{1,0:T(8,128)(2,1)} custom-call(s32[2]{0:T(128)S(1)} %get-tuple-element.58.owner_ref, f32[2,512,512]{2,1,0:T(8,128)S(1)} %get-tuple-element.53.total_ref, bf16[4096,512]{1,0:T(8,128)(2,1)S(1)} %get-tuple-element.54.column_ref, bf16[512,512]{1,0:T(8,128)(2,1)S(1)} %collective-permute-done.23.refs_0_, ...), custom_call_target="tpu_custom_call" | custom-call | tf_op jit(solution)/shard_map/last/pallas_call | solution.py:331
  111.2 2.1 %last.3 = bf16[1024,512]{1,0:T(8,128)(2,1)} custom-call(s32[2]{0:T(128)S(1)} %get-tuple-element.58.owner_ref, f32[2,512,512]{2,1,0:T(8,128)S(1)} %get-tuple-element.53.total_ref, bf16[4096,512]{1,0:T(8,128)(2,1)S(1)} %get-tuple-element.54.column_ref, bf16[512,512]{1,0:T(8,128)(2,1)S(1)} %collective-permute-done.25.refs_0_, ...), custom_call_target="tpu_custom_call", output_to_operand_aliasing={{}: (5, {})} | custom-call | tf_op jit(solution)/shard_map/last/pallas_call | solution.py:331
  (71 shorter events, 17.2 us)
Async XLA Ops:
  2.5 15.2 %collective-permute-start = (bf16[1552,128]{1,0:T(8,128)(2,1)S(1)}, bf16[1552,128]{1,0:T(8,128)(2,1)S(1)}, u32[]{:S(2)}, u32[]{:S(2)}) collective-permute-start(bf16[1552,128]{1,0:T(8,128)(2,1)S(1)} %pad_maximum_fusion.refs_0_), channel_id=1, source_target_pairs={{0,6},{1,7},{2,4},{3,5},{4,2},{5,3},{6,0},{7,1},{8,14},{9,15},{10,... | collective-permute-start | bytes 1191944 | tf_op jit(solution)/shard_map/slots_far/ppermute | solution.py:366
  7.6 17.8 %collective-permute-start.5 = (bf16[1552,128]{1,0:T(8,128)(2,1)S(1)}, bf16[1552,128]{1,0:T(8,128)(2,1)S(1)}, u32[]{:S(2)}, u32[]{:S(2)}) collective-permute-start(bf16[1552,128]{1,0:T(8,128)(2,1)S(1)} %pad_maximum_fusion.refs_0_), channel_id=1, source_target_pairs={{0,2},{1,3},{2,0},{3,1},{4,6},{5,7},{6,4},{7,5},{8,10},{9,11},{10,... | collective-permute-start | bytes 1191944 | tf_op jit(solution)/shard_map/slots_near/ppermute | solution.py:366
  10.5 29.3 %collective-permute-start.7 = (bf16[2,512,512]{2,1,0:T(8,128)(2,1)}, bf16[2,512,512]{2,1,0:T(8,128)(2,1)S(1)}, u32[]{:S(2)}, u32[]{:S(2)}) collective-permute-start(bf16[2,512,512]{2,1,0:T(8,128)(2,1)} %get-tuple-element.41.own_ref.refs_3_.refs_2_), channel_id=1, source_target_pairs={{0,8},{8,0},{16,24},{24,16},{1,9},{9,1},{17,25},{25,17},{2,10},{10... | collective-permute-start | bytes 3145736 | tf_op jit(solution)/shard_map/g0_x/ppermute | solution.py:363
  12.0 26.8 %collective-permute-start.2 = (bf16[2,512,512]{2,1,0:T(8,128)(2,1)}, bf16[2,512,512]{2,1,0:T(8,128)(2,1)S(1)}, u32[]{:S(2)}, u32[]{:S(2)}) collective-permute-start(bf16[2,512,512]{2,1,0:T(8,128)(2,1)} %get-tuple-element.41.own_ref.refs_3_.refs_2_), channel_id=1, source_target_pairs={{0,16},{8,24},{16,0},{24,8},{1,17},{9,25},{17,1},{25,9},{2,18},{10... | collective-permute-start | bytes 3145736 | tf_op jit(solution)/shard_map/g0_y/ppermute | solution.py:363
  17.7 7.7 %collective-permute-start.4 = (bf16[1552,128]{1,0:T(8,128)(2,1)S(1)}, bf16[1552,128]{1,0:T(8,128)(2,1)}, u32[]{:S(2)}, u32[]{:S(2)}) collective-permute-start(bf16[1552,128]{1,0:T(8,128)(2,1)S(1)} %pad_maximum_fusion.refs_0_), channel_id=1, source_target_pairs={{0,1},{1,0},{2,3},{3,2},{4,5},{5,4},{6,7},{7,6},{8,9},{9,8},{10,11... | collective-permute-start | bytes 1191944 | tf_op jit(solution)/shard_map/slots_twin/ppermute | solution.py:371
  17.7 17.3 %collective-permute-start.1 = (bf16[1552,128]{1,0:T(8,128)(2,1)S(1)}, bf16[1552,128]{1,0:T(8,128)(2,1)}, u32[]{:S(2)}, u32[]{:S(2)}) collective-permute-start(bf16[1552,128]{1,0:T(8,128)(2,1)S(1)} %collective-permute-done.refs_4_), channel_id=1, source_target_pairs={{0,2},{1,3},{2,0},{3,1},{4,6},{5,7},{6,4},{7,5},{8,10},{9,11},{10,... | collective-permute-start | bytes 1191944 | tf_op jit(solution)/shard_map/slots_cross/ppermute | solution.py:366
  25.4 36.0 %collective-permute-start.11 = (bf16[2,512,512]{2,1,0:T(8,128)(2,1)}, bf16[2,512,512]{2,1,0:T(8,128)(2,1)S(1)}, u32[]{:S(2)}, u32[]{:S(2)}) collective-permute-start(bf16[2,512,512]{2,1,0:T(8,128)(2,1)} %get-tuple-element.41.own_ref.refs_3_.refs_2_), channel_id=1, source_target_pairs={{0,1},{1,0},{2,3},{3,2},{4,5},{5,4},{6,7},{7,6},{8,9},{9,8},{10,11... | collective-permute-start | bytes 3145736 | tf_op jit(solution)/shard_map/g0_twin/ppermute | solution.py:371
  25.4 14.4 %collective-permute-start.6 = (bf16[1552,128]{1,0:T(8,128)(2,1)S(1)}, bf16[1552,128]{1,0:T(8,128)(2,1)S(1)}, u32[]{:S(2)}, u32[]{:S(2)}) collective-permute-start(bf16[1552,128]{1,0:T(8,128)(2,1)S(1)} %collective-permute-done.5.refs_2_), channel_id=1, source_target_pairs={{0,1},{1,0},{2,3},{3,2},{4,5},{5,4},{6,7},{7,6},{8,9},{9,8},{10,11... | collective-permute-start | bytes 1191944 | tf_op jit(solution)/shard_map/slots_near_twin/ppermute | solution.py:371
  35.0 26.4 %collective-permute-start.16 = (bf16[512,512]{1,0:T(8,128)(2,1)}, bf16[512,512]{1,0:T(8,128)(2,1)S(1)}, u32[]{:S(2)}, u32[]{:S(2)}) collective-permute-start(bf16[512,512]{1,0:T(8,128)(2,1)} %get-tuple-element.43), channel_id=1, source_target_pairs={{0,6},{1,7},{2,4},{3,5},{4,2},{5,3},{6,0},{7,1},{8,14},{9,15},{10,... | collective-permute-start | bytes 1572872 | tf_op jit(solution)/shard_map/g0_far_upper/ppermute | solution.py:366
  38.8 35.5 %collective-permute-start.15 = (bf16[2,512,512]{2,1,0:T(8,128)(2,1)}, bf16[2,512,512]{2,1,0:T(8,128)(2,1)S(1)}, u32[]{:S(2)}, u32[]{:S(2)}) collective-permute-start(bf16[2,512,512]{2,1,0:T(8,128)(2,1)} %get-tuple-element.41.own_ref.refs_3_.refs_2_), channel_id=1, source_target_pairs={{0,2},{1,3},{2,0},{3,1},{4,6},{5,7},{6,4},{7,5},{8,10},{9,11},{10,... | collective-permute-start | bytes 3145736 | tf_op jit(solution)/shard_map/g0_near/ppermute | solution.py:366
  39.9 14.6 %collective-permute-start.10 = (bf16[512,512]{1,0:T(8,128)(2,1)S(1)}, bf16[512,512]{1,0:T(8,128)(2,1)S(1)}, u32[]{:S(2)}, u32[]{:S(2)}) collective-permute-start(bf16[512,512]{1,0:T(8,128)(2,1)S(1)} %slice_bitcast_fusion.1), channel_id=1, source_target_pairs={{0,8},{8,0},{16,24},{24,16},{1,9},{9,1},{17,25},{25,17},{2,10},{10... | collective-permute-start | bytes 1572872 | tf_op jit(solution)/shard_map/g0_xy_lower/ppermute | solution.py:363
  43.5 14.0 %collective-permute-start.9 = (bf16[512,512]{1,0:T(8,128)(2,1)S(1)}, bf16[512,512]{1,0:T(8,128)(2,1)S(1)}, u32[]{:S(2)}, u32[]{:S(2)}) collective-permute-start(bf16[512,512]{1,0:T(8,128)(2,1)S(1)} %slice_bitcast_fusion.3), channel_id=1, source_target_pairs={{0,16},{8,24},{16,0},{24,8},{1,17},{9,25},{17,1},{25,9},{2,18},{10... | collective-permute-start | bytes 1572872 | tf_op jit(solution)/shard_map/g0_xy_upper/ppermute | solution.py:363
  59.8 25.9 %collective-permute-start.14 = (bf16[2,512,512]{2,1,0:T(8,128)(2,1)S(1)}, bf16[2,512,512]{2,1,0:T(8,128)(2,1)S(1)}, u32[]{:S(2)}, u32[]{:S(2)}) collective-permute-start(bf16[2,512,512]{2,1,0:T(8,128)(2,1)S(1)} %turn_rest.1.refs_0_), channel_id=1, source_target_pairs={{0,16},{8,24},{16,0},{24,8},{1,17},{9,25},{17,1},{25,9},{2,18},{10... | collective-permute-start | bytes 3145736 | tf_op jit(solution)/shard_map/turned_y/ppermute | solution.py:363
  61.4 4.0 %collective-permute-start.17 = (bf16[512,512]{1,0:T(8,128)(2,1)S(1)}, bf16[512,512]{1,0:T(8,128)(2,1)S(1)}, u32[]{:S(2)}, u32[]{:S(2)}) collective-permute-start(bf16[512,512]{1,0:T(8,128)(2,1)S(1)} %collective-permute-done.16.refs_7_.refs_6_), channel_id=1, source_target_pairs={{0,1},{1,0},{2,3},{3,2},{4,5},{5,4},{6,7},{7,6},{8,9},{9,8},{10,11... | collective-permute-start | bytes 1572872 | tf_op jit(solution)/shard_map/g0_far_upper_twin/ppermute | solution.py:371
  62.5 25.2 %collective-permute-start.13 = (bf16[2,512,512]{2,1,0:T(8,128)(2,1)S(1)}, bf16[2,512,512]{2,1,0:T(8,128)(2,1)S(1)}, u32[]{:S(2)}, u32[]{:S(2)}) collective-permute-start(bf16[2,512,512]{2,1,0:T(8,128)(2,1)S(1)} %turn_rest.1.refs_0_), channel_id=1, source_target_pairs={{0,8},{8,0},{16,24},{24,16},{1,9},{9,1},{17,25},{25,17},{2,10},{10... | collective-permute-start | bytes 3145736 | tf_op jit(solution)/shard_map/turned_x/ppermute | solution.py:363
  64.0 21.6 %collective-permute-start.19 = (bf16[512,512]{1,0:T(8,128)(2,1)S(1)}, bf16[512,512]{1,0:T(8,128)(2,1)S(1)}, u32[]{:S(2)}, u32[]{:S(2)}) collective-permute-start(bf16[512,512]{1,0:T(8,128)(2,1)S(1)} %copy-done.1), channel_id=1, source_target_pairs={{0,6},{1,7},{2,4},{3,5},{4,2},{5,3},{6,0},{7,1},{8,14},{9,15},{10,... | collective-permute-start | bytes 1572872 | tf_op jit(solution)/shard_map/g0_far_lower/ppermute | solution.py:366
  74.3 17.2 %collective-permute-start.18 = (bf16[2,512,512]{2,1,0:T(8,128)(2,1)S(1)}, bf16[2,512,512]{2,1,0:T(8,128)(2,1)S(1)}, u32[]{:S(2)}, u32[]{:S(2)}) collective-permute-start(bf16[2,512,512]{2,1,0:T(8,128)(2,1)S(1)} %collective-permute-done.15.refs_5_.refs_4_), channel_id=1, source_target_pairs={{0,1},{1,0},{2,3},{3,2},{4,5},{5,4},{6,7},{7,6},{8,9},{9,8},{10,11... | collective-permute-start | bytes 3145736 | tf_op jit(solution)/shard_map/g0_near_twin/ppermute | solution.py:371
  74.3 21.6 %collective-permute-start.23 = (bf16[512,512]{1,0:T(8,128)(2,1)S(1)}, bf16[512,512]{1,0:T(8,128)(2,1)S(1)}, u32[]{:S(2)}, u32[]{:S(2)}) collective-permute-start(bf16[512,512]{1,0:T(8,128)(2,1)S(1)} %collective-permute-done.16.refs_7_.refs_6_), channel_id=1, source_target_pairs={{0,2},{1,3},{2,0},{3,1},{4,6},{5,7},{6,4},{7,5},{8,10},{9,11},{10,... | collective-permute-start | bytes 1572872 | tf_op jit(solution)/shard_map/g0_cross_upper/ppermute | solution.py:366
  85.6 5.3 %collective-permute-start.20 = (bf16[512,512]{1,0:T(8,128)(2,1)S(1)}, bf16[512,512]{1,0:T(8,128)(2,1)S(1)}, u32[]{:S(2)}, u32[]{:S(2)}) collective-permute-start(bf16[512,512]{1,0:T(8,128)(2,1)S(1)} %collective-permute-done.19.refs_8_.refs_7_), channel_id=1, source_target_pairs={{0,1},{1,0},{2,3},{3,2},{4,5},{5,4},{6,7},{7,6},{8,9},{9,8},{10,11... | collective-permute-start | bytes 1572872 | tf_op jit(solution)/shard_map/g0_far_lower_twin/ppermute | solution.py:371
  85.7 14.4 %collective-permute-start.22 = (bf16[512,512]{1,0:T(8,128)(2,1)S(1)}, bf16[512,512]{1,0:T(8,128)(2,1)S(1)}, u32[]{:S(2)}, u32[]{:S(2)}) collective-permute-start(bf16[512,512]{1,0:T(8,128)(2,1)S(1)} %slice_bitcast_fusion), channel_id=1, source_target_pairs={{0,8},{8,0},{16,24},{24,16},{1,9},{9,1},{17,25},{25,17},{2,10},{10... | collective-permute-start | bytes 1572872 | tf_op jit(solution)/shard_map/turned_xy_lower/ppermute | solution.py:363
  87.8 19.4 %collective-permute-start.25 = (bf16[512,512]{1,0:T(8,128)(2,1)S(1)}, bf16[512,512]{1,0:T(8,128)(2,1)S(1)}, u32[]{:S(2)}, u32[]{:S(2)}) collective-permute-start(bf16[512,512]{1,0:T(8,128)(2,1)S(1)} %collective-permute-done.19.refs_8_.refs_7_), channel_id=1, source_target_pairs={{0,2},{1,3},{2,0},{3,1},{4,6},{5,7},{6,4},{7,5},{8,10},{9,11},{10,... | collective-permute-start | bytes 1572872 | tf_op jit(solution)/shard_map/g0_cross_lower/ppermute | solution.py:366
  90.9 16.3 %collective-permute-start.21 = (bf16[512,512]{1,0:T(8,128)(2,1)S(1)}, bf16[512,512]{1,0:T(8,128)(2,1)S(1)}, u32[]{:S(2)}, u32[]{:S(2)}) collective-permute-start(bf16[512,512]{1,0:T(8,128)(2,1)S(1)} %slice_bitcast_fusion.2), channel_id=1, source_target_pairs={{0,16},{8,24},{16,0},{24,8},{1,17},{9,25},{17,1},{25,9},{2,18},{10... | collective-permute-start | bytes 1572872 | tf_op jit(solution)/shard_map/turned_xy_upper/ppermute | solution.py:363
  100.1 9.1 %collective-permute-start.24 = (bf16[512,512]{1,0:T(8,128)(2,1)S(1)}, bf16[512,512]{1,0:T(8,128)(2,1)S(1)}, u32[]{:S(2)}, u32[]{:S(2)}) collective-permute-start(bf16[512,512]{1,0:T(8,128)(2,1)S(1)} %collective-permute-done.23.refs_0_), channel_id=1, source_target_pairs={{0,1},{1,0},{2,3},{3,2},{4,5},{5,4},{6,7},{7,6},{8,9},{9,8},{10,11... | collective-permute-start | bytes 1572872 | tf_op jit(solution)/shard_map/g0_cross_upper_twin/ppermute | solution.py:371
  107.1 4.1 %collective-permute-start.26 = (bf16[512,512]{1,0:T(8,128)(2,1)S(1)}, bf16[512,512]{1,0:T(8,128)(2,1)S(1)}, u32[]{:S(2)}, u32[]{:S(2)}) collective-permute-start(bf16[512,512]{1,0:T(8,128)(2,1)S(1)} %collective-permute-done.25.refs_0_), channel_id=1, source_target_pairs={{0,1},{1,0},{2,3},{3,2},{4,5},{5,4},{6,7},{7,6},{8,9},{9,8},{10,11... | collective-permute-start | bytes 1572872 | tf_op jit(solution)/shard_map/g0_cross_lower_twin/ppermute | solution.py:371
  (5 other events, 16.0 us)

commit v13 on v12

--- a/solution.py
+++ b/solution.py
@@ -171,7 +171,7 @@
     else:
         out_ref, own, parts = refs[-1], own_ref, refs[:-1]
     half, cols = parts[0].shape
-    tile = min(256, half)
+    tile = min(512, half)
     for side in range(2):
         @pl.loop(0, half // tile)
         def _(t):

time: 114 us -> 114 us (level)
  no operation moved by 1% of the time
where the time goes in v13:
time: 114 us; the launch traced here: 113 us
  waiting for transfers between devices  52 us (46%)
  starting transfers between devices  33.5 us (29%)
  Pallas kernels  23 us (20%)
  other arithmetic  2.2 us (2%)
  local copies, waits for them, and re-layouts  1.64 us (1%)
    ppermute x8, waiting for transfers between devices, along_z(): lax.ppermute(value, 'col', [(z * self.nc + c, to * self.nc + c) for z, to...  41.8 us
    ppermute x8, starting transfers between devices, along_z(): lax.ppermute(value, 'col', [(z * self.nc + c, to * self.nc + c) for z, to...  20.8 us
    ppermute x8, starting transfers between devices, shift(): return lax.ppermute(value, 'row', pairs)  11.4 us
    ppermute x8, waiting for transfers between devices, shift(): return lax.ppermute(value, 'row', pairs)  7.75 us
    pallas_call x2, Pallas kernels, turn(): pl.pallas_call(functools.partial(turn_kernel, first), out_shape=jax.Shape...  5.84 us
    pallas_call x2, Pallas kernels, last(): pl.pallas_call(functools.partial(last_kernel, side, n_row), out_shape=jax...  4.12 us
    pallas_call x1, Pallas kernels, close(): pl.pallas_call(functools.partial(close_kernel, n_col), out_shape=(jax.Sha...  3.58 us
    pallas_call x1, Pallas kernels, spread(): pl.pallas_call(functools.partial(spread_kernel, len(parts), slots, width)...  3.14 us
  transfers between devices with their start and end apart: 27, of which 13 were waited for; matrix products, arithmetic and copies ran while one was open for 2% of the time, Pallas kernels for 19%

profile of v13, /device:TPU:0, one launch (start us, length us, event | category | flops | bytes accessed | tf_op | source)
XLA Modules:
  0.0 113.3 jit_solution(11652557100825983986)
XLA Ops:
  2.5 5.1 %collective-permute-start = (bf16[1552,128]{1,0:T(8,128)(2,1)S(1)}, bf16[1552,128]{1,0:T(8,128)(2,1)S(1)}, u32[]{:S(2)}, u32[]{:S(2)}) collective-permute-start(bf16[1552,128]{1,0:T(8,128)(2,1)S(1)} %pad_maximum_fusion.refs_0_), channel_id=1, source_target_pairs={{0,6},{1,7},{2,4},{3,5},{4,2},{5,3},{6,0},{7,1},{8,14},{9,15},{10,... | collective-permute-start | bytes 1191944 | tf_op jit(solution)/shard_map/slots_far/ppermute | solution.py:366
  7.6 2.9 %mask.1 = (bf16[2,512,512]{2,1,0:T(8,128)(2,1)}, bf16[512,512]{1,0:T(8,128)(2,1)}, bf16[512,512]{1,0:T(8,128)(2,1)}) custom-call(s32[4,8]{1,0:T(4,128)} %bitcast.73, bf16[1024,512]{1,0:T(8,128)(2,1)} %values_ref), custom_call_target="tpu_custom_call" | custom-call | tf_op jit(solution)/shard_map/mask/pallas_call | solution.py:76
  10.5 1.6 %collective-permute-start.7 = (bf16[2,512,512]{2,1,0:T(8,128)(2,1)}, bf16[2,512,512]{2,1,0:T(8,128)(2,1)S(1)}, u32[]{:S(2)}, u32[]{:S(2)}) collective-permute-start(bf16[2,512,512]{2,1,0:T(8,128)(2,1)} %get-tuple-element.41.own_ref.refs_3_.refs_2_), channel_id=1, source_target_pairs={{0,8},{8,0},{16,24},{24,16},{1,9},{9,1},{17,25},{25,17},{2,10},{10... | collective-permute-start | bytes 3145736 | tf_op jit(solution)/shard_map/g0_x/ppermute | solution.py:363
  13.6 4.1 %collective-permute-done.refs_4_ = bf16[1552,128]{1,0:T(8,128)(2,1)S(1)} collective-permute-done((bf16[1552,128]{1,0:T(8,128)(2,1)S(1)}, bf16[1552,128]{1,0:T(8,128)(2,1)S(1)}, u32[]{:S(2)}, u32[]{:S(2)}) %collective-permute-start) | collective-permute-done | bytes 397344 | tf_op jit(solution)/shard_map/slots_far/ppermute | solution.py:366
  17.7 7.3 %collective-permute-start.1 = (bf16[1552,128]{1,0:T(8,128)(2,1)S(1)}, bf16[1552,128]{1,0:T(8,128)(2,1)}, u32[]{:S(2)}, u32[]{:S(2)}) collective-permute-start(bf16[1552,128]{1,0:T(8,128)(2,1)S(1)} %collective-permute-done.refs_4_), channel_id=1, source_target_pairs={{0,2},{1,3},{2,0},{3,1},{4,6},{5,7},{6,4},{7,5},{8,10},{9,11},{10,... | collective-permute-start | bytes 1191944 | tf_op jit(solution)/shard_map/slots_cross/ppermute | solution.py:366
  25.9 9.1 %collective-permute-done.1.refs_0_ = bf16[1552,128]{1,0:T(8,128)(2,1)} collective-permute-done((bf16[1552,128]{1,0:T(8,128)(2,1)S(1)}, bf16[1552,128]{1,0:T(8,128)(2,1)}, u32[]{:S(2)}, u32[]{:S(2)}) %collective-permute-start.1) | collective-permute-done | bytes 397344 | tf_op jit(solution)/shard_map/slots_cross/ppermute | solution.py:366
  35.0 2.5 %collective-permute-start.16 = (bf16[512,512]{1,0:T(8,128)(2,1)}, bf16[512,512]{1,0:T(8,128)(2,1)S(1)}, u32[]{:S(2)}, u32[]{:S(2)}) collective-permute-start(bf16[512,512]{1,0:T(8,128)(2,1)} %get-tuple-element.43), channel_id=1, source_target_pairs={{0,6},{1,7},{2,4},{3,5},{4,2},{5,3},{6,0},{7,1},{8,14},{9,15},{10,... | collective-permute-start | bytes 1572872 | tf_op jit(solution)/shard_map/g0_far_upper/ppermute | solution.py:366
  39.9 1.6 %collective-permute-start.10 = (bf16[512,512]{1,0:T(8,128)(2,1)S(1)}, bf16[512,512]{1,0:T(8,128)(2,1)S(1)}, u32[]{:S(2)}, u32[]{:S(2)}) collective-permute-start(bf16[512,512]{1,0:T(8,128)(2,1)S(1)} %slice_bitcast_fusion.1), channel_id=1, source_target_pairs={{0,8},{8,0},{16,24},{24,16},{1,9},{9,1},{17,25},{25,17},{2,10},{10... | collective-permute-start | bytes 1572872 | tf_op jit(solution)/shard_map/g0_xy_lower/ppermute | solution.py:363
  45.2 3.1 %spread.1.refs_2_ = bf16[1024,4096]{1,0:T(8,128)(2,1)S(1)} custom-call(s32[6,12]{1,0:T(8,128)S(1)} %bitcast.69, s32[6,12]{1,0:T(8,128)S(1)} %bitcast_add_fusion.col_ref, bf16[1552,128]{1,0:T(8,128)(2,1)S(1)} %pad_maximum_fusion.refs_0_, bf16[1552,128]{1,0:T(8,128)(2,1)} %collective-permute-done.4.refs_1_, ...), custom_call_target="tpu_custom_call" | custom-call | tf_op jit(solution)/shard_map/spread/pallas_call | solution.py:121
  48.3 1.5 %fill.1.dense_ref = bf16[1024,4096]{1,0:T(8,128)(2,1)S(1)} custom-call(s32[2,12]{1,0:T(2,128)S(1)} %bitcast.70, s32[2,12]{1,0:T(2,128)S(1)} %broadcast_add_fusion.col_ref, bf16[1552,128]{1,0:T(8,128)(2,1)} %collective-permute-done.1.refs_0_, bf16[1552,128]{1,0:T(8,128)(2,1)S(1)} %collective-permute-done.3.refs_1_, ...), custom_call_target="tpu_custom_call", output_to_operand_aliasing={{}: (4, {})} | custom-call | tf_op jit(solution)/shard_map/fill/pallas_call | solution.py:140
  49.9 4.0 %turn.1.own_ref = f32[2,512,512]{2,1,0:T(8,128)S(1)} custom-call(s32[4]{0:T(128)S(1)} %pad_add_fusion.1.source_ref, bf16[1024,4096]{1,0:T(8,128)(2,1)S(1)} %fill.1.dense_ref, bf16[2,512,512]{2,1,0:T(8,128)(2,1)S(1)} %copy-done, bf16[2,512,512]{2,1,0:T(8,128)(2,1)S(1)} %collective-permute-done.7.refs_0_, bf16[2,512,512]{2,1,0:T(8,128)(2,1)S(1)} %collective-permute-done.2.refs_1_), custom_call_target="tpu_custom_call" | custom-call | tf_op jit(solution)/shard_map/turn/pallas_call | solution.py:189
  54.2 3.3 %collective-permute-done.9.refs_0_ = bf16[512,512]{1,0:T(8,128)(2,1)S(1)} collective-permute-done((bf16[512,512]{1,0:T(8,128)(2,1)S(1)}, bf16[512,512]{1,0:T(8,128)(2,1)S(1)}, u32[]{:S(2)}, u32[]{:S(2)}) %collective-permute-start.9) | collective-permute-done | bytes 524320 | tf_op jit(solution)/shard_map/g0_xy_upper/ppermute | solution.py:363
  57.5 1.8 %turn_rest.1.refs_0_ = bf16[2,512,512]{2,1,0:T(8,128)(2,1)S(1)} custom-call(s32[4]{0:T(128)S(1)} %pad_add_fusion.1.source_ref, bf16[1024,4096]{1,0:T(8,128)(2,1)S(1)} %fill.1.dense_ref, f32[2,512,512]{2,1,0:T(8,128)S(1)} %turn.1.own_ref, bf16[512,512]{1,0:T(8,128)(2,1)S(1)} %collective-permute-done.9.refs_0_, ...), custom_call_target="tpu_custom_call" | custom-call | tf_op jit(solution)/shard_map/turn_rest/pallas_call | solution.py:189
  59.3 1.6 %collective-permute-start.14 = (bf16[2,512,512]{2,1,0:T(8,128)(2,1)S(1)}, bf16[2,512,512]{2,1,0:T(8,128)(2,1)S(1)}, u32[]{:S(2)}, u32[]{:S(2)}) collective-permute-start(bf16[2,512,512]{2,1,0:T(8,128)(2,1)S(1)} %turn_rest.1.refs_0_), channel_id=1, source_target_pairs={{0,16},{8,24},{16,0},{24,8},{1,17},{9,25},{17,1},{25,9},{2,18},{10... | collective-permute-start | bytes 3145736 | tf_op jit(solution)/shard_map/turned_y/ppermute | solution.py:363
  64.9 9.5 %collective-permute-done.15.refs_5_.refs_4_ = bf16[2,512,512]{2,1,0:T(8,128)(2,1)S(1)} collective-permute-done((bf16[2,512,512]{2,1,0:T(8,128)(2,1)}, bf16[2,512,512]{2,1,0:T(8,128)(2,1)S(1)}, u32[]{:S(2)}, u32[]{:S(2)}) %collective-permute-start.15) | collective-permute-done | bytes 1048608 | tf_op jit(solution)/shard_map/g0_near/ppermute | solution.py:366
  75.0 10.6 %collective-permute-done.19.refs_8_.refs_7_ = bf16[512,512]{1,0:T(8,128)(2,1)S(1)} collective-permute-done((bf16[512,512]{1,0:T(8,128)(2,1)S(1)}, bf16[512,512]{1,0:T(8,128)(2,1)S(1)}, u32[]{:S(2)}, u32[]{:S(2)}) %collective-permute-start.19) | collective-permute-done | bytes 524320 | tf_op jit(solution)/shard_map/g0_far_lower/ppermute | solution.py:366
  85.7 1.6 %collective-permute-start.22 = (bf16[512,512]{1,0:T(8,128)(2,1)S(1)}, bf16[512,512]{1,0:T(8,128)(2,1)S(1)}, u32[]{:S(2)}, u32[]{:S(2)}) collective-permute-start(bf16[512,512]{1,0:T(8,128)(2,1)S(1)} %slice_bitcast_fusion), channel_id=1, source_target_pairs={{0,8},{8,0},{16,24},{24,16},{1,9},{9,1},{17,25},{25,17},{2,10},{10... | collective-permute-start | bytes 1572872 | tf_op jit(solution)/shard_map/turned_xy_lower/ppermute | solution.py:363
  87.3 3.0 %collective-permute-start.25 = (bf16[512,512]{1,0:T(8,128)(2,1)S(1)}, bf16[512,512]{1,0:T(8,128)(2,1)S(1)}, u32[]{:S(2)}, u32[]{:S(2)}) collective-permute-start(bf16[512,512]{1,0:T(8,128)(2,1)S(1)} %collective-permute-done.19.refs_8_.refs_7_), channel_id=1, source_target_pairs={{0,2},{1,3},{2,0},{3,1},{4,6},{5,7},{6,4},{7,5},{8,10},{9,11},{10,... | collective-permute-start | bytes 1572872 | tf_op jit(solution)/shard_map/g0_cross_lower/ppermute | solution.py:366
  91.0 3.6 %close.1 = (f32[2,512,512]{2,1,0:T(8,128)S(1)}, bf16[4096,512]{1,0:T(8,128)(2,1)S(1)}) custom-call(s32[4]{0:T(128)S(1)} %pad_add_fusion.1.source_ref, s32[6]{0:T(128)S(1)} %stack.100.owner_ref, s32[3]{0:T(128)S(1)} %compare_convert_fusion.late_ref, bf16[2,512,512]{2,1,0:T(8,128)(2,1)S(1)} %turn_rest.1.refs_0_, ...), custom_call_target="tpu_custom_call" | custom-call | tf_op jit(solution)/shard_map/close/pallas_call | solution.py:248
  95.9 4.2 %collective-permute-done.22.refs_1_ = bf16[512,512]{1,0:T(8,128)(2,1)S(1)} collective-permute-done((bf16[512,512]{1,0:T(8,128)(2,1)S(1)}, bf16[512,512]{1,0:T(8,128)(2,1)S(1)}, u32[]{:S(2)}, u32[]{:S(2)}) %collective-permute-start.22) | collective-permute-done | bytes 524320 | tf_op jit(solution)/shard_map/turned_xy_lower/ppermute | solution.py:363
  100.1 7.0 %collective-permute-done.25.refs_0_ = bf16[512,512]{1,0:T(8,128)(2,1)S(1)} collective-permute-done((bf16[512,512]{1,0:T(8,128)(2,1)S(1)}, bf16[512,512]{1,0:T(8,128)(2,1)S(1)}, u32[]{:S(2)}, u32[]{:S(2)}) %collective-permute-start.25) | collective-permute-done | bytes 524320 | tf_op jit(solution)/shard_map/g0_cross_lower/ppermute | solution.py:366
  107.2 1.9 %close_rest.1 = (f32[2,512,512]{2,1,0:T(8,128)S(1)}, bf16[4096,512]{1,0:T(8,128)(2,1)S(1)}) custom-call(s32[4]{0:T(128)S(1)} %pad_add_fusion.1.source_ref, s32[6]{0:T(128)S(1)} %stack.100.owner_ref, s32[3]{0:T(128)S(1)} %compare_convert_fusion.late_ref, f32[2,512,512]{2,1,0:T(8,128)S(1)} %get-tuple-element.48._, ...), custom_call_target="tpu_custom_call", output_to_operand_aliasing={{0}: (3, {}), {1}: (4, {})} | custom-call | tf_op jit(solution)/shard_map/close_rest/pallas_call | solution.py:288
  109.2 2.1 %last.2.refs_2_ = bf16[1024,512]{1,0:T(8,128)(2,1)} custom-call(s32[2]{0:T(128)S(1)} %get-tuple-element.58.owner_ref, f32[2,512,512]{2,1,0:T(8,128)S(1)} %get-tuple-element.53.total_ref, bf16[4096,512]{1,0:T(8,128)(2,1)S(1)} %get-tuple-element.54.column_ref, bf16[512,512]{1,0:T(8,128)(2,1)S(1)} %collective-permute-done.23.refs_0_, ...), custom_call_target="tpu_custom_call" | custom-call | tf_op jit(solution)/shard_map/last/pallas_call | solution.py:331
  111.2 2.1 %last.3 = bf16[1024,512]{1,0:T(8,128)(2,1)} custom-call(s32[2]{0:T(128)S(1)} %get-tuple-element.58.owner_ref, f32[2,512,512]{2,1,0:T(8,128)S(1)} %get-tuple-element.53.total_ref, bf16[4096,512]{1,0:T(8,128)(2,1)S(1)} %get-tuple-element.54.column_ref, bf16[512,512]{1,0:T(8,128)(2,1)S(1)} %collective-permute-done.25.refs_0_, ...), custom_call_target="tpu_custom_call", output_to_operand_aliasing={{}: (5, {})} | custom-call | tf_op jit(solution)/shard_map/last/pallas_call | solution.py:331
  (71 shorter events, 17.5 us)
Async XLA Ops:
  2.5 15.2 %collective-permute-start = (bf16[1552,128]{1,0:T(8,128)(2,1)S(1)}, bf16[1552,128]{1,0:T(8,128)(2,1)S(1)}, u32[]{:S(2)}, u32[]{:S(2)}) collective-permute-start(bf16[1552,128]{1,0:T(8,128)(2,1)S(1)} %pad_maximum_fusion.refs_0_), channel_id=1, source_target_pairs={{0,6},{1,7},{2,4},{3,5},{4,2},{5,3},{6,0},{7,1},{8,14},{9,15},{10,... | collective-permute-start | bytes 1191944 | tf_op jit(solution)/shard_map/slots_far/ppermute | solution.py:366
  7.6 17.8 %collective-permute-start.5 = (bf16[1552,128]{1,0:T(8,128)(2,1)S(1)}, bf16[1552,128]{1,0:T(8,128)(2,1)S(1)}, u32[]{:S(2)}, u32[]{:S(2)}) collective-permute-start(bf16[1552,128]{1,0:T(8,128)(2,1)S(1)} %pad_maximum_fusion.refs_0_), channel_id=1, source_target_pairs={{0,2},{1,3},{2,0},{3,1},{4,6},{5,7},{6,4},{7,5},{8,10},{9,11},{10,... | collective-permute-start | bytes 1191944 | tf_op jit(solution)/shard_map/slots_near/ppermute | solution.py:366
  10.5 29.3 %collective-permute-start.7 = (bf16[2,512,512]{2,1,0:T(8,128)(2,1)}, bf16[2,512,512]{2,1,0:T(8,128)(2,1)S(1)}, u32[]{:S(2)}, u32[]{:S(2)}) collective-permute-start(bf16[2,512,512]{2,1,0:T(8,128)(2,1)} %get-tuple-element.41.own_ref.refs_3_.refs_2_), channel_id=1, source_target_pairs={{0,8},{8,0},{16,24},{24,16},{1,9},{9,1},{17,25},{25,17},{2,10},{10... | collective-permute-start | bytes 3145736 | tf_op jit(solution)/shard_map/g0_x/ppermute | solution.py:363
  12.0 26.8 %collective-permute-start.2 = (bf16[2,512,512]{2,1,0:T(8,128)(2,1)}, bf16[2,512,512]{2,1,0:T(8,128)(2,1)S(1)}, u32[]{:S(2)}, u32[]{:S(2)}) collective-permute-start(bf16[2,512,512]{2,1,0:T(8,128)(2,1)} %get-tuple-element.41.own_ref.refs_3_.refs_2_), channel_id=1, source_target_pairs={{0,16},{8,24},{16,0},{24,8},{1,17},{9,25},{17,1},{25,9},{2,18},{10... | collective-permute-start | bytes 3145736 | tf_op jit(solution)/shard_map/g0_y/ppermute | solution.py:363
  17.7 7.7 %collective-permute-start.4 = (bf16[1552,128]{1,0:T(8,128)(2,1)S(1)}, bf16[1552,128]{1,0:T(8,128)(2,1)}, u32[]{:S(2)}, u32[]{:S(2)}) collective-permute-start(bf16[1552,128]{1,0:T(8,128)(2,1)S(1)} %pad_maximum_fusion.refs_0_), channel_id=1, source_target_pairs={{0,1},{1,0},{2,3},{3,2},{4,5},{5,4},{6,7},{7,6},{8,9},{9,8},{10,11... | collective-permute-start | bytes 1191944 | tf_op jit(solution)/shard_map/slots_twin/ppermute | solution.py:371
  17.7 17.3 %collective-permute-start.1 = (bf16[1552,128]{1,0:T(8,128)(2,1)S(1)}, bf16[1552,128]{1,0:T(8,128)(2,1)}, u32[]{:S(2)}, u32[]{:S(2)}) collective-permute-start(bf16[1552,128]{1,0:T(8,128)(2,1)S(1)} %collective-permute-done.refs_4_), channel_id=1, source_target_pairs={{0,2},{1,3},{2,0},{3,1},{4,6},{5,7},{6,4},{7,5},{8,10},{9,11},{10,... | collective-permute-start | bytes 1191944 | tf_op jit(solution)/shard_map/slots_cross/ppermute | solution.py:366
  25.4 35.5 %collective-permute-start.11 = (bf16[2,512,512]{2,1,0:T(8,128)(2,1)}, bf16[2,512,512]{2,1,0:T(8,128)(2,1)S(1)}, u32[]{:S(2)}, u32[]{:S(2)}) collective-permute-start(bf16[2,512,512]{2,1,0:T(8,128)(2,1)} %get-tuple-element.41.own_ref.refs_3_.refs_2_), channel_id=1, source_target_pairs={{0,1},{1,0},{2,3},{3,2},{4,5},{5,4},{6,7},{7,6},{8,9},{9,8},{10,11... | collective-permute-start | bytes 3145736 | tf_op jit(solution)/shard_map/g0_twin/ppermute | solution.py:371
  25.4 14.4 %collective-permute-start.6 = (bf16[1552,128]{1,0:T(8,128)(2,1)S(1)}, bf16[1552,128]{1,0:T(8,128)(2,1)S(1)}, u32[]{:S(2)}, u32[]{:S(2)}) collective-permute-start(bf16[1552,128]{1,0:T(8,128)(2,1)S(1)} %collective-permute-done.5.refs_2_), channel_id=1, source_target_pairs={{0,1},{1,0},{2,3},{3,2},{4,5},{5,4},{6,7},{7,6},{8,9},{9,8},{10,11... | collective-permute-start | bytes 1191944 | tf_op jit(solution)/shard_map/slots_near_twin/ppermute | solution.py:371
  35.0 25.9 %collective-permute-start.16 = (bf16[512,512]{1,0:T(8,128)(2,1)}, bf16[512,512]{1,0:T(8,128)(2,1)S(1)}, u32[]{:S(2)}, u32[]{:S(2)}) collective-permute-start(bf16[512,512]{1,0:T(8,128)(2,1)} %get-tuple-element.43), channel_id=1, source_target_pairs={{0,6},{1,7},{2,4},{3,5},{4,2},{5,3},{6,0},{7,1},{8,14},{9,15},{10,... | collective-permute-start | bytes 1572872 | tf_op jit(solution)/shard_map/g0_far_upper/ppermute | solution.py:366
  38.8 35.5 %collective-permute-start.15 = (bf16[2,512,512]{2,1,0:T(8,128)(2,1)}, bf16[2,512,512]{2,1,0:T(8,128)(2,1)S(1)}, u32[]{:S(2)}, u32[]{:S(2)}) collective-permute-start(bf16[2,512,512]{2,1,0:T(8,128)(2,1)} %get-tuple-element.41.own_ref.refs_3_.refs_2_), channel_id=1, source_target_pairs={{0,2},{1,3},{2,0},{3,1},{4,6},{5,7},{6,4},{7,5},{8,10},{9,11},{10,... | collective-permute-start | bytes 3145736 | tf_op jit(solution)/shard_map/g0_near/ppermute | solution.py:366
  39.9 14.3 %collective-permute-start.10 = (bf16[512,512]{1,0:T(8,128)(2,1)S(1)}, bf16[512,512]{1,0:T(8,128)(2,1)S(1)}, u32[]{:S(2)}, u32[]{:S(2)}) collective-permute-start(bf16[512,512]{1,0:T(8,128)(2,1)S(1)} %slice_bitcast_fusion.1), channel_id=1, source_target_pairs={{0,8},{8,0},{16,24},{24,16},{1,9},{9,1},{17,25},{25,17},{2,10},{10... | collective-permute-start | bytes 1572872 | tf_op jit(solution)/shard_map/g0_xy_lower/ppermute | solution.py:363
  43.5 14.0 %collective-permute-start.9 = (bf16[512,512]{1,0:T(8,128)(2,1)S(1)}, bf16[512,512]{1,0:T(8,128)(2,1)S(1)}, u32[]{:S(2)}, u32[]{:S(2)}) collective-permute-start(bf16[512,512]{1,0:T(8,128)(2,1)S(1)} %slice_bitcast_fusion.3), channel_id=1, source_target_pairs={{0,16},{8,24},{16,0},{24,8},{1,17},{9,25},{17,1},{25,9},{2,18},{10... | collective-permute-start | bytes 1572872 | tf_op jit(solution)/shard_map/g0_xy_upper/ppermute | solution.py:363
  59.3 26.4 %collective-permute-start.14 = (bf16[2,512,512]{2,1,0:T(8,128)(2,1)S(1)}, bf16[2,512,512]{2,1,0:T(8,128)(2,1)S(1)}, u32[]{:S(2)}, u32[]{:S(2)}) collective-permute-start(bf16[2,512,512]{2,1,0:T(8,128)(2,1)S(1)} %turn_rest.1.refs_0_), channel_id=1, source_target_pairs={{0,16},{8,24},{16,0},{24,8},{1,17},{9,25},{17,1},{25,9},{2,18},{10... | collective-permute-start | bytes 3145736 | tf_op jit(solution)/shard_map/turned_y/ppermute | solution.py:363
  60.9 4.0 %collective-permute-start.17 = (bf16[512,512]{1,0:T(8,128)(2,1)S(1)}, bf16[512,512]{1,0:T(8,128)(2,1)S(1)}, u32[]{:S(2)}, u32[]{:S(2)}) collective-permute-start(bf16[512,512]{1,0:T(8,128)(2,1)S(1)} %collective-permute-done.16.refs_7_.refs_6_), channel_id=1, source_target_pairs={{0,1},{1,0},{2,3},{3,2},{4,5},{5,4},{6,7},{7,6},{8,9},{9,8},{10,11... | collective-permute-start | bytes 1572872 | tf_op jit(solution)/shard_map/g0_far_upper_twin/ppermute | solution.py:371
  62.0 25.2 %collective-permute-start.13 = (bf16[2,512,512]{2,1,0:T(8,128)(2,1)S(1)}, bf16[2,512,512]{2,1,0:T(8,128)(2,1)S(1)}, u32[]{:S(2)}, u32[]{:S(2)}) collective-permute-start(bf16[2,512,512]{2,1,0:T(8,128)(2,1)S(1)} %turn_rest.1.refs_0_), channel_id=1, source_target_pairs={{0,8},{8,0},{16,24},{24,16},{1,9},{9,1},{17,25},{25,17},{2,10},{10... | collective-permute-start | bytes 3145736 | tf_op jit(solution)/shard_map/turned_x/ppermute | solution.py:363
  63.5 22.1 %collective-permute-start.19 = (bf16[512,512]{1,0:T(8,128)(2,1)S(1)}, bf16[512,512]{1,0:T(8,128)(2,1)S(1)}, u32[]{:S(2)}, u32[]{:S(2)}) collective-permute-start(bf16[512,512]{1,0:T(8,128)(2,1)S(1)} %copy-done.1), channel_id=1, source_target_pairs={{0,6},{1,7},{2,4},{3,5},{4,2},{5,3},{6,0},{7,1},{8,14},{9,15},{10,... | collective-permute-start | bytes 1572872 | tf_op jit(solution)/shard_map/g0_far_lower/ppermute | solution.py:366
  74.3 16.7 %collective-permute-start.18 = (bf16[2,512,512]{2,1,0:T(8,128)(2,1)S(1)}, bf16[2,512,512]{2,1,0:T(8,128)(2,1)S(1)}, u32[]{:S(2)}, u32[]{:S(2)}) collective-permute-start(bf16[2,512,512]{2,1,0:T(8,128)(2,1)S(1)} %collective-permute-done.15.refs_5_.refs_4_), channel_id=1, source_target_pairs={{0,1},{1,0},{2,3},{3,2},{4,5},{5,4},{6,7},{7,6},{8,9},{9,8},{10,11... | collective-permute-start | bytes 3145736 | tf_op jit(solution)/shard_map/g0_near_twin/ppermute | solution.py:371
  74.3 21.6 %collective-permute-start.23 = (bf16[512,512]{1,0:T(8,128)(2,1)S(1)}, bf16[512,512]{1,0:T(8,128)(2,1)S(1)}, u32[]{:S(2)}, u32[]{:S(2)}) collective-permute-start(bf16[512,512]{1,0:T(8,128)(2,1)S(1)} %collective-permute-done.16.refs_7_.refs_6_), channel_id=1, source_target_pairs={{0,2},{1,3},{2,0},{3,1},{4,6},{5,7},{6,4},{7,5},{8,10},{9,11},{10,... | collective-permute-start | bytes 1572872 | tf_op jit(solution)/shard_map/g0_cross_upper/ppermute | solution.py:366
  85.6 4.8 %collective-permute-start.20 = (bf16[512,512]{1,0:T(8,128)(2,1)S(1)}, bf16[512,512]{1,0:T(8,128)(2,1)S(1)}, u32[]{:S(2)}, u32[]{:S(2)}) collective-permute-start(bf16[512,512]{1,0:T(8,128)(2,1)S(1)} %collective-permute-done.19.refs_8_.refs_7_), channel_id=1, source_target_pairs={{0,1},{1,0},{2,3},{3,2},{4,5},{5,4},{6,7},{7,6},{8,9},{9,8},{10,11... | collective-permute-start | bytes 1572872 | tf_op jit(solution)/shard_map/g0_far_lower_twin/ppermute | solution.py:371
  85.7 14.4 %collective-permute-start.22 = (bf16[512,512]{1,0:T(8,128)(2,1)S(1)}, bf16[512,512]{1,0:T(8,128)(2,1)S(1)}, u32[]{:S(2)}, u32[]{:S(2)}) collective-permute-start(bf16[512,512]{1,0:T(8,128)(2,1)S(1)} %slice_bitcast_fusion), channel_id=1, source_target_pairs={{0,8},{8,0},{16,24},{24,16},{1,9},{9,1},{17,25},{25,17},{2,10},{10... | collective-permute-start | bytes 1572872 | tf_op jit(solution)/shard_map/turned_xy_lower/ppermute | solution.py:363
  87.3 19.9 %collective-permute-start.25 = (bf16[512,512]{1,0:T(8,128)(2,1)S(1)}, bf16[512,512]{1,0:T(8,128)(2,1)S(1)}, u32[]{:S(2)}, u32[]{:S(2)}) collective-permute-start(bf16[512,512]{1,0:T(8,128)(2,1)S(1)} %collective-permute-done.19.refs_8_.refs_7_), channel_id=1, source_target_pairs={{0,2},{1,3},{2,0},{3,1},{4,6},{5,7},{6,4},{7,5},{8,10},{9,11},{10,... | collective-permute-start | bytes 1572872 | tf_op jit(solution)/shard_map/g0_cross_lower/ppermute | solution.py:366
  90.4 16.8 %collective-permute-start.21 = (bf16[512,512]{1,0:T(8,128)(2,1)S(1)}, bf16[512,512]{1,0:T(8,128)(2,1)S(1)}, u32[]{:S(2)}, u32[]{:S(2)}) collective-permute-start(bf16[512,512]{1,0:T(8,128)(2,1)S(1)} %slice_bitcast_fusion.2), channel_id=1, source_target_pairs={{0,16},{8,24},{16,0},{24,8},{1,17},{9,25},{17,1},{25,9},{2,18},{10... | collective-permute-start | bytes 1572872 | tf_op jit(solution)/shard_map/turned_xy_upper/ppermute | solution.py:363
  100.1 9.1 %collective-permute-start.24 = (bf16[512,512]{1,0:T(8,128)(2,1)S(1)}, bf16[512,512]{1,0:T(8,128)(2,1)S(1)}, u32[]{:S(2)}, u32[]{:S(2)}) collective-permute-start(bf16[512,512]{1,0:T(8,128)(2,1)S(1)} %collective-permute-done.23.refs_0_), channel_id=1, source_target_pairs={{0,1},{1,0},{2,3},{3,2},{4,5},{5,4},{6,7},{7,6},{8,9},{9,8},{10,11... | collective-permute-start | bytes 1572872 | tf_op jit(solution)/shard_map/g0_cross_upper_twin/ppermute | solution.py:371
  107.1 4.1 %collective-permute-start.26 = (bf16[512,512]{1,0:T(8,128)(2,1)S(1)}, bf16[512,512]{1,0:T(8,128)(2,1)S(1)}, u32[]{:S(2)}, u32[]{:S(2)}) collective-permute-start(bf16[512,512]{1,0:T(8,128)(2,1)S(1)} %collective-permute-done.25.refs_0_), channel_id=1, source_target_pairs={{0,1},{1,0},{2,3},{3,2},{4,5},{5,4},{6,7},{7,6},{8,9},{9,8},{10,11... | collective-permute-start | bytes 1572872 | tf_op jit(solution)/shard_map/g0_cross_lower_twin/ppermute | solution.py:371
  (5 other events, 16.1 us)
